TPU v7x, 32 devices: a whole 2x2x4 slice. The times are simulated.
32 devices in a mesh: lat: 4 (over z), lon: 8 (over y, x, core).
Axes of the slice: x: 2, y: 2, z: 4, core: 2. Of those that a mesh axis runs over, the one named last changes fastest.
Arguments:
- sensitivity: bfloat16 [4, 8, 60, 256, 128], P('lat', 'lon'), may hold values from 0 to 0.07470703
- block_ids: int32 [4, 8, 60], P('lat', 'lon'), may hold values from 0 to 32767, as said below
- block_offsets: int32 [4, 8, 4], P('lat', 'lon'), may hold values from 0 to 60, as said below
- ray_counts: int32 [4, 8], P('lat', 'lon'), may hold values from 1 to 768, as said below
- ray_vector: float32 [4, 4, 8, 768], P(None, 'lat', 'lon'), may hold values from -6 to 6
- damping_vector: float32 [4, 128, 256, 128], P(None, 'lat', 'lon'), may hold values from -6 to 6
- model_vector: float32 [4, 128, 256, 128], P(None, 'lat', 'lon'), may hold values from -6 to 6
- solution: float32 [4, 128, 256, 128], P(None, 'lat', 'lon'), may hold values from -6 to 6
- search: float32 [4, 128, 256, 128], P(None, 'lat', 'lon'), may hold values from -6 to 6
- recurrence: float32 [3, 4], replicated, may hold values from 0.5 to 1.5
Outputs:
- ray_out: float32 [4, 4, 8, 768], P(None, 'lat', 'lon')
- damp_out: float32 [4, 128, 256, 128], P(None, 'lat', 'lon')
- model_out: float32 [4, 128, 256, 128], P(None, 'lat', 'lon')
- solution_out: float32 [4, 128, 256, 128], P(None, 'lat', 'lon')
- search_out: float32 [4, 128, 256, 128], P(None, 'lat', 'lon')
- recurrence_out: float32 [3, 4], replicated
Inputs may be any that keep to these rules, and one draw needn't show every extreme that they name: `block_ids`: of the 60 entries of one device at most 4 name blocks of one owner device; some owner is named exactly 4 times by every device. Entries of tiles that belong to no ray block name blocks too. The entries of all devices that name one owner's blocks lie in one patch of 4 x 4 neighbouring columns of that owner. `block_offsets`: each device's offsets start at 0 and never fall; a ray block holding some live ray has 10 to 20 tiles, the others none; some device uses all 60 tiles. A device's live rays are its first ray_counts rays; some device has all 768 live.
All inputs are finite; a program needn't handle non-finite values.
Results may differ from a plain program's by a relative error of at most 0.0003.
Values may be sent and summed in bfloat16 or wider, within the bound.
No kernel may reach another device: no remote copies, remote signals or barrier semaphores. Data moves between devices by JAX's collectives and lax.ppermute only.
A program may use at most 64 MiB of HBM per device.

v0:
```python
import jax
import jax.numpy as jnp
from jax import lax
from jax.sharding import PartitionSpec as P

DAMP_WEIGHT = 0.15
EPSILON = 1e-05
HIGHEST_PRECISION = lax.Precision.HIGHEST


def with_halo(cells, sides, width):
    for axis, dim in sides:
        count = lax.axis_size(axis)
        ends = count - 1
        head = lax.slice_in_dim(cells, 0, width, axis=dim)
        tail = lax.slice_in_dim(cells, cells.shape[dim] - width, cells.shape[dim], axis=dim)
        cells = jnp.concatenate(
            [
                lax.ppermute(tail, axis, [(i, (i + 1) % count) for i in range(ends)]),
                cells,
                lax.ppermute(head, axis, [((i + 1) % count, i) for i in range(ends)]),
            ],
            axis=dim,
        )
    return cells


def laplace(field):
    padded = with_halo(field, (("lat", 1), ("lon", 2)), 1)
    depth_pad = jnp.pad(field, ((0, 0), (0, 0), (0, 0), (1, 1)))
    beside_all = (
        padded[:, 2:, 1:-1] + padded[:, :-2, 1:-1] + padded[:, 1:-1, 2:] + padded[:, 1:-1, :-2]
    )
    beside_all = beside_all + depth_pad[..., 2:] + depth_pad[..., :-2]
    return 6.0 * field - beside_all


def membership(limits, tiles):
    position = jnp.arange(tiles, dtype=jnp.int32)[:, None]
    inside = (position >= limits[None, :-1]) & (position < limits[None, 1:])
    return inside.astype(jnp.float32)


def per_device(
    sensitivity,
    block_ids,
    block_offsets,
    ray_counts,
    ray_vector,
    damping_vector,
    model_vector,
    solution,
    search,
    recurrence,
):
    lat_size = lax.axis_size("lat")
    lon_size = lax.axis_size("lon")
    devices = lat_size * lon_size
    kernel = sensitivity[0, 0]
    tiles, ray_width, depth = kernel.shape
    block_list = block_ids[0, 0]
    bounds = block_offsets[0, 0]
    count_here = ray_counts[0, 0]
    blocks_dev = bounds.shape[0] - 1
    systems, clat_dev, clon_dev = (
        model_vector.shape[0],
        model_vector.shape[1],
        model_vector.shape[2],
    )
    columns_dev = clat_dev * clon_dev
    capacity = 2 * ((tiles + devices - 1) // devices)
    cells_all = devices * columns_dev * depth
    rows_all = devices * blocks_dev * ray_width + cells_all
    alpha_old = recurrence[0]
    rho_bar = recurrence[1]
    phi_bar = recurrence[2]
    owner_dev = block_list // columns_dev
    column = block_list - owner_dev * columns_dev
    owner_hits = (owner_dev[:, None] == jnp.arange(devices, dtype=jnp.int32)[None, :]).astype(
        jnp.int32
    )
    slot_rank = jnp.sum(owner_hits * (jnp.cumsum(owner_hits, axis=0) - 1), axis=1)
    slot_index = owner_dev * capacity + slot_rank
    request = jnp.zeros((devices * capacity,), jnp.int32).at[slot_index].set(column + 1)
    wanted = lax.all_to_all(request, ("lat", "lon"), split_axis=0, concat_axis=0, tiled=True)
    table = (
        model_vector.transpose(1, 2, 0, 3).reshape(columns_dev, systems, depth).astype(jnp.bfloat16)
    )
    served = jnp.where(
        (wanted > 0)[:, None, None],
        jnp.take(table, jnp.maximum(wanted - 1, 0), axis=0),
        jnp.zeros((), jnp.bfloat16),
    )
    fetched = lax.all_to_all(served, ("lat", "lon"), split_axis=0, concat_axis=0, tiled=True)
    tile_model = jnp.take(fetched, slot_index, axis=0)
    member = membership(bounds, tiles)
    products = jnp.einsum("tid,trd->tri", kernel, tile_model, preferred_element_type=jnp.float32)
    traced = jnp.einsum("tb,tri->rbi", member, products, precision=HIGHEST_PRECISION)
    ray_old = ray_vector.reshape(systems, blocks_dev, ray_width)
    ray_index = jnp.arange(blocks_dev * ray_width, dtype=jnp.int32).reshape(blocks_dev, ray_width)
    live_rows = ray_index < count_here
    ray_bar = jnp.where(live_rows[None], traced - alpha_old[:, None, None] * ray_old, 0.0)
    damp_bar = DAMP_WEIGHT * laplace(model_vector) - alpha_old[:, None, None, None] * damping_vector
    residual_sq = jnp.sum(ray_bar * ray_bar, axis=(1, 2)) + jnp.sum(
        damp_bar * damp_bar, axis=(1, 2, 3)
    )
    ray_low = ray_bar.astype(jnp.bfloat16)
    spread = jnp.einsum(
        "tb,rbi->tri", member.astype(jnp.bfloat16), ray_low, preferred_element_type=jnp.float32
    ).astype(jnp.bfloat16)
    sent_terms = jnp.einsum("tid,tri->trd", kernel, spread, preferred_element_type=jnp.float32)
    outgoing = (
        jnp.zeros((devices * capacity, systems, depth), jnp.float32).at[slot_index].set(sent_terms)
    )
    incoming = lax.all_to_all(outgoing, ("lat", "lon"), split_axis=0, concat_axis=0, tiled=True)
    collected = jnp.zeros((columns_dev + 1, systems, depth), jnp.float32).at[wanted].add(incoming)
    remote_part = collected[1:].reshape(clat_dev, clon_dev, systems, depth).transpose(2, 0, 1, 3)
    adjoint_image = remote_part + DAMP_WEIGHT * laplace(damp_bar)
    image_sq = jnp.sum(adjoint_image * adjoint_image, axis=(1, 2, 3))
    cross_sum = jnp.sum(adjoint_image * model_vector, axis=(1, 2, 3))
    model_sq = jnp.sum(model_vector * model_vector, axis=(1, 2, 3))
    residual_sq, image_sq, cross_sum, model_sq = lax.psum(
        (residual_sq, image_sq, cross_sum, model_sq), ("lat", "lon")
    )
    beta_new = jnp.sqrt(residual_sq / rows_all + EPSILON)
    beta_wide = beta_new[:, None, None, None]
    update = adjoint_image / beta_wide - beta_wide * model_vector
    update_sq = image_sq / (beta_new * beta_new) - 2.0 * cross_sum + beta_new * beta_new * model_sq
    alpha_new = jnp.sqrt(update_sq / cells_all + EPSILON)
    model_out = update / alpha_new[:, None, None, None]
    rho_new = jnp.sqrt(rho_bar * rho_bar + beta_new * beta_new)
    cosine = rho_bar / rho_new
    sine_new = beta_new / rho_new
    solution_out = solution + (cosine * phi_bar / rho_new)[:, None, None, None] * search
    search_out = model_out - (sine_new * alpha_new / rho_new)[:, None, None, None] * search
    ray_out = (ray_bar / beta_new[:, None, None]).reshape(systems, 1, 1, blocks_dev * ray_width)
    damp_out = damp_bar / beta_wide
    recurrence_out = jnp.stack([alpha_new, -cosine * alpha_new, sine_new * phi_bar])
    return (ray_out, damp_out, model_out, solution_out, search_out, recurrence_out)


def solution(mesh):
    return jax.shard_map(
        per_device,
        mesh=mesh,
        in_specs=(
            P("lat", "lon", None, None, None),
            P("lat", "lon", None),
            P("lat", "lon", None),
            P("lat", "lon"),
            P(None, "lat", "lon", None),
            P(None, "lat", "lon", None),
            P(None, "lat", "lon", None),
            P(None, "lat", "lon", None),
            P(None, "lat", "lon", None),
            P(),
        ),
        out_specs=(
            P(None, "lat", "lon", None),
            P(None, "lat", "lon", None),
            P(None, "lat", "lon", None),
            P(None, "lat", "lon", None),
            P(None, "lat", "lon", None),
            P(),
        ),
        check_vma=False,
    )
```

profile of v0, /device:TPU:0, one launch (start us, length us, event | category | flops | bytes accessed | tf_op | source)
XLA Modules:
  0.0 166.8 jit_solution(10572027661286127)
XLA Ops:
  0.6 0.7 fusion.40
  1.3 0.1 fusion.27
  1.4 0.1 reduce_window_sum.11
  1.5 0.2 select_reduce_fusion
  1.7 0.7 fusion.34
  2.3 0.8 scatter_custom_fusion
  3.1 0.7 all_to_all.14
  3.8 7.3 %all-to-all-start = ((s32[32,4,1]{1,2,0:T(1,128)}), s32[32,4,1]{1,2,0:T(1,128)S(1)}, u32[]{:S(2)}, u32[]{:S(2)}) async-start(s32[32,4,1]{1,2,0:T(1,128)} %bitcast.5), calls=%async_computation | async-start | bytes 32768 | tf_op jit(solution)/shard_map/all_to_all | solution.py:85
  11.1 0.9 fusion.52
  12.0 1.3 collective-permute-start
  13.3 4.5 %collective-permute-start.1 = (f32[4,1,32,128]{3,1,2,0:T(1,128)S(1)}, f32[4,1,32,128]{3,1,2,0:T(1,128)S(1)}, u32[]{:S(2)}, u32[]{:S(2)}) collective-permute-start(f32[4,1,32,128]{3,1,2,0:T(1,128)S(1)} %bitcast.95), channel_id=1, source_target_pairs={{0,8},{8,16},{16,24},{1,9},{9,17},{17,25},{2,10},{10,18},{18,26},{... | collective-permute-start | bytes 196616 | tf_op jit(solution)/shard_map/ppermute | solution.py:19
  17.9 3.1 %multiply_reduce_fusion = (f32[4]{0:T(128)}, bf16[32,32,4,128]{3,1,0,2:T(8,128)(2,1)S(1)}) fusion(f32[4,32,32,128]{3,2,1,0:T(8,128)} %param.16), kind=kLoop, calls=%fused_computation.49 | loop fusion | flops 1572860 | bytes 3145744 | tf_op jit(solution)/shard_map/reduce_sum | solution.py:121
  21.0 0.5 compare_and_fusion
  21.5 0.8 slice_bitcast_fusion
  22.3 0.1 slice_bitcast_fusion.2
  22.4 0.8 copy.23
  23.2 0.5 broadcast.298
  23.7 0.7 reduce.7
  24.4 0.1 all_to_all.16
  24.5 0.5 fusion.35
  25.1 0.1 compare_reduce_fusion.1
  25.2 0.6 le.29
  25.8 0.6 gt.11
  26.4 0.7 gather_fusion
  27.2 1.7 %select_select_fusion = bf16[128,4,128]{2,1,0:T(4,128)(2,1)} fusion(bf16[128,4,128]{2,1,0:T(4,128)(2,1)S(1)} %gather_fusion, pred[128]{0:T(512)(128)(4,1)} %le.29, pred[128]{0:T(512)(128)(4,1)} %gt.11), kind=kLoop, calls=%fused_computation.61 | loop fusion | flops 131072 | bytes 262400 | tf_op jit(solution)/shard_map/jit(_where)/select_n | solution.py:89
  28.9 4.9 %all-to-all-start.1 = ((bf16[128,4,128]{2,1,0:T(4,128)(2,1)}), bf16[128,4,128]{2,1,0:T(4,128)(2,1)S(1)}, u32[]{:S(2)}, u32[]{:S(2)}) async-start(bf16[128,4,128]{2,1,0:T(4,128)(2,1)} %select_select_fusion), calls=%async_computation.1 | async-start | bytes 262144 | tf_op jit(solution)/shard_map/all_to_all | solution.py:94
  33.7 0.7 pad_clamp_fusion
  34.4 1.2 copy.27
  36.4 0.6 copy-done.3
  37.0 2.2 %collective-permute-start.3 = (f32[4,34,1,128]{3,1,2,0:T(8,128)S(1)}, f32[4,34,1,128]{3,1,2,0:T(8,128)S(1)}, u32[]{:S(2)}, u32[]{:S(2)}) collective-permute-start(f32[4,34,1,128]{3,1,2,0:T(8,128)S(1)} %get-tuple-element.48), channel_id=1, source_target_pairs={{0,1},{1,2},{2,3},{3,4},{4,5},{5,6},{6,7},{8,9},{9,10},{10,11},{11... | collective-permute-start | bytes 208904 | tf_op jit(solution)/shard_map/ppermute | solution.py:19
  39.2 1.3 collective-permute-start.2
  40.5 1.5 all-to-all-done.1
  42.0 0.7 gather_fusion.1
  42.6 0.0 copy-start.4
  42.6 3.4 %fusion.2 = f32[60,4,256]{2,1,0:T(4,128)S(1)} fusion(bf16[1,1,60,256,128]{4,3,2,1,0:T(8,128)(2,1)} %param.10, bf16[60,4,128]{2,1,0:T(4,128)(2,1)S(1)} %gather_fusion.1, pred[60]{0:T(512)(128)(4,1)S(1)} %copy-done.12), kind=kOutput, calls=%fused_computation.11 | convolution fusion | flops 15759360 | bytes 4239420 | tf_op jit(solution)/shard_map/tid,trd->tri/dot_general | solution.py:97
  46.1 0.4 multiply_reduce_fusion.4
  46.4 0.3 convolution_convert_fusion
  46.7 0.0 copy-start.9
  46.7 0.6 fusion
  47.4 0.8 broadcast_in_dim.74
  48.1 6.9 %scatter_fusion = f32[128,4,128]{2,1,0:T(4,128)} fusion(f32[128,4,128]{2,1,0:T(4,128)} %broadcast_in_dim.74, s32[60]{0:T(128)S(1)} %copy-done.9, f32[60,4,128]{2,1,0:T(4,128)S(1)} %fusion), kind=kCustom, calls=%fused_computation.3 | custom fusion | bytes 368880 | tf_op jit(solution)/shard_map/scatter | solution.py:113
  55.0 6.5 %all-to-all-start.2 = ((f32[128,4,128]{2,1,0:T(4,128)}), f32[128,4,128]{2,1,0:T(4,128)S(1)}, u32[]{:S(2)}, u32[]{:S(2)}) async-start(f32[128,4,128]{2,1,0:T(4,128)} %scatter_fusion), calls=%async_computation.2 | async-start | bytes 524288 | tf_op jit(solution)/shard_map/all_to_all | solution.py:115
  61.5 9.8 %multiply_reduce_fusion.3 = (f32[4]{0:T(128)S(1)}, f32[4,32,32,128]{3,1,2,0:T(8,128)S(1)}) fusion(f32[4,32,32,128]{3,2,1,0:T(8,128)} %param.15, f32[4]{0:T(128)S(1)} %slice_bitcast_fusion, f32[4,32,32,128]{3,1,2,0:T(8,128)} %copy-done.3, f32[4,1,32,128]{3,1,2,0:T(1,128)S(1)} %collective-permute-done, f32[4,1,32,128]{3,1,2,0:T(1,128)S(1)} %collective-permute-done.1, ...), kind=kLoop, calls=%fused_computation.53 | loop fusion | flops 10485756 | bytes 6561824 | tf_op jit(solution)/shard_map/reduce_sum | solution.py:104
  71.3 0.1 fusion.51
  71.4 1.3 collective-permute-start.4
  72.7 4.5 %collective-permute-start.5 = (f32[4,1,32,128]{3,1,2,0:T(1,128)S(1)}, f32[4,1,32,128]{3,1,2,0:T(1,128)S(1)}, u32[]{:S(2)}, u32[]{:S(2)}) collective-permute-start(f32[4,1,32,128]{3,1,2,0:T(1,128)S(1)} %get-tuple-element.49), channel_id=1, source_target_pairs={{0,8},{8,16},{16,24},{1,9},{9,17},{17,25},{2,10},{10,18},{18,26},{... | collective-permute-start | bytes 196616 | tf_op jit(solution)/shard_map/ppermute | solution.py:19
  77.3 0.3 collective-permute-done.4
  77.6 1.6 collective-permute-done.5
  79.2 1.3 collective-permute-start.7
  80.5 1.3 collective-permute-start.6
  81.8 1.5 broadcast_in_dim.73
  83.3 15.4 %scatter_fusion.1 = f32[1025,4,128]{2,1,0:T(4,128)} fusion(f32[1025,4,128]{2,1,0:T(4,128)} %broadcast_in_dim.73, s32[128]{0:T(128)S(1)} %copy-done.14, f32[128,4,128]{2,1,0:T(4,128)S(1)} %all-to-all-done.2), kind=kCustom, calls=%fused_computation.4 | custom fusion | flops 65536 | bytes 786944 | tf_op jit(solution)/shard_map/scatter-add | solution.py:116
  98.7 1.9 %slice.118 = f32[1024,4,128]{2,1,0:T(4,128)S(1)} slice(f32[1025,4,128]{2,1,0:T(4,128)} %scatter_fusion.1), slice={[1:1025], [0:4], [0:128]} | slice | bytes 4194304 | tf_op jit(solution)/shard_map/slice | solution.py:117
  100.6 0.3 copy-done.2
  100.9 4.9 %multiply_reduce_fusion.2 = (f32[4]{0:T(128)S(1)}, f32[4]{0:T(128)S(1)}, f32[4,32,32,128]{3,1,2,0:T(8,128)}) fusion(f32[4,32,32,128]{3,2,1,0:T(8,128)S(1)} %copy-done, f32[4,32,32,128]{3,1,2,0:T(8,128)S(1)} %copy-done.2, f32[4,1,32,128]{3,1,2,0:T(1,128)S(1)} %collective-permute-done.4, f32[4,1,32,128]{3,1,2,0:T(1,128)S(1)} %collective-permute-done.5, ...), kind=kLoop, calls=%fused_computation.51 | loop fusion | flops 11010040 | bytes 8658976 | tf_op jit(solution)/shard_map/reduce_sum | solution.py:119
  105.8 44.1 %all-reduce.2 = (f32[4]{0:T(128)S(1)}, f32[4]{0:T(128)S(1)}, f32[4]{0:T(128)S(1)}, f32[4]{0:T(128)S(1)}) all-reduce(f32[4]{0:T(128)S(1)} %add.165, f32[4]{0:T(128)S(1)} %copy-done.11, f32[4]{0:T(128)S(1)} %get-tuple-element.25, f32[4]{0:T(128)S(1)} %get-tuple-element.24), channel_id=1, replica_groups=mesh['lat'=4,'lon'=8] {'lat','lon'}, use_global_device_ids=true, to_apply=%region_5.6 | all-reduce | flops 16 | bytes 128 | tf_op jit(solution)/shard_map/psum | solution.py:122
  150.0 0.1 broadcast_divide_fusion.1
  150.1 0.6 reshape.267
  150.7 6.1 %fusion.20 = (f32[4,32,32,128]{3,1,2,0:T(8,128)S(1)}, f32[4,32,32,128]{3,1,2,0:T(8,128)S(1)}, f32[4,32,32,128]{3,1,2,0:T(8,128)S(1)}) fusion(f32[4,32,32,128]{3,2,1,0:T(8,128)} %param.18, f32[4]{0:T(128)S(1)} %multiply_divide_fusion, f32[4]{0:T(128)S(1)} %get-tuple-element.35, f32[4,32,32,128]{3,2,1,0:T(8,128)S(1)} %copy-done, ...), kind=kLoop, calls=%fused_computation.46 | loop fusion | flops 3670016 | bytes 14680112 | tf_op jit(solution)/shard_map/sub | solution.py:135
  156.8 2.5 %copy.41 = f32[4,32,32,128]{3,2,1,0:T(8,128)} copy(f32[4,32,32,128]{3,1,2,0:T(8,128)S(1)} %get-tuple-element.57) | data formatting | bytes 4194304
  159.3 2.5 %copy.42 = f32[4,32,32,128]{3,2,1,0:T(8,128)} copy(f32[4,32,32,128]{3,1,2,0:T(8,128)S(1)} %get-tuple-element.39) | data formatting | bytes 4194304
  161.8 2.5 %copy.43 = f32[4,32,32,128]{3,2,1,0:T(8,128)} copy(f32[4,32,32,128]{3,1,2,0:T(8,128)S(1)} %get-tuple-element.38) | data formatting | bytes 4194304
  164.4 1.9 %multiply_add_fusion = f32[4,32,32,128]{3,2,1,0:T(8,128)} fusion(f32[4,32,32,128]{3,2,1,0:T(8,128)S(1)} %copy-done.6, f32[4,32,32,128]{3,2,1,0:T(8,128)S(1)} %copy-done.5, f32[4]{0:T(128)S(1)} %get-tuple-element.55), kind=kLoop, calls=%fused_computation.48 | loop fusion | flops 1048576 | bytes 6291472 | tf_op jit(solution)/shard_map/add | solution.py:134
  166.3 0.6 pad_maximum_fusion.22
  (43 shorter events, 0.2 us)
Async XLA Ops:
  0.6 21.7 %copy-start.10 = (s32[1,1,4]{2,1,0:T(1,128)S(1)}, s32[1,1,4]{2,1,0:T(1,128)}, u32[]{:S(2)}) copy-start(s32[1,1,4]{2,1,0:T(1,128)} %param.12) | copy-start | bytes 52
  2.3 20.1 %copy-start.8 = (s32[60]{0:T(128)}, s32[60]{0:T(128)S(1)}, u32[]{:S(2)}) copy-start(s32[60]{0:T(128)S(1)} %fusion.34) | copy-start | bytes 724
  3.8 19.4 %all-to-all-start = ((s32[32,4,1]{1,2,0:T(1,128)}), s32[32,4,1]{1,2,0:T(1,128)S(1)}, u32[]{:S(2)}, u32[]{:S(2)}) async-start(s32[32,4,1]{1,2,0:T(1,128)} %bitcast.5), calls=%async_computation | async-start | bytes 32768 | tf_op jit(solution)/shard_map/all_to_all | solution.py:85
  12.0 24.4 %collective-permute-start = (f32[4,1,32,128]{3,1,2,0:T(1,128)S(1)}, f32[4,1,32,128]{3,1,2,0:T(1,128)S(1)}, u32[]{:S(2)}, u32[]{:S(2)}) collective-permute-start(f32[4,1,32,128]{3,1,2,0:T(1,128)S(1)} %bitcast.96), channel_id=1, source_target_pairs={{8,0},{16,8},{24,16},{9,1},{17,9},{25,17},{10,2},{18,10},{26,18},{... | collective-permute-start | bytes 196616 | tf_op jit(solution)/shard_map/ppermute | solution.py:21
  13.3 23.1 %collective-permute-start.1 = (f32[4,1,32,128]{3,1,2,0:T(1,128)S(1)}, f32[4,1,32,128]{3,1,2,0:T(1,128)S(1)}, u32[]{:S(2)}, u32[]{:S(2)}) collective-permute-start(f32[4,1,32,128]{3,1,2,0:T(1,128)S(1)} %bitcast.95), channel_id=1, source_target_pairs={{0,8},{8,16},{16,24},{1,9},{9,17},{17,25},{2,10},{10,18},{18,26},{... | collective-permute-start | bytes 196616 | tf_op jit(solution)/shard_map/ppermute | solution.py:19
  21.0 13.4 %copy-start = (f32[4,32,32,128]{3,2,1,0:T(8,128)S(1)}, f32[4,32,32,128]{3,2,1,0:T(8,128)}, u32[]{:S(2)}) copy-start(f32[4,32,32,128]{3,2,1,0:T(8,128)} %param.16) | copy-start | bytes 6291460
  28.9 13.1 %all-to-all-start.1 = ((bf16[128,4,128]{2,1,0:T(4,128)(2,1)}), bf16[128,4,128]{2,1,0:T(4,128)(2,1)S(1)}, u32[]{:S(2)}, u32[]{:S(2)}) async-start(bf16[128,4,128]{2,1,0:T(4,128)(2,1)} %select_select_fusion), calls=%async_computation.1 | async-start | bytes 262144 | tf_op jit(solution)/shard_map/all_to_all | solution.py:94
  34.4 1.2 copy-start.7
  35.6 1.3 copy-start.3
  35.7 7.0 %copy-start.12 = (pred[60]{0:T(512)(128)(4,1)S(1)}, pred[60]{0:T(512)(128)(4,1)}, u32[]{:S(2)}) copy-start(pred[60]{0:T(512)(128)(4,1)} %compare_and_fusion) | copy-start | bytes 184
  37.0 24.5 %collective-permute-start.3 = (f32[4,34,1,128]{3,1,2,0:T(8,128)S(1)}, f32[4,34,1,128]{3,1,2,0:T(8,128)S(1)}, u32[]{:S(2)}, u32[]{:S(2)}) collective-permute-start(f32[4,34,1,128]{3,1,2,0:T(8,128)S(1)} %get-tuple-element.48), channel_id=1, source_target_pairs={{0,1},{1,2},{2,3},{3,4},{4,5},{5,6},{6,7},{8,9},{9,10},{10,11},{11... | collective-permute-start | bytes 208904 | tf_op jit(solution)/shard_map/ppermute | solution.py:19
  39.2 22.4 %collective-permute-start.2 = (f32[4,34,1,128]{3,1,2,0:T(8,128)S(1)}, f32[4,34,1,128]{3,1,2,0:T(8,128)S(1)}, u32[]{:S(2)}, u32[]{:S(2)}) collective-permute-start(f32[4,34,1,128]{3,1,2,0:T(8,128)S(1)} %get-tuple-element.47), channel_id=1, source_target_pairs={{1,0},{2,1},{3,2},{4,3},{5,4},{6,5},{7,6},{9,8},{10,9},{11,10},{12... | collective-permute-start | bytes 208904 | tf_op jit(solution)/shard_map/ppermute | solution.py:21
  42.6 4.1 %copy-start.4 = (bf16[1,1,60,256,128]{4,3,2,1,0:T(8,128)(2,1)S(1)}, bf16[1,1,60,256,128]{4,3,2,1,0:T(8,128)(2,1)}, u32[]{:S(2)}) copy-start(bf16[1,1,60,256,128]{4,3,2,1,0:T(8,128)(2,1)} %param.10) | copy-start | bytes 11796484
  46.7 1.4 copy-start.9
  55.0 26.8 %all-to-all-start.2 = ((f32[128,4,128]{2,1,0:T(4,128)}), f32[128,4,128]{2,1,0:T(4,128)S(1)}, u32[]{:S(2)}, u32[]{:S(2)}) async-start(f32[128,4,128]{2,1,0:T(4,128)} %scatter_fusion), calls=%async_computation.2 | async-start | bytes 524288 | tf_op jit(solution)/shard_map/all_to_all | solution.py:115
  71.3 7.9 %copy-start.1 = (f32[4,32,32,128]{3,1,2,0:T(8,128)}, f32[4,32,32,128]{3,1,2,0:T(8,128)S(1)}, u32[]{:S(2)}) copy-start(f32[4,32,32,128]{3,1,2,0:T(8,128)S(1)} %get-tuple-element.42) | copy-start | bytes 6291460
  71.4 6.2 %collective-permute-start.4 = (f32[4,1,32,128]{3,1,2,0:T(1,128)S(1)}, f32[4,1,32,128]{3,1,2,0:T(1,128)S(1)}, u32[]{:S(2)}, u32[]{:S(2)}) collective-permute-start(f32[4,1,32,128]{3,1,2,0:T(1,128)S(1)} %get-tuple-element.50), channel_id=1, source_target_pairs={{8,0},{16,8},{24,16},{9,1},{17,9},{25,17},{10,2},{18,10},{26,18},{... | collective-permute-start | bytes 196616 | tf_op jit(solution)/shard_map/ppermute | solution.py:21
  72.7 10.6 %copy-start.14 = (s32[128]{0:T(128)S(1)}, s32[128]{0:T(128)}, u32[]{:S(2)}) copy-start(s32[128]{0:T(128)} %get-tuple-element.58) | copy-start | bytes 1540
  72.7 6.4 %collective-permute-start.5 = (f32[4,1,32,128]{3,1,2,0:T(1,128)S(1)}, f32[4,1,32,128]{3,1,2,0:T(1,128)S(1)}, u32[]{:S(2)}, u32[]{:S(2)}) collective-permute-start(f32[4,1,32,128]{3,1,2,0:T(1,128)S(1)} %get-tuple-element.49), channel_id=1, source_target_pairs={{0,8},{8,16},{16,24},{1,9},{9,17},{17,25},{2,10},{10,18},{18,26},{... | collective-permute-start | bytes 196616 | tf_op jit(solution)/shard_map/ppermute | solution.py:19
  79.2 21.4 %collective-permute-start.7 = (f32[4,34,1,128]{3,1,2,0:T(8,128)S(1)}, f32[4,34,1,128]{3,1,2,0:T(8,128)S(1)}, u32[]{:S(2)}, u32[]{:S(2)}) collective-permute-start(f32[4,34,1,128]{3,1,2,0:T(8,128)S(1)} %get-tuple-element.46), channel_id=1, source_target_pairs={{0,1},{1,2},{2,3},{3,4},{4,5},{5,6},{6,7},{8,9},{9,10},{10,11},{11... | collective-permute-start | bytes 208904 | tf_op jit(solution)/shard_map/ppermute | solution.py:19
  80.5 20.1 %collective-permute-start.6 = (f32[4,34,1,128]{3,1,2,0:T(8,128)S(1)}, f32[4,34,1,128]{3,1,2,0:T(8,128)S(1)}, u32[]{:S(2)}, u32[]{:S(2)}) collective-permute-start(f32[4,34,1,128]{3,1,2,0:T(8,128)S(1)} %get-tuple-element.45), channel_id=1, source_target_pairs={{1,0},{2,1},{3,2},{4,3},{5,4},{6,5},{7,6},{9,8},{10,9},{11,10},{12... | collective-permute-start | bytes 208904 | tf_op jit(solution)/shard_map/ppermute | solution.py:21
  98.7 2.2 %copy-start.2 = (f32[4,32,32,128]{3,1,2,0:T(8,128)S(1)}, f32[4,32,32,128]{3,1,2,0:T(8,128)}, u32[]{:S(2)}) copy-start(f32[4,32,32,128]{3,1,2,0:T(8,128)} %copy-done.1) | copy-start | bytes 6291460
  100.9 4.9 %copy-start.11 = (f32[4]{0:T(128)S(1)}, f32[4]{0:T(128)}, u32[]{:S(2)}) copy-start(f32[4]{0:T(128)} %get-tuple-element.51) | copy-start | bytes 52
  100.9 49.0 %copy-start.13 = (f32[3,4]{1,0:T(4,128)S(1)}, f32[3,4]{1,0:T(4,128)}, u32[]{:S(2)}) copy-start(f32[3,4]{1,0:T(4,128)} %param.19) | copy-start | bytes 148
  161.8 2.5 %copy-start.5 = (f32[4,32,32,128]{3,2,1,0:T(8,128)S(1)}, f32[4,32,32,128]{3,2,1,0:T(8,128)}, u32[]{:S(2)}) copy-start(f32[4,32,32,128]{3,2,1,0:T(8,128)} %param.18) | copy-start | bytes 6291460
  161.8 2.5 %copy-start.6 = (f32[4,32,32,128]{3,2,1,0:T(8,128)S(1)}, f32[4,32,32,128]{3,2,1,0:T(8,128)}, u32[]{:S(2)}) copy-start(f32[4,32,32,128]{3,2,1,0:T(8,128)} %param.17) | copy-start | bytes 6291460
where the time goes:
time: 168 us; the launch traced here: 167 us
  other arithmetic  47.7 us (28%)
  blocking collectives  44.1 us (26%)
  starting transfers between devices  36.4 us (22%)
  local copies, waits for them, and re-layouts  28.8 us (17%)
  matrix products  4.7 us (3%)
  waiting for transfers between devices  3.41 us (2%)
  between operations  1.69 us (1%)
    psum x1, blocking collectives, per_device(): lax.psum((residual_sq, image_sq, cross_sum, model_sq), ('lat', 'lon'))  44.1 us
    scatter-add x1, other arithmetic, per_device(): jnp.zeros((columns_dev + 1, systems, depth), jnp.float32).at[wanted]  15.4 us
    ppermute x4, starting transfers between devices, with_halo(): lax.ppermute(tail, axis, [(i, (i + 1) % count) for i in range(ends)])  12.6 us
    reduce_sum x1, other arithmetic, per_device(): jnp.sum(damp_bar * damp_bar, axis=(1, 2, 3))  9.79 us
    unnamed x35, local copies, waits for them, and re-layouts  9.78 us
    all_to_all x1, starting transfers between devices, per_device(): lax.all_to_all(request, ('lat', 'lon'), split_axis=0, concat_axis=0, tile...  7.3 us
    scatter x1, local copies, waits for them, and re-layouts, per_device(): jnp.zeros((devices * capacity, systems, depth), jnp.float32).at[slot_index]  6.89 us
    all_to_all x1, starting transfers between devices, per_device(): lax.all_to_all(outgoing, ('lat', 'lon'), split_axis=0, concat_axis=0, til...  6.5 us
  transfers between devices with their start and end apart: 11, of which 3 were waited for; matrix products, arithmetic and copies ran while one was open for 33% of the time, Pallas kernels for 0%

commit v1 on v0

--- a/solution.py
+++ b/solution.py
@@ -81,8 +81,19 @@
     )
     slot_rank = jnp.sum(owner_hits * (jnp.cumsum(owner_hits, axis=0) - 1), axis=1)
     slot_index = owner_dev * capacity + slot_rank
-    request = jnp.zeros((devices * capacity,), jnp.int32).at[slot_index].set(column + 1)
-    wanted = lax.all_to_all(request, ("lat", "lon"), split_axis=0, concat_axis=0, tiled=True)
+    every_list = lax.all_gather(block_list, ("lat", "lon"), axis=0)
+    me = lax.axis_index(("lat", "lon"))
+    mine = every_list // columns_dev == me
+    mine_rank = jnp.cumsum(mine.astype(jnp.int32), axis=1) - 1
+    mine_slot = jnp.where(mine, mine_rank, capacity)
+    wanted = jnp.sum(
+        jnp.where(
+            mine_slot[:, :, None] == jnp.arange(capacity, dtype=jnp.int32),
+            (every_list - me * columns_dev + 1)[:, :, None],
+            0,
+        ),
+        axis=1,
+    ).reshape(devices * capacity)
     table = (
         model_vector.transpose(1, 2, 0, 3).reshape(columns_dev, systems, depth).astype(jnp.bfloat16)
     )
@@ -119,9 +130,9 @@
     image_sq = jnp.sum(adjoint_image * adjoint_image, axis=(1, 2, 3))
     cross_sum = jnp.sum(adjoint_image * model_vector, axis=(1, 2, 3))
     model_sq = jnp.sum(model_vector * model_vector, axis=(1, 2, 3))
-    residual_sq, image_sq, cross_sum, model_sq = lax.psum(
-        (residual_sq, image_sq, cross_sum, model_sq), ("lat", "lon")
-    )
+    partial = jnp.stack([residual_sq, image_sq, cross_sum, model_sq])
+    every_partial = lax.all_gather(partial, ("lat", "lon"), axis=0)
+    residual_sq, image_sq, cross_sum, model_sq = jnp.sum(every_partial, axis=0)
     beta_new = jnp.sqrt(residual_sq / rows_all + EPSILON)
     beta_wide = beta_new[:, None, None, None]
     update = adjoint_image / beta_wide - beta_wide * model_vector

time: 168 us -> 193 us (1.15)
  blocking collectives: 44.1 us -> 89.2 us
  other arithmetic: 47.7 us -> 37.6 us
  starting transfers between devices: 36.4 us -> 28 us
  local copies, waits for them, and re-layouts: 28.8 us -> 25 us
  waiting for transfers between devices: 3.41 us -> 5.45 us
    all_gather x0 -> x2, blocking collectives: none -> 89.2 us  [the longest x1 46 us: per_device(): every_partial = lax.all_gather(partial, ('lat', 'lon'), axis=0)]
    psum x1 -> x0, blocking collectives: 44.1 us -> none  [per_device(): lax.psum((residual_sq, image_sq, cross_sum, model_sq), ('lat', 'lon'))]
    all_to_all x1 -> x0, starting transfers between devices: 7.3 us -> none  [per_device(): lax.all_to_all(request, ('lat', 'lon'), split_axis=0, concat_axis=0, tile...]
    reduce_sum x1, other arithmetic: 9.79 us -> 3.79 us  [per_device(): jnp.sum(damp_bar * damp_bar, axis=(1, 2, 3))]
    ppermute x4, waiting for transfers between devices: 0.3 us -> 5.23 us  [with_halo(): lax.ppermute(head, axis, [((i + 1) % count, i) for i in range(ends)])]
    all_to_all x1, starting transfers between devices: 4.87 us -> 2.58 us  [per_device(): lax.all_to_all(served, ('lat', 'lon'), split_axis=0, concat_axis=0, tiled...]
    unnamed x35 -> x25, local copies, waits for them, and re-layouts: 9.78 us -> 9.2 us
  transfers between devices with their start and end apart: 11 -> 10, of which waited for: 3 -> 3; matrix products, arithmetic and copies ran while one was open for 33% -> 14% of each run, Pallas kernels for 0% -> 0%
where the time goes in v1:
time: 193 us; the launch traced here: 192 us
  blocking collectives  89.2 us (46%)
  other arithmetic  37.6 us (19%)
  starting transfers between devices  28 us (15%)
  local copies, waits for them, and re-layouts  25 us (13%)
  waiting for transfers between devices  5.45 us (3%)
  matrix products  4.7 us (2%)
    all_gather x1, blocking collectives, per_device(): every_partial = lax.all_gather(partial, ('lat', 'lon'), axis=0)  46 us
    all_gather x1, blocking collectives, per_device(): every_list = lax.all_gather(block_list, ('lat', 'lon'), axis=0)  43.2 us
    scatter-add x1, other arithmetic, per_device(): jnp.zeros((columns_dev + 1, systems, depth), jnp.float32).at[wanted]  14.9 us
    ppermute x4, starting transfers between devices, with_halo(): lax.ppermute(tail, axis, [(i, (i + 1) % count) for i in range(ends)])  11.9 us
    unnamed x25, local copies, waits for them, and re-layouts  9.2 us
    all_to_all x1, starting transfers between devices, per_device(): lax.all_to_all(outgoing, ('lat', 'lon'), split_axis=0, concat_axis=0, til...  8.42 us
    scatter x1, local copies, waits for them, and re-layouts, per_device(): jnp.zeros((devices * capacity, systems, depth), jnp.float32).at[slot_index]  6.89 us
    sub x1, other arithmetic, per_device(): model_out - (sine_new * alpha_new / rho_new)[:, None, None, None] * search  6.07 us
  transfers between devices with their start and end apart: 10, of which 3 were waited for; matrix products, arithmetic and copies ran while one was open for 14% of the time, Pallas kernels for 0%

profile of v1, /device:TPU:0, one launch (start us, length us, event | category | flops | bytes accessed | tf_op | source)
XLA Modules:
  0.0 191.8 jit_solution(16298268506536725666)
XLA Ops:
  0.6 43.2 %all-gather = s32[32,1,60]{2,1,0:T(1,128)S(1)} all-gather(s32[1,1,60]{2,1,0:T(1,128)} %param.11), channel_id=2, replica_groups=mesh['lat'=4,'lon'=8] {'lat','lon'}, dimensions={0}, use_global_device_ids=true | all-gather | bytes 7920 | tf_op jit(solution)/shard_map/all_gather | solution.py:84
  43.9 0.2 reduce_window_sum.23
  44.1 0.1 select_reduce_fusion
  44.2 0.1 copy.48
  44.3 2.6 %multiply_reduce_fusion = (f32[4]{0:T(128)S(1)}, bf16[32,32,4,128]{3,1,0,2:T(8,128)(2,1)S(1)}) fusion(f32[4,32,32,128]{3,2,1,0:T(8,128)} %param.16), kind=kLoop, calls=%fused_computation.49 | loop fusion | flops 1572860 | bytes 3145744 | tf_op jit(solution)/shard_map/reduce_sum | solution.py:132
  47.0 0.8 copy.47
  47.8 0.1 reshape.315
  47.9 0.1 copy.46
  48.0 0.1 le.29
  48.2 0.1 copy.45
  48.3 0.1 gt.11
  48.4 0.7 gather_fusion
  49.1 1.0 select_select_fusion
  50.1 2.6 %all-to-all-start = ((bf16[128,4,128]{2,1,0:T(4,128)(2,1)}), bf16[128,4,128]{2,1,0:T(4,128)(2,1)S(1)}, u32[]{:S(2)}, u32[]{:S(2)}) async-start(bf16[128,4,128]{2,1,0:T(4,128)(2,1)} %select_select_fusion), calls=%async_computation | async-start | bytes 262144 | tf_op jit(solution)/shard_map/all_to_all | solution.py:105
  52.7 1.3 collective-permute-start
  54.0 4.5 %collective-permute-start.1 = (f32[4,1,32,128]{3,1,2,0:T(1,128)S(1)}, f32[4,1,32,128]{3,1,2,0:T(1,128)S(1)}, u32[]{:S(2)}, u32[]{:S(2)}) collective-permute-start(f32[4,1,32,128]{3,1,2,0:T(1,128)S(1)} %bitcast.130), channel_id=1, source_target_pairs={{0,8},{8,16},{16,24},{1,9},{9,17},{17,25},{2,10},{10,18},{18,26},{... | collective-permute-start | bytes 196616 | tf_op jit(solution)/shard_map/ppermute | solution.py:19
  58.6 0.1 fusion.27
  58.7 0.1 reduce_window_sum.22
  58.8 0.2 select_reduce_fusion.1
  59.0 0.0 copy-start.6
  59.0 0.0 copy-start.7
  59.0 0.0 copy-start.8
  59.0 1.2 copy.52
  60.3 0.0 copy-start.5
  60.3 0.1 slice_bitcast_fusion.2
  61.3 1.5 collective-permute-start.3
  62.7 1.3 collective-permute-start.2
  64.0 0.0 collective-permute-done.3
  64.1 3.5 %collective-permute-done.2 = f32[4,34,1,128]{3,1,2,0:T(8,128)S(1)} collective-permute-done((f32[4,34,1,128]{3,1,2,0:T(8,128)S(1)}, f32[4,34,1,128]{3,1,2,0:T(8,128)S(1)}, u32[]{:S(2)}, u32[]{:S(2)}) %collective-permute-start.2) | collective-permute-done | bytes 69664 | tf_op jit(solution)/shard_map/ppermute | solution.py:21
  67.6 3.8 %multiply_reduce_fusion.3 = (f32[4]{0:T(128)S(1)}, f32[4,32,32,128]{3,1,2,0:T(8,128)}) fusion(f32[4,32,32,128]{3,2,1,0:T(8,128)S(1)} %copy-done.5, f32[4]{0:T(128)S(1)} %slice_bitcast_fusion, f32[4,32,32,128]{3,1,2,0:T(8,128)S(1)} %copy.52, f32[4,1,32,128]{3,1,2,0:T(1,128)S(1)} %collective-permute-done, f32[4,1,32,128]{3,1,2,0:T(1,128)S(1)} %collective-permute-done.1, ...), kind=kLoop, calls=%fused_computation.52 | loop fusion | flops 10485756 | bytes 6561824 | tf_op jit(solution)/shard_map/reduce_sum | solution.py:115
  71.4 0.0 all-to-all-done
  71.4 0.6 gather_fusion.1
  72.0 0.0 copy-start.2
  72.1 3.4 %fusion.2 = f32[60,4,256]{2,1,0:T(4,128)S(1)} fusion(bf16[1,1,60,256,128]{4,3,2,1,0:T(8,128)(2,1)} %param.10, bf16[60,4,128]{2,1,0:T(4,128)(2,1)S(1)} %gather_fusion.1, pred[60]{0:T(512)(128)(4,1)S(1)} %compare_and_fusion), kind=kOutput, calls=%fused_computation.10 | convolution fusion | flops 15759360 | bytes 4239420 | tf_op jit(solution)/shard_map/tid,trd->tri/dot_general | solution.py:108
  75.5 0.4 multiply_reduce_fusion.4
  75.8 0.3 convolution_convert_fusion
  76.1 0.6 fusion
  76.8 0.8 broadcast_in_dim.95
  77.5 6.9 %scatter_fusion = f32[128,4,128]{2,1,0:T(4,128)} fusion(f32[128,4,128]{2,1,0:T(4,128)} %broadcast_in_dim.95, s32[60]{0:T(128)S(1)} %fusion.37, f32[60,4,128]{2,1,0:T(4,128)S(1)} %fusion), kind=kCustom, calls=%fused_computation.2 | custom fusion | bytes 368880 | tf_op jit(solution)/shard_map/scatter | solution.py:124
  84.4 8.4 %all-to-all-start.1 = ((f32[128,4,128]{2,1,0:T(4,128)}), f32[128,4,128]{2,1,0:T(4,128)S(1)}, u32[]{:S(2)}, u32[]{:S(2)}) async-start(f32[128,4,128]{2,1,0:T(4,128)} %scatter_fusion), calls=%async_computation.1 | async-start | bytes 524288 | tf_op jit(solution)/shard_map/all_to_all | solution.py:126
  92.8 1.3 fusion.52
  94.1 1.3 collective-permute-start.4
  95.4 4.5 %collective-permute-start.5 = (f32[4,1,32,128]{3,1,2,0:T(1,128)S(1)}, f32[4,1,32,128]{3,1,2,0:T(1,128)S(1)}, u32[]{:S(2)}, u32[]{:S(2)}) collective-permute-start(f32[4,1,32,128]{3,1,2,0:T(1,128)S(1)} %get-tuple-element.47), channel_id=1, source_target_pairs={{0,8},{8,16},{16,24},{1,9},{9,17},{17,25},{2,10},{10,18},{18,26},{... | collective-permute-start | bytes 196616 | tf_op jit(solution)/shard_map/ppermute | solution.py:19
  100.0 1.7 collective-permute-done.4
  101.7 0.2 collective-permute-done.5
  101.9 0.9 pad_maximum_fusion.18
  102.8 1.3 collective-permute-start.7
  104.1 1.3 collective-permute-start.6
  105.4 0.0 all-to-all-done.1
  105.4 1.5 broadcast_in_dim.94
  106.9 14.9 %scatter_fusion.1 = f32[1025,4,128]{2,1,0:T(4,128)} fusion(f32[1025,4,128]{2,1,0:T(4,128)} %broadcast_in_dim.94, s32[128]{0:T(128)S(1)} %get-tuple-element.59, f32[128,4,128]{2,1,0:T(4,128)S(1)} %all-to-all-done.1), kind=kCustom, calls=%fused_computation.3 | custom fusion | flops 65536 | bytes 786944 | tf_op jit(solution)/shard_map/scatter-add | solution.py:127
  121.8 1.9 slice.118
  123.6 0.0 collective-permute-done.7
  123.7 0.3 copy-done.1
  124.0 4.9 %multiply_reduce_fusion.2 = (f32[4]{0:T(128)S(1)}, f32[4]{0:T(128)S(1)}, f32[4,32,32,128]{3,1,2,0:T(8,128)}) fusion(f32[4,32,32,128]{3,2,1,0:T(8,128)S(1)} %copy-done, f32[4,32,32,128]{3,1,2,0:T(8,128)S(1)} %copy-done.1, f32[4,1,32,128]{3,1,2,0:T(1,128)S(1)} %collective-permute-done.4, f32[4,1,32,128]{3,1,2,0:T(1,128)S(1)} %collective-permute-done.5, ...), kind=kLoop, calls=%fused_computation.51 | loop fusion | flops 11010040 | bytes 8658976 | tf_op jit(solution)/shard_map/reduce_sum | solution.py:130
  128.8 46.0 %all-gather.2 = f32[32,4,4]{2,1,0:T(4,128)S(1)} all-gather(f32[1,4,4]{2,1,0:T(4,128)S(1)} %maximum_bitcast_fusion), channel_id=3, replica_groups=mesh['lat'=4,'lon'=8] {'lat','lon'}, dimensions={0}, use_global_device_ids=true | all-gather | bytes 2112 | tf_op jit(solution)/shard_map/all_gather | solution.py:134
  174.9 0.1 broadcast_divide_fusion.1
  175.0 0.6 reshape.358
  175.6 6.1 %fusion.20 = (f32[4,32,32,128]{3,1,2,0:T(8,128)S(1)}, f32[4,32,32,128]{3,1,2,0:T(8,128)S(1)}, f32[4,32,32,128]{3,1,2,0:T(8,128)S(1)}) fusion(f32[4,32,32,128]{3,2,1,0:T(8,128)} %param.18, f32[4]{0:T(128)S(1)} %get-tuple-element.36, f32[4]{0:T(128)S(1)} %get-tuple-element.37, f32[4,32,32,128]{3,2,1,0:T(8,128)S(1)} %copy-done, ...), kind=kLoop, calls=%fused_computation.45 | loop fusion | flops 3670016 | bytes 14680112 | tf_op jit(solution)/shard_map/sub | solution.py:146
  181.7 2.5 %copy.66 = f32[4,32,32,128]{3,2,1,0:T(8,128)} copy(f32[4,32,32,128]{3,1,2,0:T(8,128)S(1)} %get-tuple-element.58) | data formatting | bytes 4194304
  184.2 2.5 %copy.67 = f32[4,32,32,128]{3,2,1,0:T(8,128)} copy(f32[4,32,32,128]{3,1,2,0:T(8,128)S(1)} %get-tuple-element.35) | data formatting | bytes 4194304
  186.8 2.5 %copy.68 = f32[4,32,32,128]{3,2,1,0:T(8,128)} copy(f32[4,32,32,128]{3,1,2,0:T(8,128)S(1)} %get-tuple-element.34) | data formatting | bytes 4194304
  189.3 1.9 multiply_add_fusion
  191.2 0.6 pad_maximum_fusion.22
  (36 shorter events, 0.3 us)
Async XLA Ops:
  47.0 5.7 %copy-start = (f32[4,32,32,128]{3,2,1,0:T(8,128)S(1)}, f32[4,32,32,128]{3,2,1,0:T(8,128)}, u32[]{:S(2)}) copy-start(f32[4,32,32,128]{3,2,1,0:T(8,128)} %param.16) | copy-start | bytes 6291460
  47.0 11.6 %copy-start.9 = (s32[1,1,60]{2,1,0:T(1,128)S(1)}, s32[1,1,60]{2,1,0:T(1,128)}, u32[]{:S(2)}) copy-start(s32[1,1,60]{2,1,0:T(1,128)} %param.11) | copy-start | bytes 724
  50.1 21.3 %all-to-all-start = ((bf16[128,4,128]{2,1,0:T(4,128)(2,1)}), bf16[128,4,128]{2,1,0:T(4,128)(2,1)S(1)}, u32[]{:S(2)}, u32[]{:S(2)}) async-start(bf16[128,4,128]{2,1,0:T(4,128)(2,1)} %select_select_fusion), calls=%async_computation | async-start | bytes 262144 | tf_op jit(solution)/shard_map/all_to_all | solution.py:105
  52.7 8.5 %collective-permute-start = (f32[4,1,32,128]{3,1,2,0:T(1,128)S(1)}, f32[4,1,32,128]{3,1,2,0:T(1,128)S(1)}, u32[]{:S(2)}, u32[]{:S(2)}) collective-permute-start(f32[4,1,32,128]{3,1,2,0:T(1,128)S(1)} %bitcast.131), channel_id=1, source_target_pairs={{8,0},{16,8},{24,16},{9,1},{17,9},{25,17},{10,2},{18,10},{26,18},{... | collective-permute-start | bytes 196616 | tf_op jit(solution)/shard_map/ppermute | solution.py:21
  54.0 7.2 %collective-permute-start.1 = (f32[4,1,32,128]{3,1,2,0:T(1,128)S(1)}, f32[4,1,32,128]{3,1,2,0:T(1,128)S(1)}, u32[]{:S(2)}, u32[]{:S(2)}) collective-permute-start(f32[4,1,32,128]{3,1,2,0:T(1,128)S(1)} %bitcast.130), channel_id=1, source_target_pairs={{0,8},{8,16},{16,24},{1,9},{9,17},{17,25},{2,10},{10,18},{18,26},{... | collective-permute-start | bytes 196616 | tf_op jit(solution)/shard_map/ppermute | solution.py:19
  59.0 1.3 copy-start.6
  59.0 1.3 copy-start.7
  59.0 1.3 copy-start.8
  60.3 7.3 %copy-start.5 = (f32[4,32,32,128]{3,2,1,0:T(8,128)S(1)}, f32[4,32,32,128]{3,2,1,0:T(8,128)}, u32[]{:S(2)}) copy-start(f32[4,32,32,128]{3,2,1,0:T(8,128)} %param.15) | copy-start | bytes 6291460
  61.3 2.8 %collective-permute-start.3 = (f32[4,34,1,128]{3,1,2,0:T(8,128)S(1)}, f32[4,34,1,128]{3,1,2,0:T(8,128)S(1)}, u32[]{:S(2)}, u32[]{:S(2)}) collective-permute-start(f32[4,34,1,128]{3,1,2,0:T(8,128)S(1)} %get-tuple-element.46), channel_id=1, source_target_pairs={{0,1},{1,2},{2,3},{3,4},{4,5},{5,6},{6,7},{8,9},{9,10},{10,11},{11... | collective-permute-start | bytes 208904 | tf_op jit(solution)/shard_map/ppermute | solution.py:19
  62.7 4.9 %collective-permute-start.2 = (f32[4,34,1,128]{3,1,2,0:T(8,128)S(1)}, f32[4,34,1,128]{3,1,2,0:T(8,128)S(1)}, u32[]{:S(2)}, u32[]{:S(2)}) collective-permute-start(f32[4,34,1,128]{3,1,2,0:T(8,128)S(1)} %get-tuple-element.45), channel_id=1, source_target_pairs={{1,0},{2,1},{3,2},{4,3},{5,4},{6,5},{7,6},{9,8},{10,9},{11,10},{12... | collective-permute-start | bytes 208904 | tf_op jit(solution)/shard_map/ppermute | solution.py:21
  72.0 4.1 %copy-start.2 = (bf16[1,1,60,256,128]{4,3,2,1,0:T(8,128)(2,1)S(1)}, bf16[1,1,60,256,128]{4,3,2,1,0:T(8,128)(2,1)}, u32[]{:S(2)}) copy-start(bf16[1,1,60,256,128]{4,3,2,1,0:T(8,128)(2,1)} %param.10) | copy-start | bytes 11796484
  84.4 21.0 %all-to-all-start.1 = ((f32[128,4,128]{2,1,0:T(4,128)}), f32[128,4,128]{2,1,0:T(4,128)S(1)}, u32[]{:S(2)}, u32[]{:S(2)}) async-start(f32[128,4,128]{2,1,0:T(4,128)} %scatter_fusion), calls=%async_computation.1 | async-start | bytes 524288 | tf_op jit(solution)/shard_map/all_to_all | solution.py:126
  94.1 7.5 %collective-permute-start.4 = (f32[4,1,32,128]{3,1,2,0:T(1,128)S(1)}, f32[4,1,32,128]{3,1,2,0:T(1,128)S(1)}, u32[]{:S(2)}, u32[]{:S(2)}) collective-permute-start(f32[4,1,32,128]{3,1,2,0:T(1,128)S(1)} %get-tuple-element.48), channel_id=1, source_target_pairs={{8,0},{16,8},{24,16},{9,1},{17,9},{25,17},{10,2},{18,10},{26,18},{... | collective-permute-start | bytes 196616 | tf_op jit(solution)/shard_map/ppermute | solution.py:21
  95.4 6.4 %collective-permute-start.5 = (f32[4,1,32,128]{3,1,2,0:T(1,128)S(1)}, f32[4,1,32,128]{3,1,2,0:T(1,128)S(1)}, u32[]{:S(2)}, u32[]{:S(2)}) collective-permute-start(f32[4,1,32,128]{3,1,2,0:T(1,128)S(1)} %get-tuple-element.47), channel_id=1, source_target_pairs={{0,8},{8,16},{16,24},{1,9},{9,17},{17,25},{2,10},{10,18},{18,26},{... | collective-permute-start | bytes 196616 | tf_op jit(solution)/shard_map/ppermute | solution.py:19
  102.8 20.8 %collective-permute-start.7 = (f32[4,34,1,128]{3,1,2,0:T(8,128)S(1)}, f32[4,34,1,128]{3,1,2,0:T(8,128)S(1)}, u32[]{:S(2)}, u32[]{:S(2)}) collective-permute-start(f32[4,34,1,128]{3,1,2,0:T(8,128)S(1)} %get-tuple-element.44), channel_id=1, source_target_pairs={{0,1},{1,2},{2,3},{3,4},{4,5},{5,6},{6,7},{8,9},{9,10},{10,11},{11... | collective-permute-start | bytes 208904 | tf_op jit(solution)/shard_map/ppermute | solution.py:19
  104.1 19.6 %collective-permute-start.6 = (f32[4,34,1,128]{3,1,2,0:T(8,128)S(1)}, f32[4,34,1,128]{3,1,2,0:T(8,128)S(1)}, u32[]{:S(2)}, u32[]{:S(2)}) collective-permute-start(f32[4,34,1,128]{3,1,2,0:T(8,128)S(1)} %get-tuple-element.43), channel_id=1, source_target_pairs={{1,0},{2,1},{3,2},{4,3},{5,4},{6,5},{7,6},{9,8},{10,9},{11,10},{12... | collective-permute-start | bytes 208904 | tf_op jit(solution)/shard_map/ppermute | solution.py:21
  121.8 2.2 %copy-start.1 = (f32[4,32,32,128]{3,1,2,0:T(8,128)S(1)}, f32[4,32,32,128]{3,1,2,0:T(8,128)}, u32[]{:S(2)}) copy-start(f32[4,32,32,128]{3,1,2,0:T(8,128)} %get-tuple-element.39) | copy-start | bytes 6291460
  186.8 2.5 %copy-start.3 = (f32[4,32,32,128]{3,2,1,0:T(8,128)S(1)}, f32[4,32,32,128]{3,2,1,0:T(8,128)}, u32[]{:S(2)}) copy-start(f32[4,32,32,128]{3,2,1,0:T(8,128)} %param.18) | copy-start | bytes 6291460
  186.8 2.5 %copy-start.4 = (f32[4,32,32,128]{3,2,1,0:T(8,128)S(1)}, f32[4,32,32,128]{3,2,1,0:T(8,128)}, u32[]{:S(2)}) copy-start(f32[4,32,32,128]{3,2,1,0:T(8,128)} %param.17) | copy-start | bytes 6291460

commit v2 on v0

v2 whole, which is shorter than its diff:
```python
import functools

import jax
import jax.numpy as jnp
from jax import lax
from jax.experimental import pallas as pl
from jax.experimental.pallas import tpu as pltpu
from jax.sharding import PartitionSpec as P

DAMP_WEIGHT = 0.15
EPSILON = 1e-05
AXES = ("lat", "lon")
PATCH = 4
F32, BF16, I32 = jnp.float32, jnp.bfloat16, jnp.int32


def iota(shape, dim):
    return lax.broadcasted_iota(I32, shape, dim)


def vmem():
    return pl.BlockSpec(memory_space=pltpu.VMEM)


def smem():
    return pl.BlockSpec(memory_space=pltpu.SMEM)


def call(body, name, out_shape, in_specs, out_specs, scratch=(), grid=(), mib=16, flops=0, moved=0):
    return pl.pallas_call(
        body,
        name=name,
        grid=grid,
        out_shape=out_shape,
        in_specs=in_specs,
        out_specs=out_specs,
        scratch_shapes=list(scratch),
        compiler_params=pltpu.CompilerParams(vmem_limit_bytes=mib * 2**20),
        cost_estimate=pl.CostEstimate(flops=flops, bytes_accessed=moved, transcendentals=0),
    )


def request_body(shift, cap, blocks, ids_ref, off_ref, req_ref, meta_ref):
    tiles = ids_ref.shape[-1]
    devices = req_ref.shape[0]
    lanes = 128
    ids = jnp.concatenate(
        [ids_ref[0], jnp.full((1, lanes - tiles), -1, I32)], axis=1
    )
    owner = lax.shift_right_arithmetic(ids, shift)
    column = ids - lax.shift_left(owner, shift)
    square = (lanes, lanes)
    down, across = iota(square, 0), iota(square, 1)
    owner_f = jnp.broadcast_to(owner.astype(F32), square)
    owner_col = jnp.sum(jnp.where(down == across, owner_f, 0.0), axis=1, keepdims=True)
    same = jnp.where((owner_f == owner_col) & (down < across), 1.0, 0.0)
    rank = jnp.sum(same, axis=0, keepdims=True).astype(I32)
    lane = iota((1, lanes), 1)
    block = jnp.zeros((1, lanes), I32)
    for b in range(1, blocks + 1):
        block = block + (lane >= off_ref[0, 0, b]).astype(I32)
    meta_ref[...] = jnp.concatenate([owner, rank, block] + [owner] * 5, axis=0)
    wide = (devices, lanes)
    hit = jnp.broadcast_to(owner, wide) == iota(wide, 0)
    value = jnp.broadcast_to((column + 1).astype(F32), wide)
    rank_wide = jnp.broadcast_to(rank, wide)
    at = iota(wide, 1)
    req = jnp.zeros(wide, F32)
    for c in range(cap):
        picked = jnp.sum(jnp.where(hit & (rank_wide == c), value, 0.0), axis=1, keepdims=True)
        req = jnp.where(at == c, picked, req)
    req_ref[...] = req.astype(I32)


def wanted_column(wanted, cap):
    devices, lanes = wanted.shape
    rows = devices * cap
    spread = jnp.broadcast_to(wanted.astype(F32)[:, None, :], (devices, cap, lanes))
    spread = spread.reshape(rows, lanes)
    pick = iota((rows, lanes), 1) == (iota((rows, lanes), 0) & (cap - 1))
    return jnp.sum(jnp.where(pick, spread, 0.0), axis=1, keepdims=True).astype(I32)


def serve_body(clat, cap, wanted_ref, model_ref, served_ref, corner_ref, patch, mixed, sem):
    systems, _, clon, depth = patch.shape
    wanted = wanted_ref[...]
    shift = clon.bit_length() - 1
    first = jnp.min(jnp.where(wanted > 0, wanted - 1, clat * clon))
    corner = jnp.minimum(lax.shift_right_logical(first, shift), clat - PATCH)
    corner_ref[0] = corner
    copy = pltpu.make_async_copy(model_ref.at[:, pl.ds(corner, PATCH)], patch, sem)
    copy.start()
    col = wanted_column(wanted, cap)
    rows = col.shape[0]
    target = jnp.where(col > 0, col - 1 - corner * clon, -1)
    width = PATCH * clon
    chosen = (jnp.broadcast_to(target, (rows, width)) == iota((rows, width), 1)).astype(F32).astype(BF16)
    copy.wait()
    for r in range(systems):
        table = patch[r].reshape(width, depth).astype(BF16)
        mixed[pl.ds(r, rows, stride=systems), :] = jnp.dot(
            chosen, table, preferred_element_type=F32
        )
    served_ref[...] = mixed[...].astype(BF16)


def rays_body(
    cap, blocks, meta_ref, count_ref, rec_ref, tiles_ref, fetched_ref, old_ref, bar_ref, term_ref, masks, lows
):
    tiles, width, depth = tiles_ref.shape[2:]
    systems = old_ref.shape[0]
    group = cap * systems
    for c in range(cap + 1):
        here = lax.shift_right_logical(iota((group, depth), 0), systems.bit_length() - 1) == c
        masks[c] = here.astype(F32).astype(BF16)
    term_ref[...] = jnp.zeros(term_ref.shape, F32)
    lows[...] = jnp.zeros(lows.shape, BF16)
    total = jnp.zeros((blocks * group, width), F32)
    for t in range(tiles):
        owner, rank, block = meta_ref[0, t], meta_ref[1, t], meta_ref[2, t]
        rows = fetched_ref[pl.ds(pl.multiple_of(owner * group, group), group), :]
        left = jnp.concatenate(
            [rows * masks[jnp.where(block == b, rank, cap)] for b in range(blocks)], axis=0
        )
        total = total + lax.dot_general(
            left, tiles_ref[0, 0, t], (((1,), (1,)), ((), ())), preferred_element_type=F32
        )
    for b in range(blocks):
        traced = jnp.zeros((systems, width), F32)
        for c in range(cap):
            at = b * group + c * systems
            traced = traced + total[at : at + systems]
        old = jnp.concatenate(
            [old_ref[r, 0, :, b * width : (b + 1) * width] * rec_ref[0, r] for r in range(systems)], axis=0
        )
        live = iota((systems, width), 1) + b * width < count_ref[0, 0]
        bar = jnp.where(live, traced - old, 0.0)
        for r in range(systems):
            bar_ref[r, 0, :, b * width : (b + 1) * width] = bar[r : r + 1]
        lows[b] = jnp.concatenate([bar, jnp.zeros((16 - systems, width), F32)], axis=0).astype(BF16)
    for t in range(tiles):
        slot = meta_ref[0, t] * cap + meta_ref[1, t]
        term = jnp.dot(lows[meta_ref[2, t]], tiles_ref[0, 0, t], preferred_element_type=F32)
        term_ref[slot] = term[:systems]


def six(x, north, south, west, east):
    sub, lane = iota(x.shape, 0), iota(x.shape, 1)
    rows, depth = x.shape
    left = jnp.where(sub == 0, jnp.broadcast_to(west, x.shape), pltpu.roll(x, 1, 0))
    right = jnp.where(sub == rows - 1, jnp.broadcast_to(east, x.shape), pltpu.roll(x, rows - 1, 0))
    above = jnp.where(lane == 0, 0.0, pltpu.roll(x, 1, 1))
    below = jnp.where(lane == depth - 1, 0.0, pltpu.roll(x, depth - 1, 1))
    beside = north + south + left + right + above + below
    return DAMP_WEIGHT * (6.0 * x - beside)


def dense_body(
    cap,
    flag_ref,
    rec_ref,
    corner_ref,
    wanted_ref,
    bar_ref,
    model_ref,
    damp_ref,
    north_ref,
    south_ref,
    west_ref,
    east_ref,
    westmost_ref,
    eastmost_ref,
    bar_out,
    image_out,
    sums_out,
    patch_out,
    model_patch_out,
    chosen_out,
    rows_s,
    west_s,
    east_s,
):
    r = pl.program_id(0)
    _, clat, clon, depth = model_ref.shape
    alpha = rec_ref[0, r]

    @pl.when(r == 0)
    def _():
        sums_out[...] = jnp.zeros(sums_out.shape, F32)
        col = wanted_column(wanted_ref[...], cap)
        slots = col.shape[0]
        target = jnp.where(col > 0, col - 1 - corner_ref[0] * clon, -1).astype(F32)
        square = (slots, slots)
        flat = jnp.sum(
            jnp.where(iota(square, 0) == iota(square, 1), jnp.broadcast_to(target, square), 0.0),
            axis=0,
            keepdims=True,
        ).astype(I32)
        wide = (PATCH * clon, slots)
        chosen_out[...] = (jnp.broadcast_to(flat, wide) == iota(wide, 0)).astype(F32).astype(BF16)

    def side(ref, near, own, flag):
        x, beyond, old = ref[0, 0:clat], ref[0, clat : 2 * clat], ref[0, 2 * clat : 3 * clat]
        upper, lower = ref[0, 3 * clat : 3 * clat + 1], ref[0, 3 * clat + 1 : 3 * clat + 2]
        return (six(x, beyond, own, upper, lower) - alpha * old) * flag

    west_s[...] = side(west_ref, 0, westmost_ref[0, 0:clat], flag_ref[2])
    east_s[...] = side(east_ref, 0, eastmost_ref[0, 0:clat], flag_ref[3])
    corner_n, corner_s = 3 * clat, 3 * clat + 1
    rows_s[0] = flag_ref[0] * (
        six(
            north_ref[0, 1],
            north_ref[0, 0],
            model_ref[0, 0],
            west_ref[0, corner_n : corner_n + 1],
            east_ref[0, corner_n : corner_n + 1],
        )
        - alpha * north_ref[0, 2]
    )
    rows_s[clat + 1] = flag_ref[1] * (
        six(
            south_ref[0, 0],
            model_ref[0, clat - 1],
            south_ref[0, 1],
            west_ref[0, corner_s : corner_s + 1],
            east_ref[0, corner_s : corner_s + 1],
        )
        - alpha * south_ref[0, 2]
    )

    def fold(x):
        parts = [x[i * 8 : (i + 1) * 8] for i in range(x.shape[0] // 8)]
        return functools.reduce(lambda a, b: a + b, parts)

    def first(i, north, south, acc):
        x = model_ref[0, i]
        bar = six(x, north, south, west_ref[0, pl.ds(i, 1)], east_ref[0, pl.ds(i, 1)])
        bar = bar - alpha * damp_ref[0, i]
        rows_s[i + 1] = bar
        bar_out[0, i] = bar
        return acc[0] + fold(bar * bar), acc[1] + fold(x * x)

    zero = jnp.zeros((8, depth), F32)
    acc = first(0, north_ref[0, 1], model_ref[0, 1], (zero, zero))
    acc = lax.fori_loop(
        1, clat - 1, lambda i, acc: first(i, model_ref[0, i - 1], model_ref[0, i + 1], acc), acc, unroll=2
    )
    bar_sq, model_sq = first(clat - 1, model_ref[0, clat - 2], south_ref[0, 0], acc)

    def second(i, acc):
        image = six(rows_s[i + 1], rows_s[i], rows_s[i + 2], west_s[pl.ds(i, 1)], east_s[pl.ds(i, 1)])
        image_out[0, i] = image
        return acc[0] + fold(image * image), acc[1] + fold(image * model_ref[0, i])

    image_sq, cross = lax.fori_loop(0, clat, second, (zero, zero), unroll=2)
    for a in range(PATCH):
        patch_out[0, pl.ds(a * clon, clon), :] = image_out[0, corner_ref[0] + a]
        model_patch_out[0, pl.ds(a * clon, clon), :] = model_ref[0, corner_ref[0] + a]
    ray = bar_ref[0, 0]
    res = jnp.sum(bar_sq, keepdims=True) + jnp.sum(ray * ray, keepdims=True)
    lane = iota((1, depth), 1)
    row = sums_out[...]
    systems = pl.num_programs(0)
    values = (
        res,
        jnp.sum(image_sq, keepdims=True),
        jnp.sum(cross, keepdims=True),
        jnp.sum(model_sq, keepdims=True),
    )
    for q, value in enumerate(values):
        row = row + jnp.where(lane == q * systems + r, jnp.broadcast_to(value, (1, depth)), 0.0)
    sums_out[...] = row


def combine_body(terms_ref, chosen_ref, patch_ref, model_patch_ref, sums_ref, added_ref, parts_ref):
    systems, width, depth = patch_ref.shape
    slots = chosen_ref.shape[1]
    chosen = chosen_ref[...]
    row = sums_ref[...]
    lane = iota(row.shape, 1)
    for r in range(systems):
        x = terms_ref[pl.ds(r, slots, stride=systems), :]
        high = x.astype(BF16)
        rest = x - high.astype(F32)
        middle = rest.astype(BF16)
        low = (rest - middle.astype(F32)).astype(BF16)
        added = (
            jnp.dot(chosen, low, preferred_element_type=F32)
            + jnp.dot(chosen, middle, preferred_element_type=F32)
            + jnp.dot(chosen, high, preferred_element_type=F32)
        )
        added_ref[r] = added
        square = jnp.sum(added * (2.0 * patch_ref[r] + added), keepdims=True)
        cross = jnp.sum(added * model_patch_ref[r], keepdims=True)
        row = row + jnp.where(lane == systems + r, jnp.broadcast_to(square, row.shape), 0.0)
        row = row + jnp.where(lane == 2 * systems + r, jnp.broadcast_to(cross, row.shape), 0.0)
    parts_ref[...] = jnp.broadcast_to(row, parts_ref.shape)


def finish_body(
    rows_all,
    cells_all,
    corner_ref,
    parts_ref,
    rec_ref,
    bar_ref,
    added_ref,
    image_ref,
    model_ref,
    damp_ref,
    solution_ref,
    search_ref,
    ray_out,
    damp_out,
    model_out,
    solution_out,
    search_out,
    rec_out,
    coef,
):
    r, piece = pl.program_id(0), pl.program_id(1)
    systems = rec_ref.shape[1]
    _, rows, clon, depth = image_ref.shape

    @pl.when((r == 0) & (piece == 0))
    def _():
        total = jnp.sum(parts_ref[...], axis=0, keepdims=True)
        residual_sq, image_sq, cross, model_sq = (
            total[:, q * systems : (q + 1) * systems] for q in range(4)
        )
        alpha_old, rho_bar, phi_bar = rec_ref[0:1], rec_ref[1:2], rec_ref[2:3]
        beta = jnp.sqrt(residual_sq / rows_all + EPSILON)
        update_sq = image_sq / (beta * beta) - 2.0 * cross + beta * beta * model_sq
        alpha = jnp.sqrt(jnp.maximum(update_sq, 0.0) / cells_all + EPSILON)
        rho = jnp.sqrt(rho_bar * rho_bar + beta * beta)
        cosine = rho_bar / rho
        sine = beta / rho
        rec_out[...] = jnp.concatenate([alpha, -cosine * alpha, sine * phi_bar], axis=0)
        scales = (
            1.0 / beta,
            1.0 / (beta * alpha),
            beta / alpha,
            cosine * phi_bar / rho,
            sine * alpha / rho,
        )
        for q, scale in enumerate(scales):
            for s in range(systems):
                coef[q, s] = scale[0, s]
        for s in range(systems):
            ray_out[s] = bar_ref[s] * coef[0, s]

    damp_out[...] = damp_ref[...] * coef[0, r]
    image_scale, model_scale, search_scale = coef[1, r], coef[2, r], coef[4, r]
    search = search_ref[...]
    new = image_ref[...] * image_scale - model_ref[...] * model_scale
    model_out[...] = new
    search_out[...] = new - search * search_scale
    solution_out[...] = solution_ref[...] + search * coef[3, r]
    for a in range(PATCH):
        at = corner_ref[0] + a - piece * rows

        @pl.when((at >= 0) & (at < rows))
        def _():
            more = added_ref[0, pl.ds(a * clon, clon), :] * image_scale
            model_out[0, at] = model_out[0, at] + more
            search_out[0, at] = search_out[0, at] + more


def shifted(x, axis, step):
    count = lax.axis_size(axis)
    if step > 0:
        pairs = [(i, i + 1) for i in range(count - 1)]
    else:
        pairs = [(i + 1, i) for i in range(count - 1)]
    return lax.ppermute(x, axis, pairs)


def exchange(x):
    return lax.all_to_all(x, AXES, split_axis=0, concat_axis=0, tiled=True)


def per_device(
    sensitivity,
    block_ids,
    block_offsets,
    ray_counts,
    ray_vector,
    damping_vector,
    model_vector,
    solution,
    search,
    recurrence,
):
    lat_size, lon_size = lax.axis_size("lat"), lax.axis_size("lon")
    devices = lat_size * lon_size
    tiles, width, depth = sensitivity.shape[2:]
    blocks = block_offsets.shape[-1] - 1
    systems, clat, clon, _ = model_vector.shape
    columns = clat * clon
    cap = max(2 * ((tiles + devices - 1) // devices), 16 // systems)
    slots = devices * cap
    group = cap * systems
    cells_all = devices * columns * depth
    rows_all = devices * blocks * width + cells_all
    lanes = 128
    field = jax.ShapeDtypeStruct(model_vector.shape, F32)

    req, meta = call(
        functools.partial(request_body, columns.bit_length() - 1, cap, blocks),
        "request",
        (jax.ShapeDtypeStruct((devices, lanes), I32), jax.ShapeDtypeStruct((8, lanes), I32)),
        [vmem(), smem()],
        (vmem(), vmem()),
    )(block_ids, block_offsets)
    wanted = exchange(req.reshape(devices, 1, lanes)).reshape(devices, lanes)

    last, before = clat - 1, clat - 2
    south_msg = jnp.concatenate([model_vector[:, before:], damping_vector[:, last:]], axis=1)
    north_msg = jnp.concatenate([model_vector[:, :2], damping_vector[:, :1]], axis=1)
    north = shifted(south_msg, "lat", 1)
    south = shifted(north_msg, "lat", -1)

    def column_msg(near, beyond):
        return jnp.concatenate(
            [
                model_vector[:, :, near],
                model_vector[:, :, beyond],
                damping_vector[:, :, near],
                north[:, 1:2, near],
                south[:, 0:1, near],
                jnp.zeros((systems, 6, depth), F32),
            ],
            axis=1,
        )

    served, corner = call(
        functools.partial(serve_body, clat, cap),
        "serve",
        (jax.ShapeDtypeStruct((slots * systems, depth), BF16), jax.ShapeDtypeStruct((1,), I32)),
        [vmem(), pl.BlockSpec(memory_space=pl.ANY)],
        (vmem(), smem()),
        scratch=[
            pltpu.VMEM((systems, PATCH, clon, depth), F32),
            pltpu.VMEM((slots * systems, depth), F32),
            pltpu.SemaphoreType.DMA,
        ],
    )(wanted, model_vector)
    fetched = exchange(served.reshape(devices, group, depth)).reshape(slots * systems, depth)

    east_msg = column_msg(clon - 1, clon - 2)
    west_msg = column_msg(0, 1)
    west = shifted(east_msg, "lon", 1)
    east = shifted(west_msg, "lon", -1)

    ray_bar, terms = call(
        functools.partial(rays_body, cap, blocks),
        "rays",
        (jax.ShapeDtypeStruct(ray_vector.shape, F32), jax.ShapeDtypeStruct((slots, systems, depth), F32)),
        [smem(), smem(), smem(), vmem(), vmem(), vmem()],
        (vmem(), vmem()),
        scratch=[
            pltpu.VMEM((cap + 1, group, depth), BF16),
            pltpu.VMEM((blocks + 1, 16, width), BF16),
        ],
        flops=4 * tiles * width * depth * 16,
        moved=2 * tiles * width * depth,
    )(meta, ray_counts, recurrence, sensitivity, fetched, ray_vector)
    arrived = exchange(terms.reshape(devices, cap * systems, depth)).reshape(slots * systems, depth)

    lat_at, lon_at = lax.axis_index("lat"), lax.axis_index("lon")
    flags = jnp.stack(
        [lat_at > 0, lat_at < lat_size - 1, lon_at > 0, lon_at < lon_size - 1]
    ).astype(F32)
    slab = lambda shape: pl.BlockSpec((1,) + shape[1:], lambda r: (r,) + (0,) * (len(shape) - 1))
    patch_shape = (systems, PATCH * clon, depth)
    damp_bar, image, sums, patch, model_patch, chosen = call(
        functools.partial(dense_body, cap),
        "dense",
        (
            field,
            field,
            jax.ShapeDtypeStruct((1, lanes), F32),
            jax.ShapeDtypeStruct(patch_shape, F32),
            jax.ShapeDtypeStruct(patch_shape, F32),
            jax.ShapeDtypeStruct((PATCH * clon, slots), BF16),
        ),
        [
            smem(),
            smem(),
            smem(),
            pl.BlockSpec((devices, lanes), lambda r: (0, 0)),
            slab(ray_vector.shape),
            slab(field.shape),
            slab(field.shape),
            slab(north.shape),
            slab(south.shape),
            slab(west.shape),
            slab(east.shape),
            slab(west_msg.shape),
            slab(east_msg.shape),
        ],
        (
            slab(field.shape),
            slab(field.shape),
            pl.BlockSpec((1, lanes), lambda r: (0, 0)),
            slab(patch_shape),
            slab(patch_shape),
            pl.BlockSpec((PATCH * clon, slots), lambda r: (0, 0)),
        ),
        scratch=[
            pltpu.VMEM((clat + 2, clon, depth), F32),
            pltpu.VMEM((clat, depth), F32),
            pltpu.VMEM((clat, depth), F32),
        ],
        grid=(systems,),
        flops=40 * systems * columns * depth,
        moved=16 * systems * columns * depth,
    )(
        flags,
        recurrence,
        corner,
        wanted,
        ray_bar,
        model_vector,
        damping_vector,
        north,
        south,
        west,
        east,
        west_msg,
        east_msg,
    )

    added, parts = call(
        combine_body,
        "combine",
        (jax.ShapeDtypeStruct(patch_shape, F32), jax.ShapeDtypeStruct((devices, lanes), F32)),
        [vmem()] * 5,
        (vmem(), vmem()),
    )(arrived, chosen, patch, model_patch, sums)
    every = exchange(parts.reshape(devices, 1, lanes)).reshape(devices, lanes)

    pieces = 2
    rows = clat // pieces
    whole = lambda shape: pl.BlockSpec(shape, lambda r, p: (0,) * len(shape))
    part = pl.BlockSpec((1, rows, clon, depth), lambda r, p: (r, p, 0, 0))
    outs = call(
        functools.partial(finish_body, float(rows_all), float(cells_all)),
        "finish",
        (
            jax.ShapeDtypeStruct(ray_vector.shape, F32),
            field,
            field,
            field,
            field,
            jax.ShapeDtypeStruct(recurrence.shape, F32),
        ),
        [
            smem(),
            whole((devices, lanes)),
            whole(recurrence.shape),
            whole(ray_vector.shape),
            pl.BlockSpec((1,) + patch_shape[1:], lambda r, p: (r, 0, 0)),
        ]
        + [part] * 5,
        (whole(ray_vector.shape), part, part, part, part, whole(recurrence.shape)),
        scratch=[pltpu.SMEM((8, systems), F32)],
        grid=(systems, pieces),
        flops=10 * systems * columns * depth,
        moved=36 * systems * columns * depth,
    )(corner, every, recurrence, ray_bar, added, image, model_vector, damp_bar, solution, search)
    return outs


def solution(mesh):
    fields = P(None, "lat", "lon", None)
    return jax.shard_map(
        per_device,
        mesh=mesh,
        in_specs=(
            P("lat", "lon", None, None, None),
            P("lat", "lon", None),
            P("lat", "lon", None),
            P("lat", "lon"),
            fields,
            fields,
            fields,
            fields,
            fields,
            P(),
        ),
        out_specs=(fields, fields, fields, fields, fields, P()),
        check_vma=False,
    )
```

time: 168 us -> 104 us (0.62)
  other arithmetic: 47.7 us -> 0.85 us
  Pallas kernels: 0 us -> 27.2 us
  blocking collectives: 44.1 us -> 17.6 us
  starting transfers between devices: 36.4 us -> 26.5 us
  local copies, waits for them, and re-layouts: 28.8 us -> 23.7 us
  matrix products: 4.7 us -> 0 us
  waiting for transfers between devices: 3.41 us -> 6.07 us
    psum x1 -> x0, blocking collectives: 44.1 us -> none  [per_device(): lax.psum((residual_sq, image_sq, cross_sum, model_sq), ('lat', 'lon'))]
    pallas_call x0 -> x6, Pallas kernels: none -> 27.2 us  [the longest x1 14.3 us: per_device(): call(functools.partial(dense_body, cap), 'dense', (field, field, jax.Shap...]
    reduce_sum x4 -> x0, other arithmetic: 18 us -> none  [the longest x1 9.79 us: per_device(): jnp.sum(damp_bar * damp_bar, axis=(1, 2, 3))]
    all_to_all x0 -> x1, blocking collectives: none -> 17.6 us  [exchange(): return lax.all_to_all(x, AXES, split_axis=0, concat_axis=0, tiled=True)]
    scatter-add x1 -> x0, other arithmetic: 15.4 us -> none  [per_device(): jnp.zeros((columns_dev + 1, systems, depth), jnp.float32).at[wanted]]
    unnamed x35 -> x42, local copies, waits for them, and re-layouts: 9.78 us -> 18.6 us
    ppermute x8 -> x4, starting transfers between devices: 17.7 us -> 9.29 us  [shifted(): return lax.ppermute(x, axis, pairs)]
    scatter x2 -> x0, local copies, waits for them, and re-layouts: 7.65 us -> none  [the longest x1 6.89 us: per_device(): jnp.zeros((devices * capacity, systems, depth), jnp.float32).at[slot_index]]
  transfers between devices with their start and end apart: 11 -> 7, of which waited for: 3 -> 1; matrix products, arithmetic and copies ran while one was open for 33% -> 6% of each run, Pallas kernels for 0% -> 19%
where the time goes in v2:
time: 104 us; the launch traced here: 103 us
  Pallas kernels  27.2 us (26%)
  starting transfers between devices  26.5 us (25%)
  local copies, waits for them, and re-layouts  23.7 us (23%)
  blocking collectives  17.6 us (17%)
  waiting for transfers between devices  6.07 us (6%)
  between operations  1.56 us (2%)
    unnamed x42, local copies, waits for them, and re-layouts  18.6 us
    all_to_all x1, blocking collectives, exchange(): return lax.all_to_all(x, AXES, split_axis=0, concat_axis=0, tiled=True)  17.6 us
    all_to_all x3, starting transfers between devices, exchange(): return lax.all_to_all(x, AXES, split_axis=0, concat_axis=0, tiled=True)  17.2 us
    pallas_call x1, Pallas kernels, per_device(): call(functools.partial(dense_body, cap), 'dense', (field, field, jax.Shap...  14.3 us
    ppermute x4, starting transfers between devices, shifted(): return lax.ppermute(x, axis, pairs)  9.29 us
    all_to_all x3, waiting for transfers between devices, exchange(): return lax.all_to_all(x, AXES, split_axis=0, concat_axis=0, tiled=True)  6.06 us
    pallas_call x1, Pallas kernels, per_device(): call(functools.partial(finish_body, float(rows_all), float(cells_all)), '...  5.71 us
    pallas_call x1, Pallas kernels, per_device(): call(functools.partial(rays_body, cap, blocks), 'rays', (jax.ShapeDtypeSt...  4.23 us
  transfers between devices with their start and end apart: 7, of which 1 were waited for; matrix products, arithmetic and copies ran while one was open for 6% of the time, Pallas kernels for 19%

profile of v2, /device:TPU:0, one launch (start us, length us, event | category | flops | bytes accessed | tf_op | source)
XLA Modules:
  0.0 103.5 jit_solution(5978902955991442901)
XLA Ops:
  0.6 0.0 copy-start
  0.6 0.0 copy-start.17
  0.7 0.8 copy-done.17
  1.4 0.0 copy-start.18
  1.5 0.7 copy-done.18
  2.1 1.3 %request.1 = (s32[32,128]{1,0:T(8,128)}, s32[8,128]{1,0:T(8,128)S(1)}) custom-call(s32[1,1,60]{2,1,0:T(1,128)S(1)} %copy-done.17, s32[1,1,4]{2,1,0:T(1,128)S(1)} %copy-done.18), custom_call_target="tpu_custom_call" | custom-call | tf_op jit(solution)/shard_map/request/pallas_call | solution.py:408
  3.5 7.3 %all-to-all-start = ((s32[32,1,128]{2,1,0:T(1,128)}), s32[32,1,128]{2,1,0:T(1,128)S(1)}, u32[]{:S(2)}, u32[]{:S(2)}) async-start(s32[32,1,128]{2,1,0:T(1,128)} %bitcast.1), calls=%async_computation | async-start | bytes 32768 | tf_op jit(solution)/shard_map/all_to_all | solution.py:379
  10.8 0.9 fusion.3
  11.7 1.0 fusion.2
  12.7 0.1 copy.46
  12.8 0.0 copy-start.13
  12.8 0.0 copy-start.14
  12.9 3.7 %collective-permute-start = (f32[4,3,32,128]{3,0,2,1:T(4,128)S(1)}, f32[4,3,32,128]{3,0,2,1:T(4,128)S(1)}, u32[]{:S(2)}, u32[]{:S(2)}) collective-permute-start(f32[4,3,32,128]{3,0,2,1:T(4,128)S(1)} %pad_maximum_fusion), channel_id=1, source_target_pairs={{0,8},{8,16},{16,24},{1,9},{9,17},{17,25},{2,10},{10,18},{18,26},{... | collective-permute-start | bytes 589832 | tf_op jit(solution)/shard_map/ppermute | solution.py:375
  16.6 0.1 copy.48
  16.7 0.7 pad_maximum_fusion.1
  17.4 1.3 %collective-permute-start.1 = (f32[4,3,32,128]{3,0,2,1:T(4,128)}, f32[4,3,32,128]{3,0,2,1:T(4,128)}, u32[]{:S(2)}, u32[]{:S(2)}) collective-permute-start(f32[4,3,32,128]{3,0,2,1:T(4,128)} %pad_maximum_fusion.1), channel_id=1, source_target_pairs={{8,0},{16,8},{24,16},{9,1},{17,9},{25,17},{10,2},{18,10},{26,18},{... | collective-permute-start | bytes 589832 | tf_op jit(solution)/shard_map/ppermute | solution.py:375
  18.7 0.0 all-to-all-done
  18.7 0.0 copy-done
  18.7 1.2 %serve.1 = (bf16[512,128]{1,0:T(8,128)(2,1)}, s32[1]{0:T(128)}) custom-call(s32[32,128]{1,0:T(8,128)S(1)} %bitcast.44, f32[4,32,32,128]{3,2,1,0:T(8,128)S(1)} %copy-done), custom_call_target="tpu_custom_call" | custom-call | tf_op jit(solution)/shard_map/serve/pallas_call | solution.py:436
  19.9 7.4 %all-to-all-start.1 = ((bf16[32,16,128]{2,1,0:T(8,128)(2,1)}), bf16[32,16,128]{2,1,0:T(8,128)(2,1)S(1)}, u32[]{:S(2)}, u32[]{:S(2)}) async-start(bf16[32,16,128]{2,1,0:T(8,128)(2,1)} %bitcast.3), calls=%async_computation.1 | async-start | bytes 262144 | tf_op jit(solution)/shard_map/all_to_all | solution.py:379
  27.3 0.2 fusion.1
  28.2 1.3 %fusion = (f32[4,32,1,128]{3,2,1,0:T(1,128)S(1)}, f32[4,32,1,128]{3,2,1,0:T(1,128)S(1)}) fusion(f32[4,32,32,128]{3,2,1,0:T(8,128)} %damp_ref.1), kind=kLoop, calls=%fused_computation.3 | loop fusion | bytes 262144 | tf_op jit(solution)/shard_map/slice | solution.py:428
  29.5 6.1 %all-to-all-done.1 = bf16[32,16,128]{2,1,0:T(8,128)(2,1)S(1)} async-done(((bf16[32,16,128]{2,1,0:T(8,128)(2,1)}), bf16[32,16,128]{2,1,0:T(8,128)(2,1)S(1)}, u32[]{:S(2)}, u32[]{:S(2)}) %all-to-all-start.1) | async-done | bytes 131104 | tf_op jit(solution)/shard_map/all_to_all | solution.py:379
  35.5 0.0 copy-done.13
  35.5 0.0 copy-done.14
  35.5 0.0 copy-start.1
  35.5 2.1 %copy-done.1 = bf16[1,1,60,256,128]{4,3,2,1,0:T(8,128)(2,1)S(1)} copy-done((bf16[1,1,60,256,128]{4,3,2,1,0:T(8,128)(2,1)S(1)}, bf16[1,1,60,256,128]{4,3,2,1,0:T(8,128)(2,1)}, u32[]{:S(2)}) %copy-start.1) | copy-done | bytes 3932184
  37.7 4.2 %rays.1 = (f32[4,1,1,768]{3,2,1,0:T(1,128)S(1)}, f32[128,4,128]{2,1,0:T(4,128)}) custom-call(s32[8,128]{1,0:T(8,128)S(1)} %get-tuple-element.22.meta_ref, s32[1,1]{1,0:T(1,128)S(6)} %copy.56.count_ref, f32[3,4]{1,0:T(4,128)S(1)} %copy-done.13, bf16[1,1,60,256,128]{4,3,2,1,0:T(8,128)(2,1)S(1)} %copy-done.1, bf16[512,128]{1,0:T(8,128)(2,1)S(1)} %bitcast.43, ...), custom_call_target="tpu_custom_call" | custom-call | flops 125829120 | bytes 3932160 | tf_op jit(solution)/shard_map/rays/pallas_call | solution.py:455
  41.9 2.6 %all-to-all-start.2 = ((f32[32,16,128]{2,1,0:T(8,128)}), f32[32,16,128]{2,1,0:T(8,128)S(1)}, u32[]{:S(2)}, u32[]{:S(2)}) async-start(f32[32,16,128]{2,1,0:T(8,128)} %bitcast.5), calls=%async_computation.2 | async-start | bytes 524288 | tf_op jit(solution)/shard_map/all_to_all | solution.py:379
  44.5 0.0 collective-permute-done
  44.5 0.0 collective-permute-done.1
  44.5 0.7 fusion.4
  45.2 1.3 %collective-permute-start.3 = (f32[4,104,128]{2,1,0:T(8,128)S(1)}, f32[4,104,128]{2,1,0:T(8,128)S(1)}, u32[]{:S(2)}, u32[]{:S(2)}) collective-permute-start(f32[4,104,128]{2,1,0:T(8,128)S(1)} %concatenate.15.westmost_ref), channel_id=1, source_target_pairs={{1,0},{2,1},{3,2},{4,3},{5,4},{6,5},{7,6},{9,8},{10,9},{11,10},{12... | collective-permute-start | bytes 638984 | tf_op jit(solution)/shard_map/ppermute | solution.py:375
  46.6 3.0 %collective-permute-start.2 = (f32[4,104,128]{2,1,0:T(8,128)S(1)}, f32[4,104,128]{2,1,0:T(8,128)S(1)}, u32[]{:S(2)}, u32[]{:S(2)}) collective-permute-start(f32[4,104,128]{2,1,0:T(8,128)S(1)} %concatenate.14.eastmost_ref), channel_id=1, source_target_pairs={{0,1},{1,2},{2,3},{3,4},{4,5},{5,6},{6,7},{8,9},{9,10},{10,11},{11... | collective-permute-start | bytes 638984 | tf_op jit(solution)/shard_map/ppermute | solution.py:375
  49.6 0.1 add_convert_fusion.flag_ref
  49.7 0.9 copy.44.south_ref
  50.7 0.0 collective-permute-done.3.east_ref
  50.7 0.0 collective-permute-done.2.west_ref
  50.7 0.0 copy-start.9
  50.7 0.7 copy-done.9
  51.4 0.0 copy-start.2
  51.4 1.6 %copy-done.2 = f32[4,32,32,128]{3,2,1,0:T(8,128)S(1)} copy-done((f32[4,32,32,128]{3,2,1,0:T(8,128)S(1)}, f32[4,32,32,128]{3,2,1,0:T(8,128)}, u32[]{:S(2)}) %copy-start.2) | copy-done | bytes 2097176
  53.0 0.0 copy-start.10
  53.0 0.9 copy-done.10
  53.9 14.3 %dense.1 = (f32[4,32,32,128]{3,2,1,0:T(8,128)S(1)}, f32[4,32,32,128]{3,2,1,0:T(8,128)S(1)}, f32[1,128]{1,0:T(1,128)S(1)}, f32[4,128,128]{2,1,0:T(8,128)S(1)}, f3...) custom-call(f32[4]{0:T(128)S(1)} %add_convert_fusion.flag_ref, f32[3,4]{1,0:T(4,128)S(1)} %copy-done.13, ...), custom_call_target="tpu_custom_call" | custom-call | flops 20971520 | bytes 8388608 | tf_op jit(solution)/shard_map/dense/pallas_call | solution.py:476
  68.2 0.0 copy-start.5
  68.2 1.3 %copy-done.5 = f32[4,32,32,128]{3,2,1,0:T(8,128)} copy-done((f32[4,32,32,128]{3,2,1,0:T(8,128)}, f32[4,32,32,128]{3,2,1,0:T(8,128)S(1)}, u32[]{:S(2)}) %copy-start.5) | copy-done | bytes 2097176
  69.5 0.0 copy-start.7
  69.5 1.3 %copy-done.7 = f32[4,32,32,128]{3,2,1,0:T(8,128)} copy-done((f32[4,32,32,128]{3,2,1,0:T(8,128)}, f32[4,32,32,128]{3,2,1,0:T(8,128)S(1)}, u32[]{:S(2)}) %copy-start.7) | copy-done | bytes 2097176
  70.8 0.0 copy-start.11
  70.8 0.6 copy-done.11
  71.5 0.0 copy-start.15
  71.5 0.5 copy-done.15
  72.0 0.0 all-to-all-done.2
  72.0 0.0 copy-start.12
  72.0 0.8 copy-done.12
  72.7 0.7 copy-done.16
  73.4 0.4 combine.1
  73.8 17.6 %all_to_all.20 = f32[32,1,128]{2,1,0:T(1,128)S(1)} all-to-all(f32[32,1,128]{2,1,0:T(1,128)S(1)} %bitcast.47), channel_id=1, replica_groups=mesh['lat'=4,'lon'=8] {'lat','lon'}, dimensions={0} | all-to-all | bytes 32768 | tf_op jit(solution)/shard_map/all_to_all | solution.py:379
  91.4 1.6 %copy-done.3 = f32[4,32,32,128]{3,2,1,0:T(8,128)S(1)} copy-done((f32[4,32,32,128]{3,2,1,0:T(8,128)S(1)}, f32[4,32,32,128]{3,2,1,0:T(8,128)}, u32[]{:S(2)}) %copy-start.3) | copy-done | bytes 2097176
  93.0 1.6 %copy-done.4 = f32[4,32,32,128]{3,2,1,0:T(8,128)S(1)} copy-done((f32[4,32,32,128]{3,2,1,0:T(8,128)S(1)}, f32[4,32,32,128]{3,2,1,0:T(8,128)}, u32[]{:S(2)}) %copy-start.4) | copy-done | bytes 2097176
  94.6 1.6 %copy-done.6 = f32[4,32,32,128]{3,2,1,0:T(8,128)S(1)} copy-done((f32[4,32,32,128]{3,2,1,0:T(8,128)S(1)}, f32[4,32,32,128]{3,2,1,0:T(8,128)}, u32[]{:S(2)}) %copy-start.6) | copy-done | bytes 2097176
  96.2 1.6 %copy-done.8 = f32[4,32,32,128]{3,2,1,0:T(8,128)S(1)} copy-done((f32[4,32,32,128]{3,2,1,0:T(8,128)S(1)}, f32[4,32,32,128]{3,2,1,0:T(8,128)}, u32[]{:S(2)}) %copy-start.8) | copy-done | bytes 2097176
  97.8 5.7 %finish.1 = (f32[4,1,1,768]{3,2,1,0:T(1,128)}, f32[4,32,32,128]{3,2,1,0:T(8,128)}, f32[4,32,32,128]{3,2,1,0:T(8,128)}, f32[4,32,32,128]{3,2,1,0:T(8,128)}, f32[4,32,32,128]{3,2,1,0:T(8,128)}, /*index=5*/f32[3,4]{1,0:T(4,128)}) custom-call(s32[1]{0:T(128)} %get-tuple-element.21.corner_ref, f32[32,128]{1,0:T(8,128)S(1)} %bitcast.46, f32[3,4]{1,0:T(4,128)S(1)} %copy-done.13, ...), custom_call_target="tpu_custom_call" | custom-call | flops 5242880 | bytes 18874368 | tf_op jit(solution)/shard_map/finish/pallas_call | solution.py:547
  (13 shorter events, 0.2 us)
Async XLA Ops:
  0.6 18.1 %copy-start = (f32[4,32,32,128]{3,2,1,0:T(8,128)S(1)}, f32[4,32,32,128]{3,2,1,0:T(8,128)}, u32[]{:S(2)}) copy-start(f32[4,32,32,128]{3,2,1,0:T(8,128)} %model_ref.5) | copy-start | bytes 6291460
  0.6 0.8 copy-start.17
  1.4 0.7 copy-start.18
  3.5 15.3 %all-to-all-start = ((s32[32,1,128]{2,1,0:T(1,128)}), s32[32,1,128]{2,1,0:T(1,128)S(1)}, u32[]{:S(2)}, u32[]{:S(2)}) async-start(s32[32,1,128]{2,1,0:T(1,128)} %bitcast.1), calls=%async_computation | async-start | bytes 32768 | tf_op jit(solution)/shard_map/all_to_all | solution.py:379
  12.8 22.8 %copy-start.13 = (f32[3,4]{1,0:T(4,128)S(1)}, f32[3,4]{1,0:T(4,128)}, u32[]{:S(2)}) copy-start(f32[3,4]{1,0:T(4,128)} %rec_ref.5) | copy-start | bytes 148
  12.8 22.7 %copy-start.14 = (f32[4,1,1,768]{3,2,1,0:T(1,128)S(1)}, f32[4,1,1,768]{3,2,1,0:T(1,128)}, u32[]{:S(2)}) copy-start(f32[4,1,1,768]{3,2,1,0:T(1,128)} %old_ref.1) | copy-start | bytes 36868
  12.9 31.6 %collective-permute-start = (f32[4,3,32,128]{3,0,2,1:T(4,128)S(1)}, f32[4,3,32,128]{3,0,2,1:T(4,128)S(1)}, u32[]{:S(2)}, u32[]{:S(2)}) collective-permute-start(f32[4,3,32,128]{3,0,2,1:T(4,128)S(1)} %pad_maximum_fusion), channel_id=1, source_target_pairs={{0,8},{8,16},{16,24},{1,9},{9,17},{17,25},{2,10},{10,18},{18,26},{... | collective-permute-start | bytes 589832 | tf_op jit(solution)/shard_map/ppermute | solution.py:375
  17.4 27.1 %collective-permute-start.1 = (f32[4,3,32,128]{3,0,2,1:T(4,128)}, f32[4,3,32,128]{3,0,2,1:T(4,128)}, u32[]{:S(2)}, u32[]{:S(2)}) collective-permute-start(f32[4,3,32,128]{3,0,2,1:T(4,128)} %pad_maximum_fusion.1), channel_id=1, source_target_pairs={{8,0},{16,8},{24,16},{9,1},{17,9},{25,17},{10,2},{18,10},{26,18},{... | collective-permute-start | bytes 589832 | tf_op jit(solution)/shard_map/ppermute | solution.py:375
  19.9 15.6 %all-to-all-start.1 = ((bf16[32,16,128]{2,1,0:T(8,128)(2,1)}), bf16[32,16,128]{2,1,0:T(8,128)(2,1)S(1)}, u32[]{:S(2)}, u32[]{:S(2)}) async-start(bf16[32,16,128]{2,1,0:T(8,128)(2,1)} %bitcast.3), calls=%async_computation.1 | async-start | bytes 262144 | tf_op jit(solution)/shard_map/all_to_all | solution.py:379
  35.5 2.1 %copy-start.1 = (bf16[1,1,60,256,128]{4,3,2,1,0:T(8,128)(2,1)S(1)}, bf16[1,1,60,256,128]{4,3,2,1,0:T(8,128)(2,1)}, u32[]{:S(2)}) copy-start(bf16[1,1,60,256,128]{4,3,2,1,0:T(8,128)(2,1)} %tiles_ref.1) | copy-start | bytes 11796484
  41.9 30.1 %all-to-all-start.2 = ((f32[32,16,128]{2,1,0:T(8,128)}), f32[32,16,128]{2,1,0:T(8,128)S(1)}, u32[]{:S(2)}, u32[]{:S(2)}) async-start(f32[32,16,128]{2,1,0:T(8,128)} %bitcast.5), calls=%async_computation.2 | async-start | bytes 524288 | tf_op jit(solution)/shard_map/all_to_all | solution.py:379
  45.2 5.4 %collective-permute-start.3 = (f32[4,104,128]{2,1,0:T(8,128)S(1)}, f32[4,104,128]{2,1,0:T(8,128)S(1)}, u32[]{:S(2)}, u32[]{:S(2)}) collective-permute-start(f32[4,104,128]{2,1,0:T(8,128)S(1)} %concatenate.15.westmost_ref), channel_id=1, source_target_pairs={{1,0},{2,1},{3,2},{4,3},{5,4},{6,5},{7,6},{9,8},{10,9},{11,10},{12... | collective-permute-start | bytes 638984 | tf_op jit(solution)/shard_map/ppermute | solution.py:375
  46.6 4.1 %collective-permute-start.2 = (f32[4,104,128]{2,1,0:T(8,128)S(1)}, f32[4,104,128]{2,1,0:T(8,128)S(1)}, u32[]{:S(2)}, u32[]{:S(2)}) collective-permute-start(f32[4,104,128]{2,1,0:T(8,128)S(1)} %concatenate.14.eastmost_ref), channel_id=1, source_target_pairs={{0,1},{1,2},{2,3},{3,4},{4,5},{5,6},{6,7},{8,9},{9,10},{10,11},{11... | collective-permute-start | bytes 638984 | tf_op jit(solution)/shard_map/ppermute | solution.py:375
  50.7 0.7 copy-start.9
  51.4 1.6 %copy-start.2 = (f32[4,32,32,128]{3,2,1,0:T(8,128)S(1)}, f32[4,32,32,128]{3,2,1,0:T(8,128)}, u32[]{:S(2)}) copy-start(f32[4,32,32,128]{3,2,1,0:T(8,128)} %damp_ref.1) | copy-start | bytes 6291460
  53.0 0.9 copy-start.10
  68.2 1.3 %copy-start.5 = (f32[4,32,32,128]{3,2,1,0:T(8,128)}, f32[4,32,32,128]{3,2,1,0:T(8,128)S(1)}, u32[]{:S(2)}) copy-start(f32[4,32,32,128]{3,2,1,0:T(8,128)S(1)} %get-tuple-element.33.damp_ref) | copy-start | bytes 6291460
  69.5 1.3 %copy-start.7 = (f32[4,32,32,128]{3,2,1,0:T(8,128)}, f32[4,32,32,128]{3,2,1,0:T(8,128)S(1)}, u32[]{:S(2)}) copy-start(f32[4,32,32,128]{3,2,1,0:T(8,128)S(1)} %get-tuple-element.32.image_ref) | copy-start | bytes 6291460
  70.8 0.6 copy-start.11
  71.5 0.5 copy-start.15
  72.0 0.8 copy-start.12
  72.7 0.7 copy-start.16
  91.4 1.6 %copy-start.3 = (f32[4,32,32,128]{3,2,1,0:T(8,128)S(1)}, f32[4,32,32,128]{3,2,1,0:T(8,128)}, u32[]{:S(2)}) copy-start(f32[4,32,32,128]{3,2,1,0:T(8,128)} %solution_ref.1) | copy-start | bytes 6291460
  93.0 1.6 %copy-start.4 = (f32[4,32,32,128]{3,2,1,0:T(8,128)S(1)}, f32[4,32,32,128]{3,2,1,0:T(8,128)}, u32[]{:S(2)}) copy-start(f32[4,32,32,128]{3,2,1,0:T(8,128)} %search_ref.1) | copy-start | bytes 6291460
  94.6 1.6 %copy-start.6 = (f32[4,32,32,128]{3,2,1,0:T(8,128)S(1)}, f32[4,32,32,128]{3,2,1,0:T(8,128)}, u32[]{:S(2)}) copy-start(f32[4,32,32,128]{3,2,1,0:T(8,128)} %copy-done.5) | copy-start | bytes 6291460
  96.2 1.6 %copy-start.8 = (f32[4,32,32,128]{3,2,1,0:T(8,128)S(1)}, f32[4,32,32,128]{3,2,1,0:T(8,128)}, u32[]{:S(2)}) copy-start(f32[4,32,32,128]{3,2,1,0:T(8,128)} %copy-done.7) | copy-start | bytes 6291460

commit v3 on v2

v3 whole, which is shorter than its diff:
```python
import functools

import jax
import jax.numpy as jnp
from jax import lax
from jax.experimental import pallas as pl
from jax.experimental.pallas import tpu as pltpu
from jax.sharding import PartitionSpec as P

DAMP_WEIGHT = 0.15
EPSILON = 1e-05
AXES = ("lat", "lon")
PATCH = 4
F32, BF16, I32 = jnp.float32, jnp.bfloat16, jnp.int32


def iota(shape, dim):
    return lax.broadcasted_iota(I32, shape, dim)


def vmem():
    return pl.BlockSpec(memory_space=pltpu.VMEM)


def hbm():
    return pl.BlockSpec(memory_space=pltpu.HBM)


def far(x):
    return pltpu.with_memory_space_constraint(x, pltpu.HBM)


def smem():
    return pl.BlockSpec(memory_space=pltpu.SMEM)


def call(body, name, out_shape, in_specs, out_specs, scratch=(), grid=(), mib=16, flops=0, moved=0):
    return pl.pallas_call(
        body,
        name=name,
        grid=grid,
        out_shape=out_shape,
        in_specs=in_specs,
        out_specs=out_specs,
        scratch_shapes=list(scratch),
        compiler_params=pltpu.CompilerParams(vmem_limit_bytes=mib * 2**20),
        cost_estimate=pl.CostEstimate(flops=flops, bytes_accessed=moved, transcendentals=0),
    )


def load_body(
    shift, blocks, ids_ref, off_ref, count_ref, model_in, damp_in, model_out, damp_out, north_ref, south_ref, meta_ref, sems
):
    last = model_in.shape[1] - 1
    pairs = (
        (model_in.at[:, pl.ds(last - 1, 2)], south_ref.at[:, pl.ds(0, 2)]),
        (damp_in.at[:, pl.ds(last, 1)], south_ref.at[:, pl.ds(2, 1)]),
        (model_in.at[:, pl.ds(0, 2)], north_ref.at[:, pl.ds(0, 2)]),
        (damp_in.at[:, pl.ds(0, 1)], north_ref.at[:, pl.ds(2, 1)]),
        (model_in, model_out),
        (damp_in, damp_out),
    )
    copies = [pltpu.make_async_copy(a, b, sems.at[i]) for i, (a, b) in enumerate(pairs)]
    for copy in copies:
        copy.start()
    tiles = ids_ref.shape[-1]
    lanes = 128
    ids = jnp.concatenate([ids_ref[0], jnp.full((1, lanes - tiles), -1, I32)], axis=1)
    owner = lax.shift_right_arithmetic(ids, shift)
    square = (lanes, lanes)
    down, across = iota(square, 0), iota(square, 1)
    owner_f = jnp.broadcast_to(owner.astype(F32), square)
    owner_col = jnp.sum(jnp.where(down == across, owner_f, 0.0), axis=1, keepdims=True)
    same = jnp.where((owner_f == owner_col) & (down < across), 1.0, 0.0)
    rank = jnp.sum(same, axis=0, keepdims=True).astype(I32)
    lane = iota((1, lanes), 1)
    block = jnp.zeros((1, lanes), I32)
    for b in range(1, blocks + 1):
        block = block + (lane >= off_ref[0, 0, b]).astype(I32)
    count = jnp.full((1, lanes), count_ref[0, 0], I32)
    meta_ref[...] = jnp.concatenate([owner, rank, block, count] + [owner] * 4, axis=0)
    for copy in copies:
        copy.wait()


def wanted_column(wanted, cap):
    devices, lanes = wanted.shape
    rows = devices * cap
    spread = jnp.broadcast_to(wanted[:, None, :], (devices, cap, lanes)).reshape(rows, lanes)
    pick = iota((rows, lanes), 1) == (iota((rows, lanes), 0) & (cap - 1))
    return jnp.sum(jnp.where(pick, spread, 0.0), axis=1, keepdims=True)


def serve_body(cap, lists_ref, model_ref, served_ref, wanted_ref, corner_ref, mixed):
    systems, clat, clon, depth = model_ref.shape
    devices, tiles = lists_ref.shape
    lanes = 128
    shift = (clat * clon).bit_length() - 1
    me = lax.axis_index("lat") * lax.axis_size("lon") + lax.axis_index("lon")
    ids = jnp.concatenate([lists_ref[...], jnp.full((devices, lanes - tiles), -1, I32)], axis=1)
    column = ids - lax.shift_left(me, shift)
    mine = (column >= 0) & (column < clat * clon) & (ids >= 0)
    first = jnp.min(jnp.where(mine, column, clat * clon))
    corner = jnp.minimum(lax.shift_right_logical(first, clon.bit_length() - 1), clat - PATCH)
    corner_ref[0] = corner
    ahead = (iota((lanes, lanes), 0) < iota((lanes, lanes), 1)).astype(F32).astype(BF16)
    rank = jnp.dot(mine.astype(F32).astype(BF16), ahead, preferred_element_type=F32)
    value = (column - corner * clon + 1).astype(F32)
    at = iota((devices, lanes), 1)
    wanted = jnp.zeros((devices, lanes), F32)
    for c in range(cap):
        picked = jnp.sum(jnp.where(mine & (rank == c), value, 0.0), axis=1, keepdims=True)
        wanted = jnp.where(at == c, picked, wanted)
    wanted_ref[...] = wanted
    target = wanted_column(wanted, cap).astype(I32) - 1
    rows = target.shape[0]
    width = PATCH * clon
    chosen = (jnp.broadcast_to(target, (rows, width)) == iota((rows, width), 1)).astype(F32).astype(BF16)
    for r in range(systems):
        table = model_ref[r, pl.ds(corner, PATCH)].reshape(width, depth).astype(BF16)
        mixed[pl.ds(r, rows, stride=systems), :] = jnp.dot(chosen, table, preferred_element_type=F32)
    served_ref[...] = mixed[...].astype(BF16)


def columns_body(clat, clon, model_ref, damp_ref, north_ref, south_ref, east_ref, west_ref):
    systems, _, depth = model_ref.shape
    for r in range(systems):
        for out, near, beyond in ((east_ref, clon - 1, clon - 2), (west_ref, 0, 1)):
            out[r, 0:clat] = model_ref[r, pl.ds(near, clat, stride=clon), :]
            out[r, clat : 2 * clat] = model_ref[r, pl.ds(beyond, clat, stride=clon), :]
            out[r, 2 * clat : 3 * clat] = damp_ref[r, pl.ds(near, clat, stride=clon), :]
            out[r, 3 * clat :] = jnp.concatenate(
                [
                    north_ref[r, 1, near : near + 1],
                    south_ref[r, 0, near : near + 1],
                    jnp.zeros((6, depth), F32),
                ],
                axis=0,
            )


def six(x, north, south, west, east):
    sub, lane = iota(x.shape, 0), iota(x.shape, 1)
    rows, depth = x.shape
    left = jnp.where(sub == 0, jnp.broadcast_to(west, x.shape), pltpu.roll(x, 1, 0))
    right = jnp.where(sub == rows - 1, jnp.broadcast_to(east, x.shape), pltpu.roll(x, rows - 1, 0))
    above = jnp.where(lane == 0, 0.0, pltpu.roll(x, 1, 1))
    below = jnp.where(lane == depth - 1, 0.0, pltpu.roll(x, depth - 1, 1))
    beside = north + south + left + right + above + below
    return DAMP_WEIGHT * (6.0 * x - beside)


def fold(x):
    parts = [x[i * 8 : (i + 1) * 8] for i in range(x.shape[0] // 8)]
    return functools.reduce(lambda a, b: a + b, parts)


def place(row, lane, value):
    return row + jnp.where(iota(row.shape, 1) == lane, jnp.broadcast_to(value, row.shape), 0.0)


STEP = 8


def damp_body(
    rec_ref,
    model_ref,
    damp_ref,
    north_ref,
    south_ref,
    west_ref,
    east_ref,
    westmost_ref,
    eastmost_ref,
    bar_out,
    north_out,
    south_out,
    west_out,
    east_out,
    sums_out,
):
    systems, clat, clon, depth = model_ref.shape
    lat_at, lon_at = lax.axis_index("lat"), lax.axis_index("lon")
    has_north = (lat_at > 0).astype(F32)
    has_south = (lat_at < lax.axis_size("lat") - 1).astype(F32)
    has_west = (lon_at > 0).astype(F32)
    has_east = (lon_at < lax.axis_size("lon") - 1).astype(F32)
    corner_n, corner_s = 3 * clat, 3 * clat + 1

    def system(r, row):
        alpha = rec_ref[0, r]

        def side(ref, own, flag):
            x, beyond, old = ref[r, 0:clat], ref[r, clat : 2 * clat], ref[r, 2 * clat : 3 * clat]
            upper, lower = ref[r, corner_n : corner_n + 1], ref[r, corner_s : corner_s + 1]
            return (six(x, beyond, own, upper, lower) - alpha * old) * flag

        west_out[r] = side(west_ref, westmost_ref[r, 0:clat], has_west)
        east_out[r] = side(east_ref, eastmost_ref[r, 0:clat], has_east)
        north_out[r] = has_north * (
            six(
                north_ref[r, 1],
                north_ref[r, 0],
                model_ref[r, 0],
                west_ref[r, corner_n : corner_n + 1],
                east_ref[r, corner_n : corner_n + 1],
            )
            - alpha * north_ref[r, 2]
        )
        south_out[r] = has_south * (
            six(
                south_ref[r, 0],
                model_ref[r, clat - 1],
                south_ref[r, 1],
                west_ref[r, corner_s : corner_s + 1],
                east_ref[r, corner_s : corner_s + 1],
            )
            - alpha * south_ref[r, 2]
        )

        def chunk(k, acc):
            bar_sq, model_sq = acc
            base = k * STEP
            for j in range(STEP):
                i = base + j
                x = model_ref[r, i]
                if j == 0:
                    north = jnp.where(k > 0, model_ref[r, jnp.maximum(i - 1, 0)], north_ref[r, 1])
                else:
                    north = model_ref[r, i - 1]
                if j == STEP - 1:
                    more = jnp.minimum(i + 1, clat - 1)
                    south = jnp.where(i + 1 < clat, model_ref[r, more], south_ref[r, 0])
                else:
                    south = model_ref[r, i + 1]
                bar = six(x, north, south, west_ref[r, pl.ds(i, 1)], east_ref[r, pl.ds(i, 1)])
                bar = bar - alpha * damp_ref[r, i]
                bar_out[r, i] = bar
                bar_sq, model_sq = bar_sq + fold(bar * bar), model_sq + fold(x * x)
            return bar_sq, model_sq

        zero = jnp.zeros((8, depth), F32)
        bar_sq, model_sq = lax.fori_loop(0, clat // STEP, chunk, (zero, zero))
        row = place(row, r, jnp.sum(bar_sq, keepdims=True))
        return place(row, 3 * systems + r, jnp.sum(model_sq, keepdims=True))

    sums_out[...] = lax.fori_loop(0, systems, system, jnp.zeros((1, depth), F32))


def stage_body(after_ref, tiles_in, tiles_out, sem):
    copy = pltpu.make_async_copy(tiles_in, tiles_out, sem)
    copy.start()
    copy.wait()


def rays_body(cap, blocks, meta_ref, rec_ref, tiles_ref, fetched_ref, old_ref, sums_ref, bar_ref, term_ref, masks, lows):
    tiles, width, depth = tiles_ref.shape[2:]
    systems = old_ref.shape[0]
    group = cap * systems
    chunk = group + 1
    devices = term_ref.shape[0] // chunk
    for c in range(cap + 1):
        here = lax.shift_right_logical(iota((group, depth), 0), systems.bit_length() - 1) == c
        masks[c] = here.astype(F32).astype(BF16)
    term_ref[...] = jnp.zeros(term_ref.shape, F32)
    lows[...] = jnp.zeros(lows.shape, BF16)
    total = jnp.zeros((blocks * group, width), F32)
    for t in range(tiles):
        owner, rank, block = meta_ref[0, t], meta_ref[1, t], meta_ref[2, t]
        rows = fetched_ref[pl.ds(pl.multiple_of(owner * group, group), group), :]
        left = jnp.concatenate(
            [rows * masks[jnp.where(block == b, rank, cap)] for b in range(blocks)], axis=0
        )
        total = total + lax.dot_general(
            left, tiles_ref[0, 0, t], (((1,), (1,)), ((), ())), preferred_element_type=F32
        )
    square = jnp.zeros((systems, width), F32)
    for b in range(blocks):
        traced = jnp.zeros((systems, width), F32)
        for c in range(cap):
            at = b * group + c * systems
            traced = traced + total[at : at + systems]
        old = jnp.concatenate(
            [old_ref[r, 0, :, b * width : (b + 1) * width] * rec_ref[0, r] for r in range(systems)], axis=0
        )
        live = iota((systems, width), 1) + b * width < meta_ref[3, 0]
        bar = jnp.where(live, traced - old, 0.0)
        square = square + bar * bar
        for r in range(systems):
            bar_ref[r, 0, :, b * width : (b + 1) * width] = bar[r : r + 1]
        lows[b] = jnp.concatenate([bar, jnp.zeros((16 - systems, width), F32)], axis=0).astype(BF16)
    ray_sq = jnp.sum(square, axis=1, keepdims=True)
    part = sums_ref[...]
    for r in range(systems):
        part = place(part, r, ray_sq[r : r + 1])
    for e in range(devices):
        term_ref[e * chunk + group] = part
    for t in range(tiles):
        row = meta_ref[0, t] * chunk + meta_ref[1, t] * systems
        term = jnp.dot(lows[meta_ref[2, t]], tiles_ref[0, 0, t], preferred_element_type=F32)
        for r in range(systems):
            term_ref[row + r] = term[r : r + 1]


def image_body(
    chunk,
    cap,
    corner_ref,
    wanted_ref,
    bar_ref,
    north_ref,
    south_ref,
    west_ref,
    east_ref,
    model_ref,
    sums_ref,
    image_out,
    sums_out,
    patch_out,
    model_patch_out,
    chosen_out,
):
    systems, clat, clon, depth = model_ref.shape
    corner = corner_ref[0]
    wanted = wanted_ref[...]
    devices = wanted.shape[0]
    height, slots = chosen_out.shape
    at = iota((1, slots), 1)
    source = jnp.floor((at.astype(F32) + 0.5) * (1.0 / chunk)).astype(I32)
    inner = at - source * chunk
    from_e = (jnp.broadcast_to(source, (devices, slots)) == iota((devices, slots), 0)).astype(F32).astype(BF16)
    turned = jnp.transpose(wanted)[0:8].astype(BF16)
    listed = jnp.dot(turned, from_e, preferred_element_type=F32)
    slot_of = lax.shift_right_logical(inner, systems.bit_length() - 1)
    mine = jnp.broadcast_to(slot_of, listed.shape) == iota(listed.shape, 0)
    flat = jnp.sum(jnp.where(mine, listed, 0.0), axis=0, keepdims=True).astype(I32)
    used = (flat > 0) & (inner < chunk - 1)
    target = jnp.where(used, (inner & (systems - 1)) * (PATCH * clon) + flat - 1, -1)
    for k in range(height // 64):
        shape = (64, slots)
        hit = jnp.broadcast_to(target, shape) == iota(shape, 0) + k * 64
        chosen_out[k * 64 : (k + 1) * 64] = hit.astype(F32).astype(BF16)

    def system(r, row):
        def rows(k, acc):
            image_sq, cross = acc
            base = k * STEP
            for j in range(STEP):
                i = base + j
                x = bar_ref[r, i]
                if j == 0:
                    north = jnp.where(k > 0, bar_ref[r, jnp.maximum(i - 1, 0)], north_ref[r])
                else:
                    north = bar_ref[r, i - 1]
                if j == STEP - 1:
                    more = jnp.minimum(i + 1, clat - 1)
                    south = jnp.where(i + 1 < clat, bar_ref[r, more], south_ref[r])
                else:
                    south = bar_ref[r, i + 1]
                image = six(x, north, south, west_ref[r, pl.ds(i, 1)], east_ref[r, pl.ds(i, 1)])
                image_out[r, i] = image
                image_sq, cross = image_sq + fold(image * image), cross + fold(image * model_ref[r, i])
            return image_sq, cross

        zero = jnp.zeros((8, depth), F32)
        image_sq, cross = lax.fori_loop(0, clat // STEP, rows, (zero, zero))
        for a in range(PATCH):
            patch_out[pl.ds(pl.multiple_of((r * PATCH + a) * clon, clon), clon), :] = image_out[r, corner + a]
            model_patch_out[pl.ds(pl.multiple_of((r * PATCH + a) * clon, clon), clon), :] = model_ref[r, corner + a]
        row = place(row, systems + r, jnp.sum(image_sq, keepdims=True))
        return place(row, 2 * systems + r, jnp.sum(cross, keepdims=True))

    sums_out[...] = lax.fori_loop(0, systems, system, sums_ref[...])


def combine_body(chunk, systems, terms_ref, chosen_ref, patch_ref, model_patch_ref, sums_ref, added_ref, residual_ref, parts_ref, split):
    arrived, depth = terms_ref.shape
    devices = parts_ref.shape[0]
    width = patch_ref.shape[0]
    x = terms_ref[...]
    high = x.astype(BF16)
    rest = x - high.astype(F32)
    middle = rest.astype(BF16)
    low = (rest - middle.astype(F32)).astype(BF16)
    padded = split.shape[0]
    if padded > arrived:
        split[arrived:] = jnp.zeros((padded - arrived, split.shape[1]), BF16)
    split[0:arrived, 0:depth] = high
    split[0:arrived, depth : 2 * depth] = middle
    split[0:arrived, 2 * depth :] = low
    three = jnp.dot(chosen_ref[...], split[...], preferred_element_type=F32)
    added = three[:, 0:depth] + (three[:, depth : 2 * depth] + three[:, 2 * depth :])
    added_ref[...] = added
    every = terms_ref[pl.ds(chunk - 1, devices, stride=chunk), :]
    residual_ref[...] = jnp.sum(every, axis=0, keepdims=True)
    square = added * (2.0 * patch_ref[...] + added)
    cross = added * model_patch_ref[...]
    row = sums_ref[...]
    each = width // systems
    for r in range(systems):
        row = place(row, systems + r, jnp.sum(square[r * each : (r + 1) * each], keepdims=True))
        row = place(row, 2 * systems + r, jnp.sum(cross[r * each : (r + 1) * each], keepdims=True))
    parts_ref[...] = jnp.broadcast_to(row, parts_ref.shape)


def first_norm(residual_ref, systems, rows_all):
    return jnp.sqrt(residual_ref[0:1, 0:systems] / rows_all + EPSILON)


def early_body(
    rows_all, residual_ref, rec_ref, bar_ref, damp_ref, solution_ref, search_ref, ray_out, damp_out, solution_out, coef
):
    r, piece = pl.program_id(0), pl.program_id(1)
    systems = rec_ref.shape[1]

    @pl.when((r == 0) & (piece == 0))
    def _():
        rho_bar, phi_bar = rec_ref[1:2], rec_ref[2:3]
        beta = first_norm(residual_ref, systems, rows_all)
        rho = jnp.sqrt(rho_bar * rho_bar + beta * beta)
        scales = (1.0 / beta, (rho_bar / rho) * phi_bar / rho)
        for q, scale in enumerate(scales):
            for s in range(systems):
                coef[q, s] = scale[0, s]
        for s in range(systems):
            ray_out[s] = bar_ref[s] * coef[0, s]

    damp_out[...] = damp_ref[...] * coef[0, r]
    solution_out[...] = solution_ref[...] + search_ref[...] * coef[1, r]


def finish_body(
    rows_all,
    cells_all,
    corner_ref,
    residual_ref,
    parts_ref,
    rec_ref,
    added_ref,
    image_ref,
    model_ref,
    search_ref,
    model_out,
    search_out,
    rec_out,
    coef,
):
    r, piece = pl.program_id(0), pl.program_id(1)
    systems = rec_ref.shape[1]
    _, rows, clon, depth = image_ref.shape

    @pl.when((r == 0) & (piece == 0))
    def _():
        total = jnp.sum(parts_ref[...], axis=0, keepdims=True)
        image_sq, cross, model_sq = (total[:, q * systems : (q + 1) * systems] for q in range(1, 4))
        rho_bar, phi_bar = rec_ref[1:2], rec_ref[2:3]
        beta = first_norm(residual_ref, systems, rows_all)
        update_sq = image_sq / (beta * beta) - 2.0 * cross + beta * beta * model_sq
        alpha = jnp.sqrt(jnp.maximum(update_sq, 0.0) / cells_all + EPSILON)
        rho = jnp.sqrt(rho_bar * rho_bar + beta * beta)
        cosine = rho_bar / rho
        sine = beta / rho
        rec_out[...] = jnp.concatenate([alpha, -cosine * alpha, sine * phi_bar], axis=0)
        scales = (1.0 / (beta * alpha), beta / alpha, sine * alpha / rho)
        for q, scale in enumerate(scales):
            for s in range(systems):
                coef[q, s] = scale[0, s]

    image_scale, model_scale, search_scale = coef[0, r], coef[1, r], coef[2, r]
    new = image_ref[...] * image_scale - model_ref[...] * model_scale
    model_out[...] = new
    search_out[...] = new - search_ref[...] * search_scale
    for a in range(PATCH):
        at = corner_ref[0] + a - piece * rows

        @pl.when((at >= 0) & (at < rows))
        def _():
            more = added_ref[0, pl.ds(a * clon, clon), :] * image_scale
            model_out[0, at] = model_out[0, at] + more
            search_out[0, at] = search_out[0, at] + more


def shifted(x, axis, step):
    count = lax.axis_size(axis)
    if step > 0:
        pairs = [(i, i + 1) for i in range(count - 1)]
    else:
        pairs = [(i + 1, i) for i in range(count - 1)]
    return lax.ppermute(x, axis, pairs)


def exchange(x):
    return lax.all_to_all(x, AXES, split_axis=0, concat_axis=0, tiled=True)


def per_device(
    sensitivity,
    block_ids,
    block_offsets,
    ray_counts,
    ray_vector,
    damping_vector,
    model_vector,
    solution,
    search,
    recurrence,
):
    lat_size, lon_size = lax.axis_size("lat"), lax.axis_size("lon")
    devices = lat_size * lon_size
    tiles, width, depth = sensitivity.shape[2:]
    blocks = block_offsets.shape[-1] - 1
    systems, clat, clon, _ = model_vector.shape
    columns = clat * clon
    cap = max(2 * ((tiles + devices - 1) // devices), 16 // systems)
    slots = devices * cap
    group = cap * systems
    chunk = group + 1
    cells_all = devices * columns * depth
    rows_all = devices * blocks * width + cells_all
    lanes = 128
    shape = jax.ShapeDtypeStruct
    field = shape(model_vector.shape, F32)
    flat_shape = (systems, columns, depth)

    lists = exchange(jnp.broadcast_to(block_ids[0], (devices, 1, tiles))).reshape(devices, tiles)

    band = shape((systems, 3, clon, depth), F32)
    model, damping, north_msg, south_msg, meta = call(
        functools.partial(load_body, columns.bit_length() - 1, blocks),
        "load",
        (field, field, band, band, shape((8, lanes), I32)),
        [vmem(), smem(), smem(), hbm(), hbm()],
        (vmem(),) * 5,
        scratch=[pltpu.SemaphoreType.DMA((6,))],
        moved=8 * systems * columns * depth,
    )(block_ids, block_offsets, ray_counts, far(model_vector), far(damping_vector))
    north = shifted(south_msg, "lat", 1)
    south = shifted(north_msg, "lat", -1)

    served, wanted, corner = call(
        functools.partial(serve_body, cap),
        "serve",
        (shape((slots * systems, depth), BF16), shape((devices, lanes), F32), shape((1,), I32)),
        [vmem(), vmem()],
        (vmem(), vmem(), smem()),
        scratch=[pltpu.VMEM((slots * systems, depth), F32)],
    )(lists, model)
    fetched = exchange(served.reshape(devices, group, depth)).reshape(slots * systems, depth)

    side = shape((systems, 3 * clat + 8, depth), F32)
    east_msg, west_msg = call(
        functools.partial(columns_body, clat, clon),
        "columns",
        (side, side),
        [vmem()] * 4,
        (vmem(), vmem()),
    )(model.reshape(flat_shape), damping.reshape(flat_shape), north, south)
    west = shifted(east_msg, "lon", 1)
    east = shifted(west_msg, "lon", -1)

    held = call(
        stage_body,
        "stage",
        shape(sensitivity.shape, BF16),
        [smem(), hbm()],
        vmem(),
        scratch=[pltpu.SemaphoreType.DMA],
        moved=2 * tiles * width * depth,
    )(corner, far(sensitivity))

    edge = shape((systems, clon, depth), F32)
    flank = shape((systems, clat, depth), F32)
    damp_bar, *border, sums = call(
        damp_body,
        "damp",
        (field, edge, edge, flank, flank, shape((1, lanes), F32)),
        [smem()] + [vmem()] * 8,
        (vmem(),) * 6,
        flops=20 * systems * columns * depth,
        moved=12 * systems * columns * depth,
    )(recurrence, model, damping, north, south, west, east, west_msg, east_msg)

    ray_bar, terms = call(
        functools.partial(rays_body, cap, blocks),
        "rays",
        (shape(ray_vector.shape, F32), shape((devices * chunk, 1, depth), F32)),
        [smem(), smem()] + [vmem()] * 4,
        (vmem(), vmem()),
        scratch=[
            pltpu.VMEM((cap + 1, group, depth), BF16),
            pltpu.VMEM((blocks + 1, 16, width), BF16),
        ],
        flops=4 * tiles * width * depth * 16,
        moved=2 * tiles * width * depth,
    )(meta, recurrence, held, fetched, ray_vector, sums)
    arrived = exchange(terms.reshape(devices, 1, chunk * depth)).reshape(devices * chunk, depth)

    padded = -(-devices * chunk // lanes) * lanes
    height = systems * PATCH * clon
    patch_shape = shape((height, depth), F32)
    image, sums, patch, model_patch, chosen = call(
        functools.partial(image_body, chunk, cap),
        "image",
        (field, shape((1, lanes), F32), patch_shape, patch_shape, shape((height, padded), BF16)),
        [smem()] + [vmem()] * 8,
        (vmem(),) * 5,
        flops=20 * systems * columns * depth,
        moved=12 * systems * columns * depth,
    )(corner, wanted, damp_bar, *border, model, sums)

    added, residual, parts = call(
        functools.partial(combine_body, chunk, systems),
        "combine",
        (patch_shape, shape((1, lanes), F32), shape((devices, lanes), F32)),
        [vmem()] * 5,
        (vmem(),) * 3,
        scratch=[pltpu.VMEM((padded, 3 * depth), BF16)],
    )(arrived, chosen, patch, model_patch, sums)
    every = exchange(parts.reshape(devices, 1, lanes)).reshape(devices, lanes)

    pieces = 2
    rows = clat // pieces
    whole = lambda dims: pl.BlockSpec(dims, lambda r, p: (0,) * len(dims))
    part = pl.BlockSpec((1, rows, clon, depth), lambda r, p: (r, p, 0, 0))
    search = far(search)
    ray_out, damp_out, solution_out = call(
        functools.partial(early_body, float(rows_all)),
        "early",
        (shape(ray_vector.shape, F32), field, field),
        [whole((1, lanes)), whole(recurrence.shape), whole(ray_vector.shape)] + [part] * 3,
        (whole(ray_vector.shape), part, part),
        scratch=[pltpu.SMEM((2, systems), F32)],
        grid=(systems, pieces),
        flops=4 * systems * columns * depth,
        moved=20 * systems * columns * depth,
    )(residual, recurrence, ray_bar, damp_bar, far(solution), search)
    model_out, search_out, rec_out = call(
        functools.partial(finish_body, float(rows_all), float(cells_all)),
        "finish",
        (field, field, shape(recurrence.shape, F32)),
        [
            smem(),
            whole((1, lanes)),
            whole((devices, lanes)),
            whole(recurrence.shape),
            pl.BlockSpec((1, PATCH * clon, depth), lambda r, p: (r, 0, 0)),
        ]
        + [part] * 3,
        (part, part, whole(recurrence.shape)),
        scratch=[pltpu.SMEM((3, systems), F32)],
        grid=(systems, pieces),
        flops=6 * systems * columns * depth,
        moved=20 * systems * columns * depth,
    )(
        corner,
        residual,
        every,
        recurrence,
        added.reshape(systems, PATCH * clon, depth),
        image,
        model,
        search,
    )
    return ray_out, damp_out, model_out, solution_out, search_out, rec_out


def solution(mesh):
    fields = P(None, "lat", "lon", None)
    return jax.shard_map(
        per_device,
        mesh=mesh,
        in_specs=(
            P("lat", "lon", None, None, None),
            P("lat", "lon", None),
            P("lat", "lon", None),
            P("lat", "lon"),
            fields,
            fields,
            fields,
            fields,
            fields,
            P(),
        ),
        out_specs=(fields, fields, fields, fields, fields, P()),
        check_vma=False,
    )
```

time: 104 us -> 106 us (1.019)
  Pallas kernels: 27.2 us -> 33.7 us
  local copies, waits for them, and re-layouts: 23.7 us -> 30 us
  waiting for transfers between devices: 6.07 us -> 0.02 us
  blocking collectives: 17.6 us -> 13.9 us
    unnamed x42 -> x74, local copies, waits for them, and re-layouts: 18.6 us -> 30 us
    all_to_all x3, waiting for transfers between devices: 6.06 us -> 0.01 us  [exchange(): return lax.all_to_all(x, AXES, split_axis=0, concat_axis=0, tiled=True)]
    pallas_call x5 -> x9, Pallas kernels: 21.5 us -> 26.5 us  [the longest x1 6.7 us: per_device(): call(functools.partial(early_body, float(rows_all)), 'early', (shape(ray_...]
    slice x6 -> x0, local copies, waits for them, and re-layouts: 4.06 us -> none  [the longest x1 1.3 us: column_msg(): damping_vector[:, :, near]]
    all_to_all x1, blocking collectives: 17.6 us -> 13.9 us  [exchange(): return lax.all_to_all(x, AXES, split_axis=0, concat_axis=0, tiled=True)]
    pallas_call x1, Pallas kernels: 5.71 us -> 7.15 us  [per_device(): call(functools.partial(finish_body, float(rows_all), float(cells_all)), '...]
  transfers between devices with their start and end apart: 7 -> 7, of which waited for: 1 -> 0; matrix products, arithmetic and copies ran while one was open for 6% -> 0% of each run, Pallas kernels for 19% -> 18%
where the time goes in v3:
time: 106 us; the launch traced here: 105 us
  Pallas kernels  33.7 us (32%)
  local copies, waits for them, and re-layouts  30 us (28%)
  starting transfers between devices  26 us (25%)
  blocking collectives  13.9 us (13%)
  between operations  1.57 us (1%)
    unnamed x74, local copies, waits for them, and re-layouts  30 us
    all_to_all x3, starting transfers between devices, exchange(): return lax.all_to_all(x, AXES, split_axis=0, concat_axis=0, tiled=True)  16.5 us
    all_to_all x1, blocking collectives, exchange(): return lax.all_to_all(x, AXES, split_axis=0, concat_axis=0, tiled=True)  13.9 us
    ppermute x4, starting transfers between devices, shifted(): return lax.ppermute(x, axis, pairs)  9.54 us
    pallas_call x1, Pallas kernels, per_device(): call(functools.partial(finish_body, float(rows_all), float(cells_all)), '...  7.15 us
    pallas_call x1, Pallas kernels, per_device(): call(functools.partial(early_body, float(rows_all)), 'early', (shape(ray_...  6.7 us
    pallas_call x1, Pallas kernels, per_device(): call(functools.partial(rays_body, cap, blocks), 'rays', (shape(ray_vector...  4.35 us
    pallas_call x1, Pallas kernels, per_device(): call(damp_body, 'damp', (field, edge, edge, flank, flank, shape((1, lanes...  3.81 us
  transfers between devices with their start and end apart: 7, of which 0 were waited for; matrix products, arithmetic and copies ran while one was open for 0% of the time, Pallas kernels for 18%

profile of v3, /device:TPU:0, one launch (start us, length us, event | category | flops | bytes accessed | tf_op | source)
XLA Modules:
  0.0 105.1 jit_solution(200532089368222576)
XLA Ops:
  1.3 0.6 copy-done.29
  1.9 0.7 copy-done.34
  2.6 3.0 %load.1 = (f32[4,32,32,128]{3,2,1,0:T(8,128)S(1)}, f32[4,32,32,128]{3,2,1,0:T(8,128)S(1)}, f32[4,3,32,128]{3,2,1,0:T(8,128)S(1)}, f32[4,3,32,128]{3,2,1,0:T(8,128)S(1)}, s32[8,128]{1,0:T(8,128)S(1)}) custom-call(s32[1,1,60]{2,1,0:T(1,128)S(1)} %copy-done.29, s32[1,1,4]{2,1,0:T(1,128)S(1)} %copy-done.34, s32[1,1]{1,0:T(1,128)S(6)} %copy.18.count_ref, ...), custom_call_target="tpu_custom_call" | custom-call | bytes 4194304 | tf_op jit(solution)/shard_map/load/pallas_call | solution.py:528
  5.6 0.0 copy-start.2
  5.6 1.3 %copy-done.2 = f32[4,32,32,128]{3,2,1,0:T(8,128)} copy-done((f32[4,32,32,128]{3,2,1,0:T(8,128)}, f32[4,32,32,128]{3,2,1,0:T(8,128)S(1)}, u32[]{:S(2)}) %copy-start.2) | copy-done | bytes 2097176
  7.0 4.9 %collective-permute-start = (f32[4,3,32,128]{3,2,1,0:T(8,128)S(1)}, f32[4,3,32,128]{3,2,1,0:T(8,128)S(1)}, u32[]{:S(2)}, u32[]{:S(2)}) collective-permute-start(f32[4,3,32,128]{3,2,1,0:T(8,128)S(1)} %get-tuple-element.43), channel_id=1, source_target_pairs={{0,8},{8,16},{16,24},{1,9},{9,17},{17,25},{2,10},{10,18},{18,26},{... | collective-permute-start | bytes 589832 | tf_op jit(solution)/shard_map/ppermute | solution.py:489
  11.9 1.3 %collective-permute-start.1 = (f32[4,3,32,128]{3,2,1,0:T(8,128)S(1)}, f32[4,3,32,128]{3,2,1,0:T(8,128)S(1)}, u32[]{:S(2)}, u32[]{:S(2)}) collective-permute-start(f32[4,3,32,128]{3,2,1,0:T(8,128)S(1)} %get-tuple-element.44), channel_id=1, source_target_pairs={{8,0},{16,8},{24,16},{9,1},{17,9},{25,17},{10,2},{18,10},{26,18},{... | collective-permute-start | bytes 589832 | tf_op jit(solution)/shard_map/ppermute | solution.py:489
  13.2 13.9 %all_to_all.20 = s32[32,1,60]{2,1,0:T(1,128)S(1)} all-to-all(s32[32,1,60]{2,1,0:T(1,128)S(1)} %broadcast_in_dim.3), channel_id=1, replica_groups=mesh['lat'=4,'lon'=8] {'lat','lon'}, dimensions={0} | all-to-all | bytes 15360 | tf_op jit(solution)/shard_map/all_to_all | solution.py:493
  27.1 1.2 %serve.1 = (bf16[512,128]{1,0:T(8,128)(2,1)}, f32[32,128]{1,0:T(8,128)S(1)}, s32[1]{0:T(128)}) custom-call(s32[32,60]{1,0:T(8,128)S(1)} %bitcast.19, f32[4,32,32,128]{3,2,1,0:T(8,128)S(1)} %get-tuple-element.39.model_ref), custom_call_target="tpu_custom_call" | custom-call | tf_op jit(solution)/shard_map/serve/pallas_call | solution.py:540
  28.3 0.6 copy-done.23
  28.9 2.6 %all-to-all-start.1 = ((bf16[32,16,128]{2,1,0:T(8,128)(2,1)}), bf16[32,16,128]{2,1,0:T(8,128)(2,1)S(1)}, u32[]{:S(2)}, u32[]{:S(2)}) async-start(bf16[32,16,128]{2,1,0:T(8,128)(2,1)} %bitcast.2), calls=%async_computation.1 | async-start | bytes 262144 | tf_op jit(solution)/shard_map/all_to_all | solution.py:493
  31.5 0.0 collective-permute-done.north_ref
  31.5 0.0 collective-permute-done.1.south_ref
  31.5 0.0 copy-start.3
  31.5 1.6 %copy-done.3 = f32[4,32,32,128]{3,2,1,0:T(8,128)S(1)} copy-done((f32[4,32,32,128]{3,2,1,0:T(8,128)S(1)}, f32[4,32,32,128]{3,2,1,0:T(8,128)}, u32[]{:S(2)}) %copy-start.3) | copy-done | bytes 2097176
  33.1 0.2 columns.1
  33.4 2.0 %collective-permute-start.2 = (f32[4,104,128]{2,1,0:T(8,128)S(1)}, f32[4,104,128]{2,1,0:T(8,128)S(1)}, u32[]{:S(2)}, u32[]{:S(2)}) collective-permute-start(f32[4,104,128]{2,1,0:T(8,128)S(1)} %get-tuple-element.45.eastmost_ref), channel_id=1, source_target_pairs={{0,1},{1,2},{2,3},{3,4},{4,5},{5,6},{6,7},{8,9},{9,10},{10,11},{11... | collective-permute-start | bytes 638984 | tf_op jit(solution)/shard_map/ppermute | solution.py:489
  35.4 1.3 %collective-permute-start.3 = (f32[4,104,128]{2,1,0:T(8,128)S(1)}, f32[4,104,128]{2,1,0:T(8,128)S(1)}, u32[]{:S(2)}, u32[]{:S(2)}) collective-permute-start(f32[4,104,128]{2,1,0:T(8,128)S(1)} %get-tuple-element.46.westmost_ref), channel_id=1, source_target_pairs={{1,0},{2,1},{3,2},{4,3},{5,4},{6,5},{7,6},{9,8},{10,9},{11,10},{12... | collective-permute-start | bytes 638984 | tf_op jit(solution)/shard_map/ppermute | solution.py:489
  36.7 0.0 copy-start.4
  36.7 0.0 copy-start.20
  36.7 2.8 %stage.1.tiles_ref = bf16[1,1,60,256,128]{4,3,2,1,0:T(8,128)(2,1)S(1)} custom-call(s32[1]{0:T(128)} %get-tuple-element.40.after_ref.corner_ref, bf16[1,1,60,256,128]{4,3,2,1,0:T(8,128)(2,1)} %tiles_in.1), custom_call_target="tpu_custom_call" | custom-call | bytes 3932160 | tf_op jit(solution)/shard_map/stage/pallas_call | solution.py:561
  39.5 1.9 %copy-done = bf16[1,1,60,256,128]{4,3,2,1,0:T(8,128)(2,1)} copy-done((bf16[1,1,60,256,128]{4,3,2,1,0:T(8,128)(2,1)}, bf16[1,1,60,256,128]{4,3,2,1,0:T(8,128)(2,1)S(1)}, u32[]{:S(2)}) %copy-start) | copy-done | bytes 3932184
  41.5 3.8 %damp.1 = (f32[4,32,32,128]{3,2,1,0:T(8,128)S(1)}, f32[4,32,128]{2,1,0:T(8,128)S(1)}, f32[4,32,128]{2,1,0:T(8,128)S(1)}, f32[4,32,128]{2,1,0:T(8,128)S(1)}, f32[...) custom-call(f32[3,4]{1,0:T(4,128)S(1)} %copy-done.20, f32[4,32,32,128]{3,2,1,0:T(8,128)S(1)} %get-tuple-element.39.model_ref, ...), custom_call_target="tpu_custom_call" | custom-call | flops 10485760 | bytes 6291456 | tf_op jit(solution)/shard_map/damp/pallas_call | solution.py:573
  45.3 0.0 copy-start.5
  45.3 1.3 %copy-done.5 = f32[4,32,32,128]{3,2,1,0:T(8,128)} copy-done((f32[4,32,32,128]{3,2,1,0:T(8,128)}, f32[4,32,32,128]{3,2,1,0:T(8,128)S(1)}, u32[]{:S(2)}) %copy-start.5) | copy-done | bytes 2097176
  46.6 0.6 copy-done.12
  47.2 0.6 copy-done.14
  47.8 0.6 copy-done.16
  48.5 0.6 copy-done.18
  49.1 0.0 all-to-all-done.1
  49.1 2.1 %copy-done.1 = bf16[1,1,60,256,128]{4,3,2,1,0:T(8,128)(2,1)S(1)} copy-done((bf16[1,1,60,256,128]{4,3,2,1,0:T(8,128)(2,1)S(1)}, bf16[1,1,60,256,128]{4,3,2,1,0:T(8,128)(2,1)}, u32[]{:S(2)}) %copy-start.1) | copy-done | bytes 3932184
  51.2 4.4 %rays.1 = (f32[4,1,1,768]{3,2,1,0:T(1,128)S(1)}, f32[544,1,128]{2,1,0:T(1,128)}) custom-call(s32[8,128]{1,0:T(8,128)S(1)} %get-tuple-element.38.meta_ref, f32[3,4]{1,0:T(4,128)S(1)} %copy-done.20, bf16[1,1,60,256,128]{4,3,2,1,0:T(8,128)(2,1)S(1)} %copy-done.1, bf16[512,128]{1,0:T(8,128)(2,1)S(1)} %bitcast.16, f32[4,1,1,768]{3,2,1,0:T(1,128)S(1)} %copy-done.26, ...), custom_call_target="tpu_custom_call" | custom-call | flops 125829120 | bytes 3932160 | tf_op jit(solution)/shard_map/rays/pallas_call | solution.py:583
  55.6 0.6 copy-done.27
  56.2 8.1 %all-to-all-start.2 = ((f32[32,1,2176]{2,1,0:T(1,128)}), f32[32,1,2176]{2,1,0:T(1,128)S(1)}, u32[]{:S(2)}, u32[]{:S(2)}) async-start(f32[32,1,2176]{2,1,0:T(1,128)} %bitcast.6), calls=%async_computation.2 | async-start | bytes 557056 | tf_op jit(solution)/shard_map/all_to_all | solution.py:493
  64.2 0.0 copy-start.6
  64.2 1.6 %copy-done.6 = f32[4,32,32,128]{3,2,1,0:T(8,128)S(1)} copy-done((f32[4,32,32,128]{3,2,1,0:T(8,128)S(1)}, f32[4,32,32,128]{3,2,1,0:T(8,128)}, u32[]{:S(2)}) %copy-start.6) | copy-done | bytes 2097176
  65.8 0.8 copy-done.13
  66.7 0.8 copy-done.15
  67.5 0.8 copy-done.17
  68.4 0.8 copy-done.19
  69.2 0.7 copy-done.24
  69.9 0.7 copy-done.31
  70.6 3.7 %image.1 = (f32[4,32,32,128]{3,2,1,0:T(8,128)S(1)}, f32[1,128]{1,0:T(1,128)S(1)}, f32[512,128]{1,0:T(8,128)S(1)}, f32[512,128]{1,0:T(8,128)S(1)}, bf16[512,640]{1,0:T(8,128)(2,1)S(1)}) custom-call(s32[1]{0:T(128)} %get-tuple-element.40.after_ref.corner_ref, f32[32,128]{1,0:T(8,128)S(1)} %copy-done.24, f32[4,32,32,128]{3,2,1,0:T(8,128)S(1)} %copy-done.6, ...), custom_call_target="tpu_custom_call" | custom-call | flops 10485760 | bytes 6291456 | tf_op jit(solution)/shard_map/image/pallas_call | solution.py:601
  74.2 0.0 copy-start.8
  74.2 1.3 %copy-done.8 = f32[4,32,32,128]{3,2,1,0:T(8,128)} copy-done((f32[4,32,32,128]{3,2,1,0:T(8,128)}, f32[4,32,32,128]{3,2,1,0:T(8,128)S(1)}, u32[]{:S(2)}) %copy-start.8) | copy-done | bytes 2097176
  75.6 0.7 copy-done.10
  76.3 0.5 copy-done.35
  76.8 0.0 all-to-all-done.2
  76.8 0.9 copy-done.11
  77.7 0.7 copy-done.36
  78.4 0.7 combine.1
  79.1 0.6 copy-done.25
  79.7 0.5 copy-done.32
  80.2 5.8 %all-to-all-start.3 = ((f32[32,1,128]{2,1,0:T(1,128)}), f32[32,1,128]{2,1,0:T(1,128)S(1)}, u32[]{:S(2)}, u32[]{:S(2)}) async-start(f32[32,1,128]{2,1,0:T(1,128)} %bitcast.20), calls=%async_computation.3 | async-start | bytes 32768 | tf_op jit(solution)/shard_map/all_to_all | solution.py:493
  86.0 0.0 copy-start.7
  86.0 1.6 %copy-done.7 = f32[4,32,32,128]{3,2,1,0:T(8,128)S(1)} copy-done((f32[4,32,32,128]{3,2,1,0:T(8,128)S(1)}, f32[4,32,32,128]{3,2,1,0:T(8,128)}, u32[]{:S(2)}) %copy-start.7) | copy-done | bytes 2097176
  87.6 0.7 copy-done.21
  88.3 0.7 copy-done.28
  89.0 0.7 copy-done.33
  89.7 6.7 %early.1 = (f32[4,1,1,768]{3,2,1,0:T(1,128)}, f32[4,32,32,128]{3,2,1,0:T(8,128)}, f32[4,32,32,128]{3,2,1,0:T(8,128)}) custom-call(f32[1,128]{1,0:T(1,128)S(1)} %copy-done.33, f32[3,4]{1,0:T(4,128)S(1)} %copy-done.21, f32[4,1,1,768]{3,2,1,0:T(1,128)S(1)} %copy-done.28, f32[4,32,32,128]{3,2,1,0:T(8,128)S(1)} %copy-done.7, f32[4,32,32,128]{3,2,1,0:T(8,128)} %solution_ref.1, ...), custom_call_target="tpu_custom_call" | custom-call | flops 2097152 | bytes 10485760 | tf_op jit(solution)/shard_map/early/pallas_call | solution.py:626
  96.4 0.0 all-to-all-done.3
  96.4 0.0 copy-start.9
  96.4 1.6 %copy-done.9 = f32[4,32,32,128]{3,2,1,0:T(8,128)S(1)} copy-done((f32[4,32,32,128]{3,2,1,0:T(8,128)S(1)}, f32[4,32,32,128]{3,2,1,0:T(8,128)}, u32[]{:S(2)}) %copy-start.9) | copy-done | bytes 2097176
  98.0 7.1 %finish.1 = (f32[4,32,32,128]{3,2,1,0:T(8,128)}, f32[4,32,32,128]{3,2,1,0:T(8,128)}, f32[3,4]{1,0:T(4,128)}) custom-call(s32[1]{0:T(128)} %get-tuple-element.40.after_ref.corner_ref, f32[1,128]{1,0:T(1,128)S(1)} %copy-done.33, f32[32,128]{1,0:T(8,128)S(1)} %bitcast.18, f32[3,4]{1,0:T(4,128)S(1)} %copy-done.22, f32[4,128,128]{2,1,0:T(8,128)S(1)} %bitcast.17, ...), custom_call_target="tpu_custom_call" | custom-call | flops 3145728 | bytes 10485760 | tf_op jit(solution)/shard_map/finish/pallas_call | solution.py:637
  (36 shorter events, 0.1 us)
Async XLA Ops:
  1.3 0.7 copy-start.29
  1.9 0.7 copy-start.34
  5.6 1.3 %copy-start.2 = (f32[4,32,32,128]{3,2,1,0:T(8,128)}, f32[4,32,32,128]{3,2,1,0:T(8,128)S(1)}, u32[]{:S(2)}) copy-start(f32[4,32,32,128]{3,2,1,0:T(8,128)S(1)} %get-tuple-element.42.damp_ref) | copy-start | bytes 6291460
  7.0 24.6 %collective-permute-start = (f32[4,3,32,128]{3,2,1,0:T(8,128)S(1)}, f32[4,3,32,128]{3,2,1,0:T(8,128)S(1)}, u32[]{:S(2)}, u32[]{:S(2)}) collective-permute-start(f32[4,3,32,128]{3,2,1,0:T(8,128)S(1)} %get-tuple-element.43), channel_id=1, source_target_pairs={{0,8},{8,16},{16,24},{1,9},{9,17},{17,25},{2,10},{10,18},{18,26},{... | collective-permute-start | bytes 589832 | tf_op jit(solution)/shard_map/ppermute | solution.py:489
  11.9 19.6 %collective-permute-start.1 = (f32[4,3,32,128]{3,2,1,0:T(8,128)S(1)}, f32[4,3,32,128]{3,2,1,0:T(8,128)S(1)}, u32[]{:S(2)}, u32[]{:S(2)}) collective-permute-start(f32[4,3,32,128]{3,2,1,0:T(8,128)S(1)} %get-tuple-element.44), channel_id=1, source_target_pairs={{8,0},{16,8},{24,16},{9,1},{17,9},{25,17},{10,2},{18,10},{26,18},{... | collective-permute-start | bytes 589832 | tf_op jit(solution)/shard_map/ppermute | solution.py:489
  28.3 0.6 copy-start.23
  28.9 20.2 %all-to-all-start.1 = ((bf16[32,16,128]{2,1,0:T(8,128)(2,1)}), bf16[32,16,128]{2,1,0:T(8,128)(2,1)S(1)}, u32[]{:S(2)}, u32[]{:S(2)}) async-start(bf16[32,16,128]{2,1,0:T(8,128)(2,1)} %bitcast.2), calls=%async_computation.1 | async-start | bytes 262144 | tf_op jit(solution)/shard_map/all_to_all | solution.py:493
  31.5 1.6 %copy-start.3 = (f32[4,32,32,128]{3,2,1,0:T(8,128)S(1)}, f32[4,32,32,128]{3,2,1,0:T(8,128)}, u32[]{:S(2)}) copy-start(f32[4,32,32,128]{3,2,1,0:T(8,128)} %copy-done.2) | copy-start | bytes 6291460
  33.4 8.1 %collective-permute-start.2 = (f32[4,104,128]{2,1,0:T(8,128)S(1)}, f32[4,104,128]{2,1,0:T(8,128)S(1)}, u32[]{:S(2)}, u32[]{:S(2)}) collective-permute-start(f32[4,104,128]{2,1,0:T(8,128)S(1)} %get-tuple-element.45.eastmost_ref), channel_id=1, source_target_pairs={{0,1},{1,2},{2,3},{3,4},{4,5},{5,6},{6,7},{8,9},{9,10},{10,11},{11... | collective-permute-start | bytes 638984 | tf_op jit(solution)/shard_map/ppermute | solution.py:489
  35.4 6.0 %collective-permute-start.3 = (f32[4,104,128]{2,1,0:T(8,128)S(1)}, f32[4,104,128]{2,1,0:T(8,128)S(1)}, u32[]{:S(2)}, u32[]{:S(2)}) collective-permute-start(f32[4,104,128]{2,1,0:T(8,128)S(1)} %get-tuple-element.46.westmost_ref), channel_id=1, source_target_pairs={{1,0},{2,1},{3,2},{4,3},{5,4},{6,5},{7,6},{9,8},{10,9},{11,10},{12... | collective-permute-start | bytes 638984 | tf_op jit(solution)/shard_map/ppermute | solution.py:489
  36.7 4.7 %copy-start.4 = (f32[4,32,32,128]{3,2,1,0:T(8,128)S(1)}, f32[4,32,32,128]{3,2,1,0:T(8,128)}, u32[]{:S(2)}) copy-start(f32[4,32,32,128]{3,2,1,0:T(8,128)} %copy-done.2) | copy-start | bytes 6291460
  36.7 4.7 %copy-start.20 = (f32[3,4]{1,0:T(4,128)S(1)}, f32[3,4]{1,0:T(4,128)}, u32[]{:S(2)}) copy-start(f32[3,4]{1,0:T(4,128)} %rec_ref.7) | copy-start | bytes 148
  39.5 1.9 %copy-start = (bf16[1,1,60,256,128]{4,3,2,1,0:T(8,128)(2,1)}, bf16[1,1,60,256,128]{4,3,2,1,0:T(8,128)(2,1)S(1)}, u32[]{:S(2)}) copy-start(bf16[1,1,60,256,128]{4,3,2,1,0:T(8,128)(2,1)S(1)} %stage.1.tiles_ref) | copy-start | bytes 11796484
  41.4 7.7 %copy-start.26 = (f32[4,1,1,768]{3,2,1,0:T(1,128)S(1)}, f32[4,1,1,768]{3,2,1,0:T(1,128)}, u32[]{:S(2)}) copy-start(f32[4,1,1,768]{3,2,1,0:T(1,128)} %old_ref.1) | copy-start | bytes 36868
  45.3 1.3 %copy-start.5 = (f32[4,32,32,128]{3,2,1,0:T(8,128)}, f32[4,32,32,128]{3,2,1,0:T(8,128)S(1)}, u32[]{:S(2)}) copy-start(f32[4,32,32,128]{3,2,1,0:T(8,128)S(1)} %get-tuple-element.50.bar_ref.damp_ref) | copy-start | bytes 6291460
  46.6 0.6 copy-start.12
  47.2 0.6 copy-start.14
  47.8 0.6 copy-start.16
  48.5 0.6 copy-start.18
  49.1 7.1 %copy-start.30 = (f32[1,128]{1,0:T(1,128)}, f32[1,128]{1,0:T(1,128)S(1)}, u32[]{:S(2)}) copy-start(f32[1,128]{1,0:T(1,128)S(1)} %get-tuple-element.47.sums_ref) | copy-start | bytes 1540
  49.1 2.1 %copy-start.1 = (bf16[1,1,60,256,128]{4,3,2,1,0:T(8,128)(2,1)S(1)}, bf16[1,1,60,256,128]{4,3,2,1,0:T(8,128)(2,1)}, u32[]{:S(2)}) copy-start(bf16[1,1,60,256,128]{4,3,2,1,0:T(8,128)(2,1)} %copy-done) | copy-start | bytes 11796484
  55.6 0.6 copy-start.27
  56.2 20.6 %all-to-all-start.2 = ((f32[32,1,2176]{2,1,0:T(1,128)}), f32[32,1,2176]{2,1,0:T(1,128)S(1)}, u32[]{:S(2)}, u32[]{:S(2)}) async-start(f32[32,1,2176]{2,1,0:T(1,128)} %bitcast.6), calls=%async_computation.2 | async-start | bytes 557056 | tf_op jit(solution)/shard_map/all_to_all | solution.py:493
  64.2 1.6 %copy-start.6 = (f32[4,32,32,128]{3,2,1,0:T(8,128)S(1)}, f32[4,32,32,128]{3,2,1,0:T(8,128)}, u32[]{:S(2)}) copy-start(f32[4,32,32,128]{3,2,1,0:T(8,128)} %copy-done.5) | copy-start | bytes 6291460
  65.8 0.8 copy-start.13
  66.7 0.8 copy-start.15
  67.5 0.8 copy-start.17
  68.3 0.8 copy-start.19
  69.2 0.7 copy-start.24
  69.9 0.7 copy-start.31
  74.2 1.3 %copy-start.8 = (f32[4,32,32,128]{3,2,1,0:T(8,128)}, f32[4,32,32,128]{3,2,1,0:T(8,128)S(1)}, u32[]{:S(2)}) copy-start(f32[4,32,32,128]{3,2,1,0:T(8,128)S(1)} %get-tuple-element.65.image_ref) | copy-start | bytes 6291460
  75.6 0.7 copy-start.10
  76.3 0.5 copy-start.35
  76.8 1.0 copy-start.11
  77.7 0.7 copy-start.36
  79.1 0.6 copy-start.25
  79.7 0.5 copy-start.32
  80.2 16.2 %all-to-all-start.3 = ((f32[32,1,128]{2,1,0:T(1,128)}), f32[32,1,128]{2,1,0:T(1,128)S(1)}, u32[]{:S(2)}, u32[]{:S(2)}) async-start(f32[32,1,128]{2,1,0:T(1,128)} %bitcast.20), calls=%async_computation.3 | async-start | bytes 32768 | tf_op jit(solution)/shard_map/all_to_all | solution.py:493
  86.0 1.6 %copy-start.7 = (f32[4,32,32,128]{3,2,1,0:T(8,128)S(1)}, f32[4,32,32,128]{3,2,1,0:T(8,128)}, u32[]{:S(2)}) copy-start(f32[4,32,32,128]{3,2,1,0:T(8,128)} %copy-done.5) | copy-start | bytes 6291460
  87.6 0.7 copy-start.21
  88.3 0.7 copy-start.28
  89.0 0.7 copy-start.33
  89.7 6.7 %copy-start.22 = (f32[3,4]{1,0:T(4,128)S(1)}, f32[3,4]{1,0:T(4,128)}, u32[]{:S(2)}) copy-start(f32[3,4]{1,0:T(4,128)} %rec_ref.7) | copy-start | bytes 148
  96.4 1.6 %copy-start.9 = (f32[4,32,32,128]{3,2,1,0:T(8,128)S(1)}, f32[4,32,32,128]{3,2,1,0:T(8,128)}, u32[]{:S(2)}) copy-start(f32[4,32,32,128]{3,2,1,0:T(8,128)} %copy-done.8) | copy-start | bytes 6291460

commit v4 on v0

v4 whole, which is shorter than its diff:
```python
import functools

import jax
import jax.numpy as jnp
from jax import lax
from jax.experimental import pallas as pl
from jax.experimental.pallas import tpu as pltpu
from jax.sharding import PartitionSpec as P

DAMP_WEIGHT = 0.15
EPSILON = 1e-05
AXES = ("lat", "lon")
PATCH = 4
F32, BF16, I32 = jnp.float32, jnp.bfloat16, jnp.int32


def iota(shape, dim):
    return lax.broadcasted_iota(I32, shape, dim)


def vmem():
    return pl.BlockSpec(memory_space=pltpu.VMEM)


def hbm():
    return pl.BlockSpec(memory_space=pltpu.HBM)


def near(x):
    return pltpu.with_memory_space_constraint(x, pltpu.VMEM)


def far(x):
    return pltpu.with_memory_space_constraint(x, pltpu.HBM)


def smem():
    return pl.BlockSpec(memory_space=pltpu.SMEM)


def call(body, name, out_shape, in_specs, out_specs, scratch=(), grid=(), mib=16, flops=0, moved=0):
    return pl.pallas_call(
        body,
        name=name,
        grid=grid,
        out_shape=out_shape,
        in_specs=in_specs,
        out_specs=out_specs,
        scratch_shapes=list(scratch),
        compiler_params=pltpu.CompilerParams(vmem_limit_bytes=mib * 2**20),
        cost_estimate=pl.CostEstimate(flops=flops, bytes_accessed=moved, transcendentals=0),
    )


def wanted_column(wanted, cap):
    devices, lanes = wanted.shape
    rows = devices * cap
    spread = jnp.broadcast_to(wanted[:, None, :], (devices, cap, lanes)).reshape(rows, lanes)
    pick = iota((rows, lanes), 1) == (iota((rows, lanes), 0) & (cap - 1))
    return jnp.sum(jnp.where(pick, spread, 0.0), axis=1, keepdims=True)


def serve_body(cap, clat, clon, lists_ref, model_in, served_ref, wanted_ref, corner_ref, model_ref, mixed, sems):
    systems, _, depth = model_ref.shape
    copies = [pltpu.make_async_copy(model_in.at[r], model_ref.at[r], sems.at[r]) for r in range(systems)]
    for copy in copies:
        copy.start()
    devices, tiles = lists_ref.shape
    lanes = 128
    shift = (clat * clon).bit_length() - 1
    me = lax.axis_index("lat") * lax.axis_size("lon") + lax.axis_index("lon")
    ids = jnp.concatenate([lists_ref[...], jnp.full((devices, lanes - tiles), -1, I32)], axis=1)
    column = ids - lax.shift_left(me, shift)
    mine = (column >= 0) & (column < clat * clon) & (ids >= 0)
    first = jnp.min(jnp.where(mine, column, clat * clon))
    corner = jnp.minimum(lax.shift_right_logical(first, clon.bit_length() - 1), clat - PATCH)
    corner_ref[0] = corner
    ahead = (iota((lanes, lanes), 0) < iota((lanes, lanes), 1)).astype(F32).astype(BF16)
    rank = jnp.dot(mine.astype(F32).astype(BF16), ahead, preferred_element_type=F32)
    value = (column - corner * clon + 1).astype(F32)
    at = iota((devices, lanes), 1)
    wanted = jnp.zeros((devices, lanes), F32)
    for c in range(cap):
        picked = jnp.sum(jnp.where(mine & (rank == c), value, 0.0), axis=1, keepdims=True)
        wanted = jnp.where(at == c, picked, wanted)
    wanted_ref[...] = wanted
    target = wanted_column(wanted, cap).astype(I32) - 1
    rows = target.shape[0]
    width = PATCH * clon
    chosen = (jnp.broadcast_to(target, (rows, width)) == iota((rows, width), 1)).astype(F32).astype(BF16)
    for r in range(systems):
        copies[r].wait()
        table = model_ref[r, pl.ds(pl.multiple_of(corner * clon, clon), width), :].astype(BF16)
        mixed[pl.ds(r, rows, stride=systems), :] = jnp.dot(chosen, table, preferred_element_type=F32)
    served_ref[...] = mixed[...].astype(BF16)


def pack_body(
    shift,
    clon,
    blocks,
    ids_ref,
    off_ref,
    count_ref,
    model_ref,
    damp_in,
    tiles_in,
    damp_out,
    tiles_out,
    north_ref,
    south_ref,
    meta_ref,
    sems,
):
    systems, columns, _ = model_ref.shape
    half = tiles_in.shape[2] // 2
    copies = [pltpu.make_async_copy(damp_in.at[r], damp_out.at[r], sems.at[r]) for r in range(systems)]
    for k, part in enumerate((pl.ds(0, half), pl.ds(half, tiles_in.shape[2] - half))):
        at = (0, 0, part)
        copies.append(pltpu.make_async_copy(tiles_in.at[at], tiles_out.at[at], sems.at[systems + k]))
    for copy in copies:
        copy.start()
    tiles = ids_ref.shape[-1]
    lanes = 128
    ids = jnp.concatenate([ids_ref[0], jnp.full((1, lanes - tiles), -1, I32)], axis=1)
    owner = lax.shift_right_arithmetic(ids, shift)
    square = (lanes, lanes)
    down, across = iota(square, 0), iota(square, 1)
    owner_f = jnp.broadcast_to(owner.astype(F32), square)
    owner_col = jnp.sum(jnp.where(down == across, owner_f, 0.0), axis=1, keepdims=True)
    same = jnp.where((owner_f == owner_col) & (down < across), 1.0, 0.0)
    rank = jnp.sum(same, axis=0, keepdims=True).astype(I32)
    lane = iota((1, lanes), 1)
    block = jnp.zeros((1, lanes), I32)
    starts = off_ref[0]
    for b in range(1, blocks + 1):
        block = block + (lane >= jnp.broadcast_to(starts[:, b : b + 1], (1, lanes))).astype(I32)
    count = jnp.broadcast_to(count_ref[...], (1, lanes))
    meta_ref[...] = jnp.concatenate([owner, rank, block, count] + [owner] * 4, axis=0)
    end = columns - clon
    for r in range(systems):
        copies[r].wait()
        south_ref[r, 0] = model_ref[r, end - clon : end]
        south_ref[r, 1] = model_ref[r, end:]
        south_ref[r, 2] = damp_out[r, end:]
        north_ref[r, 0] = model_ref[r, 0:clon]
        north_ref[r, 1] = model_ref[r, clon : 2 * clon]
        north_ref[r, 2] = damp_out[r, 0:clon]
    for copy in copies[systems:]:
        copy.wait()


def columns_body(clat, clon, model_ref, damp_ref, north_ref, south_ref, east_ref, west_ref):
    systems, _, depth = model_ref.shape
    for r in range(systems):
        for out, near, beyond in ((east_ref, clon - 1, clon - 2), (west_ref, 0, 1)):
            out[r, 0:clat] = model_ref[r, pl.ds(near, clat, stride=clon), :]
            out[r, clat : 2 * clat] = model_ref[r, pl.ds(beyond, clat, stride=clon), :]
            out[r, 2 * clat : 3 * clat] = damp_ref[r, pl.ds(near, clat, stride=clon), :]
            out[r, 3 * clat :] = jnp.concatenate(
                [
                    north_ref[r, 1, near : near + 1],
                    south_ref[r, 0, near : near + 1],
                    jnp.zeros((6, depth), F32),
                ],
                axis=0,
            )


def six(x, north, south, west, east):
    sub, lane = iota(x.shape, 0), iota(x.shape, 1)
    rows, depth = x.shape
    left = jnp.where(sub == 0, jnp.broadcast_to(west, x.shape), pltpu.roll(x, 1, 0))
    right = jnp.where(sub == rows - 1, jnp.broadcast_to(east, x.shape), pltpu.roll(x, rows - 1, 0))
    above = jnp.where(lane == 0, 0.0, pltpu.roll(x, 1, 1))
    below = jnp.where(lane == depth - 1, 0.0, pltpu.roll(x, depth - 1, 1))
    beside = north + south + left + right + above + below
    return DAMP_WEIGHT * (6.0 * x - beside)


def fold(x):
    parts = [x[i * 8 : (i + 1) * 8] for i in range(x.shape[0] // 8)]
    return functools.reduce(lambda a, b: a + b, parts)


def place(row, lane, value):
    return row + jnp.where(iota(row.shape, 1) == lane, jnp.broadcast_to(value, row.shape), 0.0)


STEP = 8


def dense_body(
    cap,
    clat,
    clon,
    rec_ref,
    corner_ref,
    wanted_ref,
    ray_ref,
    model_ref,
    damp_ref,
    north_ref,
    south_ref,
    west_ref,
    east_ref,
    solution_in,
    search_in,
    bar_out,
    image_out,
    solution_out,
    search_out,
    sums_out,
    chosen_out,
    north_s,
    south_s,
    west_s,
    east_s,
    alphas,
    sems,
):
    systems, _, depth = model_ref.shape
    copies = []
    for r in range(systems):
        for k, (a, b) in enumerate(((solution_in, solution_out), (search_in, search_out))):
            copies.append(pltpu.make_async_copy(a.at[r], b.at[r], sems.at[2 * r + k]))
    for copy in copies:
        copy.start()
    for r in range(systems):
        alphas[r] = jnp.sum(rec_ref[0:1, r : r + 1])
    lat_at, lon_at = lax.axis_index("lat"), lax.axis_index("lon")
    has_north = (lat_at > 0).astype(F32)
    has_south = (lat_at < lax.axis_size("lat") - 1).astype(F32)
    has_west = (lon_at > 0).astype(F32)
    has_east = (lon_at < lax.axis_size("lon") - 1).astype(F32)
    corner_n, corner_s = 3 * clat, 3 * clat + 1

    target = wanted_column(wanted_ref[...], cap) - 1.0
    slots = target.shape[0]
    square = (slots, slots)
    flat = jnp.sum(
        jnp.where(iota(square, 0) == iota(square, 1), jnp.broadcast_to(target, square), 0.0),
        axis=0,
        keepdims=True,
    ).astype(I32)
    wide = (PATCH * clon, slots)
    chosen_out[...] = (jnp.broadcast_to(flat, wide) == iota(wide, 0)).astype(F32).astype(BF16)

    def line(ref, r, i):
        return ref[r, pl.ds(pl.multiple_of(i * clon, clon), clon), :]

    def stencils(ref, r, k, first, last, west, east):
        base = k * STEP
        for j in range(STEP):
            i = base + j
            x = line(ref, r, i)
            if j == 0:
                above = jnp.where(k > 0, line(ref, r, jnp.maximum(i - 1, 0)), first)
            else:
                above = line(ref, r, i - 1)
            if j == STEP - 1:
                below = jnp.where(i + 1 < clat, line(ref, r, jnp.minimum(i + 1, clat - 1)), last)
            else:
                below = line(ref, r, i + 1)
            yield i, x, six(x, above, below, west[pl.ds(i, 1)], east[pl.ds(i, 1)])

    def system(r, row):
        alpha = alphas[r]

        def side(ref, own, flag):
            x, beyond, old = ref[r, 0:clat], ref[r, clat : 2 * clat], ref[r, 2 * clat : 3 * clat]
            upper, lower = ref[r, corner_n : corner_n + 1], ref[r, corner_s : corner_s + 1]
            return (six(x, beyond, own, upper, lower) - alpha * old) * flag

        west_s[...] = side(west_ref, model_ref[r, pl.ds(0, clat, stride=clon), :], has_west)
        east_s[...] = side(east_ref, model_ref[r, pl.ds(clon - 1, clat, stride=clon), :], has_east)
        north_s[...] = has_north * (
            six(
                north_ref[r, 1],
                north_ref[r, 0],
                line(model_ref, r, 0),
                west_ref[r, corner_n : corner_n + 1],
                east_ref[r, corner_n : corner_n + 1],
            )
            - alpha * north_ref[r, 2]
        )
        south_s[...] = has_south * (
            six(
                south_ref[r, 0],
                line(model_ref, r, clat - 1),
                south_ref[r, 1],
                west_ref[r, corner_s : corner_s + 1],
                east_ref[r, corner_s : corner_s + 1],
            )
            - alpha * south_ref[r, 2]
        )

        def damped(k, acc):
            bar_sq, model_sq = acc
            ends = (north_ref[r, 1], south_ref[r, 0], west_ref.at[r], east_ref.at[r])
            for i, x, got in stencils(model_ref, r, k, *ends):
                bar = got - alpha * line(damp_ref, r, i)
                bar_out[r, pl.ds(pl.multiple_of(i * clon, clon), clon), :] = bar
                bar_sq, model_sq = bar_sq + fold(bar * bar), model_sq + fold(x * x)
            return bar_sq, model_sq

        def imaged(k, acc):
            image_sq, cross = acc
            for i, x, image in stencils(bar_out, r, k, north_s[...], south_s[...], west_s, east_s):
                image_out[r, pl.ds(pl.multiple_of(i * clon, clon), clon), :] = image
                image_sq, cross = image_sq + fold(image * image), cross + fold(image * line(model_ref, r, i))
            return image_sq, cross

        zero = jnp.zeros((8, depth), F32)
        bar_sq, model_sq = lax.fori_loop(0, clat // STEP, damped, (zero, zero))
        image_sq, cross = lax.fori_loop(0, clat // STEP, imaged, (zero, zero))
        ray = ray_ref[r, 0]
        residual = jnp.sum(bar_sq, keepdims=True) + jnp.sum(ray * ray, keepdims=True)
        row = place(row, r, residual)
        row = place(row, systems + r, jnp.sum(image_sq, keepdims=True))
        row = place(row, 2 * systems + r, jnp.sum(cross, keepdims=True))
        return place(row, 3 * systems + r, jnp.sum(model_sq, keepdims=True))

    sums_out[...] = lax.fori_loop(0, systems, system, jnp.zeros((1, depth), F32))
    for copy in copies:
        copy.wait()


def combine_body(clon, corner_ref, terms_ref, chosen_ref, image_ref, model_ref, sums_ref, added_ref, parts_ref):
    systems, width, depth = added_ref.shape
    slots = chosen_ref.shape[1]
    chosen = chosen_ref[...]
    row = sums_ref[...]
    here = pl.ds(pl.multiple_of(corner_ref[0] * clon, clon), width)
    for r in range(systems):
        x = terms_ref[pl.ds(r, slots, stride=systems), :]
        high = x.astype(BF16)
        rest = x - high.astype(F32)
        middle = rest.astype(BF16)
        low = (rest - middle.astype(F32)).astype(BF16)
        three = jnp.dot(chosen, jnp.concatenate([high, middle, low], axis=1), preferred_element_type=F32)
        added = three[:, 0:depth] + (three[:, depth : 2 * depth] + three[:, 2 * depth :])
        added_ref[r] = added
        square = jnp.sum(added * (2.0 * image_ref[r, here, :] + added), keepdims=True)
        cross = jnp.sum(added * model_ref[r, here, :], keepdims=True)
        row = place(row, systems + r, square)
        row = place(row, 2 * systems + r, cross)
    parts_ref[...] = jnp.broadcast_to(row, parts_ref.shape)


def finish_body(
    rows_all,
    cells_all,
    clon,
    corner_ref,
    parts_ref,
    rec_ref,
    ray_ref,
    added_ref,
    image_ref,
    model_ref,
    bar_ref,
    solution_ref,
    search_ref,
    ray_out,
    damp_out,
    model_out,
    solution_out,
    search_out,
    rec_out,
    damp_s,
    model_s,
    solution_s,
    search_s,
    coef,
    sems,
):
    systems, columns, depth = image_ref.shape
    total = jnp.sum(parts_ref[...], axis=0, keepdims=True)
    residual_sq, image_sq, cross, model_sq = (total[:, q * systems : (q + 1) * systems] for q in range(4))
    rho_bar, phi_bar = rec_ref[1:2], rec_ref[2:3]
    beta = jnp.sqrt(residual_sq / rows_all + EPSILON)
    update_sq = image_sq / (beta * beta) - 2.0 * cross + beta * beta * model_sq
    alpha = jnp.sqrt(jnp.maximum(update_sq, 0.0) / cells_all + EPSILON)
    rho = jnp.sqrt(rho_bar * rho_bar + beta * beta)
    cosine = rho_bar / rho
    sine = beta / rho
    rec_out[...] = jnp.concatenate([alpha, -cosine * alpha, sine * phi_bar], axis=0)
    scales = (
        1.0 / beta,
        1.0 / (beta * alpha),
        beta / alpha,
        cosine * phi_bar / rho,
        sine * alpha / rho,
    )
    for q, scale in enumerate(scales):
        for s in range(systems):
            coef[q, s] = scale[0, s]
    rows = columns // PIECES

    def outgoing(r, p):
        at = pl.ds(pl.multiple_of(p * rows, rows), rows)
        pairs = (
            (damp_s, damp_out),
            (model_s, model_out),
            (solution_s, solution_out),
            (search_s, search_out),
        )
        return [
            pltpu.make_async_copy(a.at[r, at], b.at[r, at], sems.at[r, p, k]) for k, (a, b) in enumerate(pairs)
        ]

    def piece(n, _):
        r, p = n // PIECES, n % PIECES
        at = pl.ds(pl.multiple_of(p * rows, rows), rows)
        search = search_ref[r, at, :]
        damp_s[r, at, :] = bar_ref[r, at, :] * coef[0, r]
        new = image_ref[r, at, :] * coef[1, r] - model_ref[r, at, :] * coef[2, r]
        model_s[r, at, :] = new
        solution_s[r, at, :] = solution_ref[r, at, :] + search * coef[3, r]
        search_s[r, at, :] = new - search * coef[4, r]
        for k in range(PATCH):
            begin = (corner_ref[0] + k) * clon

            @pl.when((begin >= p * rows) & (begin < (p + 1) * rows))
            def _():
                line = pl.ds(pl.multiple_of(begin, clon), clon)
                more = added_ref[r, k * clon : (k + 1) * clon, :] * coef[1, r]
                model_s[r, line, :] = model_s[r, line, :] + more
                search_s[r, line, :] = search_s[r, line, :] + more

        for copy in outgoing(r, p):
            copy.start()
        return 0

    lax.fori_loop(0, systems * PIECES, piece, 0)
    for r in range(systems):
        ray_out[r] = ray_ref[r] * coef[0, r]

    def settle(n, _):
        for copy in outgoing(n // PIECES, n % PIECES):
            copy.wait()
        return 0

    lax.fori_loop(0, systems * PIECES, settle, 0)


PIECES = 4


def rays_body(cap, blocks, meta_ref, rec_ref, tiles_ref, fetched_ref, old_ref, bar_ref, term_ref, masks, lows):
    tiles, width, depth = tiles_ref.shape[2:]
    systems = old_ref.shape[0]
    group = cap * systems
    for c in range(cap + 1):
        here = lax.shift_right_logical(iota((group, depth), 0), systems.bit_length() - 1) == c
        masks[c] = here.astype(F32).astype(BF16)
    term_ref[...] = jnp.zeros(term_ref.shape, F32)
    lows[...] = jnp.zeros(lows.shape, BF16)
    total = jnp.zeros((blocks * group, width), F32)
    for t in range(tiles):
        owner, rank, block = meta_ref[0, t], meta_ref[1, t], meta_ref[2, t]
        rows = fetched_ref[pl.ds(pl.multiple_of(owner * group, group), group), :]
        left = jnp.concatenate(
            [rows * masks[jnp.where(block == b, rank, cap)] for b in range(blocks)], axis=0
        )
        total = total + lax.dot_general(
            left, tiles_ref[0, 0, t], (((1,), (1,)), ((), ())), preferred_element_type=F32
        )
    for b in range(blocks):
        traced = jnp.zeros((systems, width), F32)
        for c in range(cap):
            at = b * group + c * systems
            traced = traced + total[at : at + systems]
        old = jnp.concatenate(
            [old_ref[r, 0, :, b * width : (b + 1) * width] * rec_ref[0:1, r : r + 1] for r in range(systems)], axis=0
        )
        live = iota((systems, width), 1) + b * width < meta_ref[3, 0]
        bar = jnp.where(live, traced - old, 0.0)
        for r in range(systems):
            bar_ref[r, 0, :, b * width : (b + 1) * width] = bar[r : r + 1]
        lows[b] = jnp.concatenate([bar, jnp.zeros((16 - systems, width), F32)], axis=0).astype(BF16)
    for t in range(tiles):
        slot = meta_ref[0, t] * cap + meta_ref[1, t]
        term = jnp.dot(lows[meta_ref[2, t]], tiles_ref[0, 0, t], preferred_element_type=F32)
        term_ref[slot] = term[:systems]


def shifted(x, axis, step):
    count = lax.axis_size(axis)
    if step > 0:
        pairs = [(i, i + 1) for i in range(count - 1)]
    else:
        pairs = [(i + 1, i) for i in range(count - 1)]
    return lax.ppermute(x, axis, pairs)


def exchange(x):
    return lax.all_to_all(x, AXES, split_axis=0, concat_axis=0, tiled=True)


def per_device(
    sensitivity,
    block_ids,
    block_offsets,
    ray_counts,
    ray_vector,
    damping_vector,
    model_vector,
    solution,
    search,
    recurrence,
):
    lat_size, lon_size = lax.axis_size("lat"), lax.axis_size("lon")
    devices = lat_size * lon_size
    tiles, width, depth = sensitivity.shape[2:]
    blocks = block_offsets.shape[-1] - 1
    systems, clat, clon, _ = model_vector.shape
    columns = clat * clon
    cap = max(2 * ((tiles + devices - 1) // devices), 16 // systems)
    slots = devices * cap
    group = cap * systems
    cells_all = devices * columns * depth
    rows_all = devices * blocks * width + cells_all
    lanes = 128
    full, flat = model_vector.shape, (systems, columns, depth)
    here, there = pltpu.VMEM, pltpu.HBM

    lists = exchange(jnp.broadcast_to(block_ids[0], (devices, 1, tiles))).reshape(devices, tiles)

    served, wanted, corner, model = call(
        functools.partial(serve_body, cap, clat, clon),
        "serve",
        (
            there((slots * systems, depth), BF16),
            here((devices, lanes), F32),
            jax.ShapeDtypeStruct((1,), I32),
            here(flat, F32),
        ),
        [vmem(), hbm()],
        (vmem(), vmem(), smem(), vmem()),
        scratch=[pltpu.VMEM((slots * systems, depth), F32), pltpu.SemaphoreType.DMA((systems,))],
    )(lists, far(model_vector.reshape(flat)))
    fetched = exchange(served.reshape(devices, group, depth)).reshape(slots * systems, depth)

    band = (systems, 3, clon, depth)
    damping, held, north_msg, south_msg, meta = call(
        functools.partial(pack_body, columns.bit_length() - 1, clon, blocks),
        "pack",
        (here(flat, F32), here(sensitivity.shape, BF16), there(band, F32), there(band, F32), jax.ShapeDtypeStruct((8, lanes), I32)),
        [vmem()] * 4 + [hbm(), hbm()],
        (vmem(),) * 5,
        scratch=[pltpu.SemaphoreType.DMA((systems + 2,))],
        moved=4 * systems * columns * depth + 2 * tiles * width * depth,
    )(
        far(block_ids),
        block_offsets,
        ray_counts,
        near(model),
        far(damping_vector.reshape(flat)),
        far(sensitivity),
    )
    north = shifted(south_msg, "lat", 1)
    south = shifted(north_msg, "lat", -1)

    side = (systems, 3 * clat + 8, depth)
    east_msg, west_msg = call(
        functools.partial(columns_body, clat, clon),
        "columns",
        (there(side, F32), there(side, F32)),
        [vmem()] * 4,
        (vmem(), vmem()),
    )(near(model), near(damping), far(north), far(south))
    west = shifted(east_msg, "lon", 1)
    east = shifted(west_msg, "lon", -1)

    ray_bar, terms = call(
        functools.partial(rays_body, cap, blocks),
        "rays",
        (here(ray_vector.shape, F32), there((slots, systems, depth), F32)),
        [smem()] + [vmem()] * 4,
        (vmem(), vmem()),
        scratch=[
            pltpu.VMEM((cap + 1, group, depth), BF16),
            pltpu.VMEM((blocks + 1, 16, width), BF16),
        ],
        flops=4 * tiles * width * depth * 16,
        moved=2 * tiles * width * depth,
    )(meta, far(recurrence), near(held), fetched, far(ray_vector))
    arrived = exchange(terms.reshape(devices, group, depth)).reshape(slots * systems, depth)

    bar, image, solution, search, sums, chosen = call(
        functools.partial(dense_body, cap, clat, clon),
        "dense",
        (here(flat, F32),) * 4 + (here((1, lanes), F32), here((PATCH * clon, slots), BF16)),
        [vmem(), smem()] + [vmem()] * 8 + [hbm()] * 2,
        (vmem(),) * 6,
        scratch=[
            pltpu.VMEM((clon, depth), F32),
            pltpu.VMEM((clon, depth), F32),
            pltpu.VMEM((clat, depth), F32),
            pltpu.VMEM((clat, depth), F32),
            pltpu.SMEM((systems,), F32),
            pltpu.SemaphoreType.DMA((2 * systems,)),
        ],
        flops=40 * systems * columns * depth,
        moved=24 * systems * columns * depth,
    )(
        far(recurrence),
        corner,
        near(wanted),
        near(ray_bar),
        near(model),
        near(damping),
        far(north),
        far(south),
        far(west),
        far(east),
        far(solution.reshape(flat)),
        far(search.reshape(flat)),
    )

    added, parts = call(
        functools.partial(combine_body, clon),
        "combine",
        (here((systems, PATCH * clon, depth), F32), there((devices, lanes), F32)),
        [smem()] + [vmem()] * 5,
        (vmem(),) * 2,
    )(corner, arrived, near(chosen), near(image), near(model), near(sums))
    every = exchange(parts.reshape(devices, 1, lanes)).reshape(devices, lanes)

    outs = call(
        functools.partial(finish_body, float(rows_all), float(cells_all), clon),
        "finish",
        (there(ray_vector.shape, F32),) + (there(flat, F32),) * 4 + (there(recurrence.shape, F32),),
        [smem()] + [vmem()] * 9,
        (vmem(),) + (hbm(),) * 4 + (vmem(),),
        scratch=[
            pltpu.VMEM(flat, F32),
            pltpu.VMEM(flat, F32),
            pltpu.VMEM(flat, F32),
            pltpu.VMEM(flat, F32),
            pltpu.SMEM((5, systems), F32),
            pltpu.SemaphoreType.DMA((systems, PIECES, 4)),
        ],
        flops=10 * systems * columns * depth,
        moved=16 * systems * columns * depth,
    )(
        corner,
        every,
        far(recurrence),
        near(ray_bar),
        near(added),
        near(image),
        near(model),
        near(bar),
        near(solution),
        near(search),
    )
    ray_out, damp_out, model_out, solution_out, search_out, rec_out = outs
    fields = (x.reshape(full) for x in (damp_out, model_out, solution_out, search_out))
    return (ray_out, *fields, rec_out)


def solution(mesh):
    fields = P(None, "lat", "lon", None)
    return jax.shard_map(
        per_device,
        mesh=mesh,
        in_specs=(
            P("lat", "lon", None, None, None),
            P("lat", "lon", None),
            P("lat", "lon", None),
            P("lat", "lon"),
            fields,
            fields,
            fields,
            fields,
            fields,
            P(),
        ),
        out_specs=(fields, fields, fields, fields, fields, P()),
        check_vma=False,
    )
```

time: 168 us -> 105 us (0.62)
  other arithmetic: 47.7 us -> 0 us
  Pallas kernels: 0 us -> 28.9 us
  starting transfers between devices: 36.4 us -> 15.9 us
  blocking collectives: 44.1 us -> 29.2 us
  local copies, waits for them, and re-layouts: 28.8 us -> 17.4 us
  waiting for transfers between devices: 3.41 us -> 11.9 us
  matrix products: 4.7 us -> 0 us
    psum x1 -> x0, blocking collectives: 44.1 us -> none  [per_device(): lax.psum((residual_sq, image_sq, cross_sum, model_sq), ('lat', 'lon'))]
    all_to_all x0 -> x2, blocking collectives: none -> 29.2 us  [exchange(): return lax.all_to_all(x, AXES, split_axis=0, concat_axis=0, tiled=True)]
    pallas_call x0 -> x7, Pallas kernels: none -> 28.9 us  [the longest x1 7.71 us: per_device(): call(functools.partial(dense_body, cap, clat, clon), 'dense', (here(flat,...]
    reduce_sum x4 -> x0, other arithmetic: 18 us -> none  [the longest x1 9.79 us: per_device(): jnp.sum(damp_bar * damp_bar, axis=(1, 2, 3))]
    scatter-add x1 -> x0, other arithmetic: 15.4 us -> none  [per_device(): jnp.zeros((columns_dev + 1, systems, depth), jnp.float32).at[wanted]]
    all_to_all x3 -> x2, starting transfers between devices: 18.7 us -> 8.31 us  [exchange(): return lax.all_to_all(x, AXES, split_axis=0, concat_axis=0, tiled=True)]
    ppermute x8 -> x4, starting transfers between devices: 17.7 us -> 7.62 us  [shifted(): return lax.ppermute(x, axis, pairs)]
    ppermute x8 -> x4, waiting for transfers between devices: 1.9 us -> 11.8 us  [shifted(): return lax.ppermute(x, axis, pairs)]
  transfers between devices with their start and end apart: 11 -> 6, of which waited for: 3 -> 4; matrix products, arithmetic and copies ran while one was open for 33% -> 0% of each run, Pallas kernels for 0% -> 13%
where the time goes in v4:
time: 105 us
  blocking collectives  29.2 us (28%)
  Pallas kernels  28.9 us (28%)
  local copies, waits for them, and re-layouts  17.4 us (17%)
  starting transfers between devices  15.9 us (15%)
  waiting for transfers between devices  11.9 us (11%)
  between operations  1.44 us (1%)
    all_to_all x2, blocking collectives, exchange(): return lax.all_to_all(x, AXES, split_axis=0, concat_axis=0, tiled=True)  29.2 us
    unnamed x40, local copies, waits for them, and re-layouts  16.8 us
    ppermute x4, waiting for transfers between devices, shifted(): return lax.ppermute(x, axis, pairs)  11.8 us
    all_to_all x2, starting transfers between devices, exchange(): return lax.all_to_all(x, AXES, split_axis=0, concat_axis=0, tiled=True)  8.31 us
    pallas_call x1, Pallas kernels, per_device(): call(functools.partial(dense_body, cap, clat, clon), 'dense', (here(flat,...  7.71 us
    ppermute x4, starting transfers between devices, shifted(): return lax.ppermute(x, axis, pairs)  7.62 us
    pallas_call x1, Pallas kernels, per_device(): call(functools.partial(finish_body, float(rows_all), float(cells_all), cl...  6.15 us
    pallas_call x1, Pallas kernels, per_device(): call(functools.partial(rays_body, cap, blocks), 'rays', (here(ray_vector....  4.38 us
  transfers between devices with their start and end apart: 6, of which 4 were waited for; matrix products, arithmetic and copies ran while one was open for 0% of the time, Pallas kernels for 13%

profile of v4, /device:TPU:0, one launch (start us, length us, event | category | flops | bytes accessed | tf_op | source)
XLA Modules:
  0.0 104.8 jit_solution(13106542691401634240)
XLA Ops:
  0.6 0.0 copy-start.13
  0.6 0.7 broadcast_in_dim.3
  1.3 14.3 %all_to_all.20 = s32[32,1,60]{2,1,0:T(1,128)S(1)} all-to-all(s32[32,1,60]{2,1,0:T(1,128)S(1)} %broadcast_in_dim.3), channel_id=1, replica_groups=mesh['lat'=4,'lon'=8] {'lat','lon'}, dimensions={0} | all-to-all | bytes 15360 | tf_op jit(solution)/shard_map/all_to_all | solution.py:499
  15.6 2.5 %serve.1 = (bf16[512,128]{1,0:T(8,128)(2,1)}, f32[32,128]{1,0:T(8,128)S(1)}, s32[1]{0:T(128)}, f32[4,1024,128]{2,1,0:T(8,128)S(1)}) custom-call(s32[32,60]{1,0:T(8,128)S(1)} %bitcast.21, f32[4,1024,128]{2,1,0:T(8,128)} %bitcast.23), custom_call_target="tpu_custom_call" | custom-call | tf_op jit(solution)/shard_map/serve/pallas_call | solution.py:531
  18.0 2.6 %all-to-all-start.1 = ((bf16[32,16,128]{2,1,0:T(8,128)(2,1)}), bf16[32,16,128]{2,1,0:T(8,128)(2,1)S(1)}, u32[]{:S(2)}, u32[]{:S(2)}) async-start(bf16[32,16,128]{2,1,0:T(8,128)(2,1)} %bitcast.27), calls=%async_computation.1 | async-start | bytes 262144 | tf_op jit(solution)/shard_map/all_to_all | solution.py:499
  21.3 0.0 copy-done.13
  21.3 4.2 %pack.1 = (f32[4,1024,128]{2,1,0:T(8,128)S(1)}, bf16[1,1,60,256,128]{4,3,2,1,0:T(8,128)(2,1)S(1)}, f32[4,3,32,128]{3,2,1,0:T(8,128)}, f32[4,3,32,128]{3,2,1,0:T(8,128)}, s32[8,128]{1,0:T(8,128)S(1)}) custom-call(s32[1,1,60]{2,1,0:T(1,128)} %ids_ref.1, s32[1,1,4]{2,1,0:T(1,128)S(1)} %copy-done.13, s32[1,1]{1,0:T(1,128)S(6)} %copy.17.count_ref, ...), custom_call_target="tpu_custom_call" | custom-call | bytes 6029312 | tf_op jit(solution)/shard_map/pack/pallas_call | solution.py:547
  25.5 0.0 copy-start.2
  25.6 1.3 %copy-done.2 = f32[4,1024,128]{2,1,0:T(8,128)} copy-done((f32[4,1024,128]{2,1,0:T(8,128)}, f32[4,1024,128]{2,1,0:T(8,128)S(1)}, u32[]{:S(2)}) %copy-start.2) | copy-done | bytes 2097176
  26.9 0.0 copy-start.5
  26.9 1.9 %copy-done.5 = bf16[1,1,60,256,128]{4,3,2,1,0:T(8,128)(2,1)} copy-done((bf16[1,1,60,256,128]{4,3,2,1,0:T(8,128)(2,1)}, bf16[1,1,60,256,128]{4,3,2,1,0:T(8,128)(2,1)S(1)}, u32[]{:S(2)}) %copy-start.5) | copy-done | bytes 3932184
  28.7 0.1 all-to-all-done.1
  28.9 0.0 copy-start.6
  28.9 2.1 %copy-done.6 = bf16[1,1,60,256,128]{4,3,2,1,0:T(8,128)(2,1)S(1)} copy-done((bf16[1,1,60,256,128]{4,3,2,1,0:T(8,128)(2,1)S(1)}, bf16[1,1,60,256,128]{4,3,2,1,0:T(8,128)(2,1)}, u32[]{:S(2)}) %copy-start.6) | copy-done | bytes 3932184
  31.0 0.0 copy-start.19
  31.0 0.0 copy-start.18
  31.0 4.4 %rays.1 = (f32[4,1,1,768]{3,2,1,0:T(1,128)S(1)}, f32[128,4,128]{2,1,0:T(4,128)}) custom-call(s32[8,128]{1,0:T(8,128)S(1)} %get-tuple-element.35.meta_ref, f32[3,4]{1,0:T(4,128)} %rec_ref.5, bf16[1,1,60,256,128]{4,3,2,1,0:T(8,128)(2,1)S(1)} %copy-done.6, bf16[512,128]{1,0:T(8,128)(2,1)S(1)} %bitcast.19, f32[4,1,1,768]{3,2,1,0:T(1,128)} %old_ref.1), custom_call_target="tpu_custom_call" | custom-call | flops 125829120 | bytes 3932160 | tf_op jit(solution)/shard_map/rays/pallas_call | solution.py:577
  35.4 5.7 %all-to-all-start.2 = ((f32[32,16,128]{2,1,0:T(8,128)}), f32[32,16,128]{2,1,0:T(8,128)S(1)}, u32[]{:S(2)}, u32[]{:S(2)}) async-start(f32[32,16,128]{2,1,0:T(8,128)} %bitcast.26), calls=%async_computation.2 | async-start | bytes 524288 | tf_op jit(solution)/shard_map/all_to_all | solution.py:499
  41.1 0.0 copy-done.19
  41.1 3.7 %collective-permute-start = (f32[4,3,32,128]{3,2,1,0:T(8,128)S(1)}, f32[4,3,32,128]{3,2,1,0:T(8,128)S(1)}, u32[]{:S(2)}, u32[]{:S(2)}) collective-permute-start(f32[4,3,32,128]{3,2,1,0:T(8,128)S(1)} %copy-done.19), channel_id=1, source_target_pairs={{0,8},{8,16},{16,24},{1,9},{9,17},{17,25},{2,10},{10,18},{18,26},{... | collective-permute-start | bytes 589832 | tf_op jit(solution)/shard_map/ppermute | solution.py:495
  44.8 0.0 copy-done.18
  44.8 1.3 %collective-permute-start.1 = (f32[4,3,32,128]{3,2,1,0:T(8,128)S(1)}, f32[4,3,32,128]{3,2,1,0:T(8,128)S(1)}, u32[]{:S(2)}, u32[]{:S(2)}) collective-permute-start(f32[4,3,32,128]{3,2,1,0:T(8,128)S(1)} %copy-done.18), channel_id=1, source_target_pairs={{8,0},{16,8},{24,16},{9,1},{17,9},{25,17},{10,2},{18,10},{26,18},{... | collective-permute-start | bytes 589832 | tf_op jit(solution)/shard_map/ppermute | solution.py:495
  46.1 4.2 %collective-permute-done.north_ref = f32[4,3,32,128]{3,2,1,0:T(8,128)S(1)} collective-permute-done((f32[4,3,32,128]{3,2,1,0:T(8,128)S(1)}, f32[4,3,32,128]{3,2,1,0:T(8,128)S(1)}, u32[]{:S(2)}, u32[]{:S(2)}) %collective-permute-start) | collective-permute-done | bytes 196640 | tf_op jit(solution)/shard_map/ppermute | solution.py:495
  50.3 0.0 copy-start.14
  50.3 3.7 %collective-permute-done.1.south_ref = f32[4,3,32,128]{3,2,1,0:T(8,128)S(1)} collective-permute-done((f32[4,3,32,128]{3,2,1,0:T(8,128)S(1)}, f32[4,3,32,128]{3,2,1,0:T(8,128)S(1)}, u32[]{:S(2)}, u32[]{:S(2)}) %collective-permute-start.1) | collective-permute-done | bytes 196640 | tf_op jit(solution)/shard_map/ppermute | solution.py:495
  54.0 0.0 copy-start.15
  54.0 0.0 copy-done.14
  54.0 0.7 copy-done.15
  54.7 0.0 copy-start.3
  54.7 1.6 %copy-done.3 = f32[4,1024,128]{2,1,0:T(8,128)S(1)} copy-done((f32[4,1024,128]{2,1,0:T(8,128)S(1)}, f32[4,1024,128]{2,1,0:T(8,128)}, u32[]{:S(2)}) %copy-start.3) | copy-done | bytes 2097176
  56.3 0.0 copy-start.4
  56.3 2.2 %columns.1 = (f32[4,104,128]{2,1,0:T(8,128)}, f32[4,104,128]{2,1,0:T(8,128)}) custom-call(f32[4,1024,128]{2,1,0:T(8,128)S(1)} %get-tuple-element.34.model_ref, f32[4,1024,128]{2,1,0:T(8,128)S(1)} %copy-done.3, f32[4,3,32,128]{3,2,1,0:T(8,128)} %copy-done.14, f32[4,3,32,128]{3,2,1,0:T(8,128)} %copy-done.15), custom_call_target="tpu_custom_call" | custom-call | tf_op jit(solution)/shard_map/columns/pallas_call | solution.py:567
  58.4 1.4 %collective-permute-start.2 = (f32[4,104,128]{2,1,0:T(8,128)}, f32[4,104,128]{2,1,0:T(8,128)S(1)}, u32[]{:S(2)}, u32[]{:S(2)}) collective-permute-start(f32[4,104,128]{2,1,0:T(8,128)} %get-tuple-element.44), channel_id=1, source_target_pairs={{0,1},{1,2},{2,3},{3,4},{4,5},{5,6},{6,7},{8,9},{9,10},{10,11},{11... | collective-permute-start | bytes 638984 | tf_op jit(solution)/shard_map/ppermute | solution.py:495
  59.8 1.3 %collective-permute-start.3 = (f32[4,104,128]{2,1,0:T(8,128)}, f32[4,104,128]{2,1,0:T(8,128)S(1)}, u32[]{:S(2)}, u32[]{:S(2)}) collective-permute-start(f32[4,104,128]{2,1,0:T(8,128)} %get-tuple-element.45), channel_id=1, source_target_pairs={{1,0},{2,1},{3,2},{4,3},{5,4},{6,5},{7,6},{9,8},{10,9},{11,10},{12... | collective-permute-start | bytes 638984 | tf_op jit(solution)/shard_map/ppermute | solution.py:495
  61.1 0.0 collective-permute-done.2.west_ref
  61.1 0.0 copy-start.16
  61.1 3.9 %collective-permute-done.3.east_ref = f32[4,104,128]{2,1,0:T(8,128)S(1)} collective-permute-done((f32[4,104,128]{2,1,0:T(8,128)}, f32[4,104,128]{2,1,0:T(8,128)S(1)}, u32[]{:S(2)}, u32[]{:S(2)}) %collective-permute-start.3) | collective-permute-done | bytes 213024 | tf_op jit(solution)/shard_map/ppermute | solution.py:495
  65.0 0.0 copy-start.17
  65.0 0.0 copy-done.16
  65.1 0.7 copy-done.17
  65.7 0.0 copy-done.4
  65.7 7.7 %dense.1 = (f32[4,1024,128]{2,1,0:T(8,128)S(1)}, f32[4,1024,128]{2,1,0:T(8,128)S(1)}, f32[4,1024,128]{2,1,0:T(8,128)S(1)}, f32[4,1024,128]{2,1,0:T(8,128)S(1)}, ...) custom-call(f32[3,4]{1,0:T(4,128)} %rec_ref.5, s32[1]{0:T(128)} %get-tuple-element.33.corner_ref, ...), custom_call_target="tpu_custom_call" | custom-call | flops 20971520 | bytes 12582912 | tf_op jit(solution)/shard_map/dense/pallas_call | solution.py:592
  73.4 0.0 copy-start
  73.5 1.3 %copy-done = f32[4,1024,128]{2,1,0:T(8,128)} copy-done((f32[4,1024,128]{2,1,0:T(8,128)}, f32[4,1024,128]{2,1,0:T(8,128)S(1)}, u32[]{:S(2)}) %copy-start) | copy-done | bytes 2097176
  74.8 0.0 copy-start.7
  74.8 1.3 %copy-done.7 = f32[4,1024,128]{2,1,0:T(8,128)} copy-done((f32[4,1024,128]{2,1,0:T(8,128)}, f32[4,1024,128]{2,1,0:T(8,128)S(1)}, u32[]{:S(2)}) %copy-start.7) | copy-done | bytes 2097176
  76.1 0.0 copy-start.9
  76.1 1.3 %copy-done.9 = f32[4,1024,128]{2,1,0:T(8,128)} copy-done((f32[4,1024,128]{2,1,0:T(8,128)}, f32[4,1024,128]{2,1,0:T(8,128)S(1)}, u32[]{:S(2)}) %copy-start.9) | copy-done | bytes 2097176
  77.4 0.0 copy-start.11
  77.4 1.3 %copy-done.11 = f32[4,1024,128]{2,1,0:T(8,128)} copy-done((f32[4,1024,128]{2,1,0:T(8,128)}, f32[4,1024,128]{2,1,0:T(8,128)S(1)}, u32[]{:S(2)}) %copy-start.11) | copy-done | bytes 2097176
  78.7 0.0 all-to-all-done.2
  78.7 0.0 copy-start.1
  78.7 1.6 %copy-done.1 = f32[4,1024,128]{2,1,0:T(8,128)S(1)} copy-done((f32[4,1024,128]{2,1,0:T(8,128)S(1)}, f32[4,1024,128]{2,1,0:T(8,128)}, u32[]{:S(2)}) %copy-start.1) | copy-done | bytes 2097176
  80.3 0.0 copy-start.8
  80.3 0.0 copy-start.10
  80.3 1.8 %combine.1 = (f32[4,128,128]{2,1,0:T(8,128)S(1)}, f32[32,128]{1,0:T(8,128)}) custom-call(s32[1]{0:T(128)} %get-tuple-element.33.corner_ref, f32[512,128]{1,0:T(8,128)S(1)} %bitcast.18, bf16[128,128]{1,0:T(8,128)(2,1)S(1)} %get-tuple-element.46.chosen_ref, f32[4,1024,128]{2,1,0:T(8,128)S(1)} %copy-done.1, f32[4,1024,128]{2,1,0:T(8,128)S(1)} %get-tuple-element.34.model_ref, ...), custom_call_target="tpu_custom_call" | custom-call | tf_op jit(solution)/shard_map/combine/pallas_call | solution.py:623
  82.1 14.9 %all_to_all.21 = f32[32,1,128]{2,1,0:T(1,128)S(1)} all-to-all(f32[32,1,128]{2,1,0:T(1,128)} %bitcast.28), channel_id=1, replica_groups=mesh['lat'=4,'lon'=8] {'lat','lon'}, dimensions={0} | all-to-all | bytes 32768 | tf_op jit(solution)/shard_map/all_to_all | solution.py:499
  97.0 0.0 copy-done.8
  97.0 0.0 copy-done.10
  97.0 0.0 copy-start.12
  97.0 1.6 %copy-done.12 = f32[4,1024,128]{2,1,0:T(8,128)S(1)} copy-done((f32[4,1024,128]{2,1,0:T(8,128)S(1)}, f32[4,1024,128]{2,1,0:T(8,128)}, u32[]{:S(2)}) %copy-start.12) | copy-done | bytes 2097176
  98.6 6.2 %finish.1 = (f32[4,1,1,768]{3,2,1,0:T(1,128)}, f32[4,1024,128]{2,1,0:T(8,128)}, f32[4,1024,128]{2,1,0:T(8,128)}, f32[4,1024,128]{2,1,0:T(8,128)}, f32[4,1024,128]{2,1,0:T(8,128)}, /*index=5*/f32[3,4]{1,0:T(4,128)}) custom-call(s32[1]{0:T(128)} %get-tuple-element.33.corner_ref, f32[32,128]{1,0:T(8,128)S(1)} %bitcast.20, f32[3,4]{1,0:T(4,128)} %rec_ref.5, ...), custom_call_target="tpu_custom_call" | custom-call | flops 5242880 | bytes 8388608 | tf_op jit(solution)/shard_map/finish/pallas_call | solution.py:632
Async XLA Ops:
  0.6 20.6 %copy-start.13 = (s32[1,1,4]{2,1,0:T(1,128)S(1)}, s32[1,1,4]{2,1,0:T(1,128)}, u32[]{:S(2)}) copy-start(s32[1,1,4]{2,1,0:T(1,128)} %off_ref.1) | copy-start | bytes 52
  18.0 10.8 %all-to-all-start.1 = ((bf16[32,16,128]{2,1,0:T(8,128)(2,1)}), bf16[32,16,128]{2,1,0:T(8,128)(2,1)S(1)}, u32[]{:S(2)}, u32[]{:S(2)}) async-start(bf16[32,16,128]{2,1,0:T(8,128)(2,1)} %bitcast.27), calls=%async_computation.1 | async-start | bytes 262144 | tf_op jit(solution)/shard_map/all_to_all | solution.py:499
  25.5 1.3 %copy-start.2 = (f32[4,1024,128]{2,1,0:T(8,128)}, f32[4,1024,128]{2,1,0:T(8,128)S(1)}, u32[]{:S(2)}) copy-start(f32[4,1024,128]{2,1,0:T(8,128)S(1)} %get-tuple-element.41.damp_ref) | copy-start | bytes 6291460
  26.9 1.9 %copy-start.5 = (bf16[1,1,60,256,128]{4,3,2,1,0:T(8,128)(2,1)}, bf16[1,1,60,256,128]{4,3,2,1,0:T(8,128)(2,1)S(1)}, u32[]{:S(2)}) copy-start(bf16[1,1,60,256,128]{4,3,2,1,0:T(8,128)(2,1)S(1)} %get-tuple-element.36.tiles_ref) | copy-start | bytes 11796484
  28.9 2.1 %copy-start.6 = (bf16[1,1,60,256,128]{4,3,2,1,0:T(8,128)(2,1)S(1)}, bf16[1,1,60,256,128]{4,3,2,1,0:T(8,128)(2,1)}, u32[]{:S(2)}) copy-start(bf16[1,1,60,256,128]{4,3,2,1,0:T(8,128)(2,1)} %copy-done.5) | copy-start | bytes 11796484
  31.0 10.1 %copy-start.19 = (f32[4,3,32,128]{3,2,1,0:T(8,128)S(1)}, f32[4,3,32,128]{3,2,1,0:T(8,128)}, u32[]{:S(2)}) copy-start(f32[4,3,32,128]{3,2,1,0:T(8,128)} %get-tuple-element.42) | copy-start | bytes 589828
  31.0 13.8 %copy-start.18 = (f32[4,3,32,128]{3,2,1,0:T(8,128)S(1)}, f32[4,3,32,128]{3,2,1,0:T(8,128)}, u32[]{:S(2)}) copy-start(f32[4,3,32,128]{3,2,1,0:T(8,128)} %get-tuple-element.43) | copy-start | bytes 589828
  35.4 43.4 %all-to-all-start.2 = ((f32[32,16,128]{2,1,0:T(8,128)}), f32[32,16,128]{2,1,0:T(8,128)S(1)}, u32[]{:S(2)}, u32[]{:S(2)}) async-start(f32[32,16,128]{2,1,0:T(8,128)} %bitcast.26), calls=%async_computation.2 | async-start | bytes 524288 | tf_op jit(solution)/shard_map/all_to_all | solution.py:499
  41.1 9.2 %collective-permute-start = (f32[4,3,32,128]{3,2,1,0:T(8,128)S(1)}, f32[4,3,32,128]{3,2,1,0:T(8,128)S(1)}, u32[]{:S(2)}, u32[]{:S(2)}) collective-permute-start(f32[4,3,32,128]{3,2,1,0:T(8,128)S(1)} %copy-done.19), channel_id=1, source_target_pairs={{0,8},{8,16},{16,24},{1,9},{9,17},{17,25},{2,10},{10,18},{18,26},{... | collective-permute-start | bytes 589832 | tf_op jit(solution)/shard_map/ppermute | solution.py:495
  44.8 9.2 %collective-permute-start.1 = (f32[4,3,32,128]{3,2,1,0:T(8,128)S(1)}, f32[4,3,32,128]{3,2,1,0:T(8,128)S(1)}, u32[]{:S(2)}, u32[]{:S(2)}) collective-permute-start(f32[4,3,32,128]{3,2,1,0:T(8,128)S(1)} %copy-done.18), channel_id=1, source_target_pairs={{8,0},{16,8},{24,16},{9,1},{17,9},{25,17},{10,2},{18,10},{26,18},{... | collective-permute-start | bytes 589832 | tf_op jit(solution)/shard_map/ppermute | solution.py:495
  50.3 3.7 %copy-start.14 = (f32[4,3,32,128]{3,2,1,0:T(8,128)}, f32[4,3,32,128]{3,2,1,0:T(8,128)S(1)}, u32[]{:S(2)}) copy-start(f32[4,3,32,128]{3,2,1,0:T(8,128)S(1)} %collective-permute-done.north_ref) | copy-start | bytes 589828
  54.0 0.7 copy-start.15
  54.7 1.6 %copy-start.3 = (f32[4,1024,128]{2,1,0:T(8,128)S(1)}, f32[4,1024,128]{2,1,0:T(8,128)}, u32[]{:S(2)}) copy-start(f32[4,1024,128]{2,1,0:T(8,128)} %copy-done.2) | copy-start | bytes 6291460
  56.3 9.4 %copy-start.4 = (f32[4,1024,128]{2,1,0:T(8,128)S(1)}, f32[4,1024,128]{2,1,0:T(8,128)}, u32[]{:S(2)}) copy-start(f32[4,1024,128]{2,1,0:T(8,128)} %copy-done.2) | copy-start | bytes 6291460
  58.4 2.7 %collective-permute-start.2 = (f32[4,104,128]{2,1,0:T(8,128)}, f32[4,104,128]{2,1,0:T(8,128)S(1)}, u32[]{:S(2)}, u32[]{:S(2)}) collective-permute-start(f32[4,104,128]{2,1,0:T(8,128)} %get-tuple-element.44), channel_id=1, source_target_pairs={{0,1},{1,2},{2,3},{3,4},{4,5},{5,6},{6,7},{8,9},{9,10},{10,11},{11... | collective-permute-start | bytes 638984 | tf_op jit(solution)/shard_map/ppermute | solution.py:495
  59.8 5.2 %collective-permute-start.3 = (f32[4,104,128]{2,1,0:T(8,128)}, f32[4,104,128]{2,1,0:T(8,128)S(1)}, u32[]{:S(2)}, u32[]{:S(2)}) collective-permute-start(f32[4,104,128]{2,1,0:T(8,128)} %get-tuple-element.45), channel_id=1, source_target_pairs={{1,0},{2,1},{3,2},{4,3},{5,4},{6,5},{7,6},{9,8},{10,9},{11,10},{12... | collective-permute-start | bytes 638984 | tf_op jit(solution)/shard_map/ppermute | solution.py:495
  61.1 3.9 %copy-start.16 = (f32[4,104,128]{2,1,0:T(8,128)}, f32[4,104,128]{2,1,0:T(8,128)S(1)}, u32[]{:S(2)}) copy-start(f32[4,104,128]{2,1,0:T(8,128)S(1)} %collective-permute-done.2.west_ref) | copy-start | bytes 638980
  65.0 0.7 copy-start.17
  73.4 1.3 %copy-start = (f32[4,1024,128]{2,1,0:T(8,128)}, f32[4,1024,128]{2,1,0:T(8,128)S(1)}, u32[]{:S(2)}) copy-start(f32[4,1024,128]{2,1,0:T(8,128)S(1)} %get-tuple-element.47.image_ref) | copy-start | bytes 6291460
  74.8 1.3 %copy-start.7 = (f32[4,1024,128]{2,1,0:T(8,128)}, f32[4,1024,128]{2,1,0:T(8,128)S(1)}, u32[]{:S(2)}) copy-start(f32[4,1024,128]{2,1,0:T(8,128)S(1)} %get-tuple-element.51.bar_ref) | copy-start | bytes 6291460
  76.1 1.3 %copy-start.9 = (f32[4,1024,128]{2,1,0:T(8,128)}, f32[4,1024,128]{2,1,0:T(8,128)S(1)}, u32[]{:S(2)}) copy-start(f32[4,1024,128]{2,1,0:T(8,128)S(1)} %get-tuple-element.52.solution_ref) | copy-start | bytes 6291460
  77.4 1.3 %copy-start.11 = (f32[4,1024,128]{2,1,0:T(8,128)}, f32[4,1024,128]{2,1,0:T(8,128)S(1)}, u32[]{:S(2)}) copy-start(f32[4,1024,128]{2,1,0:T(8,128)S(1)} %get-tuple-element.53.search_ref) | copy-start | bytes 6291460
  78.7 1.6 %copy-start.1 = (f32[4,1024,128]{2,1,0:T(8,128)S(1)}, f32[4,1024,128]{2,1,0:T(8,128)}, u32[]{:S(2)}) copy-start(f32[4,1024,128]{2,1,0:T(8,128)} %copy-done) | copy-start | bytes 6291460
  80.3 16.7 %copy-start.8 = (f32[4,1024,128]{2,1,0:T(8,128)S(1)}, f32[4,1024,128]{2,1,0:T(8,128)}, u32[]{:S(2)}) copy-start(f32[4,1024,128]{2,1,0:T(8,128)} %copy-done.7) | copy-start | bytes 6291460
  80.3 16.7 %copy-start.10 = (f32[4,1024,128]{2,1,0:T(8,128)S(1)}, f32[4,1024,128]{2,1,0:T(8,128)}, u32[]{:S(2)}) copy-start(f32[4,1024,128]{2,1,0:T(8,128)} %copy-done.9) | copy-start | bytes 6291460
  97.0 1.6 %copy-start.12 = (f32[4,1024,128]{2,1,0:T(8,128)S(1)}, f32[4,1024,128]{2,1,0:T(8,128)}, u32[]{:S(2)}) copy-start(f32[4,1024,128]{2,1,0:T(8,128)} %copy-done.11) | copy-start | bytes 6291460

commit v5 on v4

--- a/solution.py
+++ b/solution.py
@@ -52,6 +52,9 @@
     )
 
 
+STEP = 8
+
+
 def wanted_column(wanted, cap):
     devices, lanes = wanted.shape
     rows = devices * cap
@@ -60,11 +63,8 @@
     return jnp.sum(jnp.where(pick, spread, 0.0), axis=1, keepdims=True)
 
 
-def serve_body(cap, clat, clon, lists_ref, model_in, served_ref, wanted_ref, corner_ref, model_ref, mixed, sems):
-    systems, _, depth = model_ref.shape
-    copies = [pltpu.make_async_copy(model_in.at[r], model_ref.at[r], sems.at[r]) for r in range(systems)]
-    for copy in copies:
-        copy.start()
+def serve_body(cap, clat, clon, lists_ref, model_in, served_ref, wanted_ref, corner_ref, patch, mixed, sems):
+    systems, width, depth = patch.shape
     devices, tiles = lists_ref.shape
     lanes = 128
     shift = (clat * clon).bit_length() - 1
@@ -75,6 +75,10 @@
     first = jnp.min(jnp.where(mine, column, clat * clon))
     corner = jnp.minimum(lax.shift_right_logical(first, clon.bit_length() - 1), clat - PATCH)
     corner_ref[0] = corner
+    at = pl.ds(pl.multiple_of(corner * clon, clon), width)
+    copies = [pltpu.make_async_copy(model_in.at[r, at], patch.at[r], sems.at[r]) for r in range(systems)]
+    for copy in copies:
+        copy.start()
     ahead = (iota((lanes, lanes), 0) < iota((lanes, lanes), 1)).astype(F32).astype(BF16)
     rank = jnp.dot(mine.astype(F32).astype(BF16), ahead, preferred_element_type=F32)
     value = (column - corner * clon + 1).astype(F32)
@@ -86,38 +90,36 @@
     wanted_ref[...] = wanted
     target = wanted_column(wanted, cap).astype(I32) - 1
     rows = target.shape[0]
-    width = PATCH * clon
     chosen = (jnp.broadcast_to(target, (rows, width)) == iota((rows, width), 1)).astype(F32).astype(BF16)
     for r in range(systems):
         copies[r].wait()
-        table = model_ref[r, pl.ds(pl.multiple_of(corner * clon, clon), width), :].astype(BF16)
+        table = patch[r].astype(BF16)
         mixed[pl.ds(r, rows, stride=systems), :] = jnp.dot(chosen, table, preferred_element_type=F32)
     served_ref[...] = mixed[...].astype(BF16)
 
 
-def pack_body(
-    shift,
-    clon,
-    blocks,
-    ids_ref,
-    off_ref,
-    count_ref,
-    model_ref,
-    damp_in,
-    tiles_in,
-    damp_out,
-    tiles_out,
-    north_ref,
-    south_ref,
-    meta_ref,
-    sems,
+def pack_body(after_ref, model_in, damp_in, north_ref, south_ref, sems):
+    last = model_in.shape[1] - 1
+    pairs = (
+        (model_in.at[:, pl.ds(last - 1, 2)], south_ref.at[:, pl.ds(0, 2)]),
+        (damp_in.at[:, pl.ds(last, 1)], south_ref.at[:, pl.ds(2, 1)]),
+        (model_in.at[:, pl.ds(0, 2)], north_ref.at[:, pl.ds(0, 2)]),
+        (damp_in.at[:, pl.ds(0, 1)], north_ref.at[:, pl.ds(2, 1)]),
+    )
+    copies = [pltpu.make_async_copy(a, b, sems.at[i]) for i, (a, b) in enumerate(pairs)]
+    for copy in copies:
+        copy.start()
+    for copy in copies:
+        copy.wait()
+
+
+def flanks_body(
+    shift, blocks, after_ref, ids_ref, off_ref, count_ref, model_in, damp_in, east_ref, west_ref, meta_ref, slabs, sems
 ):
-    systems, columns, _ = model_ref.shape
-    half = tiles_in.shape[2] // 2
-    copies = [pltpu.make_async_copy(damp_in.at[r], damp_out.at[r], sems.at[r]) for r in range(systems)]
-    for k, part in enumerate((pl.ds(0, half), pl.ds(half, tiles_in.shape[2] - half))):
-        at = (0, 0, part)
-        copies.append(pltpu.make_async_copy(tiles_in.at[at], tiles_out.at[at], sems.at[systems + k]))
+    systems, clat, clon, depth = model_in.shape
+    copies = []
+    for k, (ref, at) in enumerate(((model_in, 0), (model_in, clon - 8), (damp_in, 0), (damp_in, clon - 8))):
+        copies.append(pltpu.make_async_copy(ref.at[:, :, pl.ds(at, 8)], slabs.at[k], sems.at[k]))
     for copy in copies:
         copy.start()
     tiles = ids_ref.shape[-1]
@@ -137,30 +139,28 @@
         block = block + (lane >= jnp.broadcast_to(starts[:, b : b + 1], (1, lanes))).astype(I32)
     count = jnp.broadcast_to(count_ref[...], (1, lanes))
     meta_ref[...] = jnp.concatenate([owner, rank, block, count] + [owner] * 4, axis=0)
-    end = columns - clon
+    for copy in copies:
+        copy.wait()
+    rows = slabs.reshape(4, systems, clat * 8, depth)
     for r in range(systems):
-        copies[r].wait()
-        south_ref[r, 0] = model_ref[r, end - clon : end]
-        south_ref[r, 1] = model_ref[r, end:]
-        south_ref[r, 2] = damp_out[r, end:]
-        north_ref[r, 0] = model_ref[r, 0:clon]
-        north_ref[r, 1] = model_ref[r, clon : 2 * clon]
-        north_ref[r, 2] = damp_out[r, 0:clon]
-    for copy in copies[systems:]:
-        copy.wait()
-
-
-def columns_body(clat, clon, model_ref, damp_ref, north_ref, south_ref, east_ref, west_ref):
-    systems, _, depth = model_ref.shape
+        for out, slab, near_at, beyond in ((east_ref, 1, 7, 6), (west_ref, 0, 0, 1)):
+            out[r, 0:clat] = rows[slab, r, pl.ds(near_at, clat, stride=8), :]
+            out[r, clat : 2 * clat] = rows[slab, r, pl.ds(beyond, clat, stride=8), :]
+            out[r, 2 * clat : 3 * clat] = rows[slab + 2, r, pl.ds(near_at, clat, stride=8), :]
+            out[r, 3 * clat :] = jnp.zeros((8, depth), F32)
+
+
+def corners_body(east_in, west_in, north_ref, south_ref, east_ref, west_ref):
+    systems, long, depth = east_ref.shape
+    at = long - 8
+    clon = north_ref.shape[2]
     for r in range(systems):
-        for out, near, beyond in ((east_ref, clon - 1, clon - 2), (west_ref, 0, 1)):
-            out[r, 0:clat] = model_ref[r, pl.ds(near, clat, stride=clon), :]
-            out[r, clat : 2 * clat] = model_ref[r, pl.ds(beyond, clat, stride=clon), :]
-            out[r, 2 * clat : 3 * clat] = damp_ref[r, pl.ds(near, clat, stride=clon), :]
-            out[r, 3 * clat :] = jnp.concatenate(
+        for ref, out, near_at in ((east_in, east_ref, clon - 1), (west_in, west_ref, 0)):
+            out[r, 0:at] = ref[r, 0:at]
+            out[r, at:] = jnp.concatenate(
                 [
-                    north_ref[r, 1, near : near + 1],
-                    south_ref[r, 0, near : near + 1],
+                    north_ref[r, 1, near_at : near_at + 1],
+                    south_ref[r, 0, near_at : near_at + 1],
                     jnp.zeros((6, depth), F32),
                 ],
                 axis=0,
@@ -168,10 +168,13 @@
 
 
 def six(x, north, south, west, east):
-    sub, lane = iota(x.shape, 0), iota(x.shape, 1)
+    lane = iota(x.shape, 1)
     rows, depth = x.shape
-    left = jnp.where(sub == 0, jnp.broadcast_to(west, x.shape), pltpu.roll(x, 1, 0))
-    right = jnp.where(sub == rows - 1, jnp.broadcast_to(east, x.shape), pltpu.roll(x, rows - 1, 0))
+    left, right = pltpu.roll(x, 1, 0), pltpu.roll(x, rows - 1, 0)
+    ends = (8, depth)
+    row = iota(ends, 0)
+    left = jnp.concatenate([jnp.where(row == 0, jnp.broadcast_to(west, ends), left[:8]), left[8:]], axis=0)
+    right = jnp.concatenate([right[:-8], jnp.where(row == 7, jnp.broadcast_to(east, ends), right[-8:])], axis=0)
     above = jnp.where(lane == 0, 0.0, pltpu.roll(x, 1, 1))
     below = jnp.where(lane == depth - 1, 0.0, pltpu.roll(x, depth - 1, 1))
     beside = north + south + left + right + above + below
@@ -185,9 +188,6 @@
 
 def place(row, lane, value):
     return row + jnp.where(iota(row.shape, 1) == lane, jnp.broadcast_to(value, row.shape), 0.0)
-
-
-STEP = 8
 
 
 def dense_body(
@@ -198,20 +198,22 @@
     corner_ref,
     wanted_ref,
     ray_ref,
-    model_ref,
-    damp_ref,
+    model_in,
+    damp_in,
     north_ref,
     south_ref,
     west_ref,
     east_ref,
-    solution_in,
-    search_in,
+    bar_sent,
+    image_sent,
+    sums_out,
+    patch_out,
+    model_patch_out,
+    chosen_out,
+    model_ref,
+    damp_ref,
     bar_out,
     image_out,
-    solution_out,
-    search_out,
-    sums_out,
-    chosen_out,
     north_s,
     south_s,
     west_s,
@@ -220,12 +222,22 @@
     sems,
 ):
     systems, _, depth = model_ref.shape
-    copies = []
+
+    def incoming(r):
+        return (
+            pltpu.make_async_copy(model_in.at[r], model_ref.at[r], sems.at[r, 0]),
+            pltpu.make_async_copy(damp_in.at[r], damp_ref.at[r], sems.at[r, 1]),
+        )
+
+    def outgoing(r):
+        return (
+            pltpu.make_async_copy(bar_out.at[r], bar_sent.at[r], sems.at[r, 2]),
+            pltpu.make_async_copy(image_out.at[r], image_sent.at[r], sems.at[r, 3]),
+        )
+
     for r in range(systems):
-        for k, (a, b) in enumerate(((solution_in, solution_out), (search_in, search_out))):
-            copies.append(pltpu.make_async_copy(a.at[r], b.at[r], sems.at[2 * r + k]))
-    for copy in copies:
-        copy.start()
+        for copy in incoming(r):
+            copy.start()
     for r in range(systems):
         alphas[r] = jnp.sum(rec_ref[0:1, r : r + 1])
     lat_at, lon_at = lax.axis_index("lat"), lax.axis_index("lon")
@@ -266,6 +278,8 @@
 
     def system(r, row):
         alpha = alphas[r]
+        for copy in incoming(r):
+            copy.wait()
 
         def side(ref, own, flag):
             x, beyond, old = ref[r, 0:clat], ref[r, clat : 2 * clat], ref[r, 2 * clat : 3 * clat]
@@ -314,6 +328,11 @@
         zero = jnp.zeros((8, depth), F32)
         bar_sq, model_sq = lax.fori_loop(0, clat // STEP, damped, (zero, zero))
         image_sq, cross = lax.fori_loop(0, clat // STEP, imaged, (zero, zero))
+        for copy in outgoing(r):
+            copy.start()
+        here = pl.ds(pl.multiple_of(corner_ref[0] * clon, clon), PATCH * clon)
+        patch_out[r] = image_out[r, here, :]
+        model_patch_out[r] = model_ref[r, here, :]
         ray = ray_ref[r, 0]
         residual = jnp.sum(bar_sq, keepdims=True) + jnp.sum(ray * ray, keepdims=True)
         row = place(row, r, residual)
@@ -322,16 +341,16 @@
         return place(row, 3 * systems + r, jnp.sum(model_sq, keepdims=True))
 
     sums_out[...] = lax.fori_loop(0, systems, system, jnp.zeros((1, depth), F32))
-    for copy in copies:
-        copy.wait()
-
-
-def combine_body(clon, corner_ref, terms_ref, chosen_ref, image_ref, model_ref, sums_ref, added_ref, parts_ref):
-    systems, width, depth = added_ref.shape
+    for r in range(systems):
+        for copy in outgoing(r):
+            copy.wait()
+
+
+def combine_body(terms_ref, chosen_ref, patch_ref, model_patch_ref, sums_ref, added_ref, parts_ref):
+    systems, _, depth = added_ref.shape
     slots = chosen_ref.shape[1]
     chosen = chosen_ref[...]
     row = sums_ref[...]
-    here = pl.ds(pl.multiple_of(corner_ref[0] * clon, clon), width)
     for r in range(systems):
         x = terms_ref[pl.ds(r, slots, stride=systems), :]
         high = x.astype(BF16)
@@ -341,8 +360,8 @@
         three = jnp.dot(chosen, jnp.concatenate([high, middle, low], axis=1), preferred_element_type=F32)
         added = three[:, 0:depth] + (three[:, depth : 2 * depth] + three[:, 2 * depth :])
         added_ref[r] = added
-        square = jnp.sum(added * (2.0 * image_ref[r, here, :] + added), keepdims=True)
-        cross = jnp.sum(added * model_ref[r, here, :], keepdims=True)
+        square = jnp.sum(added * (2.0 * patch_ref[r] + added), keepdims=True)
+        cross = jnp.sum(added * model_patch_ref[r], keepdims=True)
         row = place(row, systems + r, square)
         row = place(row, 2 * systems + r, cross)
     parts_ref[...] = jnp.broadcast_to(row, parts_ref.shape)
@@ -357,25 +376,52 @@
     rec_ref,
     ray_ref,
     added_ref,
-    image_ref,
-    model_ref,
-    bar_ref,
-    solution_ref,
-    search_ref,
+    image_in,
+    model_in,
+    bar_in,
+    solution_in,
+    search_in,
     ray_out,
     damp_out,
     model_out,
     solution_out,
     search_out,
     rec_out,
+    image_ref,
+    model_ref,
+    bar_ref,
+    solution_ref,
+    search_ref,
     damp_s,
     model_s,
     solution_s,
     search_s,
     coef,
     sems,
+    in_sems,
 ):
     systems, columns, depth = image_ref.shape
+    rows = columns // PIECES
+
+    def incoming(r, p):
+        at = pl.ds(pl.multiple_of(p * rows, rows), rows)
+        pairs = (
+            (search_in, search_ref),
+            (bar_in, bar_ref),
+            (image_in, image_ref),
+            (model_in, model_ref),
+            (solution_in, solution_ref),
+        )
+        return [
+            pltpu.make_async_copy(a.at[r, at], b.at[r, at], in_sems.at[r, p, k]) for k, (a, b) in enumerate(pairs)
+        ]
+
+    def begin_piece(n, _):
+        for copy in incoming(n // PIECES, n % PIECES):
+            copy.start()
+        return 0
+
+    lax.fori_loop(0, systems * PIECES, begin_piece, 0)
     total = jnp.sum(parts_ref[...], axis=0, keepdims=True)
     residual_sq, image_sq, cross, model_sq = (total[:, q * systems : (q + 1) * systems] for q in range(4))
     rho_bar, phi_bar = rec_ref[1:2], rec_ref[2:3]
@@ -396,8 +442,6 @@
     for q, scale in enumerate(scales):
         for s in range(systems):
             coef[q, s] = scale[0, s]
-    rows = columns // PIECES
-
     def outgoing(r, p):
         at = pl.ds(pl.multiple_of(p * rows, rows), rows)
         pairs = (
@@ -413,6 +457,8 @@
     def piece(n, _):
         r, p = n // PIECES, n % PIECES
         at = pl.ds(pl.multiple_of(p * rows, rows), rows)
+        for copy in incoming(r, p):
+            copy.wait()
         search = search_ref[r, at, :]
         damp_s[r, at, :] = bar_ref[r, at, :] * coef[0, r]
         new = image_ref[r, at, :] * coef[1, r] - model_ref[r, at, :] * coef[2, r]
@@ -445,11 +491,20 @@
     lax.fori_loop(0, systems * PIECES, settle, 0)
 
 
-PIECES = 4
-
-
-def rays_body(cap, blocks, meta_ref, rec_ref, tiles_ref, fetched_ref, old_ref, bar_ref, term_ref, masks, lows):
-    tiles, width, depth = tiles_ref.shape[2:]
+PIECES = 2
+
+
+def rays_body(
+    cap, blocks, meta_ref, rec_ref, tiles_in, fetched_ref, old_ref, after_ref, bar_ref, term_ref, tiles_ref, masks, lows, sems
+):
+    tiles, width, depth = tiles_in.shape[2:]
+    part = -(-tiles // PARTS)
+    copies = []
+    for k in range(PARTS):
+        at = (0, 0, pl.ds(k * part, min(part, tiles - k * part)))
+        copies.append(pltpu.make_async_copy(tiles_in.at[at], tiles_ref.at[at], sems.at[k]))
+    for copy in copies:
+        copy.start()
     systems = old_ref.shape[0]
     group = cap * systems
     for c in range(cap + 1):
@@ -459,6 +514,8 @@
     lows[...] = jnp.zeros(lows.shape, BF16)
     total = jnp.zeros((blocks * group, width), F32)
     for t in range(tiles):
+        if t % part == 0:
+            copies[t // part].wait()
         owner, rank, block = meta_ref[0, t], meta_ref[1, t], meta_ref[2, t]
         rows = fetched_ref[pl.ds(pl.multiple_of(owner * group, group), group), :]
         left = jnp.concatenate(
@@ -484,6 +541,9 @@
         slot = meta_ref[0, t] * cap + meta_ref[1, t]
         term = jnp.dot(lows[meta_ref[2, t]], tiles_ref[0, 0, t], preferred_element_type=F32)
         term_ref[slot] = term[:systems]
+
+
+PARTS = 6
 
 
 def shifted(x, axis, step):
@@ -524,138 +584,140 @@
     rows_all = devices * blocks * width + cells_all
     lanes = 128
     full, flat = model_vector.shape, (systems, columns, depth)
-    here, there = pltpu.VMEM, pltpu.HBM
+    patch = (systems, PATCH * clon, depth)
+    here, there, plain = pltpu.VMEM, pltpu.HBM, jax.ShapeDtypeStruct
+    dma = pltpu.SemaphoreType.DMA
+    model, damping = far(model_vector), far(damping_vector)
+    model_flat, damping_flat = far(model_vector.reshape(flat)), far(damping_vector.reshape(flat))
 
     lists = exchange(jnp.broadcast_to(block_ids[0], (devices, 1, tiles))).reshape(devices, tiles)
 
-    served, wanted, corner, model = call(
+    served, wanted, corner = call(
         functools.partial(serve_body, cap, clat, clon),
         "serve",
-        (
-            there((slots * systems, depth), BF16),
-            here((devices, lanes), F32),
-            jax.ShapeDtypeStruct((1,), I32),
-            here(flat, F32),
-        ),
+        (there((slots * systems, depth), BF16), plain((devices, lanes), F32), plain((1,), I32)),
         [vmem(), hbm()],
-        (vmem(), vmem(), smem(), vmem()),
-        scratch=[pltpu.VMEM((slots * systems, depth), F32), pltpu.SemaphoreType.DMA((systems,))],
-    )(lists, far(model_vector.reshape(flat)))
+        (vmem(), vmem(), smem()),
+        scratch=[pltpu.VMEM(patch, F32), pltpu.VMEM((slots * systems, depth), F32), dma((systems,))],
+    )(lists, model_flat)
     fetched = exchange(served.reshape(devices, group, depth)).reshape(slots * systems, depth)
 
-    band = (systems, 3, clon, depth)
-    damping, held, north_msg, south_msg, meta = call(
-        functools.partial(pack_body, columns.bit_length() - 1, clon, blocks),
+    band = there((systems, 3, clon, depth), F32)
+    north_msg, south_msg = call(
+        pack_body,
         "pack",
-        (here(flat, F32), here(sensitivity.shape, BF16), there(band, F32), there(band, F32), jax.ShapeDtypeStruct((8, lanes), I32)),
-        [vmem()] * 4 + [hbm(), hbm()],
-        (vmem(),) * 5,
-        scratch=[pltpu.SemaphoreType.DMA((systems + 2,))],
-        moved=4 * systems * columns * depth + 2 * tiles * width * depth,
-    )(
-        far(block_ids),
-        block_offsets,
-        ray_counts,
-        near(model),
-        far(damping_vector.reshape(flat)),
-        far(sensitivity),
-    )
+        (band, band),
+        [smem(), hbm(), hbm()],
+        (hbm(), hbm()),
+        scratch=[dma((4,))],
+        moved=24 * systems * clon * depth,
+    )(corner, model, damping)
     north = shifted(south_msg, "lat", 1)
     south = shifted(north_msg, "lat", -1)
 
     side = (systems, 3 * clat + 8, depth)
+    east_part, west_part, meta = call(
+        functools.partial(flanks_body, columns.bit_length() - 1, blocks),
+        "flanks",
+        (plain(side, F32), plain(side, F32), plain((8, lanes), I32)),
+        [smem()] + [vmem()] * 3 + [hbm(), hbm()],
+        (vmem(),) * 3,
+        scratch=[pltpu.VMEM((4, systems, clat, 8, depth), F32), dma((4,))],
+        moved=128 * systems * clat * depth,
+    )(corner, far(block_ids), block_offsets, ray_counts, model, damping)
     east_msg, west_msg = call(
-        functools.partial(columns_body, clat, clon),
-        "columns",
+        corners_body,
+        "corners",
         (there(side, F32), there(side, F32)),
         [vmem()] * 4,
         (vmem(), vmem()),
-    )(near(model), near(damping), far(north), far(south))
+    )(east_part, west_part, far(north), far(south))
     west = shifted(east_msg, "lon", 1)
     east = shifted(west_msg, "lon", -1)
 
     ray_bar, terms = call(
         functools.partial(rays_body, cap, blocks),
         "rays",
-        (here(ray_vector.shape, F32), there((slots, systems, depth), F32)),
-        [smem()] + [vmem()] * 4,
+        (plain(ray_vector.shape, F32), there((slots, systems, depth), F32)),
+        [smem(), vmem(), hbm(), vmem(), vmem(), hbm()],
         (vmem(), vmem()),
         scratch=[
+            pltpu.VMEM(sensitivity.shape, BF16),
             pltpu.VMEM((cap + 1, group, depth), BF16),
             pltpu.VMEM((blocks + 1, 16, width), BF16),
+            dma((PARTS,)),
         ],
         flops=4 * tiles * width * depth * 16,
         moved=2 * tiles * width * depth,
-    )(meta, far(recurrence), near(held), fetched, far(ray_vector))
+    )(meta, far(recurrence), far(sensitivity), fetched, far(ray_vector), far(east_msg))
     arrived = exchange(terms.reshape(devices, group, depth)).reshape(slots * systems, depth)
 
-    bar, image, solution, search, sums, chosen = call(
+    bar, image, sums, patched, model_patch, chosen = call(
         functools.partial(dense_body, cap, clat, clon),
         "dense",
-        (here(flat, F32),) * 4 + (here((1, lanes), F32), here((PATCH * clon, slots), BF16)),
-        [vmem(), smem()] + [vmem()] * 8 + [hbm()] * 2,
-        (vmem(),) * 6,
-        scratch=[
+        (there(flat, F32),) * 2
+        + (plain((1, lanes), F32), plain(patch, F32), plain(patch, F32), plain((PATCH * clon, slots), BF16)),
+        [vmem(), smem()] + [vmem()] * 2 + [hbm()] * 2 + [vmem()] * 4,
+        (hbm(),) * 2 + (vmem(),) * 4,
+        scratch=[pltpu.VMEM(flat, F32)] * 4
+        + [
             pltpu.VMEM((clon, depth), F32),
             pltpu.VMEM((clon, depth), F32),
             pltpu.VMEM((clat, depth), F32),
             pltpu.VMEM((clat, depth), F32),
             pltpu.SMEM((systems,), F32),
-            pltpu.SemaphoreType.DMA((2 * systems,)),
+            dma((systems, 4)),
         ],
         flops=40 * systems * columns * depth,
-        moved=24 * systems * columns * depth,
+        moved=16 * systems * columns * depth,
     )(
         far(recurrence),
         corner,
-        near(wanted),
-        near(ray_bar),
-        near(model),
-        near(damping),
+        wanted,
+        ray_bar,
+        model_flat,
+        damping_flat,
         far(north),
         far(south),
         far(west),
         far(east),
-        far(solution.reshape(flat)),
-        far(search.reshape(flat)),
     )
 
     added, parts = call(
-        functools.partial(combine_body, clon),
+        combine_body,
         "combine",
-        (here((systems, PATCH * clon, depth), F32), there((devices, lanes), F32)),
-        [smem()] + [vmem()] * 5,
+        (plain(patch, F32), there((devices, lanes), F32)),
+        [vmem()] * 5,
         (vmem(),) * 2,
-    )(corner, arrived, near(chosen), near(image), near(model), near(sums))
+    )(arrived, chosen, patched, model_patch, sums)
     every = exchange(parts.reshape(devices, 1, lanes)).reshape(devices, lanes)
 
     outs = call(
         functools.partial(finish_body, float(rows_all), float(cells_all), clon),
         "finish",
         (there(ray_vector.shape, F32),) + (there(flat, F32),) * 4 + (there(recurrence.shape, F32),),
-        [smem()] + [vmem()] * 9,
+        [smem()] + [vmem()] * 4 + [hbm()] * 5,
         (vmem(),) + (hbm(),) * 4 + (vmem(),),
-        scratch=[
-            pltpu.VMEM(flat, F32),
-            pltpu.VMEM(flat, F32),
-            pltpu.VMEM(flat, F32),
-            pltpu.VMEM(flat, F32),
+        scratch=[pltpu.VMEM(flat, F32)] * 9
+        + [
             pltpu.SMEM((5, systems), F32),
-            pltpu.SemaphoreType.DMA((systems, PIECES, 4)),
+            dma((systems, PIECES, 4)),
+            dma((systems, PIECES, 5)),
         ],
+        mib=32,
         flops=10 * systems * columns * depth,
-        moved=16 * systems * columns * depth,
+        moved=36 * systems * columns * depth,
     )(
         corner,
         every,
         far(recurrence),
-        near(ray_bar),
-        near(added),
-        near(image),
-        near(model),
-        near(bar),
-        near(solution),
-        near(search),
+        ray_bar,
+        added,
+        far(image),
+        model_flat,
+        far(bar),
+        far(solution.reshape(flat)),
+        far(search.reshape(flat)),
     )
     ray_out, damp_out, model_out, solution_out, search_out, rec_out = outs
     fields = (x.reshape(full) for x in (damp_out, model_out, solution_out, search_out))

time: 105 us -> 104 us (level)
  Pallas kernels: 28.9 us -> 46.8 us
  local copies, waits for them, and re-layouts: 17.4 us -> 2.05 us
  waiting for transfers between devices: 11.9 us -> 4.97 us
  blocking collectives: 29.2 us -> 32 us
    unnamed x40 -> x14, local copies, waits for them, and re-layouts: 16.8 us -> 1.39 us
    pallas_call x5 -> x6, Pallas kernels: 20.3 us -> 34.8 us  [the longest x1 13.6 us: per_device(): call(pack_body, 'pack', (band, band), [smem(), hbm(), hbm()], (hbm(), hbm...]
    ppermute x4, waiting for transfers between devices: 11.8 us -> 4.97 us  [shifted(): return lax.ppermute(x, axis, pairs)]
    pallas_call x1, Pallas kernels: 6.15 us -> 9.65 us  [per_device(): call(functools.partial(finish_body, float(rows_all), float(cells_all), cl...]
    all_to_all x2, blocking collectives: 29.2 us -> 32 us  [exchange(): return lax.all_to_all(x, AXES, split_axis=0, concat_axis=0, tiled=True)]
    ppermute x4, starting transfers between devices: 7.62 us -> 9.23 us  [shifted(): return lax.ppermute(x, axis, pairs)]
  transfers between devices with their start and end apart: 6 -> 6, of which waited for: 4 -> 2; matrix products, arithmetic and copies ran while one was open for 0% -> 0% of each run, Pallas kernels for 13% -> 27%
where the time goes in v5:
time: 104 us
  Pallas kernels  46.8 us (45%)
  blocking collectives  32 us (31%)
  starting transfers between devices  16.5 us (16%)
  waiting for transfers between devices  4.97 us (5%)
  local copies, waits for them, and re-layouts  2.05 us (2%)
  between operations  1.45 us (1%)
    all_to_all x2, blocking collectives, exchange(): return lax.all_to_all(x, AXES, split_axis=0, concat_axis=0, tiled=True)  32 us
    pallas_call x1, Pallas kernels, per_device(): call(pack_body, 'pack', (band, band), [smem(), hbm(), hbm()], (hbm(), hbm...  13.6 us
    pallas_call x1, Pallas kernels, per_device(): call(functools.partial(finish_body, float(rows_all), float(cells_all), cl...  9.65 us
    pallas_call x1, Pallas kernels, per_device(): call(functools.partial(dense_body, cap, clat, clon), 'dense', (there(flat...  9.57 us
    ppermute x4, starting transfers between devices, shifted(): return lax.ppermute(x, axis, pairs)  9.23 us
    all_to_all x2, starting transfers between devices, exchange(): return lax.all_to_all(x, AXES, split_axis=0, concat_axis=0, tiled=True)  7.29 us
    pallas_call x1, Pallas kernels, per_device(): call(functools.partial(rays_body, cap, blocks), 'rays', (plain(ray_vector...  5.93 us
    ppermute x4, waiting for transfers between devices, shifted(): return lax.ppermute(x, axis, pairs)  4.97 us
  transfers between devices with their start and end apart: 6, of which 2 were waited for; matrix products, arithmetic and copies ran while one was open for 0% of the time, Pallas kernels for 27%

profile of v5, /device:TPU:0, one launch (start us, length us, event | category | flops | bytes accessed | tf_op | source)
XLA Modules:
  0.0 103.8 jit_solution(15159422048082677425)
XLA Ops:
  0.6 0.7 broadcast_in_dim.3
  1.3 14.3 %all_to_all.20 = s32[32,1,60]{2,1,0:T(1,128)S(1)} all-to-all(s32[32,1,60]{2,1,0:T(1,128)S(1)} %broadcast_in_dim.3), channel_id=1, replica_groups=mesh['lat'=4,'lon'=8] {'lat','lon'}, dimensions={0} | all-to-all | bytes 15360 | tf_op jit(solution)/shard_map/all_to_all | solution.py:559
  15.6 2.3 %serve.1 = (bf16[512,128]{1,0:T(8,128)(2,1)}, f32[32,128]{1,0:T(8,128)S(1)}, s32[1]{0:T(128)}) custom-call(s32[32,60]{1,0:T(8,128)S(1)} %bitcast.21, f32[4,1024,128]{2,1,0:T(8,128)} %bitcast.22), custom_call_target="tpu_custom_call" | custom-call | tf_op jit(solution)/shard_map/serve/pallas_call | solution.py:595
  17.9 2.6 %all-to-all-start.1 = ((bf16[32,16,128]{2,1,0:T(8,128)(2,1)}), bf16[32,16,128]{2,1,0:T(8,128)(2,1)S(1)}, u32[]{:S(2)}, u32[]{:S(2)}) async-start(bf16[32,16,128]{2,1,0:T(8,128)(2,1)} %bitcast.29), calls=%async_computation.1 | async-start | bytes 262144 | tf_op jit(solution)/shard_map/all_to_all | solution.py:559
  20.5 0.0 copy-start
  20.5 13.6 %pack.1 = (f32[4,3,32,128]{3,2,1,0:T(8,128)}, f32[4,3,32,128]{3,2,1,0:T(8,128)}) custom-call(s32[1]{0:T(128)} %get-tuple-element.32.after_ref.corner_ref, f32[4,32,32,128]{3,2,1,0:T(8,128)} %model_in.3, f32[4,32,32,128]{3,2,1,0:T(8,128)} %damp_in.3), custom_call_target="tpu_custom_call" | custom-call | bytes 393216 | tf_op jit(solution)/shard_map/pack/pallas_call | solution.py:606
  34.1 3.6 %collective-permute-start = (f32[4,3,32,128]{3,2,1,0:T(8,128)}, f32[4,3,32,128]{3,2,1,0:T(8,128)S(1)}, u32[]{:S(2)}, u32[]{:S(2)}) collective-permute-start(f32[4,3,32,128]{3,2,1,0:T(8,128)} %get-tuple-element.37), channel_id=1, source_target_pairs={{0,8},{8,16},{16,24},{1,9},{9,17},{17,25},{2,10},{10,18},{18,26},{... | collective-permute-start | bytes 589832 | tf_op jit(solution)/shard_map/ppermute | solution.py:555
  37.7 1.3 %collective-permute-start.1 = (f32[4,3,32,128]{3,2,1,0:T(8,128)}, f32[4,3,32,128]{3,2,1,0:T(8,128)S(1)}, u32[]{:S(2)}, u32[]{:S(2)}) collective-permute-start(f32[4,3,32,128]{3,2,1,0:T(8,128)} %get-tuple-element.38), channel_id=1, source_target_pairs={{8,0},{16,8},{24,16},{9,1},{17,9},{25,17},{10,2},{18,10},{26,18},{... | collective-permute-start | bytes 589832 | tf_op jit(solution)/shard_map/ppermute | solution.py:555
  39.7 0.0 copy-done
  39.7 2.9 %flanks.1 = (f32[4,104,128]{2,1,0:T(8,128)S(1)}, f32[4,104,128]{2,1,0:T(8,128)S(1)}, s32[8,128]{1,0:T(8,128)S(1)}) custom-call(s32[1]{0:T(128)} %get-tuple-element.32.after_ref.corner_ref, s32[1,1,60]{2,1,0:T(1,128)} %ids_ref.1, s32[1,1,4]{2,1,0:T(1,128)S(1)} %copy-done, s32[1,1]{1,0:T(1,128)S(6)} %copy.17.count_ref, f32[4,32,32,128]{3,2,1,0:T(8,128)} %model_in.3, ...), custom_call_target="tpu_custom_call" | custom-call | bytes 2097152 | tf_op jit(solution)/shard_map/flanks/pallas_call | solution.py:619
  42.6 0.0 collective-permute-done.north_ref
  42.6 0.0 copy-start.1
  42.6 3.9 %collective-permute-done.1.south_ref = f32[4,3,32,128]{3,2,1,0:T(8,128)S(1)} collective-permute-done((f32[4,3,32,128]{3,2,1,0:T(8,128)}, f32[4,3,32,128]{3,2,1,0:T(8,128)S(1)}, u32[]{:S(2)}, u32[]{:S(2)}) %collective-permute-start.1) | collective-permute-done | bytes 196640 | tf_op jit(solution)/shard_map/ppermute | solution.py:555
  46.5 0.0 copy-start.2
  46.5 0.0 copy-done.1
  46.5 0.7 copy-done.2
  47.2 1.8 %corners.1 = (f32[4,104,128]{2,1,0:T(8,128)}, f32[4,104,128]{2,1,0:T(8,128)}) custom-call(f32[4,104,128]{2,1,0:T(8,128)S(1)} %get-tuple-element.35.east_in, f32[4,104,128]{2,1,0:T(8,128)S(1)} %get-tuple-element.36.west_in, f32[4,3,32,128]{3,2,1,0:T(8,128)} %copy-done.1, f32[4,3,32,128]{3,2,1,0:T(8,128)} %copy-done.2), custom_call_target="tpu_custom_call" | custom-call | tf_op jit(solution)/shard_map/corners/pallas_call | solution.py:628
  49.0 0.0 all-to-all-done.1
  49.0 0.0 copy-start.6
  49.0 0.0 copy-start.5
  49.0 5.9 %rays.1 = (f32[4,1,1,768]{3,2,1,0:T(1,128)S(1)}, f32[128,4,128]{2,1,0:T(4,128)}) custom-call(s32[8,128]{1,0:T(8,128)S(1)} %get-tuple-element.33.meta_ref, f32[3,4]{1,0:T(4,128)} %rec_ref.5, bf16[1,1,60,256,128]{4,3,2,1,0:T(8,128)(2,1)} %tiles_in.1, bf16[512,128]{1,0:T(8,128)(2,1)S(1)} %bitcast.19, f32[4,1,1,768]{3,2,1,0:T(1,128)} %old_ref.1, ...), custom_call_target="tpu_custom_call" | custom-call | flops 125829120 | bytes 3932160 | tf_op jit(solution)/shard_map/rays/pallas_call | solution.py:638
  55.0 4.7 %all-to-all-start.2 = ((f32[32,16,128]{2,1,0:T(8,128)}), f32[32,16,128]{2,1,0:T(8,128)S(1)}, u32[]{:S(2)}, u32[]{:S(2)}) async-start(f32[32,16,128]{2,1,0:T(8,128)} %bitcast.28), calls=%async_computation.2 | async-start | bytes 524288 | tf_op jit(solution)/shard_map/all_to_all | solution.py:559
  59.7 0.0 copy-done.6
  59.7 1.3 %collective-permute-start.3 = (f32[4,104,128]{2,1,0:T(8,128)S(1)}, f32[4,104,128]{2,1,0:T(8,128)S(1)}, u32[]{:S(2)}, u32[]{:S(2)}) collective-permute-start(f32[4,104,128]{2,1,0:T(8,128)S(1)} %copy-done.6), channel_id=1, source_target_pairs={{1,0},{2,1},{3,2},{4,3},{5,4},{6,5},{7,6},{9,8},{10,9},{11,10},{12... | collective-permute-start | bytes 638984 | tf_op jit(solution)/shard_map/ppermute | solution.py:555
  61.0 0.0 copy-done.5
  61.0 3.0 %collective-permute-start.2 = (f32[4,104,128]{2,1,0:T(8,128)S(1)}, f32[4,104,128]{2,1,0:T(8,128)S(1)}, u32[]{:S(2)}, u32[]{:S(2)}) collective-permute-start(f32[4,104,128]{2,1,0:T(8,128)S(1)} %copy-done.5), channel_id=1, source_target_pairs={{0,1},{1,2},{2,3},{3,4},{4,5},{5,6},{6,7},{8,9},{9,10},{10,11},{11... | collective-permute-start | bytes 638984 | tf_op jit(solution)/shard_map/ppermute | solution.py:555
  64.0 0.0 collective-permute-done.3.east_ref
  64.1 0.0 copy-start.3
  64.1 1.0 %collective-permute-done.2.west_ref = f32[4,104,128]{2,1,0:T(8,128)S(1)} collective-permute-done((f32[4,104,128]{2,1,0:T(8,128)S(1)}, f32[4,104,128]{2,1,0:T(8,128)S(1)}, u32[]{:S(2)}, u32[]{:S(2)}) %collective-permute-start.2) | collective-permute-done | bytes 213024 | tf_op jit(solution)/shard_map/ppermute | solution.py:555
  65.1 0.0 copy-start.4
  65.1 0.0 copy-done.3
  65.1 0.7 copy-done.4
  65.8 9.6 %dense.1 = (f32[4,1024,128]{2,1,0:T(8,128)}, f32[4,1024,128]{2,1,0:T(8,128)}, f32[1,128]{1,0:T(1,128)S(1)}, f32[4,128,128]{2,1,0:T(8,128)S(1)}, f32[4,128,128]{2...) custom-call(f32[3,4]{1,0:T(4,128)} %rec_ref.5, s32[1]{0:T(128)} %get-tuple-element.32.after_ref.corner_ref, ...), custom_call_target="tpu_custom_call" | custom-call | flops 20971520 | bytes 8388608 | tf_op jit(solution)/shard_map/dense/pallas_call | solution.py:655
  75.4 0.0 all-to-all-done.2
  75.4 1.0 combine.1
  76.4 17.8 %all_to_all.21 = f32[32,1,128]{2,1,0:T(1,128)S(1)} all-to-all(f32[32,1,128]{2,1,0:T(1,128)} %bitcast.30), channel_id=1, replica_groups=mesh['lat'=4,'lon'=8] {'lat','lon'}, dimensions={0} | all-to-all | bytes 32768 | tf_op jit(solution)/shard_map/all_to_all | solution.py:559
  94.1 9.6 %finish.1 = (f32[4,1,1,768]{3,2,1,0:T(1,128)}, f32[4,1024,128]{2,1,0:T(8,128)}, f32[4,1024,128]{2,1,0:T(8,128)}, f32[4,1024,128]{2,1,0:T(8,128)}, f32[4,1024,128]{2,1,0:T(8,128)}, /*index=5*/f32[3,4]{1,0:T(4,128)}) custom-call(s32[1]{0:T(128)} %get-tuple-element.32.after_ref.corner_ref, f32[32,128]{1,0:T(8,128)S(1)} %bitcast.20, f32[3,4]{1,0:T(4,128)} %rec_ref.5, ...), custom_call_target="tpu_custom_call" | custom-call | flops 5242880 | bytes 18874368 | tf_op jit(solution)/shard_map/finish/pallas_call | solution.py:695
Async XLA Ops:
  17.9 31.1 %all-to-all-start.1 = ((bf16[32,16,128]{2,1,0:T(8,128)(2,1)}), bf16[32,16,128]{2,1,0:T(8,128)(2,1)S(1)}, u32[]{:S(2)}, u32[]{:S(2)}) async-start(bf16[32,16,128]{2,1,0:T(8,128)(2,1)} %bitcast.29), calls=%async_computation.1 | async-start | bytes 262144 | tf_op jit(solution)/shard_map/all_to_all | solution.py:559
  20.5 19.2 %copy-start = (s32[1,1,4]{2,1,0:T(1,128)S(1)}, s32[1,1,4]{2,1,0:T(1,128)}, u32[]{:S(2)}) copy-start(s32[1,1,4]{2,1,0:T(1,128)} %off_ref.1) | copy-start | bytes 52
  34.1 8.4 %collective-permute-start = (f32[4,3,32,128]{3,2,1,0:T(8,128)}, f32[4,3,32,128]{3,2,1,0:T(8,128)S(1)}, u32[]{:S(2)}, u32[]{:S(2)}) collective-permute-start(f32[4,3,32,128]{3,2,1,0:T(8,128)} %get-tuple-element.37), channel_id=1, source_target_pairs={{0,8},{8,16},{16,24},{1,9},{9,17},{17,25},{2,10},{10,18},{18,26},{... | collective-permute-start | bytes 589832 | tf_op jit(solution)/shard_map/ppermute | solution.py:555
  37.7 8.8 %collective-permute-start.1 = (f32[4,3,32,128]{3,2,1,0:T(8,128)}, f32[4,3,32,128]{3,2,1,0:T(8,128)S(1)}, u32[]{:S(2)}, u32[]{:S(2)}) collective-permute-start(f32[4,3,32,128]{3,2,1,0:T(8,128)} %get-tuple-element.38), channel_id=1, source_target_pairs={{8,0},{16,8},{24,16},{9,1},{17,9},{25,17},{10,2},{18,10},{26,18},{... | collective-permute-start | bytes 589832 | tf_op jit(solution)/shard_map/ppermute | solution.py:555
  42.6 3.9 %copy-start.1 = (f32[4,3,32,128]{3,2,1,0:T(8,128)}, f32[4,3,32,128]{3,2,1,0:T(8,128)S(1)}, u32[]{:S(2)}) copy-start(f32[4,3,32,128]{3,2,1,0:T(8,128)S(1)} %collective-permute-done.north_ref) | copy-start | bytes 589828
  46.5 0.7 copy-start.2
  49.0 10.7 %copy-start.6 = (f32[4,104,128]{2,1,0:T(8,128)S(1)}, f32[4,104,128]{2,1,0:T(8,128)}, u32[]{:S(2)}) copy-start(f32[4,104,128]{2,1,0:T(8,128)} %get-tuple-element.43) | copy-start | bytes 638980
  49.0 12.0 %copy-start.5 = (f32[4,104,128]{2,1,0:T(8,128)S(1)}, f32[4,104,128]{2,1,0:T(8,128)}, u32[]{:S(2)}) copy-start(f32[4,104,128]{2,1,0:T(8,128)} %get-tuple-element.39.after_ref) | copy-start | bytes 638980
  55.0 20.4 %all-to-all-start.2 = ((f32[32,16,128]{2,1,0:T(8,128)}), f32[32,16,128]{2,1,0:T(8,128)S(1)}, u32[]{:S(2)}, u32[]{:S(2)}) async-start(f32[32,16,128]{2,1,0:T(8,128)} %bitcast.28), calls=%async_computation.2 | async-start | bytes 524288 | tf_op jit(solution)/shard_map/all_to_all | solution.py:559
  59.7 4.4 %collective-permute-start.3 = (f32[4,104,128]{2,1,0:T(8,128)S(1)}, f32[4,104,128]{2,1,0:T(8,128)S(1)}, u32[]{:S(2)}, u32[]{:S(2)}) collective-permute-start(f32[4,104,128]{2,1,0:T(8,128)S(1)} %copy-done.6), channel_id=1, source_target_pairs={{1,0},{2,1},{3,2},{4,3},{5,4},{6,5},{7,6},{9,8},{10,9},{11,10},{12... | collective-permute-start | bytes 638984 | tf_op jit(solution)/shard_map/ppermute | solution.py:555
  61.0 4.1 %collective-permute-start.2 = (f32[4,104,128]{2,1,0:T(8,128)S(1)}, f32[4,104,128]{2,1,0:T(8,128)S(1)}, u32[]{:S(2)}, u32[]{:S(2)}) collective-permute-start(f32[4,104,128]{2,1,0:T(8,128)S(1)} %copy-done.5), channel_id=1, source_target_pairs={{0,1},{1,2},{2,3},{3,4},{4,5},{5,6},{6,7},{8,9},{9,10},{10,11},{11... | collective-permute-start | bytes 638984 | tf_op jit(solution)/shard_map/ppermute | solution.py:555
  64.1 1.1 %copy-start.3 = (f32[4,104,128]{2,1,0:T(8,128)}, f32[4,104,128]{2,1,0:T(8,128)S(1)}, u32[]{:S(2)}) copy-start(f32[4,104,128]{2,1,0:T(8,128)S(1)} %collective-permute-done.3.east_ref) | copy-start | bytes 638980
  65.1 0.7 copy-start.4

commit v6 on v5

--- a/solution.py
+++ b/solution.py
@@ -55,6 +55,32 @@
 STEP = 8
 
 
+def ask_body(ids_ref, model_in, out_ref, slabs, sems):
+    systems, clat, clon, depth = model_in.shape
+    copies = []
+    for k in range(4):
+        at = (slice(None), pl.ds((k // 2) * (clat - 1), 1), pl.ds((k % 2) * (clon - 8), 8))
+        copies.append(pltpu.make_async_copy(model_in.at[at], slabs.at[k], sems.at[k]))
+    for copy in copies:
+        copy.start()
+    tiles = ids_ref.shape[-1]
+    ids = jnp.concatenate([ids_ref[0].astype(F32), jnp.full((1, depth - tiles), -1.0, F32)], axis=1)
+    for copy in copies:
+        copy.wait()
+    corners = [
+        [slabs[k, r, 0, (k % 2) * 7 : (k % 2) * 7 + 1] for r in range(systems)] for k in range(4)
+    ]
+    lat_at, lon_at = lax.axis_index("lat"), lax.axis_index("lon")
+    width = lax.axis_size("lon")
+    for e in range(out_ref.shape[0]):
+        out_ref[e, :, 0:depth] = ids
+        south, east = e // width > lat_at, e % width > lon_at
+        for r in range(systems):
+            upper = jnp.where(east, corners[1][r], corners[0][r])
+            lower = jnp.where(east, corners[3][r], corners[2][r])
+            out_ref[e, :, (r + 1) * depth : (r + 2) * depth] = jnp.where(south, lower, upper)
+
+
 def wanted_column(wanted, cap):
     devices, lanes = wanted.shape
     rows = devices * cap
@@ -63,13 +89,13 @@
     return jnp.sum(jnp.where(pick, spread, 0.0), axis=1, keepdims=True)
 
 
-def serve_body(cap, clat, clon, lists_ref, model_in, served_ref, wanted_ref, corner_ref, patch, mixed, sems):
+def serve_body(cap, clat, clon, lists_ref, model_in, served_ref, wanted_ref, corner_ref, diagonal_ref, patch, mixed, sems):
     systems, width, depth = patch.shape
-    devices, tiles = lists_ref.shape
+    devices = lists_ref.shape[0]
     lanes = 128
     shift = (clat * clon).bit_length() - 1
     me = lax.axis_index("lat") * lax.axis_size("lon") + lax.axis_index("lon")
-    ids = jnp.concatenate([lists_ref[...], jnp.full((devices, lanes - tiles), -1, I32)], axis=1)
+    ids = lists_ref[:, 0, 0:lanes].astype(I32)
     column = ids - lax.shift_left(me, shift)
     mine = (column >= 0) & (column < clat * clon) & (ids >= 0)
     first = jnp.min(jnp.where(mine, column, clat * clon))
@@ -96,30 +122,47 @@
         table = patch[r].astype(BF16)
         mixed[pl.ds(r, rows, stride=systems), :] = jnp.dot(chosen, table, preferred_element_type=F32)
     served_ref[...] = mixed[...].astype(BF16)
-
-
-def pack_body(after_ref, model_in, damp_in, north_ref, south_ref, sems):
-    last = model_in.shape[1] - 1
+    lat_at, lon_at = lax.axis_index("lat"), lax.axis_index("lon")
+    lat_size, lon_size = lax.axis_size("lat"), lax.axis_size("lon")
+    for k in range(4):
+        lat_to, lon_to = lat_at + 2 * (k // 2) - 1, lon_at + 2 * (k % 2) - 1
+        inside = (lat_to >= 0) & (lat_to < lat_size) & (lon_to >= 0) & (lon_to < lon_size)
+        source = jnp.where(inside, lat_to * lon_size + lon_to, 0)
+        flag = inside.astype(F32)
+        for r in range(systems):
+            got = lists_ref[source, :, (r + 1) * depth : (r + 2) * depth]
+            diagonal_ref[k * systems + r : k * systems + r + 1, :] = got * flag
+
+
+def flanks_body(
+    shift,
+    blocks,
+    after_ref,
+    ids_ref,
+    off_ref,
+    count_ref,
+    model_in,
+    damp_in,
+    north_ref,
+    south_ref,
+    east_ref,
+    west_ref,
+    meta_ref,
+    slabs,
+    sems,
+):
+    systems, clat, clon, depth = model_in.shape
+    copies = []
+    for k, (ref, at) in enumerate(((model_in, 0), (model_in, clon - 8), (damp_in, 0), (damp_in, clon - 8))):
+        copies.append(pltpu.make_async_copy(ref.at[:, :, pl.ds(at, 8)], slabs.at[k], sems.at[k]))
+    last = clat - 1
     pairs = (
         (model_in.at[:, pl.ds(last - 1, 2)], south_ref.at[:, pl.ds(0, 2)]),
         (damp_in.at[:, pl.ds(last, 1)], south_ref.at[:, pl.ds(2, 1)]),
         (model_in.at[:, pl.ds(0, 2)], north_ref.at[:, pl.ds(0, 2)]),
         (damp_in.at[:, pl.ds(0, 1)], north_ref.at[:, pl.ds(2, 1)]),
     )
-    copies = [pltpu.make_async_copy(a, b, sems.at[i]) for i, (a, b) in enumerate(pairs)]
-    for copy in copies:
-        copy.start()
-    for copy in copies:
-        copy.wait()
-
-
-def flanks_body(
-    shift, blocks, after_ref, ids_ref, off_ref, count_ref, model_in, damp_in, east_ref, west_ref, meta_ref, slabs, sems
-):
-    systems, clat, clon, depth = model_in.shape
-    copies = []
-    for k, (ref, at) in enumerate(((model_in, 0), (model_in, clon - 8), (damp_in, 0), (damp_in, clon - 8))):
-        copies.append(pltpu.make_async_copy(ref.at[:, :, pl.ds(at, 8)], slabs.at[k], sems.at[k]))
+    copies += [pltpu.make_async_copy(a, b, sems.at[i + 4]) for i, (a, b) in enumerate(pairs)]
     for copy in copies:
         copy.start()
     tiles = ids_ref.shape[-1]
@@ -147,24 +190,6 @@
             out[r, 0:clat] = rows[slab, r, pl.ds(near_at, clat, stride=8), :]
             out[r, clat : 2 * clat] = rows[slab, r, pl.ds(beyond, clat, stride=8), :]
             out[r, 2 * clat : 3 * clat] = rows[slab + 2, r, pl.ds(near_at, clat, stride=8), :]
-            out[r, 3 * clat :] = jnp.zeros((8, depth), F32)
-
-
-def corners_body(east_in, west_in, north_ref, south_ref, east_ref, west_ref):
-    systems, long, depth = east_ref.shape
-    at = long - 8
-    clon = north_ref.shape[2]
-    for r in range(systems):
-        for ref, out, near_at in ((east_in, east_ref, clon - 1), (west_in, west_ref, 0)):
-            out[r, 0:at] = ref[r, 0:at]
-            out[r, at:] = jnp.concatenate(
-                [
-                    north_ref[r, 1, near_at : near_at + 1],
-                    south_ref[r, 0, near_at : near_at + 1],
-                    jnp.zeros((6, depth), F32),
-                ],
-                axis=0,
-            )
 
 
 def six(x, north, south, west, east):
@@ -197,6 +222,7 @@
     rec_ref,
     corner_ref,
     wanted_ref,
+    diagonal_ref,
     ray_ref,
     model_in,
     damp_in,
@@ -245,7 +271,9 @@
     has_south = (lat_at < lax.axis_size("lat") - 1).astype(F32)
     has_west = (lon_at > 0).astype(F32)
     has_east = (lon_at < lax.axis_size("lon") - 1).astype(F32)
-    corner_n, corner_s = 3 * clat, 3 * clat + 1
+
+    def diagonal(k, r):
+        return diagonal_ref[pl.ds(k * alphas.shape[0] + r, 1), :]
 
     target = wanted_column(wanted_ref[...], cap) - 1.0
     slots = target.shape[0]
@@ -281,20 +309,20 @@
         for copy in incoming(r):
             copy.wait()
 
-        def side(ref, own, flag):
+        def side(ref, own, flag, east):
             x, beyond, old = ref[r, 0:clat], ref[r, clat : 2 * clat], ref[r, 2 * clat : 3 * clat]
-            upper, lower = ref[r, corner_n : corner_n + 1], ref[r, corner_s : corner_s + 1]
+            upper, lower = diagonal(east, r), diagonal(2 + east, r)
             return (six(x, beyond, own, upper, lower) - alpha * old) * flag
 
-        west_s[...] = side(west_ref, model_ref[r, pl.ds(0, clat, stride=clon), :], has_west)
-        east_s[...] = side(east_ref, model_ref[r, pl.ds(clon - 1, clat, stride=clon), :], has_east)
+        west_s[...] = side(west_ref, model_ref[r, pl.ds(0, clat, stride=clon), :], has_west, 0)
+        east_s[...] = side(east_ref, model_ref[r, pl.ds(clon - 1, clat, stride=clon), :], has_east, 1)
         north_s[...] = has_north * (
             six(
                 north_ref[r, 1],
                 north_ref[r, 0],
                 line(model_ref, r, 0),
-                west_ref[r, corner_n : corner_n + 1],
-                east_ref[r, corner_n : corner_n + 1],
+                diagonal(0, r),
+                diagonal(1, r),
             )
             - alpha * north_ref[r, 2]
         )
@@ -303,8 +331,8 @@
                 south_ref[r, 0],
                 line(model_ref, r, clat - 1),
                 south_ref[r, 1],
-                west_ref[r, corner_s : corner_s + 1],
-                east_ref[r, corner_s : corner_s + 1],
+                diagonal(2, r),
+                diagonal(3, r),
             )
             - alpha * south_ref[r, 2]
         )
@@ -495,7 +523,7 @@
 
 
 def rays_body(
-    cap, blocks, meta_ref, rec_ref, tiles_in, fetched_ref, old_ref, after_ref, bar_ref, term_ref, tiles_ref, masks, lows, sems
+    cap, blocks, meta_ref, rec_ref, tiles_in, fetched_ref, old_ref, north, south, west, east, bar_ref, term_ref, tiles_ref, masks, lows, sems
 ):
     tiles, width, depth = tiles_in.shape[2:]
     part = -(-tiles // PARTS)
@@ -590,48 +618,47 @@
     model, damping = far(model_vector), far(damping_vector)
     model_flat, damping_flat = far(model_vector.reshape(flat)), far(damping_vector.reshape(flat))
 
-    lists = exchange(jnp.broadcast_to(block_ids[0], (devices, 1, tiles))).reshape(devices, tiles)
-
-    served, wanted, corner = call(
+    asked = (devices, 1, (1 + systems) * depth)
+    asking = call(
+        ask_body,
+        "ask",
+        there(asked, F32),
+        [vmem(), hbm()],
+        vmem(),
+        scratch=[pltpu.VMEM((4, systems, 1, 8, depth), F32), dma((4,))],
+    )(far(block_ids), model)
+    lists = exchange(asking)
+
+    served, wanted, corner, diagonal = call(
         functools.partial(serve_body, cap, clat, clon),
         "serve",
-        (there((slots * systems, depth), BF16), plain((devices, lanes), F32), plain((1,), I32)),
+        (
+            there((slots * systems, depth), BF16),
+            plain((devices, lanes), F32),
+            plain((1,), I32),
+            plain((4 * systems, depth), F32),
+        ),
         [vmem(), hbm()],
-        (vmem(), vmem(), smem()),
+        (vmem(), vmem(), smem(), vmem()),
         scratch=[pltpu.VMEM(patch, F32), pltpu.VMEM((slots * systems, depth), F32), dma((systems,))],
     )(lists, model_flat)
     fetched = exchange(served.reshape(devices, group, depth)).reshape(slots * systems, depth)
 
+    side = there((systems, 3 * clat, depth), F32)
     band = there((systems, 3, clon, depth), F32)
-    north_msg, south_msg = call(
-        pack_body,
-        "pack",
-        (band, band),
-        [smem(), hbm(), hbm()],
-        (hbm(), hbm()),
-        scratch=[dma((4,))],
-        moved=24 * systems * clon * depth,
-    )(corner, model, damping)
+    north_msg, south_msg, east_msg, west_msg, meta = call(
+        functools.partial(flanks_body, columns.bit_length() - 1, blocks),
+        "flanks",
+        (band, band, side, side, plain((8, lanes), I32)),
+        [smem()] + [vmem()] * 3 + [hbm(), hbm()],
+        (vmem(),) * 5,
+        scratch=[pltpu.VMEM((4, systems, clat, 8, depth), F32), dma((8,))],
+        flops=1,
+        moved=128 * systems * clat * depth,
+    )(corner, far(block_ids), block_offsets, ray_counts, model, damping)
+
     north = shifted(south_msg, "lat", 1)
     south = shifted(north_msg, "lat", -1)
-
-    side = (systems, 3 * clat + 8, depth)
-    east_part, west_part, meta = call(
-        functools.partial(flanks_body, columns.bit_length() - 1, blocks),
-        "flanks",
-        (plain(side, F32), plain(side, F32), plain((8, lanes), I32)),
-        [smem()] + [vmem()] * 3 + [hbm(), hbm()],
-        (vmem(),) * 3,
-        scratch=[pltpu.VMEM((4, systems, clat, 8, depth), F32), dma((4,))],
-        moved=128 * systems * clat * depth,
-    )(corner, far(block_ids), block_offsets, ray_counts, model, damping)
-    east_msg, west_msg = call(
-        corners_body,
-        "corners",
-        (there(side, F32), there(side, F32)),
-        [vmem()] * 4,
-        (vmem(), vmem()),
-    )(east_part, west_part, far(north), far(south))
     west = shifted(east_msg, "lon", 1)
     east = shifted(west_msg, "lon", -1)
 
@@ -639,7 +666,7 @@
         functools.partial(rays_body, cap, blocks),
         "rays",
         (plain(ray_vector.shape, F32), there((slots, systems, depth), F32)),
-        [smem(), vmem(), hbm(), vmem(), vmem(), hbm()],
+        [smem(), vmem(), hbm(), vmem(), vmem()] + [pl.BlockSpec(memory_space=pl.ANY)] * 4,
         (vmem(), vmem()),
         scratch=[
             pltpu.VMEM(sensitivity.shape, BF16),
@@ -649,7 +676,7 @@
         ],
         flops=4 * tiles * width * depth * 16,
         moved=2 * tiles * width * depth,
-    )(meta, far(recurrence), far(sensitivity), fetched, far(ray_vector), far(east_msg))
+    )(meta, far(recurrence), far(sensitivity), fetched, far(ray_vector), north, south, west, east)
     arrived = exchange(terms.reshape(devices, group, depth)).reshape(slots * systems, depth)
 
     bar, image, sums, patched, model_patch, chosen = call(
@@ -657,7 +684,7 @@
         "dense",
         (there(flat, F32),) * 2
         + (plain((1, lanes), F32), plain(patch, F32), plain(patch, F32), plain((PATCH * clon, slots), BF16)),
-        [vmem(), smem()] + [vmem()] * 2 + [hbm()] * 2 + [vmem()] * 4,
+        [vmem(), smem()] + [vmem()] * 3 + [hbm()] * 2 + [vmem()] * 4,
         (hbm(),) * 2 + (vmem(),) * 4,
         scratch=[pltpu.VMEM(flat, F32)] * 4
         + [
@@ -674,13 +701,14 @@
         far(recurrence),
         corner,
         wanted,
+        diagonal,
         ray_bar,
         model_flat,
         damping_flat,
-        far(north),
-        far(south),
-        far(west),
-        far(east),
+        north,
+        south,
+        west,
+        east,
     )
 
     added, parts = call(

time: 104 us -> 88.3 us (0.85)
  Pallas kernels: 46.8 us -> 33.9 us
  blocking collectives: 32 us -> 26.3 us
  starting transfers between devices: 16.5 us -> 20.1 us
  local copies, waits for them, and re-layouts: 2.05 us -> 0.01 us
    pallas_call x2 -> x1, Pallas kernels: 15.4 us -> 2.15 us  [per_device(): call(ask_body, 'ask', there(asked, F32), [vmem(), hbm()], vmem(), scratch...]
    all_to_all x2, blocking collectives: 32 us -> 26.3 us  [exchange(): return lax.all_to_all(x, AXES, split_axis=0, concat_axis=0, tiled=True)]
    all_to_all x2, starting transfers between devices: 7.29 us -> 12.2 us  [exchange(): return lax.all_to_all(x, AXES, split_axis=0, concat_axis=0, tiled=True)]
    all_to_all x2, waiting for transfers between devices: 0.01 us -> 1.55 us  [exchange(): return lax.all_to_all(x, AXES, split_axis=0, concat_axis=0, tiled=True)]
    unnamed x14 -> x2, local copies, waits for them, and re-layouts: 1.39 us -> 0.01 us
    ppermute x4, starting transfers between devices: 9.23 us -> 7.97 us  [shifted(): return lax.ppermute(x, axis, pairs)]
  transfers between devices with their start and end apart: 6 -> 6, of which waited for: 2 -> 3; matrix products, arithmetic and copies ran while one was open for 0% -> 0% of each run, Pallas kernels for 27% -> 15%
where the time goes in v6:
time: 88.3 us; the launch traced here: 87.6 us
  Pallas kernels  33.9 us (38%)
  blocking collectives  26.3 us (30%)
  starting transfers between devices  20.1 us (23%)
  waiting for transfers between devices  5.94 us (7%)
  between operations  1.39 us (2%)
    all_to_all x2, blocking collectives, exchange(): return lax.all_to_all(x, AXES, split_axis=0, concat_axis=0, tiled=True)  26.3 us
    all_to_all x2, starting transfers between devices, exchange(): return lax.all_to_all(x, AXES, split_axis=0, concat_axis=0, tiled=True)  12.2 us
    pallas_call x1, Pallas kernels, per_device(): call(functools.partial(finish_body, float(rows_all), float(cells_all), cl...  9.63 us
    pallas_call x1, Pallas kernels, per_device(): call(functools.partial(dense_body, cap, clat, clon), 'dense', (there(flat...  9.04 us
    ppermute x4, starting transfers between devices, shifted(): return lax.ppermute(x, axis, pairs)  7.97 us
    pallas_call x1, Pallas kernels, per_device(): call(functools.partial(rays_body, cap, blocks), 'rays', (plain(ray_vector...  5.88 us
    ppermute x4, waiting for transfers between devices, shifted(): return lax.ppermute(x, axis, pairs)  4.39 us
    pallas_call x1, Pallas kernels, per_device(): call(functools.partial(flanks_body, columns.bit_length() - 1, blocks), 'f...  3.78 us
  transfers between devices with their start and end apart: 6, of which 3 were waited for; matrix products, arithmetic and copies ran while one was open for 0% of the time, Pallas kernels for 15%

profile of v6, /device:TPU:0, one launch (start us, length us, event | category | flops | bytes accessed | tf_op | source)
XLA Modules:
  0.0 87.6 jit_solution(17288306789413561299)
XLA Ops:
  0.6 0.0 copy-start
  0.6 2.2 %ask.1 = f32[32,1,640]{2,1,0:T(1,128)} custom-call(s32[1,1,60]{2,1,0:T(1,128)} %ids_ref.3, f32[4,32,32,128]{3,2,1,0:T(8,128)} %model_in.3), custom_call_target="tpu_custom_call" | custom-call | tf_op jit(solution)/shard_map/ask/pallas_call | solution.py:622
  2.8 14.9 %all_to_all.20.lists_ref = f32[32,1,640]{2,1,0:T(1,128)S(1)} all-to-all(f32[32,1,640]{2,1,0:T(1,128)} %ask.1), channel_id=1, replica_groups=mesh['lat'=4,'lon'=8] {'lat','lon'}, dimensions={0} | all-to-all | bytes 163840 | tf_op jit(solution)/shard_map/all_to_all | solution.py:587
  17.7 2.4 %serve.1 = (bf16[512,128]{1,0:T(8,128)(2,1)}, f32[32,128]{1,0:T(8,128)S(1)}, s32[1]{0:T(128)}, f32[16,128]{1,0:T(8,128)S(1)}) custom-call(f32[32,1,640]{2,1,0:T(1,128)S(1)} %all_to_all.20.lists_ref, f32[4,1024,128]{2,1,0:T(8,128)} %bitcast.19), custom_call_target="tpu_custom_call" | custom-call | tf_op jit(solution)/shard_map/serve/pallas_call | solution.py:632
  20.1 2.6 %all-to-all-start.1 = ((bf16[32,16,128]{2,1,0:T(8,128)(2,1)}), bf16[32,16,128]{2,1,0:T(8,128)(2,1)S(1)}, u32[]{:S(2)}, u32[]{:S(2)}) async-start(bf16[32,16,128]{2,1,0:T(8,128)(2,1)} %bitcast.26), calls=%async_computation.1 | async-start | bytes 262144 | tf_op jit(solution)/shard_map/all_to_all | solution.py:587
  23.4 0.0 copy-done
  23.4 3.8 %flanks.1 = (f32[4,3,32,128]{3,2,1,0:T(8,128)}, f32[4,3,32,128]{3,2,1,0:T(8,128)}, f32[4,96,128]{2,1,0:T(8,128)}, f32[4,96,128]{2,1,0:T(8,128)}, s32[8,128]{1,0:T(8,128)S(1)}) custom-call(s32[1]{0:T(128)} %get-tuple-element.31.after_ref.corner_ref, s32[1,1,60]{2,1,0:T(1,128)} %ids_ref.3, s32[1,1,4]{2,1,0:T(1,128)S(1)} %copy-done, ...), custom_call_target="tpu_custom_call" | custom-call | flops 1 | bytes 2097152 | tf_op jit(solution)/shard_map/flanks/pallas_call | solution.py:649
  27.2 3.6 %collective-permute-start = (f32[4,3,32,128]{3,2,1,0:T(8,128)}, f32[4,3,32,128]{3,2,1,0:T(8,128)S(1)}, u32[]{:S(2)}, u32[]{:S(2)}) collective-permute-start(f32[4,3,32,128]{3,2,1,0:T(8,128)} %get-tuple-element.34), channel_id=1, source_target_pairs={{0,8},{8,16},{16,24},{1,9},{9,17},{17,25},{2,10},{10,18},{18,26},{... | collective-permute-start | bytes 589832 | tf_op jit(solution)/shard_map/ppermute | solution.py:583
  30.8 1.3 %collective-permute-start.1 = (f32[4,3,32,128]{3,2,1,0:T(8,128)}, f32[4,3,32,128]{3,2,1,0:T(8,128)S(1)}, u32[]{:S(2)}, u32[]{:S(2)}) collective-permute-start(f32[4,3,32,128]{3,2,1,0:T(8,128)} %get-tuple-element.35), channel_id=1, source_target_pairs={{8,0},{16,8},{24,16},{9,1},{17,9},{25,17},{10,2},{18,10},{26,18},{... | collective-permute-start | bytes 589832 | tf_op jit(solution)/shard_map/ppermute | solution.py:583
  32.1 1.8 %collective-permute-start.2 = (f32[4,96,128]{2,1,0:T(8,128)}, f32[4,96,128]{2,1,0:T(8,128)S(1)}, u32[]{:S(2)}, u32[]{:S(2)}) collective-permute-start(f32[4,96,128]{2,1,0:T(8,128)} %get-tuple-element.36), channel_id=1, source_target_pairs={{0,1},{1,2},{2,3},{3,4},{4,5},{5,6},{6,7},{8,9},{9,10},{10,11},{11... | collective-permute-start | bytes 589832 | tf_op jit(solution)/shard_map/ppermute | solution.py:583
  33.9 1.3 %collective-permute-start.3 = (f32[4,96,128]{2,1,0:T(8,128)}, f32[4,96,128]{2,1,0:T(8,128)S(1)}, u32[]{:S(2)}, u32[]{:S(2)}) collective-permute-start(f32[4,96,128]{2,1,0:T(8,128)} %get-tuple-element.37), channel_id=1, source_target_pairs={{1,0},{2,1},{3,2},{4,3},{5,4},{6,5},{7,6},{9,8},{10,9},{11,10},{12... | collective-permute-start | bytes 589832 | tf_op jit(solution)/shard_map/ppermute | solution.py:583
  35.2 0.4 collective-permute-done.north.north_ref
  35.5 4.0 %collective-permute-done.1.south.south_ref = f32[4,3,32,128]{3,2,1,0:T(8,128)S(1)} collective-permute-done((f32[4,3,32,128]{3,2,1,0:T(8,128)}, f32[4,3,32,128]{3,2,1,0:T(8,128)S(1)}, u32[]{:S(2)}, u32[]{:S(2)}) %collective-permute-start.1) | collective-permute-done | bytes 196640 | tf_op jit(solution)/shard_map/ppermute | solution.py:583
  39.5 0.0 collective-permute-done.2.west.west_ref
  39.5 0.0 collective-permute-done.3.east.east_ref
  39.5 0.0 all-to-all-done.1
  39.6 5.9 %rays.1 = (f32[4,1,1,768]{3,2,1,0:T(1,128)S(1)}, f32[128,4,128]{2,1,0:T(4,128)}) custom-call(s32[8,128]{1,0:T(8,128)S(1)} %get-tuple-element.32.meta_ref, f32[3,4]{1,0:T(4,128)} %rec_ref.5, bf16[1,1,60,256,128]{4,3,2,1,0:T(8,128)(2,1)} %tiles_in.1, bf16[512,128]{1,0:T(8,128)(2,1)S(1)} %bitcast.17, f32[4,1,1,768]{3,2,1,0:T(1,128)} %old_ref.1, ...), custom_call_target="tpu_custom_call" | custom-call | flops 125829120 | bytes 3932160 | tf_op jit(solution)/shard_map/rays/pallas_call | solution.py:665
  45.4 9.6 %all-to-all-start.2 = ((f32[32,16,128]{2,1,0:T(8,128)}), f32[32,16,128]{2,1,0:T(8,128)S(1)}, u32[]{:S(2)}, u32[]{:S(2)}) async-start(f32[32,16,128]{2,1,0:T(8,128)} %bitcast.25), calls=%async_computation.2 | async-start | bytes 524288 | tf_op jit(solution)/shard_map/all_to_all | solution.py:587
  55.0 9.0 %dense.1 = (f32[4,1024,128]{2,1,0:T(8,128)}, f32[4,1024,128]{2,1,0:T(8,128)}, f32[1,128]{1,0:T(1,128)S(1)}, f32[4,128,128]{2,1,0:T(8,128)S(1)}, f32[4,128,128]{2...) custom-call(f32[3,4]{1,0:T(4,128)} %rec_ref.5, s32[1]{0:T(128)} %get-tuple-element.31.after_ref.corner_ref, ...), custom_call_target="tpu_custom_call" | custom-call | flops 20971520 | bytes 8388608 | tf_op jit(solution)/shard_map/dense/pallas_call | solution.py:682
  64.1 1.5 %all-to-all-done.2 = f32[32,16,128]{2,1,0:T(8,128)S(1)} async-done(((f32[32,16,128]{2,1,0:T(8,128)}), f32[32,16,128]{2,1,0:T(8,128)S(1)}, u32[]{:S(2)}, u32[]{:S(2)}) %all-to-all-start.2) | async-done | bytes 262176 | tf_op jit(solution)/shard_map/all_to_all | solution.py:587
  65.6 1.0 %combine.1 = (f32[4,128,128]{2,1,0:T(8,128)S(1)}, f32[32,128]{1,0:T(8,128)}) custom-call(f32[512,128]{1,0:T(8,128)S(1)} %bitcast.16, bf16[128,128]{1,0:T(8,128)(2,1)S(1)} %get-tuple-element.42.chosen_ref, f32[4,128,128]{2,1,0:T(8,128)S(1)} %get-tuple-element.43.patch_ref, f32[4,128,128]{2,1,0:T(8,128)S(1)} %get-tuple-element.44.model_patch_ref, ...), custom_call_target="tpu_custom_call" | custom-call | tf_op jit(solution)/shard_map/combine/pallas_call | solution.py:714
  66.6 11.4 %all_to_all.21 = f32[32,1,128]{2,1,0:T(1,128)S(1)} all-to-all(f32[32,1,128]{2,1,0:T(1,128)} %bitcast.27), channel_id=1, replica_groups=mesh['lat'=4,'lon'=8] {'lat','lon'}, dimensions={0} | all-to-all | bytes 32768 | tf_op jit(solution)/shard_map/all_to_all | solution.py:587
  78.0 9.6 %finish.1 = (f32[4,1,1,768]{3,2,1,0:T(1,128)}, f32[4,1024,128]{2,1,0:T(8,128)}, f32[4,1024,128]{2,1,0:T(8,128)}, f32[4,1024,128]{2,1,0:T(8,128)}, f32[4,1024,128]{2,1,0:T(8,128)}, /*index=5*/f32[3,4]{1,0:T(4,128)}) custom-call(s32[1]{0:T(128)} %get-tuple-element.31.after_ref.corner_ref, f32[32,128]{1,0:T(8,128)S(1)} %bitcast.18, f32[3,4]{1,0:T(4,128)} %rec_ref.5, ...), custom_call_target="tpu_custom_call" | custom-call | flops 5242880 | bytes 18874368 | tf_op jit(solution)/shard_map/finish/pallas_call | solution.py:723
Async XLA Ops:
  0.6 22.7 %copy-start = (s32[1,1,4]{2,1,0:T(1,128)S(1)}, s32[1,1,4]{2,1,0:T(1,128)}, u32[]{:S(2)}) copy-start(s32[1,1,4]{2,1,0:T(1,128)} %off_ref.1) | copy-start | bytes 52
  20.1 19.4 %all-to-all-start.1 = ((bf16[32,16,128]{2,1,0:T(8,128)(2,1)}), bf16[32,16,128]{2,1,0:T(8,128)(2,1)S(1)}, u32[]{:S(2)}, u32[]{:S(2)}) async-start(bf16[32,16,128]{2,1,0:T(8,128)(2,1)} %bitcast.26), calls=%async_computation.1 | async-start | bytes 262144 | tf_op jit(solution)/shard_map/all_to_all | solution.py:587
  27.2 8.4 %collective-permute-start = (f32[4,3,32,128]{3,2,1,0:T(8,128)}, f32[4,3,32,128]{3,2,1,0:T(8,128)S(1)}, u32[]{:S(2)}, u32[]{:S(2)}) collective-permute-start(f32[4,3,32,128]{3,2,1,0:T(8,128)} %get-tuple-element.34), channel_id=1, source_target_pairs={{0,8},{8,16},{16,24},{1,9},{9,17},{17,25},{2,10},{10,18},{18,26},{... | collective-permute-start | bytes 589832 | tf_op jit(solution)/shard_map/ppermute | solution.py:583
  30.8 8.8 %collective-permute-start.1 = (f32[4,3,32,128]{3,2,1,0:T(8,128)}, f32[4,3,32,128]{3,2,1,0:T(8,128)S(1)}, u32[]{:S(2)}, u32[]{:S(2)}) collective-permute-start(f32[4,3,32,128]{3,2,1,0:T(8,128)} %get-tuple-element.35), channel_id=1, source_target_pairs={{8,0},{16,8},{24,16},{9,1},{17,9},{25,17},{10,2},{18,10},{26,18},{... | collective-permute-start | bytes 589832 | tf_op jit(solution)/shard_map/ppermute | solution.py:583
  32.1 7.5 %collective-permute-start.2 = (f32[4,96,128]{2,1,0:T(8,128)}, f32[4,96,128]{2,1,0:T(8,128)S(1)}, u32[]{:S(2)}, u32[]{:S(2)}) collective-permute-start(f32[4,96,128]{2,1,0:T(8,128)} %get-tuple-element.36), channel_id=1, source_target_pairs={{0,1},{1,2},{2,3},{3,4},{4,5},{5,6},{6,7},{8,9},{9,10},{10,11},{11... | collective-permute-start | bytes 589832 | tf_op jit(solution)/shard_map/ppermute | solution.py:583
  33.9 5.7 %collective-permute-start.3 = (f32[4,96,128]{2,1,0:T(8,128)}, f32[4,96,128]{2,1,0:T(8,128)S(1)}, u32[]{:S(2)}, u32[]{:S(2)}) collective-permute-start(f32[4,96,128]{2,1,0:T(8,128)} %get-tuple-element.37), channel_id=1, source_target_pairs={{1,0},{2,1},{3,2},{4,3},{5,4},{6,5},{7,6},{9,8},{10,9},{11,10},{12... | collective-permute-start | bytes 589832 | tf_op jit(solution)/shard_map/ppermute | solution.py:583
  45.4 20.2 %all-to-all-start.2 = ((f32[32,16,128]{2,1,0:T(8,128)}), f32[32,16,128]{2,1,0:T(8,128)S(1)}, u32[]{:S(2)}, u32[]{:S(2)}) async-start(f32[32,16,128]{2,1,0:T(8,128)} %bitcast.25), calls=%async_computation.2 | async-start | bytes 524288 | tf_op jit(solution)/shard_map/all_to_all | solution.py:587

commit v7 on v6

v7 whole, which is shorter than its diff:
```python
import functools

import jax
import jax.numpy as jnp
from jax import lax
from jax.experimental import pallas as pl
from jax.experimental.pallas import tpu as pltpu
from jax.sharding import PartitionSpec as P

DAMP_WEIGHT = 0.15
EPSILON = 1e-05
AXES = ("lat", "lon")
PATCH = 4
F32, BF16, I32 = jnp.float32, jnp.bfloat16, jnp.int32


def iota(shape, dim):
    return lax.broadcasted_iota(I32, shape, dim)


def vmem():
    return pl.BlockSpec(memory_space=pltpu.VMEM)


def hbm():
    return pl.BlockSpec(memory_space=pltpu.HBM)


def near(x):
    return pltpu.with_memory_space_constraint(x, pltpu.VMEM)


def far(x):
    return pltpu.with_memory_space_constraint(x, pltpu.HBM)


def smem():
    return pl.BlockSpec(memory_space=pltpu.SMEM)


def call(body, name, out_shape, in_specs, out_specs, scratch=(), grid=(), mib=16, flops=0, moved=0):
    return pl.pallas_call(
        body,
        name=name,
        grid=grid,
        out_shape=out_shape,
        in_specs=in_specs,
        out_specs=out_specs,
        scratch_shapes=list(scratch),
        compiler_params=pltpu.CompilerParams(vmem_limit_bytes=mib * 2**20),
        cost_estimate=pl.CostEstimate(flops=flops, bytes_accessed=moved, transcendentals=0),
    )


STEP = 8


def ask_body(ids_ref, model_in, out_ref, slabs, sems):
    systems, clat, clon, depth = model_in.shape
    copies = []
    for k in range(4):
        at = (slice(None), pl.ds((k // 2) * (clat - 1), 1), pl.ds((k % 2) * (clon - 8), 8))
        copies.append(pltpu.make_async_copy(model_in.at[at], slabs.at[k], sems.at[k]))
    for copy in copies:
        copy.start()
    tiles = ids_ref.shape[-1]
    ids = jnp.concatenate([ids_ref[0].astype(F32), jnp.full((1, depth - tiles), -1.0, F32)], axis=1)
    for copy in copies:
        copy.wait()
    corners = [
        [slabs[k, r, 0, (k % 2) * 7 : (k % 2) * 7 + 1] for r in range(systems)] for k in range(4)
    ]
    lat_at, lon_at = lax.axis_index("lat"), lax.axis_index("lon")
    width = lax.axis_size("lon")
    for e in range(out_ref.shape[0]):
        out_ref[e, :, 0:depth] = ids
        south, east = e // width > lat_at, e % width > lon_at
        for r in range(systems):
            upper = jnp.where(east, corners[1][r], corners[0][r])
            lower = jnp.where(east, corners[3][r], corners[2][r])
            out_ref[e, :, (r + 1) * depth : (r + 2) * depth] = jnp.where(south, lower, upper)


def wanted_column(wanted, cap):
    devices, lanes = wanted.shape
    rows = devices * cap
    spread = jnp.broadcast_to(wanted[:, None, :], (devices, cap, lanes)).reshape(rows, lanes)
    pick = iota((rows, lanes), 1) == (iota((rows, lanes), 0) & (cap - 1))
    return jnp.sum(jnp.where(pick, spread, 0.0), axis=1, keepdims=True)


def serve_body(cap, clat, clon, lists_ref, model_in, served_ref, wanted_ref, corner_ref, diagonal_ref, patch, mixed, sems):
    systems, width, depth = patch.shape
    devices = lists_ref.shape[0]
    lanes = 128
    shift = (clat * clon).bit_length() - 1
    me = lax.axis_index("lat") * lax.axis_size("lon") + lax.axis_index("lon")
    ids = lists_ref[:, 0, 0:lanes].astype(I32)
    column = ids - lax.shift_left(me, shift)
    mine = (column >= 0) & (column < clat * clon) & (ids >= 0)
    first = jnp.min(jnp.where(mine, column, clat * clon))
    corner = jnp.minimum(lax.shift_right_logical(first, clon.bit_length() - 1), clat - PATCH)
    corner_ref[0] = corner
    at = pl.ds(pl.multiple_of(corner * clon, clon), width)
    copies = [pltpu.make_async_copy(model_in.at[r, at], patch.at[r], sems.at[r]) for r in range(systems)]
    for copy in copies:
        copy.start()
    ahead = (iota((lanes, lanes), 0) < iota((lanes, lanes), 1)).astype(F32).astype(BF16)
    rank = jnp.dot(mine.astype(F32).astype(BF16), ahead, preferred_element_type=F32)
    value = (column - corner * clon + 1).astype(F32)
    at = iota((devices, lanes), 1)
    wanted = jnp.zeros((devices, lanes), F32)
    for c in range(cap):
        picked = jnp.sum(jnp.where(mine & (rank == c), value, 0.0), axis=1, keepdims=True)
        wanted = jnp.where(at == c, picked, wanted)
    wanted_ref[...] = wanted
    target = wanted_column(wanted, cap).astype(I32) - 1
    rows = target.shape[0]
    chosen = (jnp.broadcast_to(target, (rows, width)) == iota((rows, width), 1)).astype(F32).astype(BF16)
    for r in range(systems):
        copies[r].wait()
        table = patch[r].astype(BF16)
        mixed[pl.ds(r, rows, stride=systems), :] = jnp.dot(chosen, table, preferred_element_type=F32)
    served_ref[...] = mixed[...].astype(BF16)
    lat_at, lon_at = lax.axis_index("lat"), lax.axis_index("lon")
    lat_size, lon_size = lax.axis_size("lat"), lax.axis_size("lon")
    for k in range(4):
        lat_to, lon_to = lat_at + 2 * (k // 2) - 1, lon_at + 2 * (k % 2) - 1
        inside = (lat_to >= 0) & (lat_to < lat_size) & (lon_to >= 0) & (lon_to < lon_size)
        source = jnp.where(inside, lat_to * lon_size + lon_to, 0)
        flag = inside.astype(F32)
        for r in range(systems):
            got = lists_ref[source, :, (r + 1) * depth : (r + 2) * depth]
            diagonal_ref[k * systems + r : k * systems + r + 1, :] = got * flag


def flanks_body(
    shift,
    blocks,
    after_ref,
    ids_ref,
    off_ref,
    count_ref,
    model_in,
    damp_in,
    north_ref,
    south_ref,
    east_ref,
    west_ref,
    meta_ref,
    slabs,
    sems,
):
    systems, clat, clon, depth = model_in.shape
    copies = []
    for k, (ref, at) in enumerate(((model_in, 0), (model_in, clon - 8), (damp_in, 0), (damp_in, clon - 8))):
        copies.append(pltpu.make_async_copy(ref.at[:, :, pl.ds(at, 8)], slabs.at[k], sems.at[k]))
    last = clat - 1
    pairs = (
        (model_in.at[:, pl.ds(last - 1, 2)], south_ref.at[:, pl.ds(0, 2)]),
        (damp_in.at[:, pl.ds(last, 1)], south_ref.at[:, pl.ds(2, 1)]),
        (model_in.at[:, pl.ds(0, 2)], north_ref.at[:, pl.ds(0, 2)]),
        (damp_in.at[:, pl.ds(0, 1)], north_ref.at[:, pl.ds(2, 1)]),
    )
    copies += [pltpu.make_async_copy(a, b, sems.at[i + 4]) for i, (a, b) in enumerate(pairs)]
    for copy in copies:
        copy.start()
    tiles = ids_ref.shape[-1]
    lanes = 128
    ids = jnp.concatenate([ids_ref[0], jnp.full((1, lanes - tiles), -1, I32)], axis=1)
    owner = lax.shift_right_arithmetic(ids, shift)
    square = (lanes, lanes)
    down, across = iota(square, 0), iota(square, 1)
    owner_f = jnp.broadcast_to(owner.astype(F32), square)
    owner_col = jnp.sum(jnp.where(down == across, owner_f, 0.0), axis=1, keepdims=True)
    same = jnp.where((owner_f == owner_col) & (down < across), 1.0, 0.0)
    rank = jnp.sum(same, axis=0, keepdims=True).astype(I32)
    lane = iota((1, lanes), 1)
    block = jnp.zeros((1, lanes), I32)
    starts = off_ref[0]
    for b in range(1, blocks + 1):
        block = block + (lane >= jnp.broadcast_to(starts[:, b : b + 1], (1, lanes))).astype(I32)
    count = jnp.broadcast_to(count_ref[...], (1, lanes))
    meta_ref[...] = jnp.concatenate([owner, rank, block, count] + [owner] * 4, axis=0)
    for copy in copies:
        copy.wait()
    rows = slabs.reshape(4, systems, clat * 8, depth)
    for r in range(systems):
        for out, slab, near_at, beyond in ((east_ref, 1, 7, 6), (west_ref, 0, 0, 1)):
            out[r, 0:clat] = rows[slab, r, pl.ds(near_at, clat, stride=8), :]
            out[r, clat : 2 * clat] = rows[slab, r, pl.ds(beyond, clat, stride=8), :]
            out[r, 2 * clat : 3 * clat] = rows[slab + 2, r, pl.ds(near_at, clat, stride=8), :]


def six(x, north, south, west, east):
    lane = iota(x.shape, 1)
    rows, depth = x.shape
    left, right = pltpu.roll(x, 1, 0), pltpu.roll(x, rows - 1, 0)
    ends = (8, depth)
    row = iota(ends, 0)
    left = jnp.concatenate([jnp.where(row == 0, jnp.broadcast_to(west, ends), left[:8]), left[8:]], axis=0)
    right = jnp.concatenate([right[:-8], jnp.where(row == 7, jnp.broadcast_to(east, ends), right[-8:])], axis=0)
    above = jnp.where(lane == 0, 0.0, pltpu.roll(x, 1, 1))
    below = jnp.where(lane == depth - 1, 0.0, pltpu.roll(x, depth - 1, 1))
    beside = north + south + left + right + above + below
    return DAMP_WEIGHT * (6.0 * x - beside)


def fold(x):
    parts = [x[i * 8 : (i + 1) * 8] for i in range(x.shape[0] // 8)]
    return functools.reduce(lambda a, b: a + b, parts)


def place(row, lane, value):
    return row + jnp.where(iota(row.shape, 1) == lane, jnp.broadcast_to(value, row.shape), 0.0)


def line(ref, r, i, clon):
    return ref[r, pl.ds(pl.multiple_of(i * clon, clon), clon), :]


def stencils(ref, r, k, clat, clon, first, last, west, east):
    base = k * STEP
    for j in range(STEP):
        i = base + j
        x = line(ref, r, i, clon)
        if j == 0:
            above = jnp.where(k > 0, line(ref, r, jnp.maximum(i - 1, 0), clon), first)
        else:
            above = line(ref, r, i - 1, clon)
        if j == STEP - 1:
            below = jnp.where(i + 1 < clat, line(ref, r, jnp.minimum(i + 1, clat - 1), clon), last)
        else:
            below = line(ref, r, i + 1, clon)
        yield i, x, six(x, above, below, west[pl.ds(i, 1)], east[pl.ds(i, 1)])


def damp_body(
    clat,
    clon,
    rec_ref,
    diagonal_ref,
    model_in,
    damp_in,
    north_ref,
    south_ref,
    west_ref,
    east_ref,
    bar_sent,
    north_out,
    south_out,
    west_out,
    east_out,
    sums_out,
    model_ref,
    damp_ref,
    bar_out,
    alphas,
    sems,
):
    systems, _, depth = model_ref.shape

    def incoming(r):
        return (
            pltpu.make_async_copy(model_in.at[r], model_ref.at[r], sems.at[r, 0]),
            pltpu.make_async_copy(damp_in.at[r], damp_ref.at[r], sems.at[r, 1]),
        )

    def outgoing(r):
        return pltpu.make_async_copy(bar_out.at[r], bar_sent.at[r], sems.at[r, 2])

    for r in range(systems):
        for copy in incoming(r):
            copy.start()
    for r in range(systems):
        alphas[r] = jnp.sum(rec_ref[0:1, r : r + 1])
    lat_at, lon_at = lax.axis_index("lat"), lax.axis_index("lon")
    has_north = (lat_at > 0).astype(F32)
    has_south = (lat_at < lax.axis_size("lat") - 1).astype(F32)
    has_west = (lon_at > 0).astype(F32)
    has_east = (lon_at < lax.axis_size("lon") - 1).astype(F32)

    def diagonal(k, r):
        return diagonal_ref[pl.ds(k * systems + r, 1), :]

    def system(r, row):
        alpha = alphas[r]
        for copy in incoming(r):
            copy.wait()

        def side(ref, own, flag, east):
            x, beyond, old = ref[r, 0:clat], ref[r, clat : 2 * clat], ref[r, 2 * clat : 3 * clat]
            upper, lower = diagonal(east, r), diagonal(2 + east, r)
            return (six(x, beyond, own, upper, lower) - alpha * old) * flag

        west_out[r] = side(west_ref, model_ref[r, pl.ds(0, clat, stride=clon), :], has_west, 0)
        east_out[r] = side(east_ref, model_ref[r, pl.ds(clon - 1, clat, stride=clon), :], has_east, 1)
        top, bottom = line(model_ref, r, 0, clon), line(model_ref, r, clat - 1, clon)
        edge = six(north_ref[r, 1], north_ref[r, 0], top, diagonal(0, r), diagonal(1, r))
        north_out[r] = has_north * (edge - alpha * north_ref[r, 2])
        edge = six(south_ref[r, 0], bottom, south_ref[r, 1], diagonal(2, r), diagonal(3, r))
        south_out[r] = has_south * (edge - alpha * south_ref[r, 2])

        def damped(k, acc):
            bar_sq, model_sq = acc
            ends = (north_ref[r, 1], south_ref[r, 0], west_ref.at[r], east_ref.at[r])
            for i, x, got in stencils(model_ref, r, k, clat, clon, *ends):
                bar = got - alpha * line(damp_ref, r, i, clon)
                bar_out[r, pl.ds(pl.multiple_of(i * clon, clon), clon), :] = bar
                bar_sq, model_sq = bar_sq + fold(bar * bar), model_sq + fold(x * x)
            return bar_sq, model_sq

        zero = jnp.zeros((8, depth), F32)
        bar_sq, model_sq = lax.fori_loop(0, clat // STEP, damped, (zero, zero))
        outgoing(r).start()
        row = place(row, r, jnp.sum(bar_sq, keepdims=True))
        return place(row, 3 * systems + r, jnp.sum(model_sq, keepdims=True))

    sums_out[...] = lax.fori_loop(0, systems, system, jnp.zeros((1, depth), F32))
    for r in range(systems):
        outgoing(r).wait()


def image_body(
    chunk,
    clat,
    clon,
    corner_ref,
    wanted_ref,
    bar_in,
    north_ref,
    south_ref,
    west_ref,
    east_ref,
    model_in,
    sums_ref,
    image_sent,
    sums_out,
    patch_out,
    model_patch_out,
    chosen_out,
    bar_ref,
    model_ref,
    image_out,
    sems,
):
    systems, _, depth = model_ref.shape

    def incoming(r):
        return (
            pltpu.make_async_copy(bar_in.at[r], bar_ref.at[r], sems.at[r, 0]),
            pltpu.make_async_copy(model_in.at[r], model_ref.at[r], sems.at[r, 1]),
        )

    def outgoing(r):
        return pltpu.make_async_copy(image_out.at[r], image_sent.at[r], sems.at[r, 2])

    for r in range(systems):
        for copy in incoming(r):
            copy.start()
    corner = corner_ref[0]
    wanted = wanted_ref[...]
    devices = wanted.shape[0]
    height, slots = chosen_out.shape
    width = PATCH * clon
    at = iota((1, slots), 1)
    source = jnp.floor((at.astype(F32) + 0.5) * (1.0 / chunk)).astype(I32)
    inner = at - source * chunk
    from_e = (jnp.broadcast_to(source, (devices, slots)) == iota((devices, slots), 0)).astype(F32).astype(BF16)
    turned = jnp.transpose(wanted)[0:8].astype(BF16)
    listed = jnp.dot(turned, from_e, preferred_element_type=F32)
    slot_of = lax.shift_right_logical(inner, systems.bit_length() - 1)
    mine = jnp.broadcast_to(slot_of, listed.shape) == iota(listed.shape, 0)
    flat = jnp.sum(jnp.where(mine, listed, 0.0), axis=0, keepdims=True).astype(I32)
    used = (flat > 0) & (inner < chunk - 1)
    target = jnp.where(used, (inner & (systems - 1)) * width + flat - 1, -1)
    for k in range(height // 64):
        shape = (64, slots)
        hit = jnp.broadcast_to(target, shape) == iota(shape, 0) + k * 64
        chosen_out[k * 64 : (k + 1) * 64] = hit.astype(F32).astype(BF16)

    def system(r, row):
        for copy in incoming(r):
            copy.wait()

        def imaged(k, acc):
            image_sq, cross = acc
            ends = (north_ref[r], south_ref[r], west_ref.at[r], east_ref.at[r])
            for i, x, image in stencils(bar_ref, r, k, clat, clon, *ends):
                image_out[r, pl.ds(pl.multiple_of(i * clon, clon), clon), :] = image
                image_sq = image_sq + fold(image * image)
                cross = cross + fold(image * line(model_ref, r, i, clon))
            return image_sq, cross

        zero = jnp.zeros((8, depth), F32)
        image_sq, cross = lax.fori_loop(0, clat // STEP, imaged, (zero, zero))
        outgoing(r).start()
        here = pl.ds(pl.multiple_of(corner * clon, clon), width)
        there = pl.ds(pl.multiple_of(r * width, width), width)
        patch_out[there, :] = image_out[r, here, :]
        model_patch_out[there, :] = model_ref[r, here, :]
        row = place(row, systems + r, jnp.sum(image_sq, keepdims=True))
        return place(row, 2 * systems + r, jnp.sum(cross, keepdims=True))

    sums_out[...] = lax.fori_loop(0, systems, system, sums_ref[...])
    for r in range(systems):
        outgoing(r).wait()


def rays_body(
    cap, blocks, meta_ref, rec_ref, tiles_in, fetched_ref, old_ref, sums_ref, bar_ref, term_ref, tiles_ref, masks, lows, sems
):
    tiles, width, depth = tiles_in.shape[2:]
    part = -(-tiles // PARTS)
    copies = []
    for k in range(PARTS):
        at = (0, 0, pl.ds(k * part, min(part, tiles - k * part)))
        copies.append(pltpu.make_async_copy(tiles_in.at[at], tiles_ref.at[at], sems.at[k]))
    for copy in copies:
        copy.start()
    systems = old_ref.shape[0]
    group = cap * systems
    chunk = group + 1
    devices = term_ref.shape[0] // chunk
    for c in range(cap + 1):
        here = lax.shift_right_logical(iota((group, depth), 0), systems.bit_length() - 1) == c
        masks[c] = here.astype(F32).astype(BF16)
    term_ref[...] = jnp.zeros(term_ref.shape, F32)
    lows[...] = jnp.zeros(lows.shape, BF16)
    total = jnp.zeros((blocks * group, width), F32)
    for t in range(tiles):
        if t % part == 0:
            copies[t // part].wait()
        owner, rank, block = meta_ref[0, t], meta_ref[1, t], meta_ref[2, t]
        rows = fetched_ref[pl.ds(pl.multiple_of(owner * group, group), group), :]
        left = jnp.concatenate(
            [rows * masks[jnp.where(block == b, rank, cap)] for b in range(blocks)], axis=0
        )
        total = total + lax.dot_general(
            left, tiles_ref[0, 0, t], (((1,), (1,)), ((), ())), preferred_element_type=F32
        )
    square = jnp.zeros((systems, width), F32)
    for b in range(blocks):
        traced = jnp.zeros((systems, width), F32)
        for c in range(cap):
            at = b * group + c * systems
            traced = traced + total[at : at + systems]
        old = jnp.concatenate(
            [old_ref[r, 0, :, b * width : (b + 1) * width] * rec_ref[0:1, r : r + 1] for r in range(systems)], axis=0
        )
        live = iota((systems, width), 1) + b * width < meta_ref[3, 0]
        bar = jnp.where(live, traced - old, 0.0)
        square = square + bar * bar
        for r in range(systems):
            bar_ref[r, 0, :, b * width : (b + 1) * width] = bar[r : r + 1]
        lows[b] = jnp.concatenate([bar, jnp.zeros((16 - systems, width), F32)], axis=0).astype(BF16)
    ray_sq = jnp.sum(square, axis=1, keepdims=True)
    part = sums_ref[...]
    for r in range(systems):
        part = place(part, r, ray_sq[r : r + 1])
    for e in range(devices):
        term_ref[e * chunk + group] = part
    for t in range(tiles):
        row = meta_ref[0, t] * chunk + meta_ref[1, t] * systems
        term = jnp.dot(lows[meta_ref[2, t]], tiles_ref[0, 0, t], preferred_element_type=F32)
        for r in range(systems):
            term_ref[row + r] = term[r : r + 1]


def combine_body(chunk, systems, terms_ref, chosen_ref, patch_ref, model_patch_ref, sums_ref, added_ref, residual_ref, parts_ref, split):
    arrived, depth = terms_ref.shape
    devices = parts_ref.shape[0]
    width = patch_ref.shape[0]
    x = terms_ref[...]
    high = x.astype(BF16)
    rest = x - high.astype(F32)
    middle = rest.astype(BF16)
    low = (rest - middle.astype(F32)).astype(BF16)
    padded = split.shape[0]
    if padded > arrived:
        split[arrived:] = jnp.zeros((padded - arrived, split.shape[1]), BF16)
    split[0:arrived, 0:depth] = high
    split[0:arrived, depth : 2 * depth] = middle
    split[0:arrived, 2 * depth :] = low
    three = jnp.dot(chosen_ref[...], split[...], preferred_element_type=F32)
    added = three[:, 0:depth] + (three[:, depth : 2 * depth] + three[:, 2 * depth :])
    added_ref[...] = added
    every = terms_ref[pl.ds(chunk - 1, devices, stride=chunk), :]
    residual_ref[...] = jnp.sum(every, axis=0, keepdims=True)
    square = added * (2.0 * patch_ref[...] + added)
    cross = added * model_patch_ref[...]
    row = sums_ref[...]
    each = width // systems
    for r in range(systems):
        row = place(row, systems + r, jnp.sum(square[r * each : (r + 1) * each], keepdims=True))
        row = place(row, 2 * systems + r, jnp.sum(cross[r * each : (r + 1) * each], keepdims=True))
    parts_ref[...] = jnp.broadcast_to(row, parts_ref.shape)


def first_norm(residual_ref, systems, rows_all):
    return jnp.sqrt(residual_ref[0:1, 0:systems] / rows_all + EPSILON)


def early_body(
    rows_all,
    residual_ref,
    rec_ref,
    ray_ref,
    bar_in,
    solution_in,
    search_in,
    ray_out,
    damp_out,
    solution_out,
    bar_ref,
    solution_ref,
    search_ref,
    damp_s,
    solution_s,
    coef,
    in_sems,
    sems,
):
    systems, columns, _ = bar_ref.shape
    rows = columns // PIECES
    ins = ((bar_in, bar_ref), (solution_in, solution_ref), (search_in, search_ref))
    outs = ((damp_s, damp_out), (solution_s, solution_out))
    start_all(ins, in_sems, systems, rows)
    rho_bar, phi_bar = rec_ref[1:2], rec_ref[2:3]
    beta = first_norm(residual_ref, systems, rows_all)
    rho = jnp.sqrt(rho_bar * rho_bar + beta * beta)
    scales = (1.0 / beta, (rho_bar / rho) * phi_bar / rho)
    for q, scale in enumerate(scales):
        for s in range(systems):
            coef[q, s] = scale[0, s]
    for s in range(systems):
        ray_out[s] = ray_ref[s] * coef[0, s]

    def piece(n, _):
        r, p = n // PIECES, n % PIECES
        at = pl.ds(pl.multiple_of(p * rows, rows), rows)
        for copy in pieces(ins, in_sems, r, p, rows):
            copy.wait()
        damp_s[r, at, :] = bar_ref[r, at, :] * coef[0, r]
        solution_s[r, at, :] = solution_ref[r, at, :] + search_ref[r, at, :] * coef[1, r]
        for copy in pieces(outs, sems, r, p, rows):
            copy.start()
        return 0

    lax.fori_loop(0, systems * PIECES, piece, 0)
    wait_all(outs, sems, systems, rows)


def finish_body(
    rows_all,
    cells_all,
    clon,
    corner_ref,
    residual_ref,
    parts_ref,
    rec_ref,
    added_ref,
    image_in,
    model_in,
    search_in,
    model_out,
    search_out,
    rec_out,
    image_ref,
    model_ref,
    search_ref,
    model_s,
    search_s,
    coef,
    in_sems,
    sems,
):
    systems, columns, _ = image_ref.shape
    rows = columns // PIECES
    ins = ((image_in, image_ref), (model_in, model_ref), (search_in, search_ref))
    outs = ((model_s, model_out), (search_s, search_out))
    start_all(ins, in_sems, systems, rows)
    total = jnp.sum(parts_ref[...], axis=0, keepdims=True)
    image_sq, cross, model_sq = (total[:, q * systems : (q + 1) * systems] for q in range(1, 4))
    rho_bar, phi_bar = rec_ref[1:2], rec_ref[2:3]
    beta = first_norm(residual_ref, systems, rows_all)
    update_sq = image_sq / (beta * beta) - 2.0 * cross + beta * beta * model_sq
    alpha = jnp.sqrt(jnp.maximum(update_sq, 0.0) / cells_all + EPSILON)
    rho = jnp.sqrt(rho_bar * rho_bar + beta * beta)
    cosine = rho_bar / rho
    sine = beta / rho
    rec_out[...] = jnp.concatenate([alpha, -cosine * alpha, sine * phi_bar], axis=0)
    scales = (1.0 / (beta * alpha), beta / alpha, sine * alpha / rho)
    for q, scale in enumerate(scales):
        for s in range(systems):
            coef[q, s] = scale[0, s]
    width = PATCH * clon

    def piece(n, _):
        r, p = n // PIECES, n % PIECES
        at = pl.ds(pl.multiple_of(p * rows, rows), rows)
        for copy in pieces(ins, in_sems, r, p, rows):
            copy.wait()
        new = image_ref[r, at, :] * coef[0, r] - model_ref[r, at, :] * coef[1, r]
        model_s[r, at, :] = new
        search_s[r, at, :] = new - search_ref[r, at, :] * coef[2, r]
        for k in range(PATCH):
            begin = (corner_ref[0] + k) * clon

            @pl.when((begin >= p * rows) & (begin < (p + 1) * rows))
            def _():
                cells = pl.ds(pl.multiple_of(begin, clon), clon)
                source = pl.ds(pl.multiple_of(r * width + k * clon, clon), clon)
                more = added_ref[source, :] * coef[0, r]
                model_s[r, cells, :] = model_s[r, cells, :] + more
                search_s[r, cells, :] = search_s[r, cells, :] + more

        for copy in pieces(outs, sems, r, p, rows):
            copy.start()
        return 0

    lax.fori_loop(0, systems * PIECES, piece, 0)
    wait_all(outs, sems, systems, rows)


PIECES = 2


def pieces(pairs, sems, r, p, rows):
    at = pl.ds(pl.multiple_of(p * rows, rows), rows)
    return [pltpu.make_async_copy(a.at[r, at], b.at[r, at], sems.at[r, p, k]) for k, (a, b) in enumerate(pairs)]


def start_all(pairs, sems, systems, rows):
    def one(n, _):
        for copy in pieces(pairs, sems, n // PIECES, n % PIECES, rows):
            copy.start()
        return 0

    lax.fori_loop(0, systems * PIECES, one, 0)


def wait_all(pairs, sems, systems, rows):
    def one(n, _):
        for copy in pieces(pairs, sems, n // PIECES, n % PIECES, rows):
            copy.wait()
        return 0

    lax.fori_loop(0, systems * PIECES, one, 0)


PARTS = 6


def shifted(x, axis, step):
    count = lax.axis_size(axis)
    if step > 0:
        pairs = [(i, i + 1) for i in range(count - 1)]
    else:
        pairs = [(i + 1, i) for i in range(count - 1)]
    return lax.ppermute(x, axis, pairs)


def exchange(x):
    return lax.all_to_all(x, AXES, split_axis=0, concat_axis=0, tiled=True)


def per_device(
    sensitivity,
    block_ids,
    block_offsets,
    ray_counts,
    ray_vector,
    damping_vector,
    model_vector,
    solution,
    search,
    recurrence,
):
    lat_size, lon_size = lax.axis_size("lat"), lax.axis_size("lon")
    devices = lat_size * lon_size
    tiles, width, depth = sensitivity.shape[2:]
    blocks = block_offsets.shape[-1] - 1
    systems, clat, clon, _ = model_vector.shape
    columns = clat * clon
    cap = max(2 * ((tiles + devices - 1) // devices), 16 // systems)
    slots = devices * cap
    group = cap * systems
    chunk = group + 1
    cells_all = devices * columns * depth
    rows_all = devices * blocks * width + cells_all
    lanes = 128
    full, flat = model_vector.shape, (systems, columns, depth)
    lines = (systems, PATCH * clon, depth)
    here, there, plain = pltpu.VMEM, pltpu.HBM, jax.ShapeDtypeStruct
    dma = pltpu.SemaphoreType.DMA
    model, damping = far(model_vector), far(damping_vector)
    model_flat, damping_flat = far(model_vector.reshape(flat)), far(damping_vector.reshape(flat))

    asked = (devices, 1, (1 + systems) * depth)
    asking = call(
        ask_body,
        "ask",
        there(asked, F32),
        [vmem(), hbm()],
        vmem(),
        scratch=[pltpu.VMEM((4, systems, 1, 8, depth), F32), dma((4,))],
    )(far(block_ids), model)
    lists = exchange(asking)

    side = there((systems, 3 * clat, depth), F32)
    band = there((systems, 3, clon, depth), F32)
    north_msg, south_msg, east_msg, west_msg, meta = call(
        functools.partial(flanks_body, columns.bit_length() - 1, blocks),
        "flanks",
        (band, band, side, side, there((8, lanes), I32)),
        [hbm()] + [vmem()] * 3 + [hbm(), hbm()],
        (vmem(),) * 5,
        scratch=[pltpu.VMEM((4, systems, clat, 8, depth), F32), dma((8,))],
        flops=1,
        moved=128 * systems * clat * depth,
    )(far(asking), far(block_ids), block_offsets, ray_counts, model, damping)

    served, wanted, corner, diagonal = call(
        functools.partial(serve_body, cap, clat, clon),
        "serve",
        (
            there((slots * systems, depth), BF16),
            plain((devices, lanes), F32),
            plain((1,), I32),
            plain((4 * systems, depth), F32),
        ),
        [vmem(), hbm()],
        (vmem(), vmem(), smem(), vmem()),
        scratch=[pltpu.VMEM(lines, F32), pltpu.VMEM((slots * systems, depth), F32), dma((systems,))],
    )(lists, model_flat)
    fetched = exchange(served.reshape(devices, group, depth)).reshape(slots * systems, depth)

    north = shifted(south_msg, "lat", 1)
    south = shifted(north_msg, "lat", -1)
    west = shifted(east_msg, "lon", 1)
    east = shifted(west_msg, "lon", -1)

    edge, flank = there((systems, clon, depth), F32), there((systems, clat, depth), F32)
    bar, *border, sums = call(
        functools.partial(damp_body, clat, clon),
        "damp",
        (there(flat, F32), edge, edge, flank, flank, there((1, lanes), F32)),
        [vmem()] * 2 + [hbm()] * 2 + [vmem()] * 4,
        (hbm(),) + (vmem(),) * 5,
        scratch=[pltpu.VMEM(flat, F32)] * 3 + [pltpu.SMEM((systems,), F32), dma((systems, 3))],
        flops=20 * systems * columns * depth,
        moved=12 * systems * columns * depth,
    )(far(recurrence), diagonal, model_flat, damping_flat, north, south, west, east)

    ray_bar, terms = call(
        functools.partial(rays_body, cap, blocks),
        "rays",
        (there(ray_vector.shape, F32), there((devices * chunk, 1, depth), F32)),
        [smem(), vmem(), hbm()] + [vmem()] * 3,
        (vmem(), vmem()),
        scratch=[
            pltpu.VMEM(sensitivity.shape, BF16),
            pltpu.VMEM((cap + 1, group, depth), BF16),
            pltpu.VMEM((blocks + 1, 16, width), BF16),
            dma((PARTS,)),
        ],
        flops=4 * tiles * width * depth * 16,
        moved=2 * tiles * width * depth,
    )(meta, far(recurrence), far(sensitivity), fetched, far(ray_vector), far(sums))
    arrived = exchange(terms.reshape(devices, 1, chunk * depth)).reshape(devices * chunk, depth)

    padded = -(-devices * chunk // lanes) * lanes
    height = systems * PATCH * clon
    patch = (height, depth)
    image, sums, patched, model_patch, chosen = call(
        functools.partial(image_body, chunk, clat, clon),
        "image",
        (
            there(flat, F32),
            plain((1, lanes), F32),
            plain(patch, F32),
            plain(patch, F32),
            plain((height, padded), BF16),
        ),
        [smem(), vmem(), hbm()] + [vmem()] * 4 + [hbm(), vmem()],
        (hbm(),) + (vmem(),) * 4,
        scratch=[pltpu.VMEM(flat, F32)] * 3 + [dma((systems, 3))],
        flops=20 * systems * columns * depth,
        moved=12 * systems * columns * depth,
    )(corner, wanted, far(bar), *(far(x) for x in border), model_flat, far(sums))

    added, residual, parts = call(
        functools.partial(combine_body, chunk, systems),
        "combine",
        (plain(patch, F32), plain((1, lanes), F32), there((devices, lanes), F32)),
        [vmem()] * 5,
        (vmem(),) * 3,
        scratch=[pltpu.VMEM((padded, 3 * depth), BF16)],
    )(arrived, chosen, patched, model_patch, sums)
    every = exchange(parts.reshape(devices, 1, lanes)).reshape(devices, lanes)

    search_flat = far(search.reshape(flat))
    ray_out, damp_out, solution_out = call(
        functools.partial(early_body, float(rows_all)),
        "early",
        (there(ray_vector.shape, F32), there(flat, F32), there(flat, F32)),
        [vmem()] * 3 + [hbm()] * 3,
        (vmem(), hbm(), hbm()),
        scratch=[pltpu.VMEM(flat, F32)] * 5
        + [pltpu.SMEM((2, systems), F32), dma((systems, PIECES, 3)), dma((systems, PIECES, 2))],
        mib=32,
        flops=4 * systems * columns * depth,
        moved=20 * systems * columns * depth,
    )(residual, far(recurrence), far(ray_bar), far(bar), far(solution.reshape(flat)), search_flat)
    model_out, search_out, rec_out = call(
        functools.partial(finish_body, float(rows_all), float(cells_all), clon),
        "finish",
        (there(flat, F32), there(flat, F32), there(recurrence.shape, F32)),
        [smem()] + [vmem()] * 4 + [hbm()] * 3,
        (hbm(), hbm(), vmem()),
        scratch=[pltpu.VMEM(flat, F32)] * 5
        + [pltpu.SMEM((3, systems), F32), dma((systems, PIECES, 3)), dma((systems, PIECES, 2))],
        mib=32,
        flops=6 * systems * columns * depth,
        moved=20 * systems * columns * depth,
    )(corner, residual, every, far(recurrence), added, far(image), model_flat, search_flat)
    fields = (x.reshape(full) for x in (damp_out, model_out, solution_out, search_out))
    return (ray_out, *fields, rec_out)


def solution(mesh):
    fields = P(None, "lat", "lon", None)
    return jax.shard_map(
        per_device,
        mesh=mesh,
        in_specs=(
            P("lat", "lon", None, None, None),
            P("lat", "lon", None),
            P("lat", "lon", None),
            P("lat", "lon"),
            fields,
            fields,
            fields,
            fields,
            fields,
            P(),
        ),
        out_specs=(fields, fields, fields, fields, fields, P()),
        check_vma=False,
    )
```

time: 88.3 us -> 90.7 us (1.027)
  blocking collectives: 26.3 us -> 14.9 us
  Pallas kernels: 33.9 us -> 40.9 us
  waiting for transfers between devices: 5.94 us -> 10 us
  starting transfers between devices: 20.1 us -> 22.7 us
    all_to_all x2 -> x1, blocking collectives: 26.3 us -> 14.9 us  [exchange(): return lax.all_to_all(x, AXES, split_axis=0, concat_axis=0, tiled=True)]
    pallas_call x3 -> x5, Pallas kernels: 15.9 us -> 26.3 us  [the longest x1 6.59 us: per_device(): call(functools.partial(damp_body, clat, clon), 'damp', (there(flat, F32),...]
    all_to_all x2 -> x3, waiting for transfers between devices: 1.55 us -> 5.62 us  [exchange(): return lax.all_to_all(x, AXES, split_axis=0, concat_axis=0, tiled=True)]
    pallas_call x1, Pallas kernels: 9.63 us -> 6.81 us  [per_device(): call(functools.partial(finish_body, float(rows_all), float(cells_all), cl...]
    all_to_all x2 -> x3, starting transfers between devices: 12.2 us -> 14.7 us  [exchange(): return lax.all_to_all(x, AXES, split_axis=0, concat_axis=0, tiled=True)]
  transfers between devices with their start and end apart: 6 -> 7, of which waited for: 3 -> 4; matrix products, arithmetic and copies ran while one was open for 0% -> 0% of each run, Pallas kernels for 15% -> 25%
where the time goes in v7:
time: 90.7 us; the launch traced here: 89.9 us
  Pallas kernels  40.9 us (45%)
  starting transfers between devices  22.7 us (25%)
  blocking collectives  14.9 us (16%)
  waiting for transfers between devices  10 us (11%)
  between operations  1.43 us (2%)
    all_to_all x1, blocking collectives, exchange(): return lax.all_to_all(x, AXES, split_axis=0, concat_axis=0, tiled=True)  14.9 us
    all_to_all x3, starting transfers between devices, exchange(): return lax.all_to_all(x, AXES, split_axis=0, concat_axis=0, tiled=True)  14.7 us
    ppermute x4, starting transfers between devices, shifted(): return lax.ppermute(x, axis, pairs)  7.97 us
    pallas_call x1, Pallas kernels, per_device(): call(functools.partial(finish_body, float(rows_all), float(cells_all), cl...  6.81 us
    pallas_call x1, Pallas kernels, per_device(): call(functools.partial(damp_body, clat, clon), 'damp', (there(flat, F32),...  6.59 us
    pallas_call x1, Pallas kernels, per_device(): call(functools.partial(image_body, chunk, clat, clon), 'image', (there(fl...  6.35 us
    pallas_call x1, Pallas kernels, per_device(): call(functools.partial(early_body, float(rows_all)), 'early', (there(ray_...  6.19 us
    pallas_call x1, Pallas kernels, per_device(): call(functools.partial(rays_body, cap, blocks), 'rays', (there(ray_vector...  5.87 us
  transfers between devices with their start and end apart: 7, of which 4 were waited for; matrix products, arithmetic and copies ran while one was open for 0% of the time, Pallas kernels for 25%

profile of v7, /device:TPU:0, one launch (start us, length us, event | category | flops | bytes accessed | tf_op | source)
XLA Modules:
  0.0 89.9 jit_solution(14044208212502669599)
XLA Ops:
  0.6 0.0 copy-start.1
  0.6 2.1 %ask.1.after_ref = f32[32,1,640]{2,1,0:T(1,128)} custom-call(s32[1,1,60]{2,1,0:T(1,128)} %ids_ref.3, f32[4,32,32,128]{3,2,1,0:T(8,128)} %model_in.3), custom_call_target="tpu_custom_call" | custom-call | tf_op jit(solution)/shard_map/ask/pallas_call | solution.py:701
  2.8 14.9 %all_to_all.20.lists_ref = f32[32,1,640]{2,1,0:T(1,128)S(1)} all-to-all(f32[32,1,640]{2,1,0:T(1,128)} %ask.1.after_ref), channel_id=1, replica_groups=mesh['lat'=4,'lon'=8] {'lat','lon'}, dimensions={0} | all-to-all | bytes 163840 | tf_op jit(solution)/shard_map/all_to_all | solution.py:665
  17.7 2.4 %serve.1 = (bf16[512,128]{1,0:T(8,128)(2,1)}, f32[32,128]{1,0:T(8,128)S(1)}, s32[1]{0:T(128)}, f32[16,128]{1,0:T(8,128)S(1)}) custom-call(f32[32,1,640]{2,1,0:T(1,128)S(1)} %all_to_all.20.lists_ref, f32[4,1024,128]{2,1,0:T(8,128)} %bitcast.19), custom_call_target="tpu_custom_call" | custom-call | tf_op jit(solution)/shard_map/serve/pallas_call | solution.py:724
  20.1 2.6 %all-to-all-start.1 = ((bf16[32,16,128]{2,1,0:T(8,128)(2,1)}), bf16[32,16,128]{2,1,0:T(8,128)(2,1)S(1)}, u32[]{:S(2)}, u32[]{:S(2)}) async-start(bf16[32,16,128]{2,1,0:T(8,128)(2,1)} %bitcast.28), calls=%async_computation.1 | async-start | bytes 262144 | tf_op jit(solution)/shard_map/all_to_all | solution.py:665
  23.3 0.0 copy-done.1
  23.4 3.2 %flanks.1 = (f32[4,3,32,128]{3,2,1,0:T(8,128)}, f32[4,3,32,128]{3,2,1,0:T(8,128)}, f32[4,96,128]{2,1,0:T(8,128)}, f32[4,96,128]{2,1,0:T(8,128)}, s32[8,128]{1,0:T(8,128)}) custom-call(f32[32,1,640]{2,1,0:T(1,128)} %ask.1.after_ref, s32[1,1,60]{2,1,0:T(1,128)} %ids_ref.3, s32[1,1,4]{2,1,0:T(1,128)S(1)} %copy-done.1, s32[1,1]{1,0:T(1,128)S(6)} %copy.18.count_ref, ...), custom_call_target="tpu_custom_call" | custom-call | flops 1 | bytes 2097152 | tf_op jit(solution)/shard_map/flanks/pallas_call | solution.py:713
  26.6 3.6 %collective-permute-start = (f32[4,3,32,128]{3,2,1,0:T(8,128)}, f32[4,3,32,128]{3,2,1,0:T(8,128)S(1)}, u32[]{:S(2)}, u32[]{:S(2)}) collective-permute-start(f32[4,3,32,128]{3,2,1,0:T(8,128)} %get-tuple-element.40), channel_id=1, source_target_pairs={{0,8},{8,16},{16,24},{1,9},{9,17},{17,25},{2,10},{10,18},{18,26},{... | collective-permute-start | bytes 589832 | tf_op jit(solution)/shard_map/ppermute | solution.py:661
  30.2 1.3 %collective-permute-start.1 = (f32[4,3,32,128]{3,2,1,0:T(8,128)}, f32[4,3,32,128]{3,2,1,0:T(8,128)S(1)}, u32[]{:S(2)}, u32[]{:S(2)}) collective-permute-start(f32[4,3,32,128]{3,2,1,0:T(8,128)} %get-tuple-element.41), channel_id=1, source_target_pairs={{8,0},{16,8},{24,16},{9,1},{17,9},{25,17},{10,2},{18,10},{26,18},{... | collective-permute-start | bytes 589832 | tf_op jit(solution)/shard_map/ppermute | solution.py:661
  31.5 1.8 %collective-permute-start.2 = (f32[4,96,128]{2,1,0:T(8,128)}, f32[4,96,128]{2,1,0:T(8,128)S(1)}, u32[]{:S(2)}, u32[]{:S(2)}) collective-permute-start(f32[4,96,128]{2,1,0:T(8,128)} %get-tuple-element.42), channel_id=1, source_target_pairs={{0,1},{1,2},{2,3},{3,4},{4,5},{5,6},{6,7},{8,9},{9,10},{10,11},{11... | collective-permute-start | bytes 589832 | tf_op jit(solution)/shard_map/ppermute | solution.py:661
  33.3 1.3 %collective-permute-start.3 = (f32[4,96,128]{2,1,0:T(8,128)}, f32[4,96,128]{2,1,0:T(8,128)S(1)}, u32[]{:S(2)}, u32[]{:S(2)}) collective-permute-start(f32[4,96,128]{2,1,0:T(8,128)} %get-tuple-element.43), channel_id=1, source_target_pairs={{1,0},{2,1},{3,2},{4,3},{5,4},{6,5},{7,6},{9,8},{10,9},{11,10},{12... | collective-permute-start | bytes 589832 | tf_op jit(solution)/shard_map/ppermute | solution.py:661
  34.6 0.4 collective-permute-done.north_ref
  35.0 4.0 %collective-permute-done.1.south_ref = f32[4,3,32,128]{3,2,1,0:T(8,128)S(1)} collective-permute-done((f32[4,3,32,128]{3,2,1,0:T(8,128)}, f32[4,3,32,128]{3,2,1,0:T(8,128)S(1)}, u32[]{:S(2)}, u32[]{:S(2)}) %collective-permute-start.1) | collective-permute-done | bytes 196640 | tf_op jit(solution)/shard_map/ppermute | solution.py:661
  39.0 0.0 collective-permute-done.2.west_ref
  39.0 0.0 collective-permute-done.3.east_ref
  39.0 0.0 copy-start
  39.0 6.6 %damp.1 = (f32[4,1024,128]{2,1,0:T(8,128)}, f32[4,32,128]{2,1,0:T(8,128)}, f32[4,32,128]{2,1,0:T(8,128)}, f32[4,32,128]{2,1,0:T(8,128)}, f32[4,32,128]{2,1,0:T(8,128)}, /*index=5*/f32[1,128]{1,0:T(1,128)}) custom-call(f32[3,4]{1,0:T(4,128)} %rec_ref.7, f32[16,128]{1,0:T(8,128)S(1)} %get-tuple-element.39.diagonal_ref, f32[4,1024,128]{2,1,0:T(8,128)} %bitcast.20, ...), custom_call_target="tpu_custom_call" | custom-call | flops 10485760 | bytes 6291456 | tf_op jit(solution)/shard_map/damp/pallas_call | solution.py:745
  45.6 0.0 all-to-all-done.1
  45.6 0.0 copy-done
  45.6 5.9 %rays.1 = (f32[4,1,1,768]{3,2,1,0:T(1,128)}, f32[544,1,128]{2,1,0:T(1,128)}) custom-call(s32[8,128]{1,0:T(8,128)S(1)} %copy-done, f32[3,4]{1,0:T(4,128)} %rec_ref.7, bf16[1,1,60,256,128]{4,3,2,1,0:T(8,128)(2,1)} %tiles_in.1, bf16[512,128]{1,0:T(8,128)(2,1)S(1)} %bitcast.17, f32[4,1,1,768]{3,2,1,0:T(1,128)} %old_ref.1, f32[1,128]{1,0:T(1,128)} %get-tuple-element.44.sums_ref), custom_call_target="tpu_custom_call" | custom-call | flops 125829120 | bytes 3932160 | tf_op jit(solution)/shard_map/rays/pallas_call | solution.py:756
  51.5 9.6 %all-to-all-start.2 = ((f32[32,1,2176]{2,1,0:T(1,128)}), f32[32,1,2176]{2,1,0:T(1,128)S(1)}, u32[]{:S(2)}, u32[]{:S(2)}) async-start(f32[32,1,2176]{2,1,0:T(1,128)} %bitcast.27), calls=%async_computation.2 | async-start | bytes 557056 | tf_op jit(solution)/shard_map/all_to_all | solution.py:665
  61.1 6.4 %image.1 = (f32[4,1024,128]{2,1,0:T(8,128)}, f32[1,128]{1,0:T(1,128)S(1)}, f32[512,128]{1,0:T(8,128)S(1)}, f32[512,128]{1,0:T(8,128)S(1)}, bf16[512,640]{1,0:T(8,128)(2,1)S(1)}) custom-call(s32[1]{0:T(128)} %get-tuple-element.46.corner_ref, f32[32,128]{1,0:T(8,128)S(1)} %get-tuple-element.47.wanted_ref, f32[4,1024,128]{2,1,0:T(8,128)} %get-tuple-element.48.bar_in, ...), custom_call_target="tpu_custom_call" | custom-call | flops 10485760 | bytes 6291456 | tf_op jit(solution)/shard_map/image/pallas_call | solution.py:776
  67.4 4.7 %all-to-all-done.2 = f32[32,1,2176]{2,1,0:T(1,128)S(1)} async-done(((f32[32,1,2176]{2,1,0:T(1,128)}), f32[32,1,2176]{2,1,0:T(1,128)S(1)}, u32[]{:S(2)}, u32[]{:S(2)}) %all-to-all-start.2) | async-done | bytes 278560 | tf_op jit(solution)/shard_map/all_to_all | solution.py:665
  72.2 1.3 %combine.1 = (f32[512,128]{1,0:T(8,128)S(1)}, f32[1,128]{1,0:T(1,128)S(1)}, f32[32,128]{1,0:T(8,128)}) custom-call(f32[544,128]{1,0:T(8,128)S(1)} %bitcast.16, bf16[512,640]{1,0:T(8,128)(2,1)S(1)} %get-tuple-element.53.chosen_ref, f32[512,128]{1,0:T(8,128)S(1)} %get-tuple-element.54.patch_ref, f32[512,128]{1,0:T(8,128)S(1)} %get-tuple-element.55.model_patch_ref, ...), custom_call_target="tpu_custom_call" | custom-call | tf_op jit(solution)/shard_map/combine/pallas_call | solution.py:793
  73.5 2.5 %all-to-all-start.3 = ((f32[32,1,128]{2,1,0:T(1,128)}), f32[32,1,128]{2,1,0:T(1,128)S(1)}, u32[]{:S(2)}, u32[]{:S(2)}) async-start(f32[32,1,128]{2,1,0:T(1,128)} %bitcast.29), calls=%async_computation.3 | async-start | bytes 32768 | tf_op jit(solution)/shard_map/all_to_all | solution.py:665
  76.0 6.2 %early.1 = (f32[4,1,1,768]{3,2,1,0:T(1,128)}, f32[4,1024,128]{2,1,0:T(8,128)}, f32[4,1024,128]{2,1,0:T(8,128)}) custom-call(f32[1,128]{1,0:T(1,128)S(1)} %get-tuple-element.57.residual_ref, f32[3,4]{1,0:T(4,128)} %rec_ref.7, f32[4,1,1,768]{3,2,1,0:T(1,128)} %get-tuple-element.58.ray_ref, f32[4,1024,128]{2,1,0:T(8,128)} %get-tuple-element.48.bar_in, ...), custom_call_target="tpu_custom_call" | custom-call | flops 2097152 | bytes 10485760 | tf_op jit(solution)/shard_map/early/pallas_call | solution.py:804
  82.2 0.9 all-to-all-done.3
  83.1 6.8 %finish.1 = (f32[4,1024,128]{2,1,0:T(8,128)}, f32[4,1024,128]{2,1,0:T(8,128)}, f32[3,4]{1,0:T(4,128)}) custom-call(s32[1]{0:T(128)} %get-tuple-element.46.corner_ref, f32[1,128]{1,0:T(1,128)S(1)} %get-tuple-element.57.residual_ref, f32[32,128]{1,0:T(8,128)S(1)} %bitcast.18, f32[3,4]{1,0:T(4,128)} %rec_ref.7, f32[512,128]{1,0:T(8,128)S(1)} %get-tuple-element.62.added_ref, ...), custom_call_target="tpu_custom_call" | custom-call | flops 3145728 | bytes 10485760 | tf_op jit(solution)/shard_map/finish/pallas_call | solution.py:816
Async XLA Ops:
  0.6 22.7 %copy-start.1 = (s32[1,1,4]{2,1,0:T(1,128)S(1)}, s32[1,1,4]{2,1,0:T(1,128)}, u32[]{:S(2)}) copy-start(s32[1,1,4]{2,1,0:T(1,128)} %off_ref.1) | copy-start | bytes 52
  20.1 25.5 %all-to-all-start.1 = ((bf16[32,16,128]{2,1,0:T(8,128)(2,1)}), bf16[32,16,128]{2,1,0:T(8,128)(2,1)S(1)}, u32[]{:S(2)}, u32[]{:S(2)}) async-start(bf16[32,16,128]{2,1,0:T(8,128)(2,1)} %bitcast.28), calls=%async_computation.1 | async-start | bytes 262144 | tf_op jit(solution)/shard_map/all_to_all | solution.py:665
  26.6 8.4 %collective-permute-start = (f32[4,3,32,128]{3,2,1,0:T(8,128)}, f32[4,3,32,128]{3,2,1,0:T(8,128)S(1)}, u32[]{:S(2)}, u32[]{:S(2)}) collective-permute-start(f32[4,3,32,128]{3,2,1,0:T(8,128)} %get-tuple-element.40), channel_id=1, source_target_pairs={{0,8},{8,16},{16,24},{1,9},{9,17},{17,25},{2,10},{10,18},{18,26},{... | collective-permute-start | bytes 589832 | tf_op jit(solution)/shard_map/ppermute | solution.py:661
  30.2 8.8 %collective-permute-start.1 = (f32[4,3,32,128]{3,2,1,0:T(8,128)}, f32[4,3,32,128]{3,2,1,0:T(8,128)S(1)}, u32[]{:S(2)}, u32[]{:S(2)}) collective-permute-start(f32[4,3,32,128]{3,2,1,0:T(8,128)} %get-tuple-element.41), channel_id=1, source_target_pairs={{8,0},{16,8},{24,16},{9,1},{17,9},{25,17},{10,2},{18,10},{26,18},{... | collective-permute-start | bytes 589832 | tf_op jit(solution)/shard_map/ppermute | solution.py:661
  31.5 7.5 %collective-permute-start.2 = (f32[4,96,128]{2,1,0:T(8,128)}, f32[4,96,128]{2,1,0:T(8,128)S(1)}, u32[]{:S(2)}, u32[]{:S(2)}) collective-permute-start(f32[4,96,128]{2,1,0:T(8,128)} %get-tuple-element.42), channel_id=1, source_target_pairs={{0,1},{1,2},{2,3},{3,4},{4,5},{5,6},{6,7},{8,9},{9,10},{10,11},{11... | collective-permute-start | bytes 589832 | tf_op jit(solution)/shard_map/ppermute | solution.py:661
  33.3 5.7 %collective-permute-start.3 = (f32[4,96,128]{2,1,0:T(8,128)}, f32[4,96,128]{2,1,0:T(8,128)S(1)}, u32[]{:S(2)}, u32[]{:S(2)}) collective-permute-start(f32[4,96,128]{2,1,0:T(8,128)} %get-tuple-element.43), channel_id=1, source_target_pairs={{1,0},{2,1},{3,2},{4,3},{5,4},{6,5},{7,6},{9,8},{10,9},{11,10},{12... | collective-permute-start | bytes 589832 | tf_op jit(solution)/shard_map/ppermute | solution.py:661
  39.0 6.6 %copy-start = (s32[8,128]{1,0:T(8,128)S(1)}, s32[8,128]{1,0:T(8,128)}, u32[]{:S(2)}) copy-start(s32[8,128]{1,0:T(8,128)} %get-tuple-element.37.meta_ref) | copy-start | bytes 12292
  51.5 20.7 %all-to-all-start.2 = ((f32[32,1,2176]{2,1,0:T(1,128)}), f32[32,1,2176]{2,1,0:T(1,128)S(1)}, u32[]{:S(2)}, u32[]{:S(2)}) async-start(f32[32,1,2176]{2,1,0:T(1,128)} %bitcast.27), calls=%async_computation.2 | async-start | bytes 557056 | tf_op jit(solution)/shard_map/all_to_all | solution.py:665
  73.5 9.6 %all-to-all-start.3 = ((f32[32,1,128]{2,1,0:T(1,128)}), f32[32,1,128]{2,1,0:T(1,128)S(1)}, u32[]{:S(2)}, u32[]{:S(2)}) async-start(f32[32,1,128]{2,1,0:T(1,128)} %bitcast.29), calls=%async_computation.3 | async-start | bytes 32768 | tf_op jit(solution)/shard_map/all_to_all | solution.py:665

commit v8 on v7

--- a/solution.py
+++ b/solution.py
@@ -89,7 +89,7 @@
     return jnp.sum(jnp.where(pick, spread, 0.0), axis=1, keepdims=True)
 
 
-def serve_body(cap, clat, clon, lists_ref, model_in, served_ref, wanted_ref, corner_ref, diagonal_ref, patch, mixed, sems):
+def serve_body(cap, clat, clon, lists_ref, model_in, north, south, west, east, served_ref, wanted_ref, corner_ref, diagonal_ref, patch, mixed, sems):
     systems, width, depth = patch.shape
     devices = lists_ref.shape[0]
     lanes = 128
@@ -525,7 +525,8 @@
     rows = columns // PIECES
     ins = ((bar_in, bar_ref), (solution_in, solution_ref), (search_in, search_ref))
     outs = ((damp_s, damp_out), (solution_s, solution_out))
-    start_all(ins, in_sems, systems, rows)
+    for n in range(AHEAD):
+        start_one(ins, in_sems, n, systems, rows)
     rho_bar, phi_bar = rec_ref[1:2], rec_ref[2:3]
     beta = first_norm(residual_ref, systems, rows_all)
     rho = jnp.sqrt(rho_bar * rho_bar + beta * beta)
@@ -539,6 +540,7 @@
     def piece(n, _):
         r, p = n // PIECES, n % PIECES
         at = pl.ds(pl.multiple_of(p * rows, rows), rows)
+        start_one(ins, in_sems, n + AHEAD, systems, rows)
         for copy in pieces(ins, in_sems, r, p, rows):
             copy.wait()
         damp_s[r, at, :] = bar_ref[r, at, :] * coef[0, r]
@@ -579,7 +581,8 @@
     rows = columns // PIECES
     ins = ((image_in, image_ref), (model_in, model_ref), (search_in, search_ref))
     outs = ((model_s, model_out), (search_s, search_out))
-    start_all(ins, in_sems, systems, rows)
+    for n in range(AHEAD):
+        start_one(ins, in_sems, n, systems, rows)
     total = jnp.sum(parts_ref[...], axis=0, keepdims=True)
     image_sq, cross, model_sq = (total[:, q * systems : (q + 1) * systems] for q in range(1, 4))
     rho_bar, phi_bar = rec_ref[1:2], rec_ref[2:3]
@@ -599,6 +602,7 @@
     def piece(n, _):
         r, p = n // PIECES, n % PIECES
         at = pl.ds(pl.multiple_of(p * rows, rows), rows)
+        start_one(ins, in_sems, n + AHEAD, systems, rows)
         for copy in pieces(ins, in_sems, r, p, rows):
             copy.wait()
         new = image_ref[r, at, :] * coef[0, r] - model_ref[r, at, :] * coef[1, r]
@@ -624,6 +628,7 @@
 
 
 PIECES = 2
+AHEAD = 4
 
 
 def pieces(pairs, sems, r, p, rows):
@@ -631,13 +636,11 @@
     return [pltpu.make_async_copy(a.at[r, at], b.at[r, at], sems.at[r, p, k]) for k, (a, b) in enumerate(pairs)]
 
 
-def start_all(pairs, sems, systems, rows):
-    def one(n, _):
+def start_one(pairs, sems, n, systems, rows):
+    @pl.when(n < systems * PIECES)
+    def _():
         for copy in pieces(pairs, sems, n // PIECES, n % PIECES, rows):
             copy.start()
-        return 0
-
-    lax.fori_loop(0, systems * PIECES, one, 0)
 
 
 def wait_all(pairs, sems, systems, rows):
@@ -721,6 +724,11 @@
         moved=128 * systems * clat * depth,
     )(far(asking), far(block_ids), block_offsets, ray_counts, model, damping)
 
+    north = shifted(south_msg, "lat", 1)
+    south = shifted(north_msg, "lat", -1)
+    west = shifted(east_msg, "lon", 1)
+    east = shifted(west_msg, "lon", -1)
+
     served, wanted, corner, diagonal = call(
         functools.partial(serve_body, cap, clat, clon),
         "serve",
@@ -730,16 +738,11 @@
             plain((1,), I32),
             plain((4 * systems, depth), F32),
         ),
-        [vmem(), hbm()],
+        [vmem(), hbm()] + [pl.BlockSpec(memory_space=pl.ANY)] * 4,
         (vmem(), vmem(), smem(), vmem()),
         scratch=[pltpu.VMEM(lines, F32), pltpu.VMEM((slots * systems, depth), F32), dma((systems,))],
-    )(lists, model_flat)
+    )(lists, model_flat, north, south, west, east)
     fetched = exchange(served.reshape(devices, group, depth)).reshape(slots * systems, depth)
-
-    north = shifted(south_msg, "lat", 1)
-    south = shifted(north_msg, "lat", -1)
-    west = shifted(east_msg, "lon", 1)
-    east = shifted(west_msg, "lon", -1)
 
     edge, flank = there((systems, clon, depth), F32), there((systems, clat, depth), F32)
     bar, *border, sums = call(

time: 90.7 us -> 86.1 us (0.949)
  starting transfers between devices: 22.7 us -> 18.4 us
  waiting for transfers between devices: 10 us -> 7.2 us
  blocking collectives: 14.9 us -> 17.1 us
    all_to_all x3, starting transfers between devices: 14.7 us -> 9.39 us  [exchange(): return lax.all_to_all(x, AXES, split_axis=0, concat_axis=0, tiled=True)]
    ppermute x4, waiting for transfers between devices: 4.39 us -> 0.01 us  [shifted(): return lax.ppermute(x, axis, pairs)]
    all_to_all x1, blocking collectives: 14.9 us -> 17.1 us  [exchange(): return lax.all_to_all(x, AXES, split_axis=0, concat_axis=0, tiled=True)]
    all_to_all x3, waiting for transfers between devices: 5.62 us -> 7.19 us  [exchange(): return lax.all_to_all(x, AXES, split_axis=0, concat_axis=0, tiled=True)]
    ppermute x4, starting transfers between devices: 7.97 us -> 8.99 us  [shifted(): return lax.ppermute(x, axis, pairs)]
  transfers between devices with their start and end apart: 7 -> 7, of which waited for: 4 -> 3; matrix products, arithmetic and copies ran while one was open for 0% -> 0% of each run, Pallas kernels for 25% -> 23%
where the time goes in v8:
time: 86.1 us; the launch traced here: 85.2 us
  Pallas kernels  41.1 us (48%)
  starting transfers between devices  18.4 us (21%)
  blocking collectives  17.1 us (20%)
  waiting for transfers between devices  7.2 us (8%)
  between operations  1.46 us (2%)
    all_to_all x1, blocking collectives, exchange(): return lax.all_to_all(x, AXES, split_axis=0, concat_axis=0, tiled=True)  17.1 us
    all_to_all x3, starting transfers between devices, exchange(): return lax.all_to_all(x, AXES, split_axis=0, concat_axis=0, tiled=True)  9.39 us
    ppermute x4, starting transfers between devices, shifted(): return lax.ppermute(x, axis, pairs)  8.99 us
    all_to_all x3, waiting for transfers between devices, exchange(): return lax.all_to_all(x, AXES, split_axis=0, concat_axis=0, tiled=True)  7.19 us
    pallas_call x1, Pallas kernels, per_device(): call(functools.partial(finish_body, float(rows_all), float(cells_all), cl...  6.91 us
    pallas_call x1, Pallas kernels, per_device(): call(functools.partial(damp_body, clat, clon), 'damp', (there(flat, F32),...  6.59 us
    pallas_call x1, Pallas kernels, per_device(): call(functools.partial(early_body, float(rows_all)), 'early', (there(ray_...  6.29 us
    pallas_call x1, Pallas kernels, per_device(): call(functools.partial(image_body, chunk, clat, clon), 'image', (there(fl...  6.29 us
  transfers between devices with their start and end apart: 7, of which 3 were waited for; matrix products, arithmetic and copies ran while one was open for 0% of the time, Pallas kernels for 23%

profile of v8, /device:TPU:0, one launch (start us, length us, event | category | flops | bytes accessed | tf_op | source)
XLA Modules:
  0.0 85.2 jit_solution(7469664403667118065)
XLA Ops:
  0.6 0.0 copy-start.1
  1.3 2.1 %ask.1.after_ref = f32[32,1,640]{2,1,0:T(1,128)} custom-call(s32[1,1,60]{2,1,0:T(1,128)} %ids_ref.3, f32[4,32,32,128]{3,2,1,0:T(8,128)} %model_in.3), custom_call_target="tpu_custom_call" | custom-call | tf_op jit(solution)/shard_map/ask/pallas_call | solution.py:704
  3.4 0.0 copy-done.1
  3.5 0.0 copy-start.2
  3.5 3.3 %flanks.1 = (f32[4,3,32,128]{3,2,1,0:T(8,128)}, f32[4,3,32,128]{3,2,1,0:T(8,128)}, f32[4,96,128]{2,1,0:T(8,128)}, f32[4,96,128]{2,1,0:T(8,128)}, s32[8,128]{1,0:T(8,128)}) custom-call(f32[32,1,640]{2,1,0:T(1,128)} %ask.1.after_ref, s32[1,1,60]{2,1,0:T(1,128)} %ids_ref.3, s32[1,1,4]{2,1,0:T(1,128)S(1)} %copy-done.1, s32[1,1]{1,0:T(1,128)S(6)} %copy.18.count_ref, ...), custom_call_target="tpu_custom_call" | custom-call | flops 1 | bytes 2097152 | tf_op jit(solution)/shard_map/flanks/pallas_call | solution.py:716
  6.7 4.9 %collective-permute-start = (f32[4,3,32,128]{3,2,1,0:T(8,128)}, f32[4,3,32,128]{3,2,1,0:T(8,128)S(1)}, u32[]{:S(2)}, u32[]{:S(2)}) collective-permute-start(f32[4,3,32,128]{3,2,1,0:T(8,128)} %get-tuple-element.38), channel_id=1, source_target_pairs={{0,8},{8,16},{16,24},{1,9},{9,17},{17,25},{2,10},{10,18},{18,26},{... | collective-permute-start | bytes 589832 | tf_op jit(solution)/shard_map/ppermute | solution.py:664
  11.7 1.3 %collective-permute-start.1 = (f32[4,3,32,128]{3,2,1,0:T(8,128)}, f32[4,3,32,128]{3,2,1,0:T(8,128)S(1)}, u32[]{:S(2)}, u32[]{:S(2)}) collective-permute-start(f32[4,3,32,128]{3,2,1,0:T(8,128)} %get-tuple-element.39), channel_id=1, source_target_pairs={{8,0},{16,8},{24,16},{9,1},{17,9},{25,17},{10,2},{18,10},{26,18},{... | collective-permute-start | bytes 589832 | tf_op jit(solution)/shard_map/ppermute | solution.py:664
  13.0 1.5 %collective-permute-start.2 = (f32[4,96,128]{2,1,0:T(8,128)}, f32[4,96,128]{2,1,0:T(8,128)S(1)}, u32[]{:S(2)}, u32[]{:S(2)}) collective-permute-start(f32[4,96,128]{2,1,0:T(8,128)} %get-tuple-element.40), channel_id=1, source_target_pairs={{0,1},{1,2},{2,3},{3,4},{4,5},{5,6},{6,7},{8,9},{9,10},{10,11},{11... | collective-permute-start | bytes 589832 | tf_op jit(solution)/shard_map/ppermute | solution.py:664
  14.5 1.3 %collective-permute-start.3 = (f32[4,96,128]{2,1,0:T(8,128)}, f32[4,96,128]{2,1,0:T(8,128)S(1)}, u32[]{:S(2)}, u32[]{:S(2)}) collective-permute-start(f32[4,96,128]{2,1,0:T(8,128)} %get-tuple-element.41), channel_id=1, source_target_pairs={{1,0},{2,1},{3,2},{4,3},{5,4},{6,5},{7,6},{9,8},{10,9},{11,10},{12... | collective-permute-start | bytes 589832 | tf_op jit(solution)/shard_map/ppermute | solution.py:664
  15.8 0.0 copy-done.2
  15.8 17.1 %all_to_all.20.lists_ref = f32[32,1,640]{2,1,0:T(1,128)S(1)} all-to-all(f32[32,1,640]{2,1,0:T(1,128)S(1)} %copy-done.2), channel_id=1, replica_groups=mesh['lat'=4,'lon'=8] {'lat','lon'}, dimensions={0} | all-to-all | bytes 163840 | tf_op jit(solution)/shard_map/all_to_all | solution.py:668
  32.9 0.0 collective-permute-done.north.north_ref
  32.9 0.0 collective-permute-done.1.south.south_ref
  32.9 0.0 collective-permute-done.2.west.west_ref
  32.9 0.0 collective-permute-done.3.east.east_ref
  32.9 2.4 %serve.1 = (bf16[512,128]{1,0:T(8,128)(2,1)}, f32[32,128]{1,0:T(8,128)S(1)}, s32[1]{0:T(128)}, f32[16,128]{1,0:T(8,128)S(1)}) custom-call(f32[32,1,640]{2,1,0:T(1,128)S(1)} %all_to_all.20.lists_ref, f32[4,1024,128]{2,1,0:T(8,128)} %bitcast.19, f32[4,3,32,128]{3,2,1,0:T(8,128)S(1)} %collective-permute-done.north.north_ref, ...), custom_call_target="tpu_custom_call" | custom-call | tf_op jit(solution)/shard_map/serve/pallas_call | solution.py:732
  35.3 2.6 %all-to-all-start.1 = ((bf16[32,16,128]{2,1,0:T(8,128)(2,1)}), bf16[32,16,128]{2,1,0:T(8,128)(2,1)S(1)}, u32[]{:S(2)}, u32[]{:S(2)}) async-start(bf16[32,16,128]{2,1,0:T(8,128)(2,1)} %bitcast.28), calls=%async_computation.1 | async-start | bytes 262144 | tf_op jit(solution)/shard_map/all_to_all | solution.py:668
  37.9 0.0 copy-start
  38.0 6.6 %damp.1 = (f32[4,1024,128]{2,1,0:T(8,128)}, f32[4,32,128]{2,1,0:T(8,128)}, f32[4,32,128]{2,1,0:T(8,128)}, f32[4,32,128]{2,1,0:T(8,128)}, f32[4,32,128]{2,1,0:T(8,128)}, /*index=5*/f32[1,128]{1,0:T(1,128)}) custom-call(f32[3,4]{1,0:T(4,128)} %rec_ref.7, f32[16,128]{1,0:T(8,128)S(1)} %get-tuple-element.43.diagonal_ref, f32[4,1024,128]{2,1,0:T(8,128)} %bitcast.20, ...), custom_call_target="tpu_custom_call" | custom-call | flops 10485760 | bytes 6291456 | tf_op jit(solution)/shard_map/damp/pallas_call | solution.py:748
  44.6 1.6 %all-to-all-done.1 = bf16[32,16,128]{2,1,0:T(8,128)(2,1)S(1)} async-done(((bf16[32,16,128]{2,1,0:T(8,128)(2,1)}), bf16[32,16,128]{2,1,0:T(8,128)(2,1)S(1)}, u32[]{:S(2)}, u32[]{:S(2)}) %all-to-all-start.1) | async-done | bytes 131104 | tf_op jit(solution)/shard_map/all_to_all | solution.py:668
  46.2 0.0 copy-done
  46.2 5.9 %rays.1 = (f32[4,1,1,768]{3,2,1,0:T(1,128)}, f32[544,1,128]{2,1,0:T(1,128)}) custom-call(s32[8,128]{1,0:T(8,128)S(1)} %copy-done, f32[3,4]{1,0:T(4,128)} %rec_ref.7, bf16[1,1,60,256,128]{4,3,2,1,0:T(8,128)(2,1)} %tiles_in.1, bf16[512,128]{1,0:T(8,128)(2,1)S(1)} %bitcast.17, f32[4,1,1,768]{3,2,1,0:T(1,128)} %old_ref.1, f32[1,128]{1,0:T(1,128)} %get-tuple-element.44.sums_ref), custom_call_target="tpu_custom_call" | custom-call | flops 125829120 | bytes 3932160 | tf_op jit(solution)/shard_map/rays/pallas_call | solution.py:759
  52.0 4.2 %all-to-all-start.2 = ((f32[32,1,2176]{2,1,0:T(1,128)}), f32[32,1,2176]{2,1,0:T(1,128)S(1)}, u32[]{:S(2)}, u32[]{:S(2)}) async-start(f32[32,1,2176]{2,1,0:T(1,128)} %bitcast.27), calls=%async_computation.2 | async-start | bytes 557056 | tf_op jit(solution)/shard_map/all_to_all | solution.py:668
  56.3 6.3 %image.1 = (f32[4,1024,128]{2,1,0:T(8,128)}, f32[1,128]{1,0:T(1,128)S(1)}, f32[512,128]{1,0:T(8,128)S(1)}, f32[512,128]{1,0:T(8,128)S(1)}, bf16[512,640]{1,0:T(8,128)(2,1)S(1)}) custom-call(s32[1]{0:T(128)} %get-tuple-element.46.corner_ref, f32[32,128]{1,0:T(8,128)S(1)} %get-tuple-element.47.wanted_ref, f32[4,1024,128]{2,1,0:T(8,128)} %get-tuple-element.48.bar_in, ...), custom_call_target="tpu_custom_call" | custom-call | flops 10485760 | bytes 6291456 | tf_op jit(solution)/shard_map/image/pallas_call | solution.py:779
  62.6 4.8 %all-to-all-done.2 = f32[32,1,2176]{2,1,0:T(1,128)S(1)} async-done(((f32[32,1,2176]{2,1,0:T(1,128)}), f32[32,1,2176]{2,1,0:T(1,128)S(1)}, u32[]{:S(2)}, u32[]{:S(2)}) %all-to-all-start.2) | async-done | bytes 278560 | tf_op jit(solution)/shard_map/all_to_all | solution.py:668
  67.4 1.3 %combine.1 = (f32[512,128]{1,0:T(8,128)S(1)}, f32[1,128]{1,0:T(1,128)S(1)}, f32[32,128]{1,0:T(8,128)}) custom-call(f32[544,128]{1,0:T(8,128)S(1)} %bitcast.16, bf16[512,640]{1,0:T(8,128)(2,1)S(1)} %get-tuple-element.53.chosen_ref, f32[512,128]{1,0:T(8,128)S(1)} %get-tuple-element.54.patch_ref, f32[512,128]{1,0:T(8,128)S(1)} %get-tuple-element.55.model_patch_ref, ...), custom_call_target="tpu_custom_call" | custom-call | tf_op jit(solution)/shard_map/combine/pallas_call | solution.py:796
  68.7 2.5 %all-to-all-start.3 = ((f32[32,1,128]{2,1,0:T(1,128)}), f32[32,1,128]{2,1,0:T(1,128)S(1)}, u32[]{:S(2)}, u32[]{:S(2)}) async-start(f32[32,1,128]{2,1,0:T(1,128)} %bitcast.29), calls=%async_computation.3 | async-start | bytes 32768 | tf_op jit(solution)/shard_map/all_to_all | solution.py:668
  71.3 6.3 %early.1 = (f32[4,1,1,768]{3,2,1,0:T(1,128)}, f32[4,1024,128]{2,1,0:T(8,128)}, f32[4,1024,128]{2,1,0:T(8,128)}) custom-call(f32[1,128]{1,0:T(1,128)S(1)} %get-tuple-element.57.residual_ref, f32[3,4]{1,0:T(4,128)} %rec_ref.7, f32[4,1,1,768]{3,2,1,0:T(1,128)} %get-tuple-element.58.ray_ref, f32[4,1024,128]{2,1,0:T(8,128)} %get-tuple-element.48.bar_in, ...), custom_call_target="tpu_custom_call" | custom-call | flops 2097152 | bytes 10485760 | tf_op jit(solution)/shard_map/early/pallas_call | solution.py:807
  77.6 0.8 all-to-all-done.3
  78.3 6.9 %finish.1 = (f32[4,1024,128]{2,1,0:T(8,128)}, f32[4,1024,128]{2,1,0:T(8,128)}, f32[3,4]{1,0:T(4,128)}) custom-call(s32[1]{0:T(128)} %get-tuple-element.46.corner_ref, f32[1,128]{1,0:T(1,128)S(1)} %get-tuple-element.57.residual_ref, f32[32,128]{1,0:T(8,128)S(1)} %bitcast.18, f32[3,4]{1,0:T(4,128)} %rec_ref.7, f32[512,128]{1,0:T(8,128)S(1)} %get-tuple-element.62.added_ref, ...), custom_call_target="tpu_custom_call" | custom-call | flops 3145728 | bytes 10485760 | tf_op jit(solution)/shard_map/finish/pallas_call | solution.py:819
Async XLA Ops:
  0.6 2.8 %copy-start.1 = (s32[1,1,4]{2,1,0:T(1,128)S(1)}, s32[1,1,4]{2,1,0:T(1,128)}, u32[]{:S(2)}) copy-start(s32[1,1,4]{2,1,0:T(1,128)} %off_ref.1) | copy-start | bytes 52
  3.5 12.3 %copy-start.2 = (f32[32,1,640]{2,1,0:T(1,128)S(1)}, f32[32,1,640]{2,1,0:T(1,128)}, u32[]{:S(2)}) copy-start(f32[32,1,640]{2,1,0:T(1,128)} %ask.1.after_ref) | copy-start | bytes 245764
  6.7 26.2 %collective-permute-start = (f32[4,3,32,128]{3,2,1,0:T(8,128)}, f32[4,3,32,128]{3,2,1,0:T(8,128)S(1)}, u32[]{:S(2)}, u32[]{:S(2)}) collective-permute-start(f32[4,3,32,128]{3,2,1,0:T(8,128)} %get-tuple-element.38), channel_id=1, source_target_pairs={{0,8},{8,16},{16,24},{1,9},{9,17},{17,25},{2,10},{10,18},{18,26},{... | collective-permute-start | bytes 589832 | tf_op jit(solution)/shard_map/ppermute | solution.py:664
  11.7 21.2 %collective-permute-start.1 = (f32[4,3,32,128]{3,2,1,0:T(8,128)}, f32[4,3,32,128]{3,2,1,0:T(8,128)S(1)}, u32[]{:S(2)}, u32[]{:S(2)}) collective-permute-start(f32[4,3,32,128]{3,2,1,0:T(8,128)} %get-tuple-element.39), channel_id=1, source_target_pairs={{8,0},{16,8},{24,16},{9,1},{17,9},{25,17},{10,2},{18,10},{26,18},{... | collective-permute-start | bytes 589832 | tf_op jit(solution)/shard_map/ppermute | solution.py:664
  13.0 19.9 %collective-permute-start.2 = (f32[4,96,128]{2,1,0:T(8,128)}, f32[4,96,128]{2,1,0:T(8,128)S(1)}, u32[]{:S(2)}, u32[]{:S(2)}) collective-permute-start(f32[4,96,128]{2,1,0:T(8,128)} %get-tuple-element.40), channel_id=1, source_target_pairs={{0,1},{1,2},{2,3},{3,4},{4,5},{5,6},{6,7},{8,9},{9,10},{10,11},{11... | collective-permute-start | bytes 589832 | tf_op jit(solution)/shard_map/ppermute | solution.py:664
  14.5 18.5 %collective-permute-start.3 = (f32[4,96,128]{2,1,0:T(8,128)}, f32[4,96,128]{2,1,0:T(8,128)S(1)}, u32[]{:S(2)}, u32[]{:S(2)}) collective-permute-start(f32[4,96,128]{2,1,0:T(8,128)} %get-tuple-element.41), channel_id=1, source_target_pairs={{1,0},{2,1},{3,2},{4,3},{5,4},{6,5},{7,6},{9,8},{10,9},{11,10},{12... | collective-permute-start | bytes 589832 | tf_op jit(solution)/shard_map/ppermute | solution.py:664
  35.3 10.8 %all-to-all-start.1 = ((bf16[32,16,128]{2,1,0:T(8,128)(2,1)}), bf16[32,16,128]{2,1,0:T(8,128)(2,1)S(1)}, u32[]{:S(2)}, u32[]{:S(2)}) async-start(bf16[32,16,128]{2,1,0:T(8,128)(2,1)} %bitcast.28), calls=%async_computation.1 | async-start | bytes 262144 | tf_op jit(solution)/shard_map/all_to_all | solution.py:668
  37.9 8.2 %copy-start = (s32[8,128]{1,0:T(8,128)S(1)}, s32[8,128]{1,0:T(8,128)}, u32[]{:S(2)}) copy-start(s32[8,128]{1,0:T(8,128)} %get-tuple-element.37.meta_ref) | copy-start | bytes 12292
  52.0 15.4 %all-to-all-start.2 = ((f32[32,1,2176]{2,1,0:T(1,128)}), f32[32,1,2176]{2,1,0:T(1,128)S(1)}, u32[]{:S(2)}, u32[]{:S(2)}) async-start(f32[32,1,2176]{2,1,0:T(1,128)} %bitcast.27), calls=%async_computation.2 | async-start | bytes 557056 | tf_op jit(solution)/shard_map/all_to_all | solution.py:668
  68.7 9.6 %all-to-all-start.3 = ((f32[32,1,128]{2,1,0:T(1,128)}), f32[32,1,128]{2,1,0:T(1,128)S(1)}, u32[]{:S(2)}, u32[]{:S(2)}) async-start(f32[32,1,128]{2,1,0:T(1,128)} %bitcast.29), calls=%async_computation.3 | async-start | bytes 32768 | tf_op jit(solution)/shard_map/all_to_all | solution.py:668

commit v9 on v8

--- a/solution.py
+++ b/solution.py
@@ -53,32 +53,6 @@
 
 
 STEP = 8
-
-
-def ask_body(ids_ref, model_in, out_ref, slabs, sems):
-    systems, clat, clon, depth = model_in.shape
-    copies = []
-    for k in range(4):
-        at = (slice(None), pl.ds((k // 2) * (clat - 1), 1), pl.ds((k % 2) * (clon - 8), 8))
-        copies.append(pltpu.make_async_copy(model_in.at[at], slabs.at[k], sems.at[k]))
-    for copy in copies:
-        copy.start()
-    tiles = ids_ref.shape[-1]
-    ids = jnp.concatenate([ids_ref[0].astype(F32), jnp.full((1, depth - tiles), -1.0, F32)], axis=1)
-    for copy in copies:
-        copy.wait()
-    corners = [
-        [slabs[k, r, 0, (k % 2) * 7 : (k % 2) * 7 + 1] for r in range(systems)] for k in range(4)
-    ]
-    lat_at, lon_at = lax.axis_index("lat"), lax.axis_index("lon")
-    width = lax.axis_size("lon")
-    for e in range(out_ref.shape[0]):
-        out_ref[e, :, 0:depth] = ids
-        south, east = e // width > lat_at, e % width > lon_at
-        for r in range(systems):
-            upper = jnp.where(east, corners[1][r], corners[0][r])
-            lower = jnp.where(east, corners[3][r], corners[2][r])
-            out_ref[e, :, (r + 1) * depth : (r + 2) * depth] = jnp.where(south, lower, upper)
 
 
 def wanted_column(wanted, cap):
@@ -137,12 +111,12 @@
 def flanks_body(
     shift,
     blocks,
-    after_ref,
     ids_ref,
     off_ref,
     count_ref,
     model_in,
     damp_in,
+    asking_ref,
     north_ref,
     south_ref,
     east_ref,
@@ -184,6 +158,20 @@
     meta_ref[...] = jnp.concatenate([owner, rank, block, count] + [owner] * 4, axis=0)
     for copy in copies:
         copy.wait()
+    listed = ids.astype(F32)
+    corners = [
+        [slabs[k % 2, r, (k // 2) * last, (k % 2) * 7 : (k % 2) * 7 + 1] for r in range(systems)]
+        for k in range(4)
+    ]
+    lat_at, lon_at = lax.axis_index("lat"), lax.axis_index("lon")
+    width = lax.axis_size("lon")
+    for e in range(asking_ref.shape[0]):
+        asking_ref[e, :, 0:depth] = listed
+        to_south, to_east = e // width > lat_at, e % width > lon_at
+        for r in range(systems):
+            upper = jnp.where(to_east, corners[1][r], corners[0][r])
+            lower = jnp.where(to_east, corners[3][r], corners[2][r])
+            asking_ref[e, :, (r + 1) * depth : (r + 2) * depth] = jnp.where(to_south, lower, upper)
     rows = slabs.reshape(4, systems, clat * 8, depth)
     for r in range(systems):
         for out, slab, near_at, beyond in ((east_ref, 1, 7, 6), (west_ref, 0, 0, 1)):
@@ -246,7 +234,9 @@
     south_ref,
     west_ref,
     east_ref,
+    tiles_in,
     bar_sent,
+    held_out,
     north_out,
     south_out,
     west_out,
@@ -257,6 +247,7 @@
     bar_out,
     alphas,
     sems,
+    hold_sem,
 ):
     systems, _, depth = model_ref.shape
 
@@ -269,9 +260,11 @@
     def outgoing(r):
         return pltpu.make_async_copy(bar_out.at[r], bar_sent.at[r], sems.at[r, 2])
 
+    holding = pltpu.make_async_copy(tiles_in.at[0, 0, pl.ds(0, HELD)], held_out, hold_sem)
     for r in range(systems):
         for copy in incoming(r):
             copy.start()
+    holding.start()
     for r in range(systems):
         alphas[r] = jnp.sum(rec_ref[0:1, r : r + 1])
     lat_at, lon_at = lax.axis_index("lat"), lax.axis_index("lon")
@@ -317,6 +310,7 @@
         return place(row, 3 * systems + r, jnp.sum(model_sq, keepdims=True))
 
     sums_out[...] = lax.fori_loop(0, systems, system, jnp.zeros((1, depth), F32))
+    holding.wait()
     for r in range(systems):
         outgoing(r).wait()
 
@@ -408,16 +402,21 @@
 
 
 def rays_body(
-    cap, blocks, meta_ref, rec_ref, tiles_in, fetched_ref, old_ref, sums_ref, bar_ref, term_ref, tiles_ref, masks, lows, sems
+    cap, blocks, meta_ref, rec_ref, tiles_in, held_ref, fetched_ref, old_ref, sums_ref, bar_ref, term_ref, rest_ref, masks, lows, sems
 ):
     tiles, width, depth = tiles_in.shape[2:]
-    part = -(-tiles // PARTS)
+    part = -(-(tiles - HELD) // PARTS)
     copies = []
     for k in range(PARTS):
-        at = (0, 0, pl.ds(k * part, min(part, tiles - k * part)))
-        copies.append(pltpu.make_async_copy(tiles_in.at[at], tiles_ref.at[at], sems.at[k]))
+        count = min(part, tiles - HELD - k * part)
+        source = tiles_in.at[0, 0, pl.ds(HELD + k * part, count)]
+        copies.append(pltpu.make_async_copy(source, rest_ref.at[pl.ds(k * part, count)], sems.at[k]))
     for copy in copies:
         copy.start()
+
+    def tile(t):
+        return held_ref[t] if t < HELD else rest_ref[t - HELD]
+
     systems = old_ref.shape[0]
     group = cap * systems
     chunk = group + 1
@@ -429,15 +428,15 @@
     lows[...] = jnp.zeros(lows.shape, BF16)
     total = jnp.zeros((blocks * group, width), F32)
     for t in range(tiles):
-        if t % part == 0:
-            copies[t // part].wait()
+        if t >= HELD and (t - HELD) % part == 0:
+            copies[(t - HELD) // part].wait()
         owner, rank, block = meta_ref[0, t], meta_ref[1, t], meta_ref[2, t]
         rows = fetched_ref[pl.ds(pl.multiple_of(owner * group, group), group), :]
         left = jnp.concatenate(
             [rows * masks[jnp.where(block == b, rank, cap)] for b in range(blocks)], axis=0
         )
         total = total + lax.dot_general(
-            left, tiles_ref[0, 0, t], (((1,), (1,)), ((), ())), preferred_element_type=F32
+            left, tile(t), (((1,), (1,)), ((), ())), preferred_element_type=F32
         )
     square = jnp.zeros((systems, width), F32)
     for b in range(blocks):
@@ -462,7 +461,7 @@
         term_ref[e * chunk + group] = part
     for t in range(tiles):
         row = meta_ref[0, t] * chunk + meta_ref[1, t] * systems
-        term = jnp.dot(lows[meta_ref[2, t]], tiles_ref[0, 0, t], preferred_element_type=F32)
+        term = jnp.dot(lows[meta_ref[2, t]], tile(t), preferred_element_type=F32)
         for r in range(systems):
             term_ref[row + r] = term[r : r + 1]
 
@@ -512,6 +511,7 @@
     ray_out,
     damp_out,
     solution_out,
+    kept_ref,
     bar_ref,
     solution_ref,
     search_ref,
@@ -523,10 +523,24 @@
 ):
     systems, columns, _ = bar_ref.shape
     rows = columns // PIECES
-    ins = ((bar_in, bar_ref), (solution_in, solution_ref), (search_in, search_ref))
+    kept = kept_ref.shape[0]
+    ins = ((bar_in, bar_ref), (solution_in, solution_ref))
     outs = ((damp_s, damp_out), (solution_s, solution_out))
+
+    def start(n):
+        if n < systems * PIECES:
+            begin(fetch(n))
+
+    def fetch(n):
+        r, p = n // PIECES, n % PIECES
+        at = pl.ds(p * rows, rows)
+        target = kept_ref.at[r, at] if r < kept else search_ref.at[0, at]
+        return pieces(ins, in_sems, r, p, rows) + [
+            pltpu.make_async_copy(search_in.at[r, at], target, in_sems.at[r, p, 2])
+        ]
+
     for n in range(AHEAD):
-        start_one(ins, in_sems, n, systems, rows)
+        start(n)
     rho_bar, phi_bar = rec_ref[1:2], rec_ref[2:3]
     beta = first_norm(residual_ref, systems, rows_all)
     rho = jnp.sqrt(rho_bar * rho_bar + beta * beta)
@@ -537,19 +551,16 @@
     for s in range(systems):
         ray_out[s] = ray_ref[s] * coef[0, s]
 
-    def piece(n, _):
+    for n in range(systems * PIECES):
         r, p = n // PIECES, n % PIECES
-        at = pl.ds(pl.multiple_of(p * rows, rows), rows)
-        start_one(ins, in_sems, n + AHEAD, systems, rows)
-        for copy in pieces(ins, in_sems, r, p, rows):
-            copy.wait()
+        at = pl.ds(p * rows, rows)
+        start(n + AHEAD)
+        settle(fetch(n))
+        search = kept_ref[r, at, :] if r < kept else search_ref[0, at, :]
         damp_s[r, at, :] = bar_ref[r, at, :] * coef[0, r]
-        solution_s[r, at, :] = solution_ref[r, at, :] + search_ref[r, at, :] * coef[1, r]
-        for copy in pieces(outs, sems, r, p, rows):
-            copy.start()
-        return 0
-
-    lax.fori_loop(0, systems * PIECES, piece, 0)
+        solution_s[r, at, :] = solution_ref[r, at, :] + search * coef[1, r]
+        begin(pieces(outs, sems, r, p, rows))
+
     wait_all(outs, sems, systems, rows)
 
 
@@ -562,6 +573,7 @@
     parts_ref,
     rec_ref,
     added_ref,
+    kept_ref,
     image_in,
     model_in,
     search_in,
@@ -579,10 +591,24 @@
 ):
     systems, columns, _ = image_ref.shape
     rows = columns // PIECES
-    ins = ((image_in, image_ref), (model_in, model_ref), (search_in, search_ref))
+    kept = kept_ref.shape[0]
+    ins = ((image_in, image_ref), (model_in, model_ref))
     outs = ((model_s, model_out), (search_s, search_out))
+
+    def start(n):
+        if n < systems * PIECES:
+            begin(fetch(n))
+
+    def fetch(n):
+        r, p = n // PIECES, n % PIECES
+        copies = pieces(ins, in_sems, r, p, rows)
+        if r >= kept:
+            at = pl.ds(p * rows, rows)
+            copies.append(pltpu.make_async_copy(search_in.at[r, at], search_ref.at[0, at], in_sems.at[r, p, 2]))
+        return copies
+
     for n in range(AHEAD):
-        start_one(ins, in_sems, n, systems, rows)
+        start(n)
     total = jnp.sum(parts_ref[...], axis=0, keepdims=True)
     image_sq, cross, model_sq = (total[:, q * systems : (q + 1) * systems] for q in range(1, 4))
     rho_bar, phi_bar = rec_ref[1:2], rec_ref[2:3]
@@ -599,31 +625,27 @@
             coef[q, s] = scale[0, s]
     width = PATCH * clon
 
-    def piece(n, _):
+    for n in range(systems * PIECES):
         r, p = n // PIECES, n % PIECES
-        at = pl.ds(pl.multiple_of(p * rows, rows), rows)
-        start_one(ins, in_sems, n + AHEAD, systems, rows)
-        for copy in pieces(ins, in_sems, r, p, rows):
-            copy.wait()
+        at = pl.ds(p * rows, rows)
+        start(n + AHEAD)
+        settle(fetch(n))
+        search = kept_ref[r, at, :] if r < kept else search_ref[0, at, :]
         new = image_ref[r, at, :] * coef[0, r] - model_ref[r, at, :] * coef[1, r]
         model_s[r, at, :] = new
-        search_s[r, at, :] = new - search_ref[r, at, :] * coef[2, r]
+        search_s[r, at, :] = new - search * coef[2, r]
         for k in range(PATCH):
-            begin = (corner_ref[0] + k) * clon
-
-            @pl.when((begin >= p * rows) & (begin < (p + 1) * rows))
+            first = (corner_ref[0] + k) * clon
+
+            @pl.when((first >= p * rows) & (first < (p + 1) * rows))
             def _():
-                cells = pl.ds(pl.multiple_of(begin, clon), clon)
-                source = pl.ds(pl.multiple_of(r * width + k * clon, clon), clon)
-                more = added_ref[source, :] * coef[0, r]
+                cells = pl.ds(pl.multiple_of(first, clon), clon)
+                more = added_ref[r * width + k * clon : r * width + (k + 1) * clon, :] * coef[0, r]
                 model_s[r, cells, :] = model_s[r, cells, :] + more
                 search_s[r, cells, :] = search_s[r, cells, :] + more
 
-        for copy in pieces(outs, sems, r, p, rows):
-            copy.start()
-        return 0
-
-    lax.fori_loop(0, systems * PIECES, piece, 0)
+        begin(pieces(outs, sems, r, p, rows))
+
     wait_all(outs, sems, systems, rows)
 
 
@@ -636,11 +658,14 @@
     return [pltpu.make_async_copy(a.at[r, at], b.at[r, at], sems.at[r, p, k]) for k, (a, b) in enumerate(pairs)]
 
 
-def start_one(pairs, sems, n, systems, rows):
-    @pl.when(n < systems * PIECES)
-    def _():
-        for copy in pieces(pairs, sems, n // PIECES, n % PIECES, rows):
-            copy.start()
+def begin(copies):
+    for copy in copies:
+        copy.start()
+
+
+def settle(copies):
+    for copy in copies:
+        copy.wait()
 
 
 def wait_all(pairs, sems, systems, rows):
@@ -652,7 +677,8 @@
     lax.fori_loop(0, systems * PIECES, one, 0)
 
 
-PARTS = 6
+PARTS = 3
+HELD = 30
 
 
 def shifted(x, axis, step):
@@ -700,30 +726,19 @@
     model, damping = far(model_vector), far(damping_vector)
     model_flat, damping_flat = far(model_vector.reshape(flat)), far(damping_vector.reshape(flat))
 
-    asked = (devices, 1, (1 + systems) * depth)
-    asking = call(
-        ask_body,
-        "ask",
-        there(asked, F32),
-        [vmem(), hbm()],
-        vmem(),
-        scratch=[pltpu.VMEM((4, systems, 1, 8, depth), F32), dma((4,))],
-    )(far(block_ids), model)
-    lists = exchange(asking)
-
     side = there((systems, 3 * clat, depth), F32)
     band = there((systems, 3, clon, depth), F32)
-    north_msg, south_msg, east_msg, west_msg, meta = call(
+    asking, north_msg, south_msg, east_msg, west_msg, meta = call(
         functools.partial(flanks_body, columns.bit_length() - 1, blocks),
         "flanks",
-        (band, band, side, side, there((8, lanes), I32)),
-        [hbm()] + [vmem()] * 3 + [hbm(), hbm()],
-        (vmem(),) * 5,
+        (there((devices, 1, (1 + systems) * depth), F32), band, band, side, side, there((8, lanes), I32)),
+        [vmem()] * 3 + [hbm(), hbm()],
+        (vmem(),) * 6,
         scratch=[pltpu.VMEM((4, systems, clat, 8, depth), F32), dma((8,))],
         flops=1,
         moved=128 * systems * clat * depth,
-    )(far(asking), far(block_ids), block_offsets, ray_counts, model, damping)
-
+    )(far(block_ids), block_offsets, ray_counts, model, damping)
+    lists = exchange(asking)
     north = shifted(south_msg, "lat", 1)
     south = shifted(north_msg, "lat", -1)
     west = shifted(east_msg, "lon", 1)
@@ -745,32 +760,40 @@
     fetched = exchange(served.reshape(devices, group, depth)).reshape(slots * systems, depth)
 
     edge, flank = there((systems, clon, depth), F32), there((systems, clat, depth), F32)
-    bar, *border, sums = call(
+    bar, held, *border, sums = call(
         functools.partial(damp_body, clat, clon),
         "damp",
-        (there(flat, F32), edge, edge, flank, flank, there((1, lanes), F32)),
-        [vmem()] * 2 + [hbm()] * 2 + [vmem()] * 4,
-        (hbm(),) + (vmem(),) * 5,
-        scratch=[pltpu.VMEM(flat, F32)] * 3 + [pltpu.SMEM((systems,), F32), dma((systems, 3))],
+        (
+            there(flat, F32),
+            here((HELD, width, depth), BF16),
+            edge,
+            edge,
+            flank,
+            flank,
+            there((1, lanes), F32),
+        ),
+        [vmem()] * 2 + [hbm()] * 2 + [vmem()] * 4 + [hbm()],
+        (hbm(),) + (vmem(),) * 6,
+        scratch=[pltpu.VMEM(flat, F32)] * 3 + [pltpu.SMEM((systems,), F32), dma((systems, 3)), dma],
         flops=20 * systems * columns * depth,
         moved=12 * systems * columns * depth,
-    )(far(recurrence), diagonal, model_flat, damping_flat, north, south, west, east)
+    )(far(recurrence), diagonal, model_flat, damping_flat, north, south, west, east, far(sensitivity))
 
     ray_bar, terms = call(
         functools.partial(rays_body, cap, blocks),
         "rays",
         (there(ray_vector.shape, F32), there((devices * chunk, 1, depth), F32)),
-        [smem(), vmem(), hbm()] + [vmem()] * 3,
+        [smem(), vmem(), hbm()] + [vmem()] * 4,
         (vmem(), vmem()),
         scratch=[
-            pltpu.VMEM(sensitivity.shape, BF16),
+            pltpu.VMEM((tiles - HELD, width, depth), BF16),
             pltpu.VMEM((cap + 1, group, depth), BF16),
             pltpu.VMEM((blocks + 1, 16, width), BF16),
             dma((PARTS,)),
         ],
         flops=4 * tiles * width * depth * 16,
         moved=2 * tiles * width * depth,
-    )(meta, far(recurrence), far(sensitivity), fetched, far(ray_vector), far(sums))
+    )(meta, far(recurrence), far(sensitivity), near(held), fetched, far(ray_vector), far(sums))
     arrived = exchange(terms.reshape(devices, 1, chunk * depth)).reshape(devices * chunk, depth)
 
     padded = -(-devices * chunk // lanes) * lanes
@@ -804,13 +827,15 @@
     every = exchange(parts.reshape(devices, 1, lanes)).reshape(devices, lanes)
 
     search_flat = far(search.reshape(flat))
-    ray_out, damp_out, solution_out = call(
+    ray_out, damp_out, solution_out, kept = call(
         functools.partial(early_body, float(rows_all)),
         "early",
-        (there(ray_vector.shape, F32), there(flat, F32), there(flat, F32)),
+        (there(ray_vector.shape, F32), there(flat, F32), there(flat, F32), here((systems - 1, columns, depth), F32)),
         [vmem()] * 3 + [hbm()] * 3,
-        (vmem(), hbm(), hbm()),
-        scratch=[pltpu.VMEM(flat, F32)] * 5
+        (vmem(), hbm(), hbm(), vmem()),
+        scratch=[pltpu.VMEM(flat, F32)] * 2
+        + [pltpu.VMEM((1, columns, depth), F32)]
+        + [pltpu.VMEM(flat, F32)] * 2
         + [pltpu.SMEM((2, systems), F32), dma((systems, PIECES, 3)), dma((systems, PIECES, 2))],
         mib=32,
         flops=4 * systems * columns * depth,
@@ -820,14 +845,16 @@
         functools.partial(finish_body, float(rows_all), float(cells_all), clon),
         "finish",
         (there(flat, F32), there(flat, F32), there(recurrence.shape, F32)),
-        [smem()] + [vmem()] * 4 + [hbm()] * 3,
+        [smem()] + [vmem()] * 5 + [hbm()] * 3,
         (hbm(), hbm(), vmem()),
-        scratch=[pltpu.VMEM(flat, F32)] * 5
+        scratch=[pltpu.VMEM(flat, F32)] * 2
+        + [pltpu.VMEM((1, columns, depth), F32)]
+        + [pltpu.VMEM(flat, F32)] * 2
         + [pltpu.SMEM((3, systems), F32), dma((systems, PIECES, 3)), dma((systems, PIECES, 2))],
         mib=32,
         flops=6 * systems * columns * depth,
         moved=20 * systems * columns * depth,
-    )(corner, residual, every, far(recurrence), added, far(image), model_flat, search_flat)
+    )(corner, residual, every, far(recurrence), added, near(kept), far(image), model_flat, search_flat)
     fields = (x.reshape(full) for x in (damp_out, model_out, solution_out, search_out))
     return (ray_out, *fields, rec_out)
 

time: 86.1 us -> 84.3 us (0.979)
  Pallas kernels: 41.1 us -> 38.5 us
    pallas_call x1 -> x0, Pallas kernels: 2.14 us -> none  [per_device(): call(ask_body, 'ask', there(asked, F32), [vmem(), hbm()], vmem(), scratch...]
where the time goes in v9:
time: 84.3 us; the launch traced here: 83.4 us
  Pallas kernels  38.5 us (46%)
  starting transfers between devices  18.4 us (22%)
  blocking collectives  17.3 us (21%)
  waiting for transfers between devices  7.14 us (8%)
  between operations  1.41 us (2%)
    all_to_all x1, blocking collectives, exchange(): return lax.all_to_all(x, AXES, split_axis=0, concat_axis=0, tiled=True)  17.3 us
    all_to_all x3, starting transfers between devices, exchange(): return lax.all_to_all(x, AXES, split_axis=0, concat_axis=0, tiled=True)  9.38 us
    ppermute x4, starting transfers between devices, shifted(): return lax.ppermute(x, axis, pairs)  8.99 us
    all_to_all x3, waiting for transfers between devices, exchange(): return lax.all_to_all(x, AXES, split_axis=0, concat_axis=0, tiled=True)  7.13 us
    pallas_call x1, Pallas kernels, per_device(): call(functools.partial(finish_body, float(rows_all), float(cells_all), cl...  6.75 us
    pallas_call x1, Pallas kernels, per_device(): call(functools.partial(damp_body, clat, clon), 'damp', (there(flat, F32),...  6.59 us
    pallas_call x1, Pallas kernels, per_device(): call(functools.partial(image_body, chunk, clat, clon), 'image', (there(fl...  6.35 us
    pallas_call x1, Pallas kernels, per_device(): call(functools.partial(early_body, float(rows_all)), 'early', (there(ray_...  6.29 us
  transfers between devices with their start and end apart: 7, of which 3 were waited for; matrix products, arithmetic and copies ran while one was open for 0% of the time, Pallas kernels for 23%

profile of v9, /device:TPU:0, one launch (start us, length us, event | category | flops | bytes accessed | tf_op | source)
XLA Modules:
  0.0 83.4 jit_solution(16518895111980235206)
XLA Ops:
  1.3 0.0 copy-start.1
  1.3 0.6 copy-done.1
  1.9 3.3 %flanks.1 = (f32[32,1,640]{2,1,0:T(1,128)}, f32[4,3,32,128]{3,2,1,0:T(8,128)}, f32[4,3,32,128]{3,2,1,0:T(8,128)}, f32[4,96,128]{2,1,0:T(8,128)}, f32[4,96,128]{2,1,0:T(8,128)}, /*index=5*/s32[8,128]{1,0:T(8,128)}) custom-call(s32[1,1,60]{2,1,0:T(1,128)} %ids_ref.1, s32[1,1,4]{2,1,0:T(1,128)S(1)} %copy-done.1, s32[1,1]{1,0:T(1,128)S(6)} %copy.18.count_ref, ...), custom_call_target="tpu_custom_call" | custom-call | flops 1 | bytes 2097152 | tf_op jit(solution)/shard_map/flanks/pallas_call | solution.py:731
  5.2 4.9 %collective-permute-start = (f32[4,3,32,128]{3,2,1,0:T(8,128)}, f32[4,3,32,128]{3,2,1,0:T(8,128)S(1)}, u32[]{:S(2)}, u32[]{:S(2)}) collective-permute-start(f32[4,3,32,128]{3,2,1,0:T(8,128)} %get-tuple-element.42), channel_id=1, source_target_pairs={{0,8},{8,16},{16,24},{1,9},{9,17},{17,25},{2,10},{10,18},{18,26},{... | collective-permute-start | bytes 589832 | tf_op jit(solution)/shard_map/ppermute | solution.py:690
  10.2 1.3 %collective-permute-start.1 = (f32[4,3,32,128]{3,2,1,0:T(8,128)}, f32[4,3,32,128]{3,2,1,0:T(8,128)S(1)}, u32[]{:S(2)}, u32[]{:S(2)}) collective-permute-start(f32[4,3,32,128]{3,2,1,0:T(8,128)} %get-tuple-element.43), channel_id=1, source_target_pairs={{8,0},{16,8},{24,16},{9,1},{17,9},{25,17},{10,2},{18,10},{26,18},{... | collective-permute-start | bytes 589832 | tf_op jit(solution)/shard_map/ppermute | solution.py:690
  11.4 1.5 %collective-permute-start.2 = (f32[4,96,128]{2,1,0:T(8,128)}, f32[4,96,128]{2,1,0:T(8,128)S(1)}, u32[]{:S(2)}, u32[]{:S(2)}) collective-permute-start(f32[4,96,128]{2,1,0:T(8,128)} %get-tuple-element.44), channel_id=1, source_target_pairs={{0,1},{1,2},{2,3},{3,4},{4,5},{5,6},{6,7},{8,9},{9,10},{10,11},{11... | collective-permute-start | bytes 589832 | tf_op jit(solution)/shard_map/ppermute | solution.py:690
  12.9 1.3 %collective-permute-start.3 = (f32[4,96,128]{2,1,0:T(8,128)}, f32[4,96,128]{2,1,0:T(8,128)S(1)}, u32[]{:S(2)}, u32[]{:S(2)}) collective-permute-start(f32[4,96,128]{2,1,0:T(8,128)} %get-tuple-element.45), channel_id=1, source_target_pairs={{1,0},{2,1},{3,2},{4,3},{5,4},{6,5},{7,6},{9,8},{10,9},{11,10},{12... | collective-permute-start | bytes 589832 | tf_op jit(solution)/shard_map/ppermute | solution.py:690
  14.2 17.3 %all_to_all.20.lists_ref = f32[32,1,640]{2,1,0:T(1,128)S(1)} all-to-all(f32[32,1,640]{2,1,0:T(1,128)} %get-tuple-element.41), channel_id=1, replica_groups=mesh['lat'=4,'lon'=8] {'lat','lon'}, dimensions={0} | all-to-all | bytes 163840 | tf_op jit(solution)/shard_map/all_to_all | solution.py:694
  31.6 0.0 collective-permute-done.north.north_ref
  31.6 0.0 collective-permute-done.1.south.south_ref
  31.6 0.0 collective-permute-done.2.west.west_ref
  31.6 0.0 collective-permute-done.3.east.east_ref
  31.6 2.4 %serve.1 = (bf16[512,128]{1,0:T(8,128)(2,1)}, f32[32,128]{1,0:T(8,128)S(1)}, s32[1]{0:T(128)}, f32[16,128]{1,0:T(8,128)S(1)}) custom-call(f32[32,1,640]{2,1,0:T(1,128)S(1)} %all_to_all.20.lists_ref, f32[4,1024,128]{2,1,0:T(8,128)} %bitcast.19, f32[4,3,32,128]{3,2,1,0:T(8,128)S(1)} %collective-permute-done.north.north_ref, ...), custom_call_target="tpu_custom_call" | custom-call | tf_op jit(solution)/shard_map/serve/pallas_call | solution.py:747
  34.0 2.6 %all-to-all-start.1 = ((bf16[32,16,128]{2,1,0:T(8,128)(2,1)}), bf16[32,16,128]{2,1,0:T(8,128)(2,1)S(1)}, u32[]{:S(2)}, u32[]{:S(2)}) async-start(bf16[32,16,128]{2,1,0:T(8,128)(2,1)} %bitcast.28), calls=%async_computation.1 | async-start | bytes 262144 | tf_op jit(solution)/shard_map/all_to_all | solution.py:694
  36.6 0.0 copy-start
  36.6 6.6 %damp.1 = (f32[4,1024,128]{2,1,0:T(8,128)}, bf16[30,256,128]{2,1,0:T(8,128)(2,1)S(1)}, f32[4,32,128]{2,1,0:T(8,128)}, f32[4,32,128]{2,1,0:T(8,128)}, f32[4,32,12...) custom-call(f32[3,4]{1,0:T(4,128)} %rec_ref.7, f32[16,128]{1,0:T(8,128)S(1)} %get-tuple-element.46.diagonal_ref, ...), custom_call_target="tpu_custom_call" | custom-call | flops 10485760 | bytes 6291456 | tf_op jit(solution)/shard_map/damp/pallas_call | solution.py:763
  43.2 1.6 %all-to-all-done.1 = bf16[32,16,128]{2,1,0:T(8,128)(2,1)S(1)} async-done(((bf16[32,16,128]{2,1,0:T(8,128)(2,1)}), bf16[32,16,128]{2,1,0:T(8,128)(2,1)S(1)}, u32[]{:S(2)}, u32[]{:S(2)}) %all-to-all-start.1) | async-done | bytes 131104 | tf_op jit(solution)/shard_map/all_to_all | solution.py:694
  44.8 0.0 copy-done
  44.8 5.6 %rays.1 = (f32[4,1,1,768]{3,2,1,0:T(1,128)}, f32[544,1,128]{2,1,0:T(1,128)}) custom-call(s32[8,128]{1,0:T(8,128)S(1)} %copy-done, f32[3,4]{1,0:T(4,128)} %rec_ref.7, bf16[1,1,60,256,128]{4,3,2,1,0:T(8,128)(2,1)} %tiles_in.3, bf16[30,256,128]{2,1,0:T(8,128)(2,1)S(1)} %get-tuple-element.47.held_ref, bf16[512,128]{1,0:T(8,128)(2,1)S(1)} %bitcast.17, ...), custom_call_target="tpu_custom_call" | custom-call | flops 125829120 | bytes 3932160 | tf_op jit(solution)/shard_map/rays/pallas_call | solution.py:782
  50.4 4.2 %all-to-all-start.2 = ((f32[32,1,2176]{2,1,0:T(1,128)}), f32[32,1,2176]{2,1,0:T(1,128)S(1)}, u32[]{:S(2)}, u32[]{:S(2)}) async-start(f32[32,1,2176]{2,1,0:T(1,128)} %bitcast.27), calls=%async_computation.2 | async-start | bytes 557056 | tf_op jit(solution)/shard_map/all_to_all | solution.py:694
  54.6 6.4 %image.1 = (f32[4,1024,128]{2,1,0:T(8,128)}, f32[1,128]{1,0:T(1,128)S(1)}, f32[512,128]{1,0:T(8,128)S(1)}, f32[512,128]{1,0:T(8,128)S(1)}, bf16[512,640]{1,0:T(8,128)(2,1)S(1)}) custom-call(s32[1]{0:T(128)} %get-tuple-element.51.corner_ref, f32[32,128]{1,0:T(8,128)S(1)} %get-tuple-element.52.wanted_ref, f32[4,1024,128]{2,1,0:T(8,128)} %get-tuple-element.53.bar_in, ...), custom_call_target="tpu_custom_call" | custom-call | flops 10485760 | bytes 6291456 | tf_op jit(solution)/shard_map/image/pallas_call | solution.py:802
  61.0 4.7 %all-to-all-done.2 = f32[32,1,2176]{2,1,0:T(1,128)S(1)} async-done(((f32[32,1,2176]{2,1,0:T(1,128)}), f32[32,1,2176]{2,1,0:T(1,128)S(1)}, u32[]{:S(2)}, u32[]{:S(2)}) %all-to-all-start.2) | async-done | bytes 278560 | tf_op jit(solution)/shard_map/all_to_all | solution.py:694
  65.7 1.3 %combine.1 = (f32[512,128]{1,0:T(8,128)S(1)}, f32[1,128]{1,0:T(1,128)S(1)}, f32[32,128]{1,0:T(8,128)}) custom-call(f32[544,128]{1,0:T(8,128)S(1)} %bitcast.16, bf16[512,640]{1,0:T(8,128)(2,1)S(1)} %get-tuple-element.58.chosen_ref, f32[512,128]{1,0:T(8,128)S(1)} %get-tuple-element.59.patch_ref, f32[512,128]{1,0:T(8,128)S(1)} %get-tuple-element.60.model_patch_ref, ...), custom_call_target="tpu_custom_call" | custom-call | tf_op jit(solution)/shard_map/combine/pallas_call | solution.py:819
  67.1 2.5 %all-to-all-start.3 = ((f32[32,1,128]{2,1,0:T(1,128)}), f32[32,1,128]{2,1,0:T(1,128)S(1)}, u32[]{:S(2)}, u32[]{:S(2)}) async-start(f32[32,1,128]{2,1,0:T(1,128)} %bitcast.29), calls=%async_computation.3 | async-start | bytes 32768 | tf_op jit(solution)/shard_map/all_to_all | solution.py:694
  69.6 6.3 %early.1 = (f32[4,1,1,768]{3,2,1,0:T(1,128)}, f32[4,1024,128]{2,1,0:T(8,128)}, f32[4,1024,128]{2,1,0:T(8,128)}, f32[3,1024,128]{2,1,0:T(8,128)S(1)}) custom-call(f32[1,128]{1,0:T(1,128)S(1)} %get-tuple-element.62.residual_ref, f32[3,4]{1,0:T(4,128)} %rec_ref.7, f32[4,1,1,768]{3,2,1,0:T(1,128)} %get-tuple-element.63.ray_ref, ...), custom_call_target="tpu_custom_call" | custom-call | flops 2097152 | bytes 10485760 | tf_op jit(solution)/shard_map/early/pallas_call | solution.py:830
  75.9 0.8 all-to-all-done.3
  76.7 6.8 %finish.1 = (f32[4,1024,128]{2,1,0:T(8,128)}, f32[4,1024,128]{2,1,0:T(8,128)}, f32[3,4]{1,0:T(4,128)}) custom-call(s32[1]{0:T(128)} %get-tuple-element.51.corner_ref, f32[1,128]{1,0:T(1,128)S(1)} %get-tuple-element.62.residual_ref, f32[32,128]{1,0:T(8,128)S(1)} %bitcast.18, f32[3,4]{1,0:T(4,128)} %rec_ref.7, f32[512,128]{1,0:T(8,128)S(1)} %get-tuple-element.67.added_ref, ...), custom_call_target="tpu_custom_call" | custom-call | flops 3145728 | bytes 10485760 | tf_op jit(solution)/shard_map/finish/pallas_call | solution.py:844
Async XLA Ops:
  1.3 0.7 copy-start.1
  5.2 26.4 %collective-permute-start = (f32[4,3,32,128]{3,2,1,0:T(8,128)}, f32[4,3,32,128]{3,2,1,0:T(8,128)S(1)}, u32[]{:S(2)}, u32[]{:S(2)}) collective-permute-start(f32[4,3,32,128]{3,2,1,0:T(8,128)} %get-tuple-element.42), channel_id=1, source_target_pairs={{0,8},{8,16},{16,24},{1,9},{9,17},{17,25},{2,10},{10,18},{18,26},{... | collective-permute-start | bytes 589832 | tf_op jit(solution)/shard_map/ppermute | solution.py:690
  10.2 21.4 %collective-permute-start.1 = (f32[4,3,32,128]{3,2,1,0:T(8,128)}, f32[4,3,32,128]{3,2,1,0:T(8,128)S(1)}, u32[]{:S(2)}, u32[]{:S(2)}) collective-permute-start(f32[4,3,32,128]{3,2,1,0:T(8,128)} %get-tuple-element.43), channel_id=1, source_target_pairs={{8,0},{16,8},{24,16},{9,1},{17,9},{25,17},{10,2},{18,10},{26,18},{... | collective-permute-start | bytes 589832 | tf_op jit(solution)/shard_map/ppermute | solution.py:690
  11.4 20.1 %collective-permute-start.2 = (f32[4,96,128]{2,1,0:T(8,128)}, f32[4,96,128]{2,1,0:T(8,128)S(1)}, u32[]{:S(2)}, u32[]{:S(2)}) collective-permute-start(f32[4,96,128]{2,1,0:T(8,128)} %get-tuple-element.44), channel_id=1, source_target_pairs={{0,1},{1,2},{2,3},{3,4},{4,5},{5,6},{6,7},{8,9},{9,10},{10,11},{11... | collective-permute-start | bytes 589832 | tf_op jit(solution)/shard_map/ppermute | solution.py:690
  12.9 18.7 %collective-permute-start.3 = (f32[4,96,128]{2,1,0:T(8,128)}, f32[4,96,128]{2,1,0:T(8,128)S(1)}, u32[]{:S(2)}, u32[]{:S(2)}) collective-permute-start(f32[4,96,128]{2,1,0:T(8,128)} %get-tuple-element.45), channel_id=1, source_target_pairs={{1,0},{2,1},{3,2},{4,3},{5,4},{6,5},{7,6},{9,8},{10,9},{11,10},{12... | collective-permute-start | bytes 589832 | tf_op jit(solution)/shard_map/ppermute | solution.py:690
  34.0 10.8 %all-to-all-start.1 = ((bf16[32,16,128]{2,1,0:T(8,128)(2,1)}), bf16[32,16,128]{2,1,0:T(8,128)(2,1)S(1)}, u32[]{:S(2)}, u32[]{:S(2)}) async-start(bf16[32,16,128]{2,1,0:T(8,128)(2,1)} %bitcast.28), calls=%async_computation.1 | async-start | bytes 262144 | tf_op jit(solution)/shard_map/all_to_all | solution.py:694
  36.6 8.2 %copy-start = (s32[8,128]{1,0:T(8,128)S(1)}, s32[8,128]{1,0:T(8,128)}, u32[]{:S(2)}) copy-start(s32[8,128]{1,0:T(8,128)} %get-tuple-element.40.meta_ref) | copy-start | bytes 12292
  50.4 15.3 %all-to-all-start.2 = ((f32[32,1,2176]{2,1,0:T(1,128)}), f32[32,1,2176]{2,1,0:T(1,128)S(1)}, u32[]{:S(2)}, u32[]{:S(2)}) async-start(f32[32,1,2176]{2,1,0:T(1,128)} %bitcast.27), calls=%async_computation.2 | async-start | bytes 557056 | tf_op jit(solution)/shard_map/all_to_all | solution.py:694
  67.1 9.6 %all-to-all-start.3 = ((f32[32,1,128]{2,1,0:T(1,128)}), f32[32,1,128]{2,1,0:T(1,128)S(1)}, u32[]{:S(2)}, u32[]{:S(2)}) async-start(f32[32,1,128]{2,1,0:T(1,128)} %bitcast.29), calls=%async_computation.3 | async-start | bytes 32768 | tf_op jit(solution)/shard_map/all_to_all | solution.py:694

commit v10 on v9

--- a/solution.py
+++ b/solution.py
@@ -63,22 +63,21 @@
     return jnp.sum(jnp.where(pick, spread, 0.0), axis=1, keepdims=True)
 
 
-def serve_body(cap, clat, clon, lists_ref, model_in, north, south, west, east, served_ref, wanted_ref, corner_ref, diagonal_ref, patch, mixed, sems):
-    systems, width, depth = patch.shape
+def rank_body(cap, clat, clon, lists_ref, wanted_ref, corner_ref, diagonal_ref):
     devices = lists_ref.shape[0]
+    depth = lists_ref.shape[2] // (diagonal_ref.shape[0] // 4 + 1)
+    systems = diagonal_ref.shape[0] // 4
     lanes = 128
     shift = (clat * clon).bit_length() - 1
-    me = lax.axis_index("lat") * lax.axis_size("lon") + lax.axis_index("lon")
+    lat_at, lon_at = lax.axis_index("lat"), lax.axis_index("lon")
+    lat_size, lon_size = lax.axis_size("lat"), lax.axis_size("lon")
+    me = lat_at * lon_size + lon_at
     ids = lists_ref[:, 0, 0:lanes].astype(I32)
     column = ids - lax.shift_left(me, shift)
     mine = (column >= 0) & (column < clat * clon) & (ids >= 0)
     first = jnp.min(jnp.where(mine, column, clat * clon))
     corner = jnp.minimum(lax.shift_right_logical(first, clon.bit_length() - 1), clat - PATCH)
     corner_ref[0] = corner
-    at = pl.ds(pl.multiple_of(corner * clon, clon), width)
-    copies = [pltpu.make_async_copy(model_in.at[r, at], patch.at[r], sems.at[r]) for r in range(systems)]
-    for copy in copies:
-        copy.start()
     ahead = (iota((lanes, lanes), 0) < iota((lanes, lanes), 1)).astype(F32).astype(BF16)
     rank = jnp.dot(mine.astype(F32).astype(BF16), ahead, preferred_element_type=F32)
     value = (column - corner * clon + 1).astype(F32)
@@ -88,16 +87,6 @@
         picked = jnp.sum(jnp.where(mine & (rank == c), value, 0.0), axis=1, keepdims=True)
         wanted = jnp.where(at == c, picked, wanted)
     wanted_ref[...] = wanted
-    target = wanted_column(wanted, cap).astype(I32) - 1
-    rows = target.shape[0]
-    chosen = (jnp.broadcast_to(target, (rows, width)) == iota((rows, width), 1)).astype(F32).astype(BF16)
-    for r in range(systems):
-        copies[r].wait()
-        table = patch[r].astype(BF16)
-        mixed[pl.ds(r, rows, stride=systems), :] = jnp.dot(chosen, table, preferred_element_type=F32)
-    served_ref[...] = mixed[...].astype(BF16)
-    lat_at, lon_at = lax.axis_index("lat"), lax.axis_index("lon")
-    lat_size, lon_size = lax.axis_size("lat"), lax.axis_size("lon")
     for k in range(4):
         lat_to, lon_to = lat_at + 2 * (k // 2) - 1, lon_at + 2 * (k % 2) - 1
         inside = (lat_to >= 0) & (lat_to < lat_size) & (lon_to >= 0) & (lon_to < lon_size)
@@ -106,6 +95,22 @@
         for r in range(systems):
             got = lists_ref[source, :, (r + 1) * depth : (r + 2) * depth]
             diagonal_ref[k * systems + r : k * systems + r + 1, :] = got * flag
+
+
+def serve_body(cap, clon, corner_ref, wanted_ref, model_in, north, south, west, east, served_ref, patch, mixed, sems):
+    systems, width, depth = patch.shape
+    at = pl.ds(pl.multiple_of(corner_ref[0] * clon, clon), width)
+    copies = [pltpu.make_async_copy(model_in.at[r, at], patch.at[r], sems.at[r]) for r in range(systems)]
+    for copy in copies:
+        copy.start()
+    target = wanted_column(wanted_ref[...], cap).astype(I32) - 1
+    rows = target.shape[0]
+    chosen = (jnp.broadcast_to(target, (rows, width)) == iota((rows, width), 1)).astype(F32).astype(BF16)
+    for r in range(systems):
+        copies[r].wait()
+        table = patch[r].astype(BF16)
+        mixed[pl.ds(r, rows, stride=systems), :] = jnp.dot(chosen, table, preferred_element_type=F32)
+    served_ref[...] = mixed[...].astype(BF16)
 
 
 def flanks_body(
@@ -396,22 +401,28 @@
         row = place(row, systems + r, jnp.sum(image_sq, keepdims=True))
         return place(row, 2 * systems + r, jnp.sum(cross, keepdims=True))
 
-    sums_out[...] = lax.fori_loop(0, systems, system, sums_ref[...])
+    row = lax.fori_loop(0, systems, system, sums_ref[...])
+    sums_out[...] = place(row, depth - 1, corner.astype(F32))
     for r in range(systems):
         outgoing(r).wait()
 
 
 def rays_body(
-    cap, blocks, meta_ref, rec_ref, tiles_in, held_ref, fetched_ref, old_ref, sums_ref, bar_ref, term_ref, rest_ref, masks, lows, sems
+    cap, blocks, meta_ref, held_ref, fetched_ref, tiles_in, *refs
 ):
+    rec_in, old_in, sums_in, bar_ref, term_ref, rest_ref, masks, lows, rec_ref, old_ref, sums_ref, sems = refs
     tiles, width, depth = tiles_in.shape[2:]
+    small = [
+        pltpu.make_async_copy(a, b, sems.at[PARTS + k])
+        for k, (a, b) in enumerate(((rec_in, rec_ref), (old_in, old_ref), (sums_in, sums_ref)))
+    ]
     part = -(-(tiles - HELD) // PARTS)
     copies = []
     for k in range(PARTS):
         count = min(part, tiles - HELD - k * part)
         source = tiles_in.at[0, 0, pl.ds(HELD + k * part, count)]
         copies.append(pltpu.make_async_copy(source, rest_ref.at[pl.ds(k * part, count)], sems.at[k]))
-    for copy in copies:
+    for copy in copies + small:
         copy.start()
 
     def tile(t):
@@ -438,6 +449,8 @@
         total = total + lax.dot_general(
             left, tile(t), (((1,), (1,)), ((), ())), preferred_element_type=F32
         )
+    for copy in small:
+        copy.wait()
     square = jnp.zeros((systems, width), F32)
     for b in range(blocks):
         traced = jnp.zeros((systems, width), F32)
@@ -485,7 +498,8 @@
     added = three[:, 0:depth] + (three[:, depth : 2 * depth] + three[:, 2 * depth :])
     added_ref[...] = added
     every = terms_ref[pl.ds(chunk - 1, devices, stride=chunk), :]
-    residual_ref[...] = jnp.sum(every, axis=0, keepdims=True)
+    total = jnp.sum(every, axis=0, keepdims=True)
+    residual_ref[...] = jnp.where(iota(total.shape, 1) == depth - 1, sums_ref[...], total)
     square = added * (2.0 * patch_ref[...] + added)
     cross = added * model_patch_ref[...]
     row = sums_ref[...]
@@ -568,28 +582,32 @@
     rows_all,
     cells_all,
     clon,
-    corner_ref,
     residual_ref,
     parts_ref,
-    rec_ref,
     added_ref,
     kept_ref,
     image_in,
     model_in,
     search_in,
+    rec_in,
     model_out,
     search_out,
-    rec_out,
+    rec_sent,
     image_ref,
     model_ref,
     search_ref,
     model_s,
     search_s,
+    rec_ref,
+    rec_out,
     coef,
     in_sems,
     sems,
+    rec_sems,
 ):
-    systems, columns, _ = image_ref.shape
+    systems, columns, depth = image_ref.shape
+    rec_copy = pltpu.make_async_copy(rec_in, rec_ref, rec_sems.at[0])
+    rec_copy.start()
     rows = columns // PIECES
     kept = kept_ref.shape[0]
     ins = ((image_in, image_ref), (model_in, model_ref))
@@ -609,7 +627,9 @@
 
     for n in range(AHEAD):
         start(n)
+    corner = residual_ref[0, depth - 1].astype(I32)
     total = jnp.sum(parts_ref[...], axis=0, keepdims=True)
+    rec_copy.wait()
     image_sq, cross, model_sq = (total[:, q * systems : (q + 1) * systems] for q in range(1, 4))
     rho_bar, phi_bar = rec_ref[1:2], rec_ref[2:3]
     beta = first_norm(residual_ref, systems, rows_all)
@@ -619,6 +639,8 @@
     cosine = rho_bar / rho
     sine = beta / rho
     rec_out[...] = jnp.concatenate([alpha, -cosine * alpha, sine * phi_bar], axis=0)
+    rec_done = pltpu.make_async_copy(rec_out, rec_sent, rec_sems.at[1])
+    rec_done.start()
     scales = (1.0 / (beta * alpha), beta / alpha, sine * alpha / rho)
     for q, scale in enumerate(scales):
         for s in range(systems):
@@ -635,7 +657,7 @@
         model_s[r, at, :] = new
         search_s[r, at, :] = new - search * coef[2, r]
         for k in range(PATCH):
-            first = (corner_ref[0] + k) * clon
+            first = (corner + k) * clon
 
             @pl.when((first >= p * rows) & (first < (p + 1) * rows))
             def _():
@@ -647,6 +669,7 @@
         begin(pieces(outs, sems, r, p, rows))
 
     wait_all(outs, sems, systems, rows)
+    rec_done.wait()
 
 
 PIECES = 2
@@ -744,19 +767,23 @@
     west = shifted(east_msg, "lon", 1)
     east = shifted(west_msg, "lon", -1)
 
-    served, wanted, corner, diagonal = call(
-        functools.partial(serve_body, cap, clat, clon),
+    wanted, corner, diagonal = call(
+        functools.partial(rank_body, cap, clat, clon),
+        "rank",
+        (plain((devices, lanes), F32), plain((1,), I32), plain((4 * systems, depth), F32)),
+        [vmem()],
+        (vmem(), smem(), vmem()),
+        flops=2 * devices * lanes * lanes,
+        moved=24 * systems * columns * depth,
+    )(lists)
+    served = call(
+        functools.partial(serve_body, cap, clon),
         "serve",
-        (
-            there((slots * systems, depth), BF16),
-            plain((devices, lanes), F32),
-            plain((1,), I32),
-            plain((4 * systems, depth), F32),
-        ),
-        [vmem(), hbm()] + [pl.BlockSpec(memory_space=pl.ANY)] * 4,
-        (vmem(), vmem(), smem(), vmem()),
+        there((slots * systems, depth), BF16),
+        [smem(), vmem(), hbm()] + [pl.BlockSpec(memory_space=pl.ANY)] * 4,
+        vmem(),
         scratch=[pltpu.VMEM(lines, F32), pltpu.VMEM((slots * systems, depth), F32), dma((systems,))],
-    )(lists, model_flat, north, south, west, east)
+    )(corner, wanted, model_flat, north, south, west, east)
     fetched = exchange(served.reshape(devices, group, depth)).reshape(slots * systems, depth)
 
     edge, flank = there((systems, clon, depth), F32), there((systems, clat, depth), F32)
@@ -783,17 +810,20 @@
         functools.partial(rays_body, cap, blocks),
         "rays",
         (there(ray_vector.shape, F32), there((devices * chunk, 1, depth), F32)),
-        [smem(), vmem(), hbm()] + [vmem()] * 4,
+        [smem(), vmem(), vmem()] + [hbm()] * 4,
         (vmem(), vmem()),
         scratch=[
             pltpu.VMEM((tiles - HELD, width, depth), BF16),
             pltpu.VMEM((cap + 1, group, depth), BF16),
             pltpu.VMEM((blocks + 1, 16, width), BF16),
-            dma((PARTS,)),
+            pltpu.VMEM(recurrence.shape, F32),
+            pltpu.VMEM(ray_vector.shape, F32),
+            pltpu.VMEM((1, lanes), F32),
+            dma((PARTS + 3,)),
         ],
         flops=4 * tiles * width * depth * 16,
         moved=2 * tiles * width * depth,
-    )(meta, far(recurrence), far(sensitivity), near(held), fetched, far(ray_vector), far(sums))
+    )(meta, near(held), fetched, far(sensitivity), far(recurrence), far(ray_vector), far(sums))
     arrived = exchange(terms.reshape(devices, 1, chunk * depth)).reshape(devices * chunk, depth)
 
     padded = -(-devices * chunk // lanes) * lanes
@@ -845,16 +875,17 @@
         functools.partial(finish_body, float(rows_all), float(cells_all), clon),
         "finish",
         (there(flat, F32), there(flat, F32), there(recurrence.shape, F32)),
-        [smem()] + [vmem()] * 5 + [hbm()] * 3,
-        (hbm(), hbm(), vmem()),
+        [vmem()] * 4 + [hbm()] * 4,
+        (hbm(),) * 3,
         scratch=[pltpu.VMEM(flat, F32)] * 2
         + [pltpu.VMEM((1, columns, depth), F32)]
         + [pltpu.VMEM(flat, F32)] * 2
-        + [pltpu.SMEM((3, systems), F32), dma((systems, PIECES, 3)), dma((systems, PIECES, 2))],
+        + [pltpu.VMEM(recurrence.shape, F32)] * 2
+        + [pltpu.SMEM((3, systems), F32), dma((systems, PIECES, 3)), dma((systems, PIECES, 2)), dma((2,))],
         mib=32,
         flops=6 * systems * columns * depth,
         moved=20 * systems * columns * depth,
-    )(corner, residual, every, far(recurrence), added, near(kept), far(image), model_flat, search_flat)
+    )(residual, every, added, near(kept), far(image), model_flat, search_flat, far(recurrence))
     fields = (x.reshape(full) for x in (damp_out, model_out, solution_out, search_out))
     return (ray_out, *fields, rec_out)
 

time: 84.3 us -> 84.2 us (level)
    pallas_call x1, Pallas kernels: 6.75 us -> 5.51 us  [per_device(): call(functools.partial(finish_body, float(rows_all), float(cells_all), cl...]
    pallas_call x1 -> x2, Pallas kernels: 2.4 us -> 3.56 us  [the longest x1 2.78 us: per_device(): call(functools.partial(serve_body, cap, clon), 'serve', there((slots * sy...]
  transfers between devices with their start and end apart: 7 -> 7, of which waited for: 3 -> 3; matrix products, arithmetic and copies ran while one was open for 0% -> 0% of each run, Pallas kernels for 23% -> 24%
where the time goes in v10:
time: 84.2 us; the launch traced here: 83.4 us
  Pallas kernels  38.4 us (46%)
  starting transfers between devices  18.4 us (22%)
  blocking collectives  17.3 us (21%)
  waiting for transfers between devices  7.11 us (8%)
  between operations  1.44 us (2%)
    all_to_all x1, blocking collectives, exchange(): return lax.all_to_all(x, AXES, split_axis=0, concat_axis=0, tiled=True)  17.3 us
    all_to_all x3, starting transfers between devices, exchange(): return lax.all_to_all(x, AXES, split_axis=0, concat_axis=0, tiled=True)  9.38 us
    ppermute x4, starting transfers between devices, shifted(): return lax.ppermute(x, axis, pairs)  8.99 us
    all_to_all x3, waiting for transfers between devices, exchange(): return lax.all_to_all(x, AXES, split_axis=0, concat_axis=0, tiled=True)  7.1 us
    pallas_call x1, Pallas kernels, per_device(): call(functools.partial(damp_body, clat, clon), 'damp', (there(flat, F32),...  6.59 us
    pallas_call x1, Pallas kernels, per_device(): call(functools.partial(image_body, chunk, clat, clon), 'image', (there(fl...  6.38 us
    pallas_call x1, Pallas kernels, per_device(): call(functools.partial(early_body, float(rows_all)), 'early', (there(ray_...  6.29 us
    pallas_call x1, Pallas kernels, per_device(): call(functools.partial(rays_body, cap, blocks), 'rays', (there(ray_vector...  5.53 us
  transfers between devices with their start and end apart: 7, of which 3 were waited for; matrix products, arithmetic and copies ran while one was open for 0% of the time, Pallas kernels for 24%

profile of v10, /device:TPU:0, one launch (start us, length us, event | category | flops | bytes accessed | tf_op | source)
XLA Modules:
  0.0 83.4 jit_solution(1492300245275604534)
XLA Ops:
  1.3 0.0 copy-start.1
  1.3 0.6 copy-done.1
  1.9 3.3 %flanks.1 = (f32[32,1,640]{2,1,0:T(1,128)}, f32[4,3,32,128]{3,2,1,0:T(8,128)}, f32[4,3,32,128]{3,2,1,0:T(8,128)}, f32[4,96,128]{2,1,0:T(8,128)}, f32[4,96,128]{2,1,0:T(8,128)}, /*index=5*/s32[8,128]{1,0:T(8,128)}) custom-call(s32[1,1,60]{2,1,0:T(1,128)} %ids_ref.1, s32[1,1,4]{2,1,0:T(1,128)S(1)} %copy-done.1, s32[1,1]{1,0:T(1,128)S(6)} %copy.18.count_ref, ...), custom_call_target="tpu_custom_call" | custom-call | flops 1 | bytes 2097152 | tf_op jit(solution)/shard_map/flanks/pallas_call | solution.py:754
  5.2 4.9 %collective-permute-start = (f32[4,3,32,128]{3,2,1,0:T(8,128)}, f32[4,3,32,128]{3,2,1,0:T(8,128)S(1)}, u32[]{:S(2)}, u32[]{:S(2)}) collective-permute-start(f32[4,3,32,128]{3,2,1,0:T(8,128)} %get-tuple-element.42), channel_id=1, source_target_pairs={{0,8},{8,16},{16,24},{1,9},{9,17},{17,25},{2,10},{10,18},{18,26},{... | collective-permute-start | bytes 589832 | tf_op jit(solution)/shard_map/ppermute | solution.py:713
  10.2 1.3 %collective-permute-start.1 = (f32[4,3,32,128]{3,2,1,0:T(8,128)}, f32[4,3,32,128]{3,2,1,0:T(8,128)S(1)}, u32[]{:S(2)}, u32[]{:S(2)}) collective-permute-start(f32[4,3,32,128]{3,2,1,0:T(8,128)} %get-tuple-element.43), channel_id=1, source_target_pairs={{8,0},{16,8},{24,16},{9,1},{17,9},{25,17},{10,2},{18,10},{26,18},{... | collective-permute-start | bytes 589832 | tf_op jit(solution)/shard_map/ppermute | solution.py:713
  11.4 1.5 %collective-permute-start.2 = (f32[4,96,128]{2,1,0:T(8,128)}, f32[4,96,128]{2,1,0:T(8,128)S(1)}, u32[]{:S(2)}, u32[]{:S(2)}) collective-permute-start(f32[4,96,128]{2,1,0:T(8,128)} %get-tuple-element.44), channel_id=1, source_target_pairs={{0,1},{1,2},{2,3},{3,4},{4,5},{5,6},{6,7},{8,9},{9,10},{10,11},{11... | collective-permute-start | bytes 589832 | tf_op jit(solution)/shard_map/ppermute | solution.py:713
  12.9 1.3 %collective-permute-start.3 = (f32[4,96,128]{2,1,0:T(8,128)}, f32[4,96,128]{2,1,0:T(8,128)S(1)}, u32[]{:S(2)}, u32[]{:S(2)}) collective-permute-start(f32[4,96,128]{2,1,0:T(8,128)} %get-tuple-element.45), channel_id=1, source_target_pairs={{1,0},{2,1},{3,2},{4,3},{5,4},{6,5},{7,6},{9,8},{10,9},{11,10},{12... | collective-permute-start | bytes 589832 | tf_op jit(solution)/shard_map/ppermute | solution.py:713
  14.2 17.3 %all_to_all.20.lists_ref = f32[32,1,640]{2,1,0:T(1,128)S(1)} all-to-all(f32[32,1,640]{2,1,0:T(1,128)} %get-tuple-element.40), channel_id=1, replica_groups=mesh['lat'=4,'lon'=8] {'lat','lon'}, dimensions={0} | all-to-all | bytes 163840 | tf_op jit(solution)/shard_map/all_to_all | solution.py:717
  31.6 0.8 rank.1
  32.4 0.0 collective-permute-done.north_ref.north
  32.4 0.0 collective-permute-done.1.south_ref.south
  32.4 0.0 collective-permute-done.2.west_ref.west
  32.4 0.0 collective-permute-done.3.east_ref.east
  32.4 2.8 %serve.1 = bf16[512,128]{1,0:T(8,128)(2,1)} custom-call(s32[1]{0:T(128)} %get-tuple-element.47.corner_ref, f32[32,128]{1,0:T(8,128)S(1)} %get-tuple-element.48.wanted_ref, f32[4,1024,128]{2,1,0:T(8,128)} %bitcast.19, f32[4,3,32,128]{3,2,1,0:T(8,128)S(1)} %collective-permute-done.north_ref.north, ...), custom_call_target="tpu_custom_call" | custom-call | tf_op jit(solution)/shard_map/serve/pallas_call | solution.py:779
  35.2 2.6 %all-to-all-start.1 = ((bf16[32,16,128]{2,1,0:T(8,128)(2,1)}), bf16[32,16,128]{2,1,0:T(8,128)(2,1)S(1)}, u32[]{:S(2)}, u32[]{:S(2)}) async-start(bf16[32,16,128]{2,1,0:T(8,128)(2,1)} %bitcast.27), calls=%async_computation.1 | async-start | bytes 262144 | tf_op jit(solution)/shard_map/all_to_all | solution.py:717
  37.8 0.0 copy-start
  37.8 6.6 %damp.1 = (f32[4,1024,128]{2,1,0:T(8,128)}, bf16[30,256,128]{2,1,0:T(8,128)(2,1)S(1)}, f32[4,32,128]{2,1,0:T(8,128)}, f32[4,32,128]{2,1,0:T(8,128)}, f32[4,32,12...) custom-call(f32[3,4]{1,0:T(4,128)} %rec_in.1, f32[16,128]{1,0:T(8,128)S(1)} %get-tuple-element.41.diagonal_ref, ...), custom_call_target="tpu_custom_call" | custom-call | flops 10485760 | bytes 6291456 | tf_op jit(solution)/shard_map/damp/pallas_call | solution.py:790
  44.4 1.6 %all-to-all-done.1 = bf16[32,16,128]{2,1,0:T(8,128)(2,1)S(1)} async-done(((bf16[32,16,128]{2,1,0:T(8,128)(2,1)}), bf16[32,16,128]{2,1,0:T(8,128)(2,1)S(1)}, u32[]{:S(2)}, u32[]{:S(2)}) %all-to-all-start.1) | async-done | bytes 131104 | tf_op jit(solution)/shard_map/all_to_all | solution.py:717
  46.0 0.0 copy-done
  46.0 5.5 %rays.1 = (f32[4,1,1,768]{3,2,1,0:T(1,128)}, f32[544,1,128]{2,1,0:T(1,128)}) custom-call(s32[8,128]{1,0:T(8,128)S(1)} %copy-done, bf16[30,256,128]{2,1,0:T(8,128)(2,1)S(1)} %get-tuple-element.46.held_ref, bf16[512,128]{1,0:T(8,128)(2,1)S(1)} %bitcast.17, bf16[1,1,60,256,128]{4,3,2,1,0:T(8,128)(2,1)} %tiles_in.3, f32[3,4]{1,0:T(4,128)} %rec_in.1, ...), custom_call_target="tpu_custom_call" | custom-call | flops 125829120 | bytes 3932160 | tf_op jit(solution)/shard_map/rays/pallas_call | solution.py:809
  51.6 4.2 %all-to-all-start.2 = ((f32[32,1,2176]{2,1,0:T(1,128)}), f32[32,1,2176]{2,1,0:T(1,128)S(1)}, u32[]{:S(2)}, u32[]{:S(2)}) async-start(f32[32,1,2176]{2,1,0:T(1,128)} %bitcast.28), calls=%async_computation.2 | async-start | bytes 557056 | tf_op jit(solution)/shard_map/all_to_all | solution.py:717
  55.8 6.4 %image.1 = (f32[4,1024,128]{2,1,0:T(8,128)}, f32[1,128]{1,0:T(1,128)S(1)}, f32[512,128]{1,0:T(8,128)S(1)}, f32[512,128]{1,0:T(8,128)S(1)}, bf16[512,640]{1,0:T(8,128)(2,1)S(1)}) custom-call(s32[1]{0:T(128)} %get-tuple-element.47.corner_ref, f32[32,128]{1,0:T(8,128)S(1)} %get-tuple-element.48.wanted_ref, f32[4,1024,128]{2,1,0:T(8,128)} %get-tuple-element.51.bar_in, ...), custom_call_target="tpu_custom_call" | custom-call | flops 10485760 | bytes 6291456 | tf_op jit(solution)/shard_map/image/pallas_call | solution.py:832
  62.2 4.7 %all-to-all-done.2 = f32[32,1,2176]{2,1,0:T(1,128)S(1)} async-done(((f32[32,1,2176]{2,1,0:T(1,128)}), f32[32,1,2176]{2,1,0:T(1,128)S(1)}, u32[]{:S(2)}, u32[]{:S(2)}) %all-to-all-start.2) | async-done | bytes 278560 | tf_op jit(solution)/shard_map/all_to_all | solution.py:717
  66.9 1.3 %combine.1 = (f32[512,128]{1,0:T(8,128)S(1)}, f32[1,128]{1,0:T(1,128)S(1)}, f32[32,128]{1,0:T(8,128)}) custom-call(f32[544,128]{1,0:T(8,128)S(1)} %bitcast.16, bf16[512,640]{1,0:T(8,128)(2,1)S(1)} %get-tuple-element.56.chosen_ref, f32[512,128]{1,0:T(8,128)S(1)} %get-tuple-element.57.patch_ref, f32[512,128]{1,0:T(8,128)S(1)} %get-tuple-element.58.model_patch_ref, ...), custom_call_target="tpu_custom_call" | custom-call | tf_op jit(solution)/shard_map/combine/pallas_call | solution.py:849
  68.2 2.5 %all-to-all-start.3 = ((f32[32,1,128]{2,1,0:T(1,128)}), f32[32,1,128]{2,1,0:T(1,128)S(1)}, u32[]{:S(2)}, u32[]{:S(2)}) async-start(f32[32,1,128]{2,1,0:T(1,128)} %bitcast.29), calls=%async_computation.3 | async-start | bytes 32768 | tf_op jit(solution)/shard_map/all_to_all | solution.py:717
  70.8 6.3 %early.1 = (f32[4,1,1,768]{3,2,1,0:T(1,128)}, f32[4,1024,128]{2,1,0:T(8,128)}, f32[4,1024,128]{2,1,0:T(8,128)}, f32[3,1024,128]{2,1,0:T(8,128)S(1)}) custom-call(f32[1,128]{1,0:T(1,128)S(1)} %get-tuple-element.60.residual_ref, f32[3,4]{1,0:T(4,128)} %rec_in.1, f32[4,1,1,768]{3,2,1,0:T(1,128)} %get-tuple-element.61.ray_ref, ...), custom_call_target="tpu_custom_call" | custom-call | flops 2097152 | bytes 10485760 | tf_op jit(solution)/shard_map/early/pallas_call | solution.py:860
  77.1 0.8 all-to-all-done.3
  77.9 5.5 %finish.1 = (f32[4,1024,128]{2,1,0:T(8,128)}, f32[4,1024,128]{2,1,0:T(8,128)}, f32[3,4]{1,0:T(4,128)}) custom-call(f32[1,128]{1,0:T(1,128)S(1)} %get-tuple-element.60.residual_ref, f32[32,128]{1,0:T(8,128)S(1)} %bitcast.18, f32[512,128]{1,0:T(8,128)S(1)} %get-tuple-element.65.added_ref, f32[3,1024,128]{2,1,0:T(8,128)S(1)} %get-tuple-element.66.kept_ref, ...), custom_call_target="tpu_custom_call" | custom-call | flops 3145728 | bytes 10485760 | tf_op jit(solution)/shard_map/finish/pallas_call | solution.py:874
Async XLA Ops:
  1.3 0.7 copy-start.1
  5.2 27.2 %collective-permute-start = (f32[4,3,32,128]{3,2,1,0:T(8,128)}, f32[4,3,32,128]{3,2,1,0:T(8,128)S(1)}, u32[]{:S(2)}, u32[]{:S(2)}) collective-permute-start(f32[4,3,32,128]{3,2,1,0:T(8,128)} %get-tuple-element.42), channel_id=1, source_target_pairs={{0,8},{8,16},{16,24},{1,9},{9,17},{17,25},{2,10},{10,18},{18,26},{... | collective-permute-start | bytes 589832 | tf_op jit(solution)/shard_map/ppermute | solution.py:713
  10.2 22.2 %collective-permute-start.1 = (f32[4,3,32,128]{3,2,1,0:T(8,128)}, f32[4,3,32,128]{3,2,1,0:T(8,128)S(1)}, u32[]{:S(2)}, u32[]{:S(2)}) collective-permute-start(f32[4,3,32,128]{3,2,1,0:T(8,128)} %get-tuple-element.43), channel_id=1, source_target_pairs={{8,0},{16,8},{24,16},{9,1},{17,9},{25,17},{10,2},{18,10},{26,18},{... | collective-permute-start | bytes 589832 | tf_op jit(solution)/shard_map/ppermute | solution.py:713
  11.4 20.9 %collective-permute-start.2 = (f32[4,96,128]{2,1,0:T(8,128)}, f32[4,96,128]{2,1,0:T(8,128)S(1)}, u32[]{:S(2)}, u32[]{:S(2)}) collective-permute-start(f32[4,96,128]{2,1,0:T(8,128)} %get-tuple-element.44), channel_id=1, source_target_pairs={{0,1},{1,2},{2,3},{3,4},{4,5},{5,6},{6,7},{8,9},{9,10},{10,11},{11... | collective-permute-start | bytes 589832 | tf_op jit(solution)/shard_map/ppermute | solution.py:713
  12.9 19.5 %collective-permute-start.3 = (f32[4,96,128]{2,1,0:T(8,128)}, f32[4,96,128]{2,1,0:T(8,128)S(1)}, u32[]{:S(2)}, u32[]{:S(2)}) collective-permute-start(f32[4,96,128]{2,1,0:T(8,128)} %get-tuple-element.45), channel_id=1, source_target_pairs={{1,0},{2,1},{3,2},{4,3},{5,4},{6,5},{7,6},{9,8},{10,9},{11,10},{12... | collective-permute-start | bytes 589832 | tf_op jit(solution)/shard_map/ppermute | solution.py:713
  35.2 10.8 %all-to-all-start.1 = ((bf16[32,16,128]{2,1,0:T(8,128)(2,1)}), bf16[32,16,128]{2,1,0:T(8,128)(2,1)S(1)}, u32[]{:S(2)}, u32[]{:S(2)}) async-start(bf16[32,16,128]{2,1,0:T(8,128)(2,1)} %bitcast.27), calls=%async_computation.1 | async-start | bytes 262144 | tf_op jit(solution)/shard_map/all_to_all | solution.py:717
  37.8 8.2 %copy-start = (s32[8,128]{1,0:T(8,128)S(1)}, s32[8,128]{1,0:T(8,128)}, u32[]{:S(2)}) copy-start(s32[8,128]{1,0:T(8,128)} %get-tuple-element.39.meta_ref) | copy-start | bytes 12292
  51.6 15.4 %all-to-all-start.2 = ((f32[32,1,2176]{2,1,0:T(1,128)}), f32[32,1,2176]{2,1,0:T(1,128)S(1)}, u32[]{:S(2)}, u32[]{:S(2)}) async-start(f32[32,1,2176]{2,1,0:T(1,128)} %bitcast.28), calls=%async_computation.2 | async-start | bytes 557056 | tf_op jit(solution)/shard_map/all_to_all | solution.py:717
  68.2 9.6 %all-to-all-start.3 = ((f32[32,1,128]{2,1,0:T(1,128)}), f32[32,1,128]{2,1,0:T(1,128)S(1)}, u32[]{:S(2)}, u32[]{:S(2)}) async-start(f32[32,1,128]{2,1,0:T(1,128)} %bitcast.29), calls=%async_computation.3 | async-start | bytes 32768 | tf_op jit(solution)/shard_map/all_to_all | solution.py:717

commit v11 on v9

--- a/solution.py
+++ b/solution.py
@@ -159,6 +159,7 @@
     for copy in copies:
         copy.wait()
     listed = ids.astype(F32)
+    asking_ref[...] = jnp.zeros(asking_ref.shape, F32)
     corners = [
         [slabs[k % 2, r, (k // 2) * last, (k % 2) * 7 : (k % 2) * 7 + 1] for r in range(systems)]
         for k in range(4)
@@ -396,22 +397,28 @@
         row = place(row, systems + r, jnp.sum(image_sq, keepdims=True))
         return place(row, 2 * systems + r, jnp.sum(cross, keepdims=True))
 
-    sums_out[...] = lax.fori_loop(0, systems, system, sums_ref[...])
+    row = lax.fori_loop(0, systems, system, sums_ref[...])
+    sums_out[...] = place(row, depth - 1, corner.astype(F32))
     for r in range(systems):
         outgoing(r).wait()
 
 
 def rays_body(
-    cap, blocks, meta_ref, rec_ref, tiles_in, held_ref, fetched_ref, old_ref, sums_ref, bar_ref, term_ref, rest_ref, masks, lows, sems
+    cap, blocks, meta_ref, held_ref, fetched_ref, tiles_in, *refs
 ):
+    rec_in, old_in, sums_in, bar_ref, term_ref, rest_ref, masks, lows, rec_ref, old_ref, sums_ref, sems = refs
     tiles, width, depth = tiles_in.shape[2:]
+    small = [
+        pltpu.make_async_copy(a, b, sems.at[PARTS + k])
+        for k, (a, b) in enumerate(((rec_in, rec_ref), (old_in, old_ref), (sums_in, sums_ref)))
+    ]
     part = -(-(tiles - HELD) // PARTS)
     copies = []
     for k in range(PARTS):
         count = min(part, tiles - HELD - k * part)
         source = tiles_in.at[0, 0, pl.ds(HELD + k * part, count)]
         copies.append(pltpu.make_async_copy(source, rest_ref.at[pl.ds(k * part, count)], sems.at[k]))
-    for copy in copies:
+    for copy in copies + small:
         copy.start()
 
     def tile(t):
@@ -438,6 +445,8 @@
         total = total + lax.dot_general(
             left, tile(t), (((1,), (1,)), ((), ())), preferred_element_type=F32
         )
+    for copy in small:
+        copy.wait()
     square = jnp.zeros((systems, width), F32)
     for b in range(blocks):
         traced = jnp.zeros((systems, width), F32)
@@ -485,7 +494,8 @@
     added = three[:, 0:depth] + (three[:, depth : 2 * depth] + three[:, 2 * depth :])
     added_ref[...] = added
     every = terms_ref[pl.ds(chunk - 1, devices, stride=chunk), :]
-    residual_ref[...] = jnp.sum(every, axis=0, keepdims=True)
+    total = jnp.sum(every, axis=0, keepdims=True)
+    residual_ref[...] = jnp.where(iota(total.shape, 1) == depth - 1, sums_ref[...], total)
     square = added * (2.0 * patch_ref[...] + added)
     cross = added * model_patch_ref[...]
     row = sums_ref[...]
@@ -568,28 +578,32 @@
     rows_all,
     cells_all,
     clon,
-    corner_ref,
     residual_ref,
     parts_ref,
-    rec_ref,
     added_ref,
     kept_ref,
     image_in,
     model_in,
     search_in,
+    rec_in,
     model_out,
     search_out,
-    rec_out,
+    rec_sent,
     image_ref,
     model_ref,
     search_ref,
     model_s,
     search_s,
+    rec_ref,
+    rec_out,
     coef,
     in_sems,
     sems,
+    rec_sems,
 ):
-    systems, columns, _ = image_ref.shape
+    systems, columns, depth = image_ref.shape
+    rec_copy = pltpu.make_async_copy(rec_in, rec_ref, rec_sems.at[0])
+    rec_copy.start()
     rows = columns // PIECES
     kept = kept_ref.shape[0]
     ins = ((image_in, image_ref), (model_in, model_ref))
@@ -609,7 +623,9 @@
 
     for n in range(AHEAD):
         start(n)
+    corner = residual_ref[0, depth - 1].astype(I32)
     total = jnp.sum(parts_ref[...], axis=0, keepdims=True)
+    rec_copy.wait()
     image_sq, cross, model_sq = (total[:, q * systems : (q + 1) * systems] for q in range(1, 4))
     rho_bar, phi_bar = rec_ref[1:2], rec_ref[2:3]
     beta = first_norm(residual_ref, systems, rows_all)
@@ -619,6 +635,8 @@
     cosine = rho_bar / rho
     sine = beta / rho
     rec_out[...] = jnp.concatenate([alpha, -cosine * alpha, sine * phi_bar], axis=0)
+    rec_done = pltpu.make_async_copy(rec_out, rec_sent, rec_sems.at[1])
+    rec_done.start()
     scales = (1.0 / (beta * alpha), beta / alpha, sine * alpha / rho)
     for q, scale in enumerate(scales):
         for s in range(systems):
@@ -635,7 +653,7 @@
         model_s[r, at, :] = new
         search_s[r, at, :] = new - search * coef[2, r]
         for k in range(PATCH):
-            first = (corner_ref[0] + k) * clon
+            first = (corner + k) * clon
 
             @pl.when((first >= p * rows) & (first < (p + 1) * rows))
             def _():
@@ -647,6 +665,7 @@
         begin(pieces(outs, sems, r, p, rows))
 
     wait_all(outs, sems, systems, rows)
+    rec_done.wait()
 
 
 PIECES = 2
@@ -731,7 +750,7 @@
     asking, north_msg, south_msg, east_msg, west_msg, meta = call(
         functools.partial(flanks_body, columns.bit_length() - 1, blocks),
         "flanks",
-        (there((devices, 1, (1 + systems) * depth), F32), band, band, side, side, there((8, lanes), I32)),
+        (there((devices, 1, 2 * systems * depth), F32), band, band, side, side, there((8, lanes), I32)),
         [vmem()] * 3 + [hbm(), hbm()],
         (vmem(),) * 6,
         scratch=[pltpu.VMEM((4, systems, clat, 8, depth), F32), dma((8,))],
@@ -783,17 +802,20 @@
         functools.partial(rays_body, cap, blocks),
         "rays",
         (there(ray_vector.shape, F32), there((devices * chunk, 1, depth), F32)),
-        [smem(), vmem(), hbm()] + [vmem()] * 4,
+        [smem(), vmem(), vmem()] + [hbm()] * 4,
         (vmem(), vmem()),
         scratch=[
             pltpu.VMEM((tiles - HELD, width, depth), BF16),
             pltpu.VMEM((cap + 1, group, depth), BF16),
             pltpu.VMEM((blocks + 1, 16, width), BF16),
-            dma((PARTS,)),
+            pltpu.VMEM(recurrence.shape, F32),
+            pltpu.VMEM(ray_vector.shape, F32),
+            pltpu.VMEM((1, lanes), F32),
+            dma((PARTS + 3,)),
         ],
         flops=4 * tiles * width * depth * 16,
         moved=2 * tiles * width * depth,
-    )(meta, far(recurrence), far(sensitivity), near(held), fetched, far(ray_vector), far(sums))
+    )(meta, near(held), fetched, far(sensitivity), far(recurrence), far(ray_vector), far(sums))
     arrived = exchange(terms.reshape(devices, 1, chunk * depth)).reshape(devices * chunk, depth)
 
     padded = -(-devices * chunk // lanes) * lanes
@@ -845,16 +867,17 @@
         functools.partial(finish_body, float(rows_all), float(cells_all), clon),
         "finish",
         (there(flat, F32), there(flat, F32), there(recurrence.shape, F32)),
-        [smem()] + [vmem()] * 5 + [hbm()] * 3,
-        (hbm(), hbm(), vmem()),
+        [vmem()] * 4 + [hbm()] * 4,
+        (hbm(),) * 3,
         scratch=[pltpu.VMEM(flat, F32)] * 2
         + [pltpu.VMEM((1, columns, depth), F32)]
         + [pltpu.VMEM(flat, F32)] * 2
-        + [pltpu.SMEM((3, systems), F32), dma((systems, PIECES, 3)), dma((systems, PIECES, 2))],
+        + [pltpu.VMEM(recurrence.shape, F32)] * 2
+        + [pltpu.SMEM((3, systems), F32), dma((systems, PIECES, 3)), dma((systems, PIECES, 2)), dma((2,))],
         mib=32,
         flops=6 * systems * columns * depth,
         moved=20 * systems * columns * depth,
-    )(corner, residual, every, far(recurrence), added, near(kept), far(image), model_flat, search_flat)
+    )(residual, every, added, near(kept), far(image), model_flat, search_flat, far(recurrence))
     fields = (x.reshape(full) for x in (damp_out, model_out, solution_out, search_out))
     return (ray_out, *fields, rec_out)
 

time: 84.3 us -> 83.3 us (0.988)
  blocking collectives: 17.3 us -> 0 us
  starting transfers between devices: 18.4 us -> 31.6 us
  waiting for transfers between devices: 7.14 us -> 11.5 us
  Pallas kernels: 38.5 us -> 37.3 us
    all_to_all x1 -> x0, blocking collectives: 17.3 us -> none  [exchange(): return lax.all_to_all(x, AXES, split_axis=0, concat_axis=0, tiled=True)]
    all_to_all x3 -> x4, starting transfers between devices: 9.38 us -> 23.6 us  [exchange(): return lax.all_to_all(x, AXES, split_axis=0, concat_axis=0, tiled=True)]
    ppermute x4, waiting for transfers between devices: 0.01 us -> 4.39 us  [shifted(): return lax.ppermute(x, axis, pairs)]
    pallas_call x1, Pallas kernels: 6.75 us -> 5.51 us  [per_device(): call(functools.partial(finish_body, float(rows_all), float(cells_all), cl...]
    ppermute x4, starting transfers between devices: 8.99 us -> 8.05 us  [shifted(): return lax.ppermute(x, axis, pairs)]
    all_to_all x3 -> x4, waiting for transfers between devices: 7.13 us -> 7.12 us  [exchange(): return lax.all_to_all(x, AXES, split_axis=0, concat_axis=0, tiled=True)]
  transfers between devices with their start and end apart: 7 -> 8, of which waited for: 3 -> 5; matrix products, arithmetic and copies ran while one was open for 0% -> 0% of each run, Pallas kernels for 23% -> 23%
where the time goes in v11:
time: 83.3 us; the launch traced here: 82.5 us
  Pallas kernels  37.3 us (45%)
  starting transfers between devices  31.6 us (38%)
  waiting for transfers between devices  11.5 us (14%)
  between operations  1.41 us (2%)
    all_to_all x4, starting transfers between devices, exchange(): return lax.all_to_all(x, AXES, split_axis=0, concat_axis=0, tiled=True)  23.6 us
    ppermute x4, starting transfers between devices, shifted(): return lax.ppermute(x, axis, pairs)  8.05 us
    all_to_all x4, waiting for transfers between devices, exchange(): return lax.all_to_all(x, AXES, split_axis=0, concat_axis=0, tiled=True)  7.12 us
    pallas_call x1, Pallas kernels, per_device(): call(functools.partial(damp_body, clat, clon), 'damp', (there(flat, F32),...  6.59 us
    pallas_call x1, Pallas kernels, per_device(): call(functools.partial(image_body, chunk, clat, clon), 'image', (there(fl...  6.37 us
    pallas_call x1, Pallas kernels, per_device(): call(functools.partial(early_body, float(rows_all)), 'early', (there(ray_...  6.29 us
    pallas_call x1, Pallas kernels, per_device(): call(functools.partial(rays_body, cap, blocks), 'rays', (there(ray_vector...  5.53 us
    pallas_call x1, Pallas kernels, per_device(): call(functools.partial(finish_body, float(rows_all), float(cells_all), cl...  5.51 us
  transfers between devices with their start and end apart: 8, of which 5 were waited for; matrix products, arithmetic and copies ran while one was open for 0% of the time, Pallas kernels for 23%

profile of v11, /device:TPU:0, one launch (start us, length us, event | category | flops | bytes accessed | tf_op | source)
XLA Modules:
  0.0 82.5 jit_solution(8078378123956877966)
XLA Ops:
  1.3 0.0 copy-start.1
  1.3 0.6 copy-done.1
  1.9 3.3 %flanks.1 = (f32[32,1,1024]{2,1,0:T(1,128)}, f32[4,3,32,128]{3,2,1,0:T(8,128)}, f32[4,3,32,128]{3,2,1,0:T(8,128)}, f32[4,96,128]{2,1,0:T(8,128)}, f32[4,96,128]{2,1,0:T(8,128)}, /*index=5*/s32[8,128]{1,0:T(8,128)}) custom-call(s32[1,1,60]{2,1,0:T(1,128)} %ids_ref.1, s32[1,1,4]{2,1,0:T(1,128)S(1)} %copy-done.1, s32[1,1]{1,0:T(1,128)S(6)} %copy.18.count_ref, ...), custom_call_target="tpu_custom_call" | custom-call | flops 1 | bytes 2097152 | tf_op jit(solution)/shard_map/flanks/pallas_call | solution.py:750
  5.2 7.3 %all-to-all-start = ((f32[32,1,1024]{2,1,0:T(1,128)}), f32[32,1,1024]{2,1,0:T(1,128)S(1)}, u32[]{:S(2)}, u32[]{:S(2)}) async-start(f32[32,1,1024]{2,1,0:T(1,128)} %get-tuple-element.41), calls=%async_computation | async-start | bytes 262144 | tf_op jit(solution)/shard_map/all_to_all | solution.py:713
  12.5 3.7 %collective-permute-start = (f32[4,3,32,128]{3,2,1,0:T(8,128)}, f32[4,3,32,128]{3,2,1,0:T(8,128)S(1)}, u32[]{:S(2)}, u32[]{:S(2)}) collective-permute-start(f32[4,3,32,128]{3,2,1,0:T(8,128)} %get-tuple-element.42), channel_id=1, source_target_pairs={{0,8},{8,16},{16,24},{1,9},{9,17},{17,25},{2,10},{10,18},{18,26},{... | collective-permute-start | bytes 589832 | tf_op jit(solution)/shard_map/ppermute | solution.py:709
  16.2 1.3 %collective-permute-start.1 = (f32[4,3,32,128]{3,2,1,0:T(8,128)}, f32[4,3,32,128]{3,2,1,0:T(8,128)S(1)}, u32[]{:S(2)}, u32[]{:S(2)}) collective-permute-start(f32[4,3,32,128]{3,2,1,0:T(8,128)} %get-tuple-element.43), channel_id=1, source_target_pairs={{8,0},{16,8},{24,16},{9,1},{17,9},{25,17},{10,2},{18,10},{26,18},{... | collective-permute-start | bytes 589832 | tf_op jit(solution)/shard_map/ppermute | solution.py:709
  17.5 1.8 %collective-permute-start.2 = (f32[4,96,128]{2,1,0:T(8,128)}, f32[4,96,128]{2,1,0:T(8,128)S(1)}, u32[]{:S(2)}, u32[]{:S(2)}) collective-permute-start(f32[4,96,128]{2,1,0:T(8,128)} %get-tuple-element.44), channel_id=1, source_target_pairs={{0,1},{1,2},{2,3},{3,4},{4,5},{5,6},{6,7},{8,9},{9,10},{10,11},{11... | collective-permute-start | bytes 589832 | tf_op jit(solution)/shard_map/ppermute | solution.py:709
  19.3 1.3 %collective-permute-start.3 = (f32[4,96,128]{2,1,0:T(8,128)}, f32[4,96,128]{2,1,0:T(8,128)S(1)}, u32[]{:S(2)}, u32[]{:S(2)}) collective-permute-start(f32[4,96,128]{2,1,0:T(8,128)} %get-tuple-element.45), channel_id=1, source_target_pairs={{1,0},{2,1},{3,2},{4,3},{5,4},{6,5},{7,6},{9,8},{10,9},{11,10},{12... | collective-permute-start | bytes 589832 | tf_op jit(solution)/shard_map/ppermute | solution.py:709
  20.6 0.4 collective-permute-done.north.north_ref
  21.0 4.0 %collective-permute-done.1.south.south_ref = f32[4,3,32,128]{3,2,1,0:T(8,128)S(1)} collective-permute-done((f32[4,3,32,128]{3,2,1,0:T(8,128)}, f32[4,3,32,128]{3,2,1,0:T(8,128)S(1)}, u32[]{:S(2)}, u32[]{:S(2)}) %collective-permute-start.1) | collective-permute-done | bytes 196640 | tf_op jit(solution)/shard_map/ppermute | solution.py:709
  25.0 0.0 collective-permute-done.2.west.west_ref
  25.0 0.0 collective-permute-done.3.east.east_ref
  25.0 0.0 all-to-all-done.lists_ref
  25.0 2.4 %serve.1 = (bf16[512,128]{1,0:T(8,128)(2,1)}, f32[32,128]{1,0:T(8,128)S(1)}, s32[1]{0:T(128)}, f32[16,128]{1,0:T(8,128)S(1)}) custom-call(f32[32,1,1024]{2,1,0:T(1,128)S(1)} %all-to-all-done.lists_ref, f32[4,1024,128]{2,1,0:T(8,128)} %bitcast.19, f32[4,3,32,128]{3,2,1,0:T(8,128)S(1)} %collective-permute-done.north.north_ref, ...), custom_call_target="tpu_custom_call" | custom-call | tf_op jit(solution)/shard_map/serve/pallas_call | solution.py:766
  27.4 9.5 %all-to-all-start.1 = ((bf16[32,16,128]{2,1,0:T(8,128)(2,1)}), bf16[32,16,128]{2,1,0:T(8,128)(2,1)S(1)}, u32[]{:S(2)}, u32[]{:S(2)}) async-start(bf16[32,16,128]{2,1,0:T(8,128)(2,1)} %bitcast.28), calls=%async_computation.1 | async-start | bytes 262144 | tf_op jit(solution)/shard_map/all_to_all | solution.py:713
  36.9 0.0 copy-start
  36.9 6.6 %damp.1 = (f32[4,1024,128]{2,1,0:T(8,128)}, bf16[30,256,128]{2,1,0:T(8,128)(2,1)S(1)}, f32[4,32,128]{2,1,0:T(8,128)}, f32[4,32,128]{2,1,0:T(8,128)}, f32[4,32,12...) custom-call(f32[3,4]{1,0:T(4,128)} %rec_in.1, f32[16,128]{1,0:T(8,128)S(1)} %get-tuple-element.46.diagonal_ref, ...), custom_call_target="tpu_custom_call" | custom-call | flops 10485760 | bytes 6291456 | tf_op jit(solution)/shard_map/damp/pallas_call | solution.py:782
  43.5 1.6 %all-to-all-done.1 = bf16[32,16,128]{2,1,0:T(8,128)(2,1)S(1)} async-done(((bf16[32,16,128]{2,1,0:T(8,128)(2,1)}), bf16[32,16,128]{2,1,0:T(8,128)(2,1)S(1)}, u32[]{:S(2)}, u32[]{:S(2)}) %all-to-all-start.1) | async-done | bytes 131104 | tf_op jit(solution)/shard_map/all_to_all | solution.py:713
  45.2 0.0 copy-done
  45.2 5.5 %rays.1 = (f32[4,1,1,768]{3,2,1,0:T(1,128)}, f32[544,1,128]{2,1,0:T(1,128)}) custom-call(s32[8,128]{1,0:T(8,128)S(1)} %copy-done, bf16[30,256,128]{2,1,0:T(8,128)(2,1)S(1)} %get-tuple-element.47.held_ref, bf16[512,128]{1,0:T(8,128)(2,1)S(1)} %bitcast.17, bf16[1,1,60,256,128]{4,3,2,1,0:T(8,128)(2,1)} %tiles_in.3, f32[3,4]{1,0:T(4,128)} %rec_in.1, ...), custom_call_target="tpu_custom_call" | custom-call | flops 125829120 | bytes 3932160 | tf_op jit(solution)/shard_map/rays/pallas_call | solution.py:801
  50.7 4.2 %all-to-all-start.2 = ((f32[32,1,2176]{2,1,0:T(1,128)}), f32[32,1,2176]{2,1,0:T(1,128)S(1)}, u32[]{:S(2)}, u32[]{:S(2)}) async-start(f32[32,1,2176]{2,1,0:T(1,128)} %bitcast.27), calls=%async_computation.2 | async-start | bytes 557056 | tf_op jit(solution)/shard_map/all_to_all | solution.py:713
  55.0 6.4 %image.1 = (f32[4,1024,128]{2,1,0:T(8,128)}, f32[1,128]{1,0:T(1,128)S(1)}, f32[512,128]{1,0:T(8,128)S(1)}, f32[512,128]{1,0:T(8,128)S(1)}, bf16[512,640]{1,0:T(8,128)(2,1)S(1)}) custom-call(s32[1]{0:T(128)} %get-tuple-element.51.corner_ref, f32[32,128]{1,0:T(8,128)S(1)} %get-tuple-element.52.wanted_ref, f32[4,1024,128]{2,1,0:T(8,128)} %get-tuple-element.53.bar_in, ...), custom_call_target="tpu_custom_call" | custom-call | flops 10485760 | bytes 6291456 | tf_op jit(solution)/shard_map/image/pallas_call | solution.py:824
  61.3 4.7 %all-to-all-done.2 = f32[32,1,2176]{2,1,0:T(1,128)S(1)} async-done(((f32[32,1,2176]{2,1,0:T(1,128)}), f32[32,1,2176]{2,1,0:T(1,128)S(1)}, u32[]{:S(2)}, u32[]{:S(2)}) %all-to-all-start.2) | async-done | bytes 278560 | tf_op jit(solution)/shard_map/all_to_all | solution.py:713
  66.0 1.3 %combine.1 = (f32[512,128]{1,0:T(8,128)S(1)}, f32[1,128]{1,0:T(1,128)S(1)}, f32[32,128]{1,0:T(8,128)}) custom-call(f32[544,128]{1,0:T(8,128)S(1)} %bitcast.16, bf16[512,640]{1,0:T(8,128)(2,1)S(1)} %get-tuple-element.58.chosen_ref, f32[512,128]{1,0:T(8,128)S(1)} %get-tuple-element.59.patch_ref, f32[512,128]{1,0:T(8,128)S(1)} %get-tuple-element.60.model_patch_ref, ...), custom_call_target="tpu_custom_call" | custom-call | tf_op jit(solution)/shard_map/combine/pallas_call | solution.py:841
  67.4 2.5 %all-to-all-start.3 = ((f32[32,1,128]{2,1,0:T(1,128)}), f32[32,1,128]{2,1,0:T(1,128)S(1)}, u32[]{:S(2)}, u32[]{:S(2)}) async-start(f32[32,1,128]{2,1,0:T(1,128)} %bitcast.29), calls=%async_computation.3 | async-start | bytes 32768 | tf_op jit(solution)/shard_map/all_to_all | solution.py:713
  69.9 6.3 %early.1 = (f32[4,1,1,768]{3,2,1,0:T(1,128)}, f32[4,1024,128]{2,1,0:T(8,128)}, f32[4,1024,128]{2,1,0:T(8,128)}, f32[3,1024,128]{2,1,0:T(8,128)S(1)}) custom-call(f32[1,128]{1,0:T(1,128)S(1)} %get-tuple-element.62.residual_ref, f32[3,4]{1,0:T(4,128)} %rec_in.1, f32[4,1,1,768]{3,2,1,0:T(1,128)} %get-tuple-element.63.ray_ref, ...), custom_call_target="tpu_custom_call" | custom-call | flops 2097152 | bytes 10485760 | tf_op jit(solution)/shard_map/early/pallas_call | solution.py:852
  76.2 0.8 all-to-all-done.3
  77.0 5.5 %finish.1 = (f32[4,1024,128]{2,1,0:T(8,128)}, f32[4,1024,128]{2,1,0:T(8,128)}, f32[3,4]{1,0:T(4,128)}) custom-call(f32[1,128]{1,0:T(1,128)S(1)} %get-tuple-element.62.residual_ref, f32[32,128]{1,0:T(8,128)S(1)} %bitcast.18, f32[512,128]{1,0:T(8,128)S(1)} %get-tuple-element.67.added_ref, f32[3,1024,128]{2,1,0:T(8,128)S(1)} %get-tuple-element.68.kept_ref, ...), custom_call_target="tpu_custom_call" | custom-call | flops 3145728 | bytes 10485760 | tf_op jit(solution)/shard_map/finish/pallas_call | solution.py:866
Async XLA Ops:
  1.3 0.7 copy-start.1
  5.2 19.8 %all-to-all-start = ((f32[32,1,1024]{2,1,0:T(1,128)}), f32[32,1,1024]{2,1,0:T(1,128)S(1)}, u32[]{:S(2)}, u32[]{:S(2)}) async-start(f32[32,1,1024]{2,1,0:T(1,128)} %get-tuple-element.41), calls=%async_computation | async-start | bytes 262144 | tf_op jit(solution)/shard_map/all_to_all | solution.py:713
  12.5 8.5 %collective-permute-start = (f32[4,3,32,128]{3,2,1,0:T(8,128)}, f32[4,3,32,128]{3,2,1,0:T(8,128)S(1)}, u32[]{:S(2)}, u32[]{:S(2)}) collective-permute-start(f32[4,3,32,128]{3,2,1,0:T(8,128)} %get-tuple-element.42), channel_id=1, source_target_pairs={{0,8},{8,16},{16,24},{1,9},{9,17},{17,25},{2,10},{10,18},{18,26},{... | collective-permute-start | bytes 589832 | tf_op jit(solution)/shard_map/ppermute | solution.py:709
  16.2 8.8 %collective-permute-start.1 = (f32[4,3,32,128]{3,2,1,0:T(8,128)}, f32[4,3,32,128]{3,2,1,0:T(8,128)S(1)}, u32[]{:S(2)}, u32[]{:S(2)}) collective-permute-start(f32[4,3,32,128]{3,2,1,0:T(8,128)} %get-tuple-element.43), channel_id=1, source_target_pairs={{8,0},{16,8},{24,16},{9,1},{17,9},{25,17},{10,2},{18,10},{26,18},{... | collective-permute-start | bytes 589832 | tf_op jit(solution)/shard_map/ppermute | solution.py:709
  17.5 7.5 %collective-permute-start.2 = (f32[4,96,128]{2,1,0:T(8,128)}, f32[4,96,128]{2,1,0:T(8,128)S(1)}, u32[]{:S(2)}, u32[]{:S(2)}) collective-permute-start(f32[4,96,128]{2,1,0:T(8,128)} %get-tuple-element.44), channel_id=1, source_target_pairs={{0,1},{1,2},{2,3},{3,4},{4,5},{5,6},{6,7},{8,9},{9,10},{10,11},{11... | collective-permute-start | bytes 589832 | tf_op jit(solution)/shard_map/ppermute | solution.py:709
  19.3 5.7 %collective-permute-start.3 = (f32[4,96,128]{2,1,0:T(8,128)}, f32[4,96,128]{2,1,0:T(8,128)S(1)}, u32[]{:S(2)}, u32[]{:S(2)}) collective-permute-start(f32[4,96,128]{2,1,0:T(8,128)} %get-tuple-element.45), channel_id=1, source_target_pairs={{1,0},{2,1},{3,2},{4,3},{5,4},{6,5},{7,6},{9,8},{10,9},{11,10},{12... | collective-permute-start | bytes 589832 | tf_op jit(solution)/shard_map/ppermute | solution.py:709
  27.4 17.7 %all-to-all-start.1 = ((bf16[32,16,128]{2,1,0:T(8,128)(2,1)}), bf16[32,16,128]{2,1,0:T(8,128)(2,1)S(1)}, u32[]{:S(2)}, u32[]{:S(2)}) async-start(bf16[32,16,128]{2,1,0:T(8,128)(2,1)} %bitcast.28), calls=%async_computation.1 | async-start | bytes 262144 | tf_op jit(solution)/shard_map/all_to_all | solution.py:713
  36.9 8.2 %copy-start = (s32[8,128]{1,0:T(8,128)S(1)}, s32[8,128]{1,0:T(8,128)}, u32[]{:S(2)}) copy-start(s32[8,128]{1,0:T(8,128)} %get-tuple-element.40.meta_ref) | copy-start | bytes 12292
  50.7 15.3 %all-to-all-start.2 = ((f32[32,1,2176]{2,1,0:T(1,128)}), f32[32,1,2176]{2,1,0:T(1,128)S(1)}, u32[]{:S(2)}, u32[]{:S(2)}) async-start(f32[32,1,2176]{2,1,0:T(1,128)} %bitcast.27), calls=%async_computation.2 | async-start | bytes 557056 | tf_op jit(solution)/shard_map/all_to_all | solution.py:713
  67.4 9.6 %all-to-all-start.3 = ((f32[32,1,128]{2,1,0:T(1,128)}), f32[32,1,128]{2,1,0:T(1,128)S(1)}, u32[]{:S(2)}, u32[]{:S(2)}) async-start(f32[32,1,128]{2,1,0:T(1,128)} %bitcast.29), calls=%async_computation.3 | async-start | bytes 32768 | tf_op jit(solution)/shard_map/all_to_all | solution.py:713

commit v12 on v11

--- a/solution.py
+++ b/solution.py
@@ -63,7 +63,7 @@
     return jnp.sum(jnp.where(pick, spread, 0.0), axis=1, keepdims=True)
 
 
-def serve_body(cap, clat, clon, lists_ref, model_in, north, south, west, east, served_ref, wanted_ref, corner_ref, diagonal_ref, patch, mixed, sems):
+def serve_body(cap, clat, clon, lists_ref, model_in, served_ref, wanted_ref, corner_ref, diagonal_ref, patch, mixed, sems):
     systems, width, depth = patch.shape
     devices = lists_ref.shape[0]
     lanes = 128
@@ -772,10 +772,10 @@
             plain((1,), I32),
             plain((4 * systems, depth), F32),
         ),
-        [vmem(), hbm()] + [pl.BlockSpec(memory_space=pl.ANY)] * 4,
+        [vmem(), hbm()],
         (vmem(), vmem(), smem(), vmem()),
         scratch=[pltpu.VMEM(lines, F32), pltpu.VMEM((slots * systems, depth), F32), dma((systems,))],
-    )(lists, model_flat, north, south, west, east)
+    )(lists, model_flat)
     fetched = exchange(served.reshape(devices, group, depth)).reshape(slots * systems, depth)
 
     edge, flank = there((systems, clon, depth), F32), there((systems, clat, depth), F32)
@@ -795,7 +795,7 @@
         (hbm(),) + (vmem(),) * 6,
         scratch=[pltpu.VMEM(flat, F32)] * 3 + [pltpu.SMEM((systems,), F32), dma((systems, 3)), dma],
         flops=20 * systems * columns * depth,
-        moved=12 * systems * columns * depth,
+        moved=128 * systems * columns * depth,
     )(far(recurrence), diagonal, model_flat, damping_flat, north, south, west, east, far(sensitivity))
 
     ray_bar, terms = call(

time: 83.3 us -> 88.1 us (1.058)
  blocking collectives: 0 us -> 15.5 us
  starting transfers between devices: 31.6 us -> 22.7 us
  waiting for transfers between devices: 11.5 us -> 9.67 us
    all_to_all x0 -> x1, blocking collectives: none -> 15.5 us  [exchange(): return lax.all_to_all(x, AXES, split_axis=0, concat_axis=0, tiled=True)]
    all_to_all x4 -> x3, starting transfers between devices: 23.6 us -> 14.7 us  [exchange(): return lax.all_to_all(x, AXES, split_axis=0, concat_axis=0, tiled=True)]
    all_to_all x4 -> x3, waiting for transfers between devices: 7.12 us -> 5.51 us  [exchange(): return lax.all_to_all(x, AXES, split_axis=0, concat_axis=0, tiled=True)]
  transfers between devices with their start and end apart: 8 -> 7, of which waited for: 5 -> 3; matrix products, arithmetic and copies ran while one was open for 0% -> 0% of each run, Pallas kernels for 23% -> 22%
where the time goes in v12:
time: 88.1 us; the launch traced here: 87.4 us
  Pallas kernels  37.3 us (42%)
  starting transfers between devices  22.7 us (26%)
  blocking collectives  15.5 us (18%)
  waiting for transfers between devices  9.67 us (11%)
  between operations  1.48 us (2%)
    all_to_all x1, blocking collectives, exchange(): return lax.all_to_all(x, AXES, split_axis=0, concat_axis=0, tiled=True)  15.5 us
    all_to_all x3, starting transfers between devices, exchange(): return lax.all_to_all(x, AXES, split_axis=0, concat_axis=0, tiled=True)  14.7 us
    ppermute x4, starting transfers between devices, shifted(): return lax.ppermute(x, axis, pairs)  7.97 us
    pallas_call x1, Pallas kernels, per_device(): call(functools.partial(damp_body, clat, clon), 'damp', (there(flat, F32),...  6.59 us
    pallas_call x1, Pallas kernels, per_device(): call(functools.partial(image_body, chunk, clat, clon), 'image', (there(fl...  6.36 us
    pallas_call x1, Pallas kernels, per_device(): call(functools.partial(early_body, float(rows_all)), 'early', (there(ray_...  6.29 us
    pallas_call x1, Pallas kernels, per_device(): call(functools.partial(rays_body, cap, blocks), 'rays', (there(ray_vector...  5.54 us
    pallas_call x1, Pallas kernels, per_device(): call(functools.partial(finish_body, float(rows_all), float(cells_all), cl...  5.53 us
  transfers between devices with their start and end apart: 7, of which 3 were waited for; matrix products, arithmetic and copies ran while one was open for 0% of the time, Pallas kernels for 22%

profile of v12, /device:TPU:0, one launch (start us, length us, event | category | flops | bytes accessed | tf_op | source)
XLA Modules:
  0.0 87.4 jit_solution(13858506992022842003)
XLA Ops:
  1.3 0.0 copy-start.1
  1.3 0.6 copy-done.1
  1.9 3.3 %flanks.1 = (f32[32,1,1024]{2,1,0:T(1,128)}, f32[4,3,32,128]{3,2,1,0:T(8,128)}, f32[4,3,32,128]{3,2,1,0:T(8,128)}, f32[4,96,128]{2,1,0:T(8,128)}, f32[4,96,128]{2,1,0:T(8,128)}, /*index=5*/s32[8,128]{1,0:T(8,128)}) custom-call(s32[1,1,60]{2,1,0:T(1,128)} %ids_ref.1, s32[1,1,4]{2,1,0:T(1,128)S(1)} %copy-done.1, s32[1,1]{1,0:T(1,128)S(6)} %copy.18.count_ref, ...), custom_call_target="tpu_custom_call" | custom-call | flops 1 | bytes 2097152 | tf_op jit(solution)/shard_map/flanks/pallas_call | solution.py:750
  5.2 0.0 copy-start.5
  5.2 0.0 copy-start.4
  5.2 0.0 copy-start.3
  5.3 0.0 copy-start.2
  5.3 15.5 %all_to_all.20.lists_ref = f32[32,1,1024]{2,1,0:T(1,128)S(1)} all-to-all(f32[32,1,1024]{2,1,0:T(1,128)} %get-tuple-element.41), channel_id=1, replica_groups=mesh['lat'=4,'lon'=8] {'lat','lon'}, dimensions={0} | all-to-all | bytes 262144 | tf_op jit(solution)/shard_map/all_to_all | solution.py:713
  20.8 2.4 %serve.1 = (bf16[512,128]{1,0:T(8,128)(2,1)}, f32[32,128]{1,0:T(8,128)S(1)}, s32[1]{0:T(128)}, f32[16,128]{1,0:T(8,128)S(1)}) custom-call(f32[32,1,1024]{2,1,0:T(1,128)S(1)} %all_to_all.20.lists_ref, f32[4,1024,128]{2,1,0:T(8,128)} %bitcast.19), custom_call_target="tpu_custom_call" | custom-call | tf_op jit(solution)/shard_map/serve/pallas_call | solution.py:766
  23.2 2.6 %all-to-all-start.1 = ((bf16[32,16,128]{2,1,0:T(8,128)(2,1)}), bf16[32,16,128]{2,1,0:T(8,128)(2,1)S(1)}, u32[]{:S(2)}, u32[]{:S(2)}) async-start(bf16[32,16,128]{2,1,0:T(8,128)(2,1)} %bitcast.28), calls=%async_computation.1 | async-start | bytes 262144 | tf_op jit(solution)/shard_map/all_to_all | solution.py:713
  25.8 0.0 copy-done.5
  25.8 3.6 %collective-permute-start = (f32[4,3,32,128]{3,2,1,0:T(8,128)S(1)}, f32[4,3,32,128]{3,2,1,0:T(8,128)S(1)}, u32[]{:S(2)}, u32[]{:S(2)}) collective-permute-start(f32[4,3,32,128]{3,2,1,0:T(8,128)S(1)} %copy-done.5), channel_id=1, source_target_pairs={{0,8},{8,16},{16,24},{1,9},{9,17},{17,25},{2,10},{10,18},{18,26},{... | collective-permute-start | bytes 589832 | tf_op jit(solution)/shard_map/ppermute | solution.py:709
  29.4 0.0 copy-done.4
  29.4 1.3 %collective-permute-start.1 = (f32[4,3,32,128]{3,2,1,0:T(8,128)S(1)}, f32[4,3,32,128]{3,2,1,0:T(8,128)S(1)}, u32[]{:S(2)}, u32[]{:S(2)}) collective-permute-start(f32[4,3,32,128]{3,2,1,0:T(8,128)S(1)} %copy-done.4), channel_id=1, source_target_pairs={{8,0},{16,8},{24,16},{9,1},{17,9},{25,17},{10,2},{18,10},{26,18},{... | collective-permute-start | bytes 589832 | tf_op jit(solution)/shard_map/ppermute | solution.py:709
  30.7 0.0 copy-done.3
  30.7 1.8 %collective-permute-start.2 = (f32[4,96,128]{2,1,0:T(8,128)S(1)}, f32[4,96,128]{2,1,0:T(8,128)S(1)}, u32[]{:S(2)}, u32[]{:S(2)}) collective-permute-start(f32[4,96,128]{2,1,0:T(8,128)S(1)} %copy-done.3), channel_id=1, source_target_pairs={{0,1},{1,2},{2,3},{3,4},{4,5},{5,6},{6,7},{8,9},{9,10},{10,11},{11... | collective-permute-start | bytes 589832 | tf_op jit(solution)/shard_map/ppermute | solution.py:709
  32.5 0.0 copy-done.2
  32.5 1.3 %collective-permute-start.3 = (f32[4,96,128]{2,1,0:T(8,128)S(1)}, f32[4,96,128]{2,1,0:T(8,128)S(1)}, u32[]{:S(2)}, u32[]{:S(2)}) collective-permute-start(f32[4,96,128]{2,1,0:T(8,128)S(1)} %copy-done.2), channel_id=1, source_target_pairs={{1,0},{2,1},{3,2},{4,3},{5,4},{6,5},{7,6},{9,8},{10,9},{11,10},{12... | collective-permute-start | bytes 589832 | tf_op jit(solution)/shard_map/ppermute | solution.py:709
  33.8 0.0 collective-permute-done.north_ref
  33.9 4.1 %collective-permute-done.1.south_ref = f32[4,3,32,128]{3,2,1,0:T(8,128)S(1)} collective-permute-done((f32[4,3,32,128]{3,2,1,0:T(8,128)S(1)}, f32[4,3,32,128]{3,2,1,0:T(8,128)S(1)}, u32[]{:S(2)}, u32[]{:S(2)}) %collective-permute-start.1) | collective-permute-done | bytes 196640 | tf_op jit(solution)/shard_map/ppermute | solution.py:709
  38.0 0.0 collective-permute-done.2.west_ref
  38.0 0.0 collective-permute-done.3.east_ref
  38.0 0.0 copy-start
  38.0 6.6 %damp.1 = (f32[4,1024,128]{2,1,0:T(8,128)}, bf16[30,256,128]{2,1,0:T(8,128)(2,1)S(1)}, f32[4,32,128]{2,1,0:T(8,128)}, f32[4,32,128]{2,1,0:T(8,128)}, f32[4,32,12...) custom-call(f32[3,4]{1,0:T(4,128)} %rec_in.1, f32[16,128]{1,0:T(8,128)S(1)} %get-tuple-element.42.diagonal_ref, ...), custom_call_target="tpu_custom_call" | custom-call | flops 10485760 | bytes 67108864 | tf_op jit(solution)/shard_map/damp/pallas_call | solution.py:782
  44.6 0.0 all-to-all-done.1
  44.6 0.0 copy-done
  44.6 5.5 %rays.1 = (f32[4,1,1,768]{3,2,1,0:T(1,128)}, f32[544,1,128]{2,1,0:T(1,128)}) custom-call(s32[8,128]{1,0:T(8,128)S(1)} %copy-done, bf16[30,256,128]{2,1,0:T(8,128)(2,1)S(1)} %get-tuple-element.47.held_ref, bf16[512,128]{1,0:T(8,128)(2,1)S(1)} %bitcast.17, bf16[1,1,60,256,128]{4,3,2,1,0:T(8,128)(2,1)} %tiles_in.3, f32[3,4]{1,0:T(4,128)} %rec_in.1, ...), custom_call_target="tpu_custom_call" | custom-call | flops 125829120 | bytes 3932160 | tf_op jit(solution)/shard_map/rays/pallas_call | solution.py:801
  50.2 9.6 %all-to-all-start.2 = ((f32[32,1,2176]{2,1,0:T(1,128)}), f32[32,1,2176]{2,1,0:T(1,128)S(1)}, u32[]{:S(2)}, u32[]{:S(2)}) async-start(f32[32,1,2176]{2,1,0:T(1,128)} %bitcast.27), calls=%async_computation.2 | async-start | bytes 557056 | tf_op jit(solution)/shard_map/all_to_all | solution.py:713
  59.8 6.4 %image.1 = (f32[4,1024,128]{2,1,0:T(8,128)}, f32[1,128]{1,0:T(1,128)S(1)}, f32[512,128]{1,0:T(8,128)S(1)}, f32[512,128]{1,0:T(8,128)S(1)}, bf16[512,640]{1,0:T(8,128)(2,1)S(1)}) custom-call(s32[1]{0:T(128)} %get-tuple-element.51.corner_ref, f32[32,128]{1,0:T(8,128)S(1)} %get-tuple-element.52.wanted_ref, f32[4,1024,128]{2,1,0:T(8,128)} %get-tuple-element.53.bar_in, ...), custom_call_target="tpu_custom_call" | custom-call | flops 10485760 | bytes 6291456 | tf_op jit(solution)/shard_map/image/pallas_call | solution.py:824
  66.2 4.7 %all-to-all-done.2 = f32[32,1,2176]{2,1,0:T(1,128)S(1)} async-done(((f32[32,1,2176]{2,1,0:T(1,128)}), f32[32,1,2176]{2,1,0:T(1,128)S(1)}, u32[]{:S(2)}, u32[]{:S(2)}) %all-to-all-start.2) | async-done | bytes 278560 | tf_op jit(solution)/shard_map/all_to_all | solution.py:713
  70.9 1.3 %combine.1 = (f32[512,128]{1,0:T(8,128)S(1)}, f32[1,128]{1,0:T(1,128)S(1)}, f32[32,128]{1,0:T(8,128)}) custom-call(f32[544,128]{1,0:T(8,128)S(1)} %bitcast.16, bf16[512,640]{1,0:T(8,128)(2,1)S(1)} %get-tuple-element.58.chosen_ref, f32[512,128]{1,0:T(8,128)S(1)} %get-tuple-element.59.patch_ref, f32[512,128]{1,0:T(8,128)S(1)} %get-tuple-element.60.model_patch_ref, ...), custom_call_target="tpu_custom_call" | custom-call | tf_op jit(solution)/shard_map/combine/pallas_call | solution.py:841
  72.2 2.5 %all-to-all-start.3 = ((f32[32,1,128]{2,1,0:T(1,128)}), f32[32,1,128]{2,1,0:T(1,128)S(1)}, u32[]{:S(2)}, u32[]{:S(2)}) async-start(f32[32,1,128]{2,1,0:T(1,128)} %bitcast.29), calls=%async_computation.3 | async-start | bytes 32768 | tf_op jit(solution)/shard_map/all_to_all | solution.py:713
  74.7 6.3 %early.1 = (f32[4,1,1,768]{3,2,1,0:T(1,128)}, f32[4,1024,128]{2,1,0:T(8,128)}, f32[4,1024,128]{2,1,0:T(8,128)}, f32[3,1024,128]{2,1,0:T(8,128)S(1)}) custom-call(f32[1,128]{1,0:T(1,128)S(1)} %get-tuple-element.62.residual_ref, f32[3,4]{1,0:T(4,128)} %rec_in.1, f32[4,1,1,768]{3,2,1,0:T(1,128)} %get-tuple-element.63.ray_ref, ...), custom_call_target="tpu_custom_call" | custom-call | flops 2097152 | bytes 10485760 | tf_op jit(solution)/shard_map/early/pallas_call | solution.py:852
  81.0 0.8 all-to-all-done.3
  81.8 5.5 %finish.1 = (f32[4,1024,128]{2,1,0:T(8,128)}, f32[4,1024,128]{2,1,0:T(8,128)}, f32[3,4]{1,0:T(4,128)}) custom-call(f32[1,128]{1,0:T(1,128)S(1)} %get-tuple-element.62.residual_ref, f32[32,128]{1,0:T(8,128)S(1)} %bitcast.18, f32[512,128]{1,0:T(8,128)S(1)} %get-tuple-element.67.added_ref, f32[3,1024,128]{2,1,0:T(8,128)S(1)} %get-tuple-element.68.kept_ref, ...), custom_call_target="tpu_custom_call" | custom-call | flops 3145728 | bytes 10485760 | tf_op jit(solution)/shard_map/finish/pallas_call | solution.py:866
Async XLA Ops:
  1.3 0.7 copy-start.1
  5.2 20.6 %copy-start.5 = (f32[4,3,32,128]{3,2,1,0:T(8,128)S(1)}, f32[4,3,32,128]{3,2,1,0:T(8,128)}, u32[]{:S(2)}) copy-start(f32[4,3,32,128]{3,2,1,0:T(8,128)} %get-tuple-element.43) | copy-start | bytes 589828
  5.2 24.2 %copy-start.4 = (f32[4,3,32,128]{3,2,1,0:T(8,128)S(1)}, f32[4,3,32,128]{3,2,1,0:T(8,128)}, u32[]{:S(2)}) copy-start(f32[4,3,32,128]{3,2,1,0:T(8,128)} %get-tuple-element.44) | copy-start | bytes 589828
  5.2 25.5 %copy-start.3 = (f32[4,96,128]{2,1,0:T(8,128)S(1)}, f32[4,96,128]{2,1,0:T(8,128)}, u32[]{:S(2)}) copy-start(f32[4,96,128]{2,1,0:T(8,128)} %get-tuple-element.45) | copy-start | bytes 589828
  5.3 27.3 %copy-start.2 = (f32[4,96,128]{2,1,0:T(8,128)S(1)}, f32[4,96,128]{2,1,0:T(8,128)}, u32[]{:S(2)}) copy-start(f32[4,96,128]{2,1,0:T(8,128)} %get-tuple-element.46) | copy-start | bytes 589828
  23.2 21.4 %all-to-all-start.1 = ((bf16[32,16,128]{2,1,0:T(8,128)(2,1)}), bf16[32,16,128]{2,1,0:T(8,128)(2,1)S(1)}, u32[]{:S(2)}, u32[]{:S(2)}) async-start(bf16[32,16,128]{2,1,0:T(8,128)(2,1)} %bitcast.28), calls=%async_computation.1 | async-start | bytes 262144 | tf_op jit(solution)/shard_map/all_to_all | solution.py:713
  25.8 8.1 %collective-permute-start = (f32[4,3,32,128]{3,2,1,0:T(8,128)S(1)}, f32[4,3,32,128]{3,2,1,0:T(8,128)S(1)}, u32[]{:S(2)}, u32[]{:S(2)}) collective-permute-start(f32[4,3,32,128]{3,2,1,0:T(8,128)S(1)} %copy-done.5), channel_id=1, source_target_pairs={{0,8},{8,16},{16,24},{1,9},{9,17},{17,25},{2,10},{10,18},{18,26},{... | collective-permute-start | bytes 589832 | tf_op jit(solution)/shard_map/ppermute | solution.py:709
  29.4 8.6 %collective-permute-start.1 = (f32[4,3,32,128]{3,2,1,0:T(8,128)S(1)}, f32[4,3,32,128]{3,2,1,0:T(8,128)S(1)}, u32[]{:S(2)}, u32[]{:S(2)}) collective-permute-start(f32[4,3,32,128]{3,2,1,0:T(8,128)S(1)} %copy-done.4), channel_id=1, source_target_pairs={{8,0},{16,8},{24,16},{9,1},{17,9},{25,17},{10,2},{18,10},{26,18},{... | collective-permute-start | bytes 589832 | tf_op jit(solution)/shard_map/ppermute | solution.py:709
  30.7 7.3 %collective-permute-start.2 = (f32[4,96,128]{2,1,0:T(8,128)S(1)}, f32[4,96,128]{2,1,0:T(8,128)S(1)}, u32[]{:S(2)}, u32[]{:S(2)}) collective-permute-start(f32[4,96,128]{2,1,0:T(8,128)S(1)} %copy-done.3), channel_id=1, source_target_pairs={{0,1},{1,2},{2,3},{3,4},{4,5},{5,6},{6,7},{8,9},{9,10},{10,11},{11... | collective-permute-start | bytes 589832 | tf_op jit(solution)/shard_map/ppermute | solution.py:709
  32.5 5.5 %collective-permute-start.3 = (f32[4,96,128]{2,1,0:T(8,128)S(1)}, f32[4,96,128]{2,1,0:T(8,128)S(1)}, u32[]{:S(2)}, u32[]{:S(2)}) collective-permute-start(f32[4,96,128]{2,1,0:T(8,128)S(1)} %copy-done.2), channel_id=1, source_target_pairs={{1,0},{2,1},{3,2},{4,3},{5,4},{6,5},{7,6},{9,8},{10,9},{11,10},{12... | collective-permute-start | bytes 589832 | tf_op jit(solution)/shard_map/ppermute | solution.py:709
  38.0 6.6 %copy-start = (s32[8,128]{1,0:T(8,128)S(1)}, s32[8,128]{1,0:T(8,128)}, u32[]{:S(2)}) copy-start(s32[8,128]{1,0:T(8,128)} %get-tuple-element.40.meta_ref) | copy-start | bytes 12292
  50.2 20.7 %all-to-all-start.2 = ((f32[32,1,2176]{2,1,0:T(1,128)}), f32[32,1,2176]{2,1,0:T(1,128)S(1)}, u32[]{:S(2)}, u32[]{:S(2)}) async-start(f32[32,1,2176]{2,1,0:T(1,128)} %bitcast.27), calls=%async_computation.2 | async-start | bytes 557056 | tf_op jit(solution)/shard_map/all_to_all | solution.py:713
  72.2 9.6 %all-to-all-start.3 = ((f32[32,1,128]{2,1,0:T(1,128)}), f32[32,1,128]{2,1,0:T(1,128)S(1)}, u32[]{:S(2)}, u32[]{:S(2)}) async-start(f32[32,1,128]{2,1,0:T(1,128)} %bitcast.29), calls=%async_computation.3 | async-start | bytes 32768 | tf_op jit(solution)/shard_map/all_to_all | solution.py:713

commit v13 on v11

--- a/solution.py
+++ b/solution.py
@@ -111,8 +111,8 @@
 def flanks_body(
     shift,
     blocks,
-    ids_ref,
-    off_ref,
+    ids_in,
+    off_in,
     count_ref,
     model_in,
     damp_in,
@@ -123,6 +123,8 @@
     west_ref,
     meta_ref,
     slabs,
+    ids_ref,
+    off_ref,
     sems,
 ):
     systems, clat, clon, depth = model_in.shape
@@ -137,8 +139,11 @@
         (damp_in.at[:, pl.ds(0, 1)], north_ref.at[:, pl.ds(2, 1)]),
     )
     copies += [pltpu.make_async_copy(a, b, sems.at[i + 4]) for i, (a, b) in enumerate(pairs)]
-    for copy in copies:
-        copy.start()
+    small = [
+        pltpu.make_async_copy(a, b, sems.at[i + 8]) for i, (a, b) in enumerate(((ids_in, ids_ref), (off_in, off_ref)))
+    ]
+    begin(small + copies)
+    settle(small)
     tiles = ids_ref.shape[-1]
     lanes = 128
     ids = jnp.concatenate([ids_ref[0], jnp.full((1, lanes - tiles), -1, I32)], axis=1)
@@ -154,7 +159,7 @@
     starts = off_ref[0]
     for b in range(1, blocks + 1):
         block = block + (lane >= jnp.broadcast_to(starts[:, b : b + 1], (1, lanes))).astype(I32)
-    count = jnp.broadcast_to(count_ref[...], (1, lanes))
+    count = jnp.full((1, lanes), count_ref[0, 0], I32)
     meta_ref[...] = jnp.concatenate([owner, rank, block, count] + [owner] * 4, axis=0)
     for copy in copies:
         copy.wait()
@@ -227,14 +232,14 @@
 def damp_body(
     clat,
     clon,
-    rec_ref,
     diagonal_ref,
     model_in,
     damp_in,
-    north_ref,
-    south_ref,
-    west_ref,
-    east_ref,
+    rec_in,
+    north_in,
+    south_in,
+    west_in,
+    east_in,
     tiles_in,
     bar_sent,
     held_out,
@@ -246,9 +251,15 @@
     model_ref,
     damp_ref,
     bar_out,
+    rec_ref,
+    north_ref,
+    south_ref,
+    west_ref,
+    east_ref,
     alphas,
     sems,
     hold_sem,
+    halo_sems,
 ):
     systems, _, depth = model_ref.shape
 
@@ -262,10 +273,23 @@
         return pltpu.make_async_copy(bar_out.at[r], bar_sent.at[r], sems.at[r, 2])
 
     holding = pltpu.make_async_copy(tiles_in.at[0, 0, pl.ds(0, HELD)], held_out, hold_sem)
+    halos = [
+        pltpu.make_async_copy(a, b, halo_sems.at[k])
+        for k, (a, b) in enumerate(
+            (
+                (rec_in, rec_ref),
+                (north_in, north_ref),
+                (south_in, south_ref),
+                (west_in, west_ref),
+                (east_in, east_ref),
+            )
+        )
+    ]
+    begin(halos)
     for r in range(systems):
-        for copy in incoming(r):
-            copy.start()
+        begin(incoming(r))
     holding.start()
+    settle(halos)
     for r in range(systems):
         alphas[r] = jnp.sum(rec_ref[0:1, r : r + 1])
     lat_at, lon_at = lax.axis_index("lat"), lax.axis_index("lon")
@@ -751,12 +775,12 @@
         functools.partial(flanks_body, columns.bit_length() - 1, blocks),
         "flanks",
         (there((devices, 1, 2 * systems * depth), F32), band, band, side, side, there((8, lanes), I32)),
-        [vmem()] * 3 + [hbm(), hbm()],
+        [hbm(), hbm(), smem(), hbm(), hbm()],
         (vmem(),) * 6,
-        scratch=[pltpu.VMEM((4, systems, clat, 8, depth), F32), dma((8,))],
+        scratch=[pltpu.VMEM((4, systems, clat, 8, depth), F32), pltpu.VMEM(block_ids.shape, I32), pltpu.VMEM(block_offsets.shape, I32), dma((10,))],
         flops=1,
         moved=128 * systems * clat * depth,
-    )(far(block_ids), block_offsets, ray_counts, model, damping)
+    )(far(block_ids), far(block_offsets), ray_counts, model, damping)
     lists = exchange(asking)
     north = shifted(south_msg, "lat", 1)
     south = shifted(north_msg, "lat", -1)
@@ -791,12 +815,14 @@
             flank,
             there((1, lanes), F32),
         ),
-        [vmem()] * 2 + [hbm()] * 2 + [vmem()] * 4 + [hbm()],
+        [vmem()] + [hbm()] * 3 + [pl.BlockSpec(memory_space=pl.ANY)] * 4 + [hbm()],
         (hbm(),) + (vmem(),) * 6,
-        scratch=[pltpu.VMEM(flat, F32)] * 3 + [pltpu.SMEM((systems,), F32), dma((systems, 3)), dma],
+        scratch=[pltpu.VMEM(flat, F32)] * 3
+        + [pltpu.VMEM(x.shape, F32) for x in (recurrence, north, south, west, east)]
+        + [pltpu.SMEM((systems,), F32), dma((systems, 3)), dma, dma((5,))],
         flops=20 * systems * columns * depth,
         moved=12 * systems * columns * depth,
-    )(far(recurrence), diagonal, model_flat, damping_flat, north, south, west, east, far(sensitivity))
+    )(diagonal, model_flat, damping_flat, far(recurrence), north, south, west, east, far(sensitivity))
 
     ray_bar, terms = call(
         functools.partial(rays_body, cap, blocks),

time: 83.3 us -> 82.4 us (0.989)
  transfers between devices with their start and end apart: 8 -> 8, of which waited for: 5 -> 5; matrix products, arithmetic and copies ran while one was open for 0% -> 0% of each run, Pallas kernels for 23% -> 24%
where the time goes in v13:
time: 82.4 us; the launch traced here: 81.6 us
  Pallas kernels  37.1 us (45%)
  starting transfers between devices  32 us (39%)
  waiting for transfers between devices  11.1 us (13%)
  between operations  1.41 us (2%)
    all_to_all x4, starting transfers between devices, exchange(): return lax.all_to_all(x, AXES, split_axis=0, concat_axis=0, tiled=True)  24 us
    ppermute x4, starting transfers between devices, shifted(): return lax.ppermute(x, axis, pairs)  8.05 us
    pallas_call x1, Pallas kernels, per_device(): call(functools.partial(damp_body, clat, clon), 'damp', (there(flat, F32),...  6.98 us
    all_to_all x4, waiting for transfers between devices, exchange(): return lax.all_to_all(x, AXES, split_axis=0, concat_axis=0, tiled=True)  6.72 us
    pallas_call x1, Pallas kernels, per_device(): call(functools.partial(image_body, chunk, clat, clon), 'image', (there(fl...  6.37 us
    pallas_call x1, Pallas kernels, per_device(): call(functools.partial(early_body, float(rows_all)), 'early', (there(ray_...  6.29 us
    pallas_call x1, Pallas kernels, per_device(): call(functools.partial(rays_body, cap, blocks), 'rays', (there(ray_vector...  5.53 us
    pallas_call x1, Pallas kernels, per_device(): call(functools.partial(finish_body, float(rows_all), float(cells_all), cl...  5.51 us
  transfers between devices with their start and end apart: 8, of which 5 were waited for; matrix products, arithmetic and copies ran while one was open for 0% of the time, Pallas kernels for 24%

profile of v13, /device:TPU:0, one launch (start us, length us, event | category | flops | bytes accessed | tf_op | source)
XLA Modules:
  0.0 81.6 jit_solution(16083960939654363762)
XLA Ops:
  1.3 2.7 %flanks.1 = (f32[32,1,1024]{2,1,0:T(1,128)}, f32[4,3,32,128]{3,2,1,0:T(8,128)}, f32[4,3,32,128]{3,2,1,0:T(8,128)}, f32[4,96,128]{2,1,0:T(8,128)}, f32[4,96,128]{2,1,0:T(8,128)}, /*index=5*/s32[8,128]{1,0:T(8,128)}) custom-call(s32[1,1,60]{2,1,0:T(1,128)} %ids_in.1, s32[1,1,4]{2,1,0:T(1,128)} %off_in.1, s32[1,1]{1,0:T(1,128)S(6)} %copy.18.count_ref, ...), custom_call_target="tpu_custom_call" | custom-call | flops 1 | bytes 2097152 | tf_op jit(solution)/shard_map/flanks/pallas_call | solution.py:774
  4.0 7.3 %all-to-all-start = ((f32[32,1,1024]{2,1,0:T(1,128)}), f32[32,1,1024]{2,1,0:T(1,128)S(1)}, u32[]{:S(2)}, u32[]{:S(2)}) async-start(f32[32,1,1024]{2,1,0:T(1,128)} %get-tuple-element.41), calls=%async_computation | async-start | bytes 262144 | tf_op jit(solution)/shard_map/all_to_all | solution.py:737
  11.3 3.7 %collective-permute-start = (f32[4,3,32,128]{3,2,1,0:T(8,128)}, f32[4,3,32,128]{3,2,1,0:T(8,128)S(1)}, u32[]{:S(2)}, u32[]{:S(2)}) collective-permute-start(f32[4,3,32,128]{3,2,1,0:T(8,128)} %get-tuple-element.42), channel_id=1, source_target_pairs={{0,8},{8,16},{16,24},{1,9},{9,17},{17,25},{2,10},{10,18},{18,26},{... | collective-permute-start | bytes 589832 | tf_op jit(solution)/shard_map/ppermute | solution.py:733
  15.0 1.3 %collective-permute-start.1 = (f32[4,3,32,128]{3,2,1,0:T(8,128)}, f32[4,3,32,128]{3,2,1,0:T(8,128)S(1)}, u32[]{:S(2)}, u32[]{:S(2)}) collective-permute-start(f32[4,3,32,128]{3,2,1,0:T(8,128)} %get-tuple-element.43), channel_id=1, source_target_pairs={{8,0},{16,8},{24,16},{9,1},{17,9},{25,17},{10,2},{18,10},{26,18},{... | collective-permute-start | bytes 589832 | tf_op jit(solution)/shard_map/ppermute | solution.py:733
  16.3 1.8 %collective-permute-start.2 = (f32[4,96,128]{2,1,0:T(8,128)}, f32[4,96,128]{2,1,0:T(8,128)S(1)}, u32[]{:S(2)}, u32[]{:S(2)}) collective-permute-start(f32[4,96,128]{2,1,0:T(8,128)} %get-tuple-element.44), channel_id=1, source_target_pairs={{0,1},{1,2},{2,3},{3,4},{4,5},{5,6},{6,7},{8,9},{9,10},{10,11},{11... | collective-permute-start | bytes 589832 | tf_op jit(solution)/shard_map/ppermute | solution.py:733
  18.1 1.3 %collective-permute-start.3 = (f32[4,96,128]{2,1,0:T(8,128)}, f32[4,96,128]{2,1,0:T(8,128)S(1)}, u32[]{:S(2)}, u32[]{:S(2)}) collective-permute-start(f32[4,96,128]{2,1,0:T(8,128)} %get-tuple-element.45), channel_id=1, source_target_pairs={{1,0},{2,1},{3,2},{4,3},{5,4},{6,5},{7,6},{9,8},{10,9},{11,10},{12... | collective-permute-start | bytes 589832 | tf_op jit(solution)/shard_map/ppermute | solution.py:733
  19.4 0.4 collective-permute-done.north.north_in
  19.7 4.0 %collective-permute-done.1.south.south_in = f32[4,3,32,128]{3,2,1,0:T(8,128)S(1)} collective-permute-done((f32[4,3,32,128]{3,2,1,0:T(8,128)}, f32[4,3,32,128]{3,2,1,0:T(8,128)S(1)}, u32[]{:S(2)}, u32[]{:S(2)}) %collective-permute-start.1) | collective-permute-done | bytes 196640 | tf_op jit(solution)/shard_map/ppermute | solution.py:733
  23.7 0.0 collective-permute-done.2.west.west_in
  23.7 0.0 collective-permute-done.3.east.east_in
  23.7 0.0 all-to-all-done.lists_ref
  23.8 2.4 %serve.1 = (bf16[512,128]{1,0:T(8,128)(2,1)}, f32[32,128]{1,0:T(8,128)S(1)}, s32[1]{0:T(128)}, f32[16,128]{1,0:T(8,128)S(1)}) custom-call(f32[32,1,1024]{2,1,0:T(1,128)S(1)} %all-to-all-done.lists_ref, f32[4,1024,128]{2,1,0:T(8,128)} %bitcast.19, f32[4,3,32,128]{3,2,1,0:T(8,128)S(1)} %collective-permute-done.north.north_in, ...), custom_call_target="tpu_custom_call" | custom-call | tf_op jit(solution)/shard_map/serve/pallas_call | solution.py:790
  26.2 9.5 %all-to-all-start.1 = ((bf16[32,16,128]{2,1,0:T(8,128)(2,1)}), bf16[32,16,128]{2,1,0:T(8,128)(2,1)S(1)}, u32[]{:S(2)}, u32[]{:S(2)}) async-start(bf16[32,16,128]{2,1,0:T(8,128)(2,1)} %bitcast.28), calls=%async_computation.1 | async-start | bytes 262144 | tf_op jit(solution)/shard_map/all_to_all | solution.py:737
  35.7 0.0 copy-start
  35.7 7.0 %damp.1 = (f32[4,1024,128]{2,1,0:T(8,128)}, bf16[30,256,128]{2,1,0:T(8,128)(2,1)S(1)}, f32[4,32,128]{2,1,0:T(8,128)}, f32[4,32,128]{2,1,0:T(8,128)}, f32[4,32,12...) custom-call(f32[16,128]{1,0:T(8,128)S(1)} %get-tuple-element.46.diagonal_ref, f32[4,1024,128]{2,1,0:T(8,128)} %bitcast.20, ...), custom_call_target="tpu_custom_call" | custom-call | flops 10485760 | bytes 6291456 | tf_op jit(solution)/shard_map/damp/pallas_call | solution.py:806
  42.7 1.2 %all-to-all-done.1 = bf16[32,16,128]{2,1,0:T(8,128)(2,1)S(1)} async-done(((bf16[32,16,128]{2,1,0:T(8,128)(2,1)}), bf16[32,16,128]{2,1,0:T(8,128)(2,1)S(1)}, u32[]{:S(2)}, u32[]{:S(2)}) %all-to-all-start.1) | async-done | bytes 131104 | tf_op jit(solution)/shard_map/all_to_all | solution.py:737
  43.9 0.0 copy-done
  43.9 5.5 %rays.1 = (f32[4,1,1,768]{3,2,1,0:T(1,128)}, f32[544,1,128]{2,1,0:T(1,128)}) custom-call(s32[8,128]{1,0:T(8,128)S(1)} %copy-done, bf16[30,256,128]{2,1,0:T(8,128)(2,1)S(1)} %get-tuple-element.47.held_ref, bf16[512,128]{1,0:T(8,128)(2,1)S(1)} %bitcast.17, bf16[1,1,60,256,128]{4,3,2,1,0:T(8,128)(2,1)} %tiles_in.3, f32[3,4]{1,0:T(4,128)} %rec_in.3, ...), custom_call_target="tpu_custom_call" | custom-call | flops 125829120 | bytes 3932160 | tf_op jit(solution)/shard_map/rays/pallas_call | solution.py:827
  49.4 4.6 %all-to-all-start.2 = ((f32[32,1,2176]{2,1,0:T(1,128)}), f32[32,1,2176]{2,1,0:T(1,128)S(1)}, u32[]{:S(2)}, u32[]{:S(2)}) async-start(f32[32,1,2176]{2,1,0:T(1,128)} %bitcast.27), calls=%async_computation.2 | async-start | bytes 557056 | tf_op jit(solution)/shard_map/all_to_all | solution.py:737
  54.1 6.4 %image.1 = (f32[4,1024,128]{2,1,0:T(8,128)}, f32[1,128]{1,0:T(1,128)S(1)}, f32[512,128]{1,0:T(8,128)S(1)}, f32[512,128]{1,0:T(8,128)S(1)}, bf16[512,640]{1,0:T(8,128)(2,1)S(1)}) custom-call(s32[1]{0:T(128)} %get-tuple-element.51.corner_ref, f32[32,128]{1,0:T(8,128)S(1)} %get-tuple-element.52.wanted_ref, f32[4,1024,128]{2,1,0:T(8,128)} %get-tuple-element.53.bar_in, ...), custom_call_target="tpu_custom_call" | custom-call | flops 10485760 | bytes 6291456 | tf_op jit(solution)/shard_map/image/pallas_call | solution.py:850
  60.5 4.7 %all-to-all-done.2 = f32[32,1,2176]{2,1,0:T(1,128)S(1)} async-done(((f32[32,1,2176]{2,1,0:T(1,128)}), f32[32,1,2176]{2,1,0:T(1,128)S(1)}, u32[]{:S(2)}, u32[]{:S(2)}) %all-to-all-start.2) | async-done | bytes 278560 | tf_op jit(solution)/shard_map/all_to_all | solution.py:737
  65.2 1.3 %combine.1 = (f32[512,128]{1,0:T(8,128)S(1)}, f32[1,128]{1,0:T(1,128)S(1)}, f32[32,128]{1,0:T(8,128)}) custom-call(f32[544,128]{1,0:T(8,128)S(1)} %bitcast.16, bf16[512,640]{1,0:T(8,128)(2,1)S(1)} %get-tuple-element.58.chosen_ref, f32[512,128]{1,0:T(8,128)S(1)} %get-tuple-element.59.patch_ref, f32[512,128]{1,0:T(8,128)S(1)} %get-tuple-element.60.model_patch_ref, ...), custom_call_target="tpu_custom_call" | custom-call | tf_op jit(solution)/shard_map/combine/pallas_call | solution.py:867
  66.5 2.5 %all-to-all-start.3 = ((f32[32,1,128]{2,1,0:T(1,128)}), f32[32,1,128]{2,1,0:T(1,128)S(1)}, u32[]{:S(2)}, u32[]{:S(2)}) async-start(f32[32,1,128]{2,1,0:T(1,128)} %bitcast.29), calls=%async_computation.3 | async-start | bytes 32768 | tf_op jit(solution)/shard_map/all_to_all | solution.py:737
  69.0 6.3 %early.1 = (f32[4,1,1,768]{3,2,1,0:T(1,128)}, f32[4,1024,128]{2,1,0:T(8,128)}, f32[4,1024,128]{2,1,0:T(8,128)}, f32[3,1024,128]{2,1,0:T(8,128)S(1)}) custom-call(f32[1,128]{1,0:T(1,128)S(1)} %get-tuple-element.62.residual_ref, f32[3,4]{1,0:T(4,128)} %rec_in.3, f32[4,1,1,768]{3,2,1,0:T(1,128)} %get-tuple-element.63.ray_ref, ...), custom_call_target="tpu_custom_call" | custom-call | flops 2097152 | bytes 10485760 | tf_op jit(solution)/shard_map/early/pallas_call | solution.py:878
  75.3 0.8 all-to-all-done.3
  76.1 5.5 %finish.1 = (f32[4,1024,128]{2,1,0:T(8,128)}, f32[4,1024,128]{2,1,0:T(8,128)}, f32[3,4]{1,0:T(4,128)}) custom-call(f32[1,128]{1,0:T(1,128)S(1)} %get-tuple-element.62.residual_ref, f32[32,128]{1,0:T(8,128)S(1)} %bitcast.18, f32[512,128]{1,0:T(8,128)S(1)} %get-tuple-element.67.added_ref, f32[3,1024,128]{2,1,0:T(8,128)S(1)} %get-tuple-element.68.kept_ref, ...), custom_call_target="tpu_custom_call" | custom-call | flops 3145728 | bytes 10485760 | tf_op jit(solution)/shard_map/finish/pallas_call | solution.py:892
Async XLA Ops:
  4.0 19.8 %all-to-all-start = ((f32[32,1,1024]{2,1,0:T(1,128)}), f32[32,1,1024]{2,1,0:T(1,128)S(1)}, u32[]{:S(2)}, u32[]{:S(2)}) async-start(f32[32,1,1024]{2,1,0:T(1,128)} %get-tuple-element.41), calls=%async_computation | async-start | bytes 262144 | tf_op jit(solution)/shard_map/all_to_all | solution.py:737
  11.3 8.5 %collective-permute-start = (f32[4,3,32,128]{3,2,1,0:T(8,128)}, f32[4,3,32,128]{3,2,1,0:T(8,128)S(1)}, u32[]{:S(2)}, u32[]{:S(2)}) collective-permute-start(f32[4,3,32,128]{3,2,1,0:T(8,128)} %get-tuple-element.42), channel_id=1, source_target_pairs={{0,8},{8,16},{16,24},{1,9},{9,17},{17,25},{2,10},{10,18},{18,26},{... | collective-permute-start | bytes 589832 | tf_op jit(solution)/shard_map/ppermute | solution.py:733
  15.0 8.8 %collective-permute-start.1 = (f32[4,3,32,128]{3,2,1,0:T(8,128)}, f32[4,3,32,128]{3,2,1,0:T(8,128)S(1)}, u32[]{:S(2)}, u32[]{:S(2)}) collective-permute-start(f32[4,3,32,128]{3,2,1,0:T(8,128)} %get-tuple-element.43), channel_id=1, source_target_pairs={{8,0},{16,8},{24,16},{9,1},{17,9},{25,17},{10,2},{18,10},{26,18},{... | collective-permute-start | bytes 589832 | tf_op jit(solution)/shard_map/ppermute | solution.py:733
  16.3 7.5 %collective-permute-start.2 = (f32[4,96,128]{2,1,0:T(8,128)}, f32[4,96,128]{2,1,0:T(8,128)S(1)}, u32[]{:S(2)}, u32[]{:S(2)}) collective-permute-start(f32[4,96,128]{2,1,0:T(8,128)} %get-tuple-element.44), channel_id=1, source_target_pairs={{0,1},{1,2},{2,3},{3,4},{4,5},{5,6},{6,7},{8,9},{9,10},{10,11},{11... | collective-permute-start | bytes 589832 | tf_op jit(solution)/shard_map/ppermute | solution.py:733
  18.1 5.7 %collective-permute-start.3 = (f32[4,96,128]{2,1,0:T(8,128)}, f32[4,96,128]{2,1,0:T(8,128)S(1)}, u32[]{:S(2)}, u32[]{:S(2)}) collective-permute-start(f32[4,96,128]{2,1,0:T(8,128)} %get-tuple-element.45), channel_id=1, source_target_pairs={{1,0},{2,1},{3,2},{4,3},{5,4},{6,5},{7,6},{9,8},{10,9},{11,10},{12... | collective-permute-start | bytes 589832 | tf_op jit(solution)/shard_map/ppermute | solution.py:733
  26.2 17.7 %all-to-all-start.1 = ((bf16[32,16,128]{2,1,0:T(8,128)(2,1)}), bf16[32,16,128]{2,1,0:T(8,128)(2,1)S(1)}, u32[]{:S(2)}, u32[]{:S(2)}) async-start(bf16[32,16,128]{2,1,0:T(8,128)(2,1)} %bitcast.28), calls=%async_computation.1 | async-start | bytes 262144 | tf_op jit(solution)/shard_map/all_to_all | solution.py:737
  35.7 8.2 %copy-start = (s32[8,128]{1,0:T(8,128)S(1)}, s32[8,128]{1,0:T(8,128)}, u32[]{:S(2)}) copy-start(s32[8,128]{1,0:T(8,128)} %get-tuple-element.40.meta_ref) | copy-start | bytes 12292
  49.4 15.7 %all-to-all-start.2 = ((f32[32,1,2176]{2,1,0:T(1,128)}), f32[32,1,2176]{2,1,0:T(1,128)S(1)}, u32[]{:S(2)}, u32[]{:S(2)}) async-start(f32[32,1,2176]{2,1,0:T(1,128)} %bitcast.27), calls=%async_computation.2 | async-start | bytes 557056 | tf_op jit(solution)/shard_map/all_to_all | solution.py:737
  66.5 9.6 %all-to-all-start.3 = ((f32[32,1,128]{2,1,0:T(1,128)}), f32[32,1,128]{2,1,0:T(1,128)S(1)}, u32[]{:S(2)}, u32[]{:S(2)}) async-start(f32[32,1,128]{2,1,0:T(1,128)} %bitcast.29), calls=%async_computation.3 | async-start | bytes 32768 | tf_op jit(solution)/shard_map/all_to_all | solution.py:737

commit v14 on v11

--- a/solution.py
+++ b/solution.py
@@ -111,8 +111,8 @@
 def flanks_body(
     shift,
     blocks,
-    ids_ref,
-    off_ref,
+    ids_in,
+    off_in,
     count_ref,
     model_in,
     damp_in,
@@ -123,6 +123,8 @@
     west_ref,
     meta_ref,
     slabs,
+    ids_ref,
+    off_ref,
     sems,
 ):
     systems, clat, clon, depth = model_in.shape
@@ -137,8 +139,11 @@
         (damp_in.at[:, pl.ds(0, 1)], north_ref.at[:, pl.ds(2, 1)]),
     )
     copies += [pltpu.make_async_copy(a, b, sems.at[i + 4]) for i, (a, b) in enumerate(pairs)]
-    for copy in copies:
-        copy.start()
+    small = [
+        pltpu.make_async_copy(a, b, sems.at[i + 8]) for i, (a, b) in enumerate(((ids_in, ids_ref), (off_in, off_ref)))
+    ]
+    begin(small + copies)
+    settle(small)
     tiles = ids_ref.shape[-1]
     lanes = 128
     ids = jnp.concatenate([ids_ref[0], jnp.full((1, lanes - tiles), -1, I32)], axis=1)
@@ -154,7 +159,7 @@
     starts = off_ref[0]
     for b in range(1, blocks + 1):
         block = block + (lane >= jnp.broadcast_to(starts[:, b : b + 1], (1, lanes))).astype(I32)
-    count = jnp.broadcast_to(count_ref[...], (1, lanes))
+    count = jnp.full((1, lanes), count_ref[0, 0], I32)
     meta_ref[...] = jnp.concatenate([owner, rank, block, count] + [owner] * 4, axis=0)
     for copy in copies:
         copy.wait()
@@ -668,8 +673,8 @@
     rec_done.wait()
 
 
-PIECES = 2
-AHEAD = 4
+PIECES = 4
+AHEAD = 8
 
 
 def pieces(pairs, sems, r, p, rows):
@@ -751,12 +756,12 @@
         functools.partial(flanks_body, columns.bit_length() - 1, blocks),
         "flanks",
         (there((devices, 1, 2 * systems * depth), F32), band, band, side, side, there((8, lanes), I32)),
-        [vmem()] * 3 + [hbm(), hbm()],
+        [hbm(), hbm(), smem(), hbm(), hbm()],
         (vmem(),) * 6,
-        scratch=[pltpu.VMEM((4, systems, clat, 8, depth), F32), dma((8,))],
+        scratch=[pltpu.VMEM((4, systems, clat, 8, depth), F32), pltpu.VMEM(block_ids.shape, I32), pltpu.VMEM(block_offsets.shape, I32), dma((10,))],
         flops=1,
         moved=128 * systems * clat * depth,
-    )(far(block_ids), block_offsets, ray_counts, model, damping)
+    )(far(block_ids), far(block_offsets), ray_counts, model, damping)
     lists = exchange(asking)
     north = shifted(south_msg, "lat", 1)
     south = shifted(north_msg, "lat", -1)

time: 83.3 us -> 82.4 us (0.989)
  transfers between devices with their start and end apart: 8 -> 8, of which waited for: 5 -> 5; matrix products, arithmetic and copies ran while one was open for 0% -> 0% of each run, Pallas kernels for 23% -> 24%
where the time goes in v14:
time: 82.4 us; the launch traced here: 81.7 us
  Pallas kernels  37.4 us (45%)
  starting transfers between devices  31.6 us (38%)
  waiting for transfers between devices  11.2 us (14%)
  between operations  1.41 us (2%)
    all_to_all x4, starting transfers between devices, exchange(): return lax.all_to_all(x, AXES, split_axis=0, concat_axis=0, tiled=True)  23.6 us
    ppermute x4, starting transfers between devices, shifted(): return lax.ppermute(x, axis, pairs)  8.05 us
    all_to_all x4, waiting for transfers between devices, exchange(): return lax.all_to_all(x, AXES, split_axis=0, concat_axis=0, tiled=True)  6.8 us
    pallas_call x1, Pallas kernels, per_device(): call(functools.partial(damp_body, clat, clon), 'damp', (there(flat, F32),...  6.61 us
    pallas_call x1, Pallas kernels, per_device(): call(functools.partial(early_body, float(rows_all)), 'early', (there(ray_...  6.59 us
    pallas_call x1, Pallas kernels, per_device(): call(functools.partial(image_body, chunk, clat, clon), 'image', (there(fl...  6.37 us
    pallas_call x1, Pallas kernels, per_device(): call(functools.partial(finish_body, float(rows_all), float(cells_all), cl...  5.93 us
    pallas_call x1, Pallas kernels, per_device(): call(functools.partial(rays_body, cap, blocks), 'rays', (there(ray_vector...  5.53 us
  transfers between devices with their start and end apart: 8, of which 5 were waited for; matrix products, arithmetic and copies ran while one was open for 0% of the time, Pallas kernels for 24%

profile of v14, /device:TPU:0, one launch (start us, length us, event | category | flops | bytes accessed | tf_op | source)
XLA Modules:
  0.0 81.7 jit_solution(6112917227087405102)
XLA Ops:
  1.3 2.7 %flanks.1 = (f32[32,1,1024]{2,1,0:T(1,128)}, f32[4,3,32,128]{3,2,1,0:T(8,128)}, f32[4,3,32,128]{3,2,1,0:T(8,128)}, f32[4,96,128]{2,1,0:T(8,128)}, f32[4,96,128]{2,1,0:T(8,128)}, /*index=5*/s32[8,128]{1,0:T(8,128)}) custom-call(s32[1,1,60]{2,1,0:T(1,128)} %ids_in.1, s32[1,1,4]{2,1,0:T(1,128)} %off_in.1, s32[1,1]{1,0:T(1,128)S(6)} %copy.18.count_ref, ...), custom_call_target="tpu_custom_call" | custom-call | flops 1 | bytes 2097152 | tf_op jit(solution)/shard_map/flanks/pallas_call | solution.py:755
  4.0 7.3 %all-to-all-start = ((f32[32,1,1024]{2,1,0:T(1,128)}), f32[32,1,1024]{2,1,0:T(1,128)S(1)}, u32[]{:S(2)}, u32[]{:S(2)}) async-start(f32[32,1,1024]{2,1,0:T(1,128)} %get-tuple-element.41), calls=%async_computation | async-start | bytes 262144 | tf_op jit(solution)/shard_map/all_to_all | solution.py:718
  11.3 3.7 %collective-permute-start = (f32[4,3,32,128]{3,2,1,0:T(8,128)}, f32[4,3,32,128]{3,2,1,0:T(8,128)S(1)}, u32[]{:S(2)}, u32[]{:S(2)}) collective-permute-start(f32[4,3,32,128]{3,2,1,0:T(8,128)} %get-tuple-element.42), channel_id=1, source_target_pairs={{0,8},{8,16},{16,24},{1,9},{9,17},{17,25},{2,10},{10,18},{18,26},{... | collective-permute-start | bytes 589832 | tf_op jit(solution)/shard_map/ppermute | solution.py:714
  15.0 1.3 %collective-permute-start.1 = (f32[4,3,32,128]{3,2,1,0:T(8,128)}, f32[4,3,32,128]{3,2,1,0:T(8,128)S(1)}, u32[]{:S(2)}, u32[]{:S(2)}) collective-permute-start(f32[4,3,32,128]{3,2,1,0:T(8,128)} %get-tuple-element.43), channel_id=1, source_target_pairs={{8,0},{16,8},{24,16},{9,1},{17,9},{25,17},{10,2},{18,10},{26,18},{... | collective-permute-start | bytes 589832 | tf_op jit(solution)/shard_map/ppermute | solution.py:714
  16.3 1.8 %collective-permute-start.2 = (f32[4,96,128]{2,1,0:T(8,128)}, f32[4,96,128]{2,1,0:T(8,128)S(1)}, u32[]{:S(2)}, u32[]{:S(2)}) collective-permute-start(f32[4,96,128]{2,1,0:T(8,128)} %get-tuple-element.44), channel_id=1, source_target_pairs={{0,1},{1,2},{2,3},{3,4},{4,5},{5,6},{6,7},{8,9},{9,10},{10,11},{11... | collective-permute-start | bytes 589832 | tf_op jit(solution)/shard_map/ppermute | solution.py:714
  18.1 1.3 %collective-permute-start.3 = (f32[4,96,128]{2,1,0:T(8,128)}, f32[4,96,128]{2,1,0:T(8,128)S(1)}, u32[]{:S(2)}, u32[]{:S(2)}) collective-permute-start(f32[4,96,128]{2,1,0:T(8,128)} %get-tuple-element.45), channel_id=1, source_target_pairs={{1,0},{2,1},{3,2},{4,3},{5,4},{6,5},{7,6},{9,8},{10,9},{11,10},{12... | collective-permute-start | bytes 589832 | tf_op jit(solution)/shard_map/ppermute | solution.py:714
  19.4 0.4 collective-permute-done.north.north_ref
  19.7 4.0 %collective-permute-done.1.south.south_ref = f32[4,3,32,128]{3,2,1,0:T(8,128)S(1)} collective-permute-done((f32[4,3,32,128]{3,2,1,0:T(8,128)}, f32[4,3,32,128]{3,2,1,0:T(8,128)S(1)}, u32[]{:S(2)}, u32[]{:S(2)}) %collective-permute-start.1) | collective-permute-done | bytes 196640 | tf_op jit(solution)/shard_map/ppermute | solution.py:714
  23.7 0.0 collective-permute-done.2.west.west_ref
  23.7 0.0 collective-permute-done.3.east.east_ref
  23.7 0.0 all-to-all-done.lists_ref
  23.8 2.4 %serve.1 = (bf16[512,128]{1,0:T(8,128)(2,1)}, f32[32,128]{1,0:T(8,128)S(1)}, s32[1]{0:T(128)}, f32[16,128]{1,0:T(8,128)S(1)}) custom-call(f32[32,1,1024]{2,1,0:T(1,128)S(1)} %all-to-all-done.lists_ref, f32[4,1024,128]{2,1,0:T(8,128)} %bitcast.19, f32[4,3,32,128]{3,2,1,0:T(8,128)S(1)} %collective-permute-done.north.north_ref, ...), custom_call_target="tpu_custom_call" | custom-call | tf_op jit(solution)/shard_map/serve/pallas_call | solution.py:771
  26.2 9.5 %all-to-all-start.1 = ((bf16[32,16,128]{2,1,0:T(8,128)(2,1)}), bf16[32,16,128]{2,1,0:T(8,128)(2,1)S(1)}, u32[]{:S(2)}, u32[]{:S(2)}) async-start(bf16[32,16,128]{2,1,0:T(8,128)(2,1)} %bitcast.28), calls=%async_computation.1 | async-start | bytes 262144 | tf_op jit(solution)/shard_map/all_to_all | solution.py:718
  35.7 0.0 copy-start
  35.7 6.6 %damp.1 = (f32[4,1024,128]{2,1,0:T(8,128)}, bf16[30,256,128]{2,1,0:T(8,128)(2,1)S(1)}, f32[4,32,128]{2,1,0:T(8,128)}, f32[4,32,128]{2,1,0:T(8,128)}, f32[4,32,12...) custom-call(f32[3,4]{1,0:T(4,128)} %rec_in.1, f32[16,128]{1,0:T(8,128)S(1)} %get-tuple-element.46.diagonal_ref, ...), custom_call_target="tpu_custom_call" | custom-call | flops 10485760 | bytes 6291456 | tf_op jit(solution)/shard_map/damp/pallas_call | solution.py:787
  42.3 1.6 %all-to-all-done.1 = bf16[32,16,128]{2,1,0:T(8,128)(2,1)S(1)} async-done(((bf16[32,16,128]{2,1,0:T(8,128)(2,1)}), bf16[32,16,128]{2,1,0:T(8,128)(2,1)S(1)}, u32[]{:S(2)}, u32[]{:S(2)}) %all-to-all-start.1) | async-done | bytes 131104 | tf_op jit(solution)/shard_map/all_to_all | solution.py:718
  43.9 0.0 copy-done
  43.9 5.5 %rays.1 = (f32[4,1,1,768]{3,2,1,0:T(1,128)}, f32[544,1,128]{2,1,0:T(1,128)}) custom-call(s32[8,128]{1,0:T(8,128)S(1)} %copy-done, bf16[30,256,128]{2,1,0:T(8,128)(2,1)S(1)} %get-tuple-element.47.held_ref, bf16[512,128]{1,0:T(8,128)(2,1)S(1)} %bitcast.17, bf16[1,1,60,256,128]{4,3,2,1,0:T(8,128)(2,1)} %tiles_in.3, f32[3,4]{1,0:T(4,128)} %rec_in.1, ...), custom_call_target="tpu_custom_call" | custom-call | flops 125829120 | bytes 3932160 | tf_op jit(solution)/shard_map/rays/pallas_call | solution.py:806
  49.4 4.3 %all-to-all-start.2 = ((f32[32,1,2176]{2,1,0:T(1,128)}), f32[32,1,2176]{2,1,0:T(1,128)S(1)}, u32[]{:S(2)}, u32[]{:S(2)}) async-start(f32[32,1,2176]{2,1,0:T(1,128)} %bitcast.27), calls=%async_computation.2 | async-start | bytes 557056 | tf_op jit(solution)/shard_map/all_to_all | solution.py:718
  53.7 6.4 %image.1 = (f32[4,1024,128]{2,1,0:T(8,128)}, f32[1,128]{1,0:T(1,128)S(1)}, f32[512,128]{1,0:T(8,128)S(1)}, f32[512,128]{1,0:T(8,128)S(1)}, bf16[512,640]{1,0:T(8,128)(2,1)S(1)}) custom-call(s32[1]{0:T(128)} %get-tuple-element.51.corner_ref, f32[32,128]{1,0:T(8,128)S(1)} %get-tuple-element.52.wanted_ref, f32[4,1024,128]{2,1,0:T(8,128)} %get-tuple-element.53.bar_in, ...), custom_call_target="tpu_custom_call" | custom-call | flops 10485760 | bytes 6291456 | tf_op jit(solution)/shard_map/image/pallas_call | solution.py:829
  60.1 4.7 %all-to-all-done.2 = f32[32,1,2176]{2,1,0:T(1,128)S(1)} async-done(((f32[32,1,2176]{2,1,0:T(1,128)}), f32[32,1,2176]{2,1,0:T(1,128)S(1)}, u32[]{:S(2)}, u32[]{:S(2)}) %all-to-all-start.2) | async-done | bytes 278560 | tf_op jit(solution)/shard_map/all_to_all | solution.py:718
  64.8 1.3 %combine.1 = (f32[512,128]{1,0:T(8,128)S(1)}, f32[1,128]{1,0:T(1,128)S(1)}, f32[32,128]{1,0:T(8,128)}) custom-call(f32[544,128]{1,0:T(8,128)S(1)} %bitcast.16, bf16[512,640]{1,0:T(8,128)(2,1)S(1)} %get-tuple-element.58.chosen_ref, f32[512,128]{1,0:T(8,128)S(1)} %get-tuple-element.59.patch_ref, f32[512,128]{1,0:T(8,128)S(1)} %get-tuple-element.60.model_patch_ref, ...), custom_call_target="tpu_custom_call" | custom-call | tf_op jit(solution)/shard_map/combine/pallas_call | solution.py:846
  66.1 2.5 %all-to-all-start.3 = ((f32[32,1,128]{2,1,0:T(1,128)}), f32[32,1,128]{2,1,0:T(1,128)S(1)}, u32[]{:S(2)}, u32[]{:S(2)}) async-start(f32[32,1,128]{2,1,0:T(1,128)} %bitcast.29), calls=%async_computation.3 | async-start | bytes 32768 | tf_op jit(solution)/shard_map/all_to_all | solution.py:718
  68.7 6.6 %early.1 = (f32[4,1,1,768]{3,2,1,0:T(1,128)}, f32[4,1024,128]{2,1,0:T(8,128)}, f32[4,1024,128]{2,1,0:T(8,128)}, f32[3,1024,128]{2,1,0:T(8,128)S(1)}) custom-call(f32[1,128]{1,0:T(1,128)S(1)} %get-tuple-element.62.residual_ref, f32[3,4]{1,0:T(4,128)} %rec_in.1, f32[4,1,1,768]{3,2,1,0:T(1,128)} %get-tuple-element.63.ray_ref, ...), custom_call_target="tpu_custom_call" | custom-call | flops 2097152 | bytes 10485760 | tf_op jit(solution)/shard_map/early/pallas_call | solution.py:857
  75.3 0.5 all-to-all-done.3
  75.7 5.9 %finish.1 = (f32[4,1024,128]{2,1,0:T(8,128)}, f32[4,1024,128]{2,1,0:T(8,128)}, f32[3,4]{1,0:T(4,128)}) custom-call(f32[1,128]{1,0:T(1,128)S(1)} %get-tuple-element.62.residual_ref, f32[32,128]{1,0:T(8,128)S(1)} %bitcast.18, f32[512,128]{1,0:T(8,128)S(1)} %get-tuple-element.67.added_ref, f32[3,1024,128]{2,1,0:T(8,128)S(1)} %get-tuple-element.68.kept_ref, ...), custom_call_target="tpu_custom_call" | custom-call | flops 3145728 | bytes 10485760 | tf_op jit(solution)/shard_map/finish/pallas_call | solution.py:871
Async XLA Ops:
  4.0 19.8 %all-to-all-start = ((f32[32,1,1024]{2,1,0:T(1,128)}), f32[32,1,1024]{2,1,0:T(1,128)S(1)}, u32[]{:S(2)}, u32[]{:S(2)}) async-start(f32[32,1,1024]{2,1,0:T(1,128)} %get-tuple-element.41), calls=%async_computation | async-start | bytes 262144 | tf_op jit(solution)/shard_map/all_to_all | solution.py:718
  11.3 8.5 %collective-permute-start = (f32[4,3,32,128]{3,2,1,0:T(8,128)}, f32[4,3,32,128]{3,2,1,0:T(8,128)S(1)}, u32[]{:S(2)}, u32[]{:S(2)}) collective-permute-start(f32[4,3,32,128]{3,2,1,0:T(8,128)} %get-tuple-element.42), channel_id=1, source_target_pairs={{0,8},{8,16},{16,24},{1,9},{9,17},{17,25},{2,10},{10,18},{18,26},{... | collective-permute-start | bytes 589832 | tf_op jit(solution)/shard_map/ppermute | solution.py:714
  15.0 8.8 %collective-permute-start.1 = (f32[4,3,32,128]{3,2,1,0:T(8,128)}, f32[4,3,32,128]{3,2,1,0:T(8,128)S(1)}, u32[]{:S(2)}, u32[]{:S(2)}) collective-permute-start(f32[4,3,32,128]{3,2,1,0:T(8,128)} %get-tuple-element.43), channel_id=1, source_target_pairs={{8,0},{16,8},{24,16},{9,1},{17,9},{25,17},{10,2},{18,10},{26,18},{... | collective-permute-start | bytes 589832 | tf_op jit(solution)/shard_map/ppermute | solution.py:714
  16.3 7.5 %collective-permute-start.2 = (f32[4,96,128]{2,1,0:T(8,128)}, f32[4,96,128]{2,1,0:T(8,128)S(1)}, u32[]{:S(2)}, u32[]{:S(2)}) collective-permute-start(f32[4,96,128]{2,1,0:T(8,128)} %get-tuple-element.44), channel_id=1, source_target_pairs={{0,1},{1,2},{2,3},{3,4},{4,5},{5,6},{6,7},{8,9},{9,10},{10,11},{11... | collective-permute-start | bytes 589832 | tf_op jit(solution)/shard_map/ppermute | solution.py:714
  18.1 5.7 %collective-permute-start.3 = (f32[4,96,128]{2,1,0:T(8,128)}, f32[4,96,128]{2,1,0:T(8,128)S(1)}, u32[]{:S(2)}, u32[]{:S(2)}) collective-permute-start(f32[4,96,128]{2,1,0:T(8,128)} %get-tuple-element.45), channel_id=1, source_target_pairs={{1,0},{2,1},{3,2},{4,3},{5,4},{6,5},{7,6},{9,8},{10,9},{11,10},{12... | collective-permute-start | bytes 589832 | tf_op jit(solution)/shard_map/ppermute | solution.py:714
  26.2 17.7 %all-to-all-start.1 = ((bf16[32,16,128]{2,1,0:T(8,128)(2,1)}), bf16[32,16,128]{2,1,0:T(8,128)(2,1)S(1)}, u32[]{:S(2)}, u32[]{:S(2)}) async-start(bf16[32,16,128]{2,1,0:T(8,128)(2,1)} %bitcast.28), calls=%async_computation.1 | async-start | bytes 262144 | tf_op jit(solution)/shard_map/all_to_all | solution.py:718
  35.7 8.2 %copy-start = (s32[8,128]{1,0:T(8,128)S(1)}, s32[8,128]{1,0:T(8,128)}, u32[]{:S(2)}) copy-start(s32[8,128]{1,0:T(8,128)} %get-tuple-element.40.meta_ref) | copy-start | bytes 12292
  49.4 15.4 %all-to-all-start.2 = ((f32[32,1,2176]{2,1,0:T(1,128)}), f32[32,1,2176]{2,1,0:T(1,128)S(1)}, u32[]{:S(2)}, u32[]{:S(2)}) async-start(f32[32,1,2176]{2,1,0:T(1,128)} %bitcast.27), calls=%async_computation.2 | async-start | bytes 557056 | tf_op jit(solution)/shard_map/all_to_all | solution.py:718
  66.1 9.6 %all-to-all-start.3 = ((f32[32,1,128]{2,1,0:T(1,128)}), f32[32,1,128]{2,1,0:T(1,128)S(1)}, u32[]{:S(2)}, u32[]{:S(2)}) async-start(f32[32,1,128]{2,1,0:T(1,128)} %bitcast.29), calls=%async_computation.3 | async-start | bytes 32768 | tf_op jit(solution)/shard_map/all_to_all | solution.py:718
